TPU v7x, 128 devices: a whole 4x4x4 slice. The times are simulated.
128 devices in a mesh: row: 16 (over y, x_lo, core), col: 8 (over z, x_hi).
Axes of the slice: x: 4 (x_hi: 2, x_lo: 2; x = x_hi * 2 + x_lo), y: 4, z: 4, core: 2. Of those that a mesh axis runs over, the one named last changes fastest.
Arguments:
- value_matrix: float32 [16384, 16384], P('row', 'col'), may hold values from -1 to 3, as said below
- inputs: float32 [16384, 1024], P('row'), may hold values from -0.09375 to 0.09375
- plant_diag: float32 [128, 128], replicated, may hold values from 0.3 to 0.9
- state_cost: float32 [16384], P('row'), may hold values from 0.05 to 1
- control_weight: float32 [1], replicated, may hold values from 0.25 to 40
Outputs:
- value_next: float32 [16384, 16384], P('row', 'col')
Inputs may be any that keep to these rules, and one draw needn't show every extreme that they name: value_matrix is symmetric and positive definite.
All inputs are finite; a program needn't handle non-finite values.
Results may differ from a plain program's by a relative error of at most 0.00005.
Values sent between devices are 32-bit elements; how exact they have to be, the bound alone decides.
No kernel may reach another device: no remote copies, remote signals or barrier semaphores. Data moves between devices by JAX's collectives and lax.ppermute only.
A program may use at most 192 MiB of HBM per device.

v0:
```python
import jax
import jax.numpy as jnp
from jax import lax
from jax.sharding import PartitionSpec as P

COUPLING = 0.25
HIGHEST_PRECISION = lax.Precision.HIGHEST


def broadcast(value, axis, source):
    kept = jnp.where(lax.axis_index(axis) == source, value, 0).astype(value.dtype)
    return lax.psum(kept, axis)


def extended(cells, sides, width):
    for axis, dim in sides:
        count = lax.axis_size(axis)
        ends = count - 1
        head = lax.slice_in_dim(cells, 0, width, axis=dim)
        tail = lax.slice_in_dim(cells, cells.shape[dim] - width, cells.shape[dim], axis=dim)
        cells = jnp.concatenate(
            [
                lax.ppermute(tail, axis, [(i, (i + 1) % count) for i in range(ends)]),
                cells,
                lax.ppermute(head, axis, [((i + 1) % count, i) for i in range(ends)]),
            ],
            axis=dim,
        )
    return cells


def stencil_first(field, diagonal):
    centre = field[1:-1]
    side_padded = jnp.pad(centre, ((0, 0), (1, 1), (0, 0)))
    neighbours = field[:-2] + field[2:] + side_padded[:, :-2] + side_padded[:, 2:]
    return diagonal[:, :, None] * centre + COUPLING * neighbours


def stencil_last(field, diagonal):
    centre = field[:, 1:-1]
    side_padded = jnp.pad(centre, ((0, 0), (0, 0), (1, 1)))
    neighbours = field[:, :-2] + field[:, 2:] + side_padded[:, :, :-2] + side_padded[:, :, 2:]
    return diagonal[None] * centre + COUPLING * neighbours


def local(value_matrix, inputs, plant_diag, state_cost, control_weight):
    row_devices = lax.axis_size("row")
    col_devices = lax.axis_size("col")
    row_index = lax.axis_index("row")
    col_index = lax.axis_index("col")
    grid_side = plant_diag.shape[0]
    rows_block, cols_block = value_matrix.shape
    actuators = inputs.shape[1]
    lines_rows = rows_block // grid_side
    lines_cols = cols_block // grid_side
    per_column = row_devices // col_devices
    diag_rows = lax.dynamic_slice_in_dim(plant_diag, row_index * lines_rows, lines_rows, 0)
    diag_cols = lax.dynamic_slice_in_dim(plant_diag, col_index * lines_cols, lines_cols, 0)
    contract_first = (((0,), (0,)), ((), ()))
    pieces = []
    for member in range(per_column):
        pieces.append(broadcast(inputs, "row", col_index * per_column + member))
    panel_rows = jnp.concatenate(pieces, 0)
    local_term = jnp.dot(value_matrix, panel_rows, precision=HIGHEST_PRECISION)
    pb_rows = lax.psum(local_term, "col")
    share_rows = rows_block // col_devices
    mine_inputs = lax.dynamic_slice_in_dim(inputs, col_index * share_rows, share_rows, 0)
    mine_pb = lax.dynamic_slice_in_dim(pb_rows, col_index * share_rows, share_rows, 0)
    gram_term = lax.dot_general(mine_inputs, mine_pb, contract_first, precision=HIGHEST_PRECISION)
    gram_matrix = lax.psum(gram_term, ("row", "col"))
    padded_pb = extended(pb_rows, (("row", 0),), grid_side)
    gain_rows = stencil_first(padded_pb.reshape(lines_rows + 2, grid_side, actuators), diag_rows)
    gain_trans = gain_rows.reshape(rows_block, actuators).T
    gram_matrix = gram_matrix + control_weight[0] * jnp.eye(actuators, dtype=jnp.float32)
    factor = jnp.linalg.cholesky(gram_matrix)
    scaled_gain = jax.scipy.linalg.solve_triangular(factor, gain_trans, lower=True)
    columns = []
    for member in range(per_column):
        columns.append(broadcast(scaled_gain, "row", col_index * per_column + member))
    scaled_cols = jnp.concatenate(columns, 1)
    downdate = lax.dot_general(
        scaled_gain, scaled_cols, contract_first, precision=HIGHEST_PRECISION
    )
    padded_value = extended(value_matrix, (("col", 1),), grid_side)
    product = stencil_last(padded_value.reshape(rows_block, lines_cols + 2, grid_side), diag_cols)
    padded_product = extended(product.reshape(rows_block, cols_block), (("row", 0),), grid_side)
    propagated = stencil_first(
        padded_product.reshape(lines_rows + 2, grid_side, cols_block), diag_rows
    )
    propagated = propagated.reshape(rows_block, cols_block)
    row_states = row_index * rows_block + jnp.arange(rows_block, dtype=jnp.int32)
    col_states = col_index * cols_block + jnp.arange(cols_block, dtype=jnp.int32)
    diagonal_mask = row_states[:, None] == col_states[None, :]
    cost_term = jnp.where(diagonal_mask, state_cost[:, None], jnp.float32(0.0))
    return propagated + cost_term - downdate


def solution(mesh):
    in_specs = (P("row", "col"), P("row", None), P(), P("row"), P())
    out_specs = P("row", "col")
    return jax.shard_map(local, mesh=mesh, in_specs=in_specs, out_specs=out_specs, check_vma=False)
```

profile of v0, /device:TPU:1, one launch (start us, length us, event | category | flops | bytes accessed | tf_op | source)
XLA Modules:
  0.0 1242.9 jit_solution(13887878850725653745)
XLA Ops:
  6.5 5.4 copy.40
  11.9 7.1 broadcast_select_fusion.3
  19.0 197.3 %all-reduce.17.cloned.1.call-done = (f32[1024,1024]{0,1:T(8,128)}, f32[1024,1024]{0,1:T(8,128)}) async-done(((f32[1024,1024]{0,1:T(8,128)}, f32[1024,1024]{0,1:T(8,128)}), (f32[1024,1024]{0,1:T(8,128)}, f32[1024,1024]{0,1:T(8,128)})) %all-reduce.17.cloned.1.call-update) | async-done | bytes 8388624 | tf_op jit(solution)/shard_map/psum | solution.py:12
  216.3 32.0 %fusion.27 = f32[1024,1024]{0,1:T(8,128)} fusion(f32[1024,2048]{1,0:T(8,128)} %param.5, f32[1024,1024]{0,1:T(8,128)} %get-tuple-element.31, f32[1024,1024]{0,1:T(8,128)} %get-tuple-element.32), kind=kOutput, calls=%fused_computation.46 | convolution fusion | flops 25771900928 | bytes 20971520 | tf_op jit(solution)/shard_map/dot_general | solution.py:64
  248.4 185.3 %all-reduce.11.cloned.1.call-done = f32[1024,1024]{0,1:T(8,128)} async-done(((f32[1024,1024]{0,1:T(8,128)}), f32[1024,1024]{0,1:T(8,128)}) %all-reduce.11.cloned.1.call-update) | async-done | bytes 4194320 | tf_op jit(solution)/shard_map/psum | solution.py:65
  433.7 6.6 fusion.60
  451.7 10.5 collective-permute-done.5
  469.1 126.2 %all-reduce.13.cloned.1.call-done = f32[1024,1024]{0,1:T(8,128)} async-done(((f32[1024,1024]{0,1:T(8,128)}), f32[1024,1024]{0,1:T(8,128)}) %all-reduce.13.cloned.1.call-update) | async-done | bytes 4194320 | tf_op jit(solution)/shard_map/psum | solution.py:70
  595.3 4.8 select_add_fusion
  600.1 5.5 copy.43
  605.6 4.5 fusion.24
  612.0 11.7 cholesky.222
  623.8 9.8 custom-call.63
  636.7 11.7 cholesky.243
  649.3 9.8 custom-call.64
  664.6 11.7 cholesky.466
  677.1 9.8 custom-call.65
  691.4 11.7 cholesky.485
  703.9 9.8 custom-call.66
  718.1 12.1 cholesky.504
  731.0 9.8 custom-call.67
  745.0 11.7 cholesky.524
  757.5 9.8 custom-call.68
  771.1 11.7 cholesky.544
  783.6 9.8 custom-call.69
  796.5 11.7 cholesky.562
  818.5 4.8 select_select_fusion
  823.3 24.7 %while.1 = (s32[]{:T(128)}, f32[1024,1024]{0,1:T(8,128)}, s32[8,2]{0,1:T(2,128)S(1)}, f32[8,128,128]{2,1,0:T(8,128)S(1)}, s32[]{:T(128)}) while((s32[]{:T(128)}, f32[1024,1024]{0,1:T(8,128)}, s32[8,2]{0,1:T(2,128)S(1)}, f32[8,128,128]{2,1,0:T(8,128)S(1)}, s32[]{:T(128)}) %tuple.52), condition=%wide.while_cond, body=%wide.while_body.sunk | while | flops 2 | bytes 393321 | solution.py:76
  848.1 79.0 %custom-call.70 = f32[8,128,128]{1,2,0:T(8,128)S(1)} custom-call(f32[8,128,128]{2,1,0:T(8,128)S(1)} %get-tuple-element.12), custom_call_target="InvertDiagBlocksLowerTriangular" | custom-call | tf_op jit(solution)/shard_map/jit(_solve_triangular)/triangular_solve | solution.py:76
  948.8 3.7 convolution_subtract_fusion.2
  955.2 4.0 convolution_subtract_fusion.1
  961.5 4.7 convolution_subtract_fusion.3
  974.6 4.5 broadcast_select_fusion
  979.1 9.3 copy.34
  994.5 20.6 %collective-permute-done = f32[1024,128]{0,1:T(8,128)S(1)} collective-permute-done((f32[1024,128]{0,1:T(8,128)S(1)}, f32[1024,128]{0,1:T(8,128)S(1)}, u32[]{:S(2)}, u32[]{:S(2)}) %collective-permute-start) | collective-permute-done | bytes 524320 | tf_op jit(solution)/shard_map/ppermute | solution.py:23
  1015.1 24.7 %collective-permute-done.1 = f32[1024,128]{0,1:T(8,128)S(1)} collective-permute-done((f32[1024,128]{0,1:T(8,128)S(1)}, f32[1024,128]{0,1:T(8,128)S(1)}, u32[]{:S(2)}, u32[]{:S(2)}) %collective-permute-start.1) | collective-permute-done | bytes 524320 | tf_op jit(solution)/shard_map/ppermute | solution.py:25
  1039.8 9.1 pad_maximum_fusion
  1048.9 8.5 slice.361
  1057.4 20.1 %fusion.3 = f32[1024,16,128]{0,2,1:T(8,128)} fusion(f32[1024,16,128]{0,2,1:T(8,128)} %slice.361, f32[1024,18,128]{0,2,1:T(8,128)} %bitcast.140, f32[16,128]{1,0:T(8,128)S(1)} %constant_dynamic-slice_fusion.1), kind=kLoop, calls=%fused_computation.12 | loop fusion | flops 12582912 | bytes 33562624 | tf_op jit(solution)/shard_map/add | solution.py:43
  1080.3 4.4 collective-permute-start.2
  1086.7 8.9 copy.77
  1095.6 9.6 copy.37
  1105.1 4.3 collective-permute-done.3
  1109.4 8.6 fusion.8
  1118.0 9.2 copy.38
  1127.2 17.6 %fusion.7 = f32[8,128,2048]{2,1,0:T(8,128)} fusion(f32[8,128,2048]{2,1,0:T(8,128)} %bitcast.143, f32[8,128,2048]{2,1,0:T(8,128)} %copy.37, f32[8,128]{1,0:T(8,128)S(1)} %constant_dynamic-slice_fusion.2), kind=kLoop, calls=%fused_computation.16 | loop fusion | flops 10485760 | bytes 25169920 | tf_op jit(solution)/shard_map/add | solution.py:36
  1144.8 58.5 %all-reduce.15.cloned.1.call-done = (f32[1024,1024]{0,1:T(8,128)}, f32[1024,1024]{0,1:T(8,128)}) async-done(((f32[1024,1024]{0,1:T(8,128)}, f32[1024,1024]{0,1:T(8,128)}), (f32[1024,1024]{0,1:T(8,128)}, f32[1024,1024]{0,1:T(8,128)})) %all-reduce.15.cloned.1.call-update) | async-done | bytes 8388624 | tf_op jit(solution)/shard_map/psum | solution.py:12
  1203.3 32.8 %fusion.17 = f32[1024,2048]{1,0:T(8,128)} fusion(f32[8,128,2048]{2,1,0:T(8,128)} %fusion.7, f32[1024]{0:T(1024)S(1)} %copy-done.10, s32[2048]{0:T(1024)S(1)} %iota_add_fusion, s32[1024]{0:T(1024)S(1)} %iota_add_fusion.1, f32[1024,1024]{0,1:T(8,128)} %copy-done.5, f32[1024,1024]{0,1:T(8,128)} %get-tuple-element.29, f32[1024,1024]{0,1:T(8,128)} %get-tuple-element.30), kind=kOutput, calls=%fused_computation.30 | convolution fusion | flops 25780289536 | bytes 29376512 | tf_op jit(solution)/shard_map/dot_general | solution.py:81
  (172 shorter events, 128.4 us)
Async XLA Ops:
  6.5 440.9 %copy-start = (f32[128,128]{1,0:T(8,128)S(1)}, f32[128,128]{1,0:T(8,128)}, u32[]{:S(2)}) copy-start(f32[128,128]{1,0:T(8,128)} %param.7) | copy-start | bytes 196612
  6.5 209.8 %all-reduce.17.cloned.1.call-start = ((), (), s32[]{:S(2)}) async-start(), calls=%async_computation.3 | async-start | bytes 16777216 | tf_op jit(solution)/shard_map/psum | solution.py:12
  19.0 414.7 %all-reduce.11.cloned.1.call-start = ((), (), s32[]{:S(2)}) async-start(), calls=%async_computation | async-start | bytes 8388608 | tf_op jit(solution)/shard_map/psum | solution.py:65
  248.3 346.9 %all-reduce.13.cloned.1.call-start = ((), (), s32[]{:S(2)}) async-start(), calls=%async_computation.1 | async-start | bytes 8388608 | tf_op jit(solution)/shard_map/psum | solution.py:70
  440.3 762.9 %all-reduce.15.cloned.1.call-start = ((), (), s32[]{:S(2)}) async-start(), calls=%async_computation.2 | async-start | bytes 16777216 | tf_op jit(solution)/shard_map/psum | solution.py:12
  441.7 10.1 collective-permute-start.4
  444.8 17.4 %collective-permute-start.5 = (f32[128,1024]{0,1:T(8,128)S(1)}, f32[128,1024]{0,1:T(8,128)S(1)}, u32[]{:S(2)}, u32[]{:S(2)}) collective-permute-start(f32[128,1024]{0,1:T(8,128)S(1)} %get-tuple-element.42), channel_id=1, source_target_pairs={{8,0},{16,8},{24,16},{32,24},{40,32},{48,40},{56,48},{64,56},{72,6... | collective-permute-start | bytes 1572872 | tf_op jit(solution)/shard_map/ppermute | solution.py:25
  447.5 14.8 %copy-start.3 = (f32[1024,1024]{0,1:T(8,128)S(1)}, f32[1024,1024]{0,1:T(8,128)}, u32[]{:S(2)}) copy-start(f32[1024,1024]{0,1:T(8,128)} %all-reduce.11.cloned.1.call-done) | copy-start | bytes 12582916
  610.1 1.9 copy-start.4
  660.2 2.0 copy-start.2
  927.1 12.7 %copy-start.9 = (f32[8,128,128]{1,2,0:T(8,128)}, f32[8,128,128]{1,2,0:T(8,128)S(1)}, u32[]{:S(2)}) copy-start(f32[8,128,128]{1,2,0:T(8,128)S(1)} %custom-call.70) | copy-start | bytes 1572868
  967.2 5.4 copy-start.6
  971.4 1.0 copy-start.8
  971.4 1.2 copy-start.7
  974.6 4.5 copy-start.5
  989.7 25.5 %collective-permute-start = (f32[1024,128]{0,1:T(8,128)S(1)}, f32[1024,128]{0,1:T(8,128)S(1)}, u32[]{:S(2)}, u32[]{:S(2)}) collective-permute-start(f32[1024,128]{0,1:T(8,128)S(1)} %get-tuple-element.37), channel_id=1, source_target_pairs={{0,1},{1,2},{2,3},{3,4},{4,5},{5,6},{6,7},{8,9},{9,10},{10,11},{11... | collective-permute-start | bytes 1572872 | tf_op jit(solution)/shard_map/ppermute | solution.py:23
  993.2 46.6 %collective-permute-start.1 = (f32[1024,128]{0,1:T(8,128)S(1)}, f32[1024,128]{0,1:T(8,128)S(1)}, u32[]{:S(2)}, u32[]{:S(2)}) collective-permute-start(f32[1024,128]{0,1:T(8,128)S(1)} %get-tuple-element.38), channel_id=1, source_target_pairs={{1,0},{2,1},{3,2},{4,3},{5,4},{6,5},{7,6},{9,8},{10,9},{11,10},{12... | collective-permute-start | bytes 1572872 | tf_op jit(solution)/shard_map/ppermute | solution.py:25
  1080.3 24.8 %collective-permute-start.2 = (f32[128,2048]{0,1:T(8,128)}, f32[128,2048]{0,1:T(8,128)S(1)}, u32[]{:S(2)}, u32[]{:S(2)}) collective-permute-start(f32[128,2048]{0,1:T(8,128)} %bitcast.1), channel_id=1, source_target_pairs={{0,8},{8,16},{16,24},{24,32},{32,40},{40,48},{48,56},{56,64},{64,7... | collective-permute-start | bytes 3145736 | tf_op jit(solution)/shard_map/ppermute | solution.py:23
  1084.7 24.7 %collective-permute-start.3 = (f32[128,2048]{0,1:T(8,128)S(1)}, f32[128,2048]{0,1:T(8,128)S(1)}, u32[]{:S(2)}, u32[]{:S(2)}) collective-permute-start(f32[128,2048]{0,1:T(8,128)S(1)} %bitcast.156), channel_id=1, source_target_pairs={{8,0},{16,8},{24,16},{32,24},{40,32},{48,40},{56,48},{64,56},{72,6... | collective-permute-start | bytes 3145736 | tf_op jit(solution)/shard_map/ppermute | solution.py:25
  1127.2 76.1 %copy-start.10 = (f32[1024]{0:T(1024)S(1)}, f32[1024]{0:T(1024)}, u32[]{:S(2)}) copy-start(f32[1024]{0:T(1024)} %param.8) | copy-start | bytes 12292
  1203.3 32.8 %copy-start.1 = (f32[128,128]{1,0:T(8,128)S(1)}, f32[128,128]{1,0:T(8,128)}, u32[]{:S(2)}) copy-start(f32[128,128]{1,0:T(8,128)} %param.7) | copy-start | bytes 196612
Sparse Core Ops, SparseCore 0:
  19.1 197.1 all-reduce.16
  248.5 185.2 all-reduce.10
  440.5 154.7 all-reduce.12
  979.2 223.9 all-reduce.14
where the time goes:
time: 1250 us; the launch traced here: 1240 us
  waiting for transfers between devices  628 us (50%)
  other arithmetic  331 us (26%)
  matrix products  137 us (11%)
  local copies, waits for them, and re-layouts  111 us (9%)
  between operations  19.5 us (2%)
  starting transfers between devices  16.3 us (1%)
    psum x2, waiting for transfers between devices, broadcast(): return lax.psum(kept, axis)  256 us
    psum x1, waiting for transfers between devices, local(): pb_rows = lax.psum(local_term, 'col')  185 us
    another operation x30, other arithmetic, local(): factor = jnp.linalg.cholesky(gram_matrix)  168 us
    psum x1, waiting for transfers between devices, local(): gram_matrix = lax.psum(gram_term, ('row', 'col'))  126 us
    another operation x3, other arithmetic, local(): jax.scipy.linalg.solve_triangular(factor, gain_trans, lower=True)  83.8 us
    another operation x15, matrix products, local(): jax.scipy.linalg.solve_triangular(factor, gain_trans, lower=True)  40.1 us
    ppermute x3, waiting for transfers between devices, extended(): lax.ppermute(head, axis, [((i + 1) % count, i) for i in range(ends)])  39.5 us
    unnamed x35, local copies, waits for them, and re-layouts  36.2 us
  transfers between devices with their start and end apart: 10, of which 9 were waited for; matrix products, arithmetic and copies ran while one was open for 9% of the time, Pallas kernels for 0%

commit v1 on v0

v1 whole, which is shorter than its diff:
```python
import functools

import jax
import jax.numpy as jnp
from jax import lax
from jax.experimental import pallas as pl
from jax.experimental.pallas import tpu as pltpu
from jax.sharding import PartitionSpec as P

COUPLING = 0.25
HIGHEST_PRECISION = lax.Precision.HIGHEST
F32 = jnp.float32
BF16 = jnp.bfloat16
NN = (((1,), (0,)), ((), ()))
NT = (((1,), (1,)), ((), ()))
TN = (((0,), (0,)), ((), ()))
LINE = 128
PANEL = 256
VMEM_LIMIT = 56 << 20


def split(x):
    high = x.astype(BF16)
    return high, (x - high.astype(F32)).astype(BF16)


def dot1(a, b, dims):
    return lax.dot_general(a, b, dims, preferred_element_type=F32)


def dot3(a, b, dims):
    (a_high, a_low), (b_high, b_low) = a, b
    return dot1(a_high, b_high, dims) + dot1(a_high, b_low, dims) + dot1(a_low, b_high, dims)


def line_of(device):
    return (device & 1) * 8 + (device >> 1)


def product_kernel(me_ref, first, second, inputs, out, high, low):
    @pl.when(pl.program_id(0) == 0)
    def _():
        high[...], low[...] = split(inputs[...])

    lines = split(jnp.concatenate([first[...], second[...]], 1))
    out[...] = dot3(lines, (high[...], low[...]), TN).reshape(out.shape)


def product_lines(me, value_matrix, inputs, odd):
    rows, acts = inputs.shape
    return pl.pallas_call(
        product_kernel,
        grid_spec=pltpu.PrefetchScalarGridSpec(
            num_scalar_prefetch=1,
            grid=(4,),
            in_specs=[
                pl.BlockSpec((rows, LINE), lambda i, m: (0, line_of(m[0] ^ (4 * i + odd)))),
                pl.BlockSpec((rows, LINE), lambda i, m: (0, line_of(m[0] ^ (4 * i + 2 + odd)))),
                pl.BlockSpec((rows, acts), lambda i, m: (0, 0)),
            ],
            out_specs=pl.BlockSpec((2, LINE, acts), lambda i, m: (i, 0, 0)),
            scratch_shapes=[pltpu.VMEM((rows, acts), BF16)] * 2,
        ),
        out_shape=jax.ShapeDtypeStruct((8, LINE, acts), F32),
        compiler_params=pltpu.CompilerParams(vmem_limit_bytes=VMEM_LIMIT),
        cost_estimate=pl.CostEstimate(flops=6 * 1024 * rows * acts, bytes_accessed=12 << 20, transcendentals=0),
    )(me, value_matrix, value_matrix, inputs)


def swap(x, mask, axis="row"):
    count = 16 if axis == "row" else 8
    return lax.ppermute(x, axis, [(i, i ^ mask) for i in range(count)])


def reduce_y(near, far, blocks):
    kept = [blocks[0], blocks[far]]
    got = swap(jnp.stack([blocks[near], blocks[near ^ far]]), near * 4)
    kept = [kept[0] + got[0], kept[1] + got[1]]
    return kept[0] + swap(kept[1], far * 4)


def scatter_lines(even, odd):
    got = swap(odd, 1)
    quarter = LINE // 4
    cut = lambda i, q: even[i, q * quarter : (q + 1) * quarter] + got[i, q * quarter : (q + 1) * quarter]
    half = lambda i, q: jnp.concatenate([cut(i, q), cut(i, q + 1)], 0)
    came = swap(jnp.stack([half(2 * m + 1, 0) for m in range(4)]), 2)
    own = [half(2 * m, 0) + came[m] for m in range(4)]
    a = reduce_y(1, 3, [o[:quarter] for o in own])
    b = reduce_y(3, 1, [o[quarter:] for o in own])
    pair = lambda m, q: jnp.stack([cut(2 * m, q), cut(2 * m + 1, q)])
    c = reduce_y(1, 3, [pair(m, 2) for m in range(4)])
    d = reduce_y(3, 1, [pair(m, 3) for m in range(4)])
    rest = jnp.concatenate([c[0], d[0]], 0) + swap(jnp.concatenate([c[1], d[1]], 0), 2)
    return jnp.concatenate([a, b, rest], 0)


def halves(x, bit):
    count = x.shape[0] // 2
    low, high = x[:count], x[count:]
    return jnp.where(bit, high, low), jnp.where(bit, low, high)


def joined(mine, got, bit):
    return jnp.concatenate([jnp.where(bit, got, mine), jnp.where(bit, mine, got)], 0)


def sum_all(x, row_index, col_index):
    bit = lambda k: (row_index >> k) & 1 == 1
    keep, send = halves(x, bit(0))
    x = keep + swap(send, 1)
    y = row_index >> 2
    count = x.shape[0] // 4
    own = lambda m: lax.dynamic_slice_in_dim(x, (y ^ m) * count, count, 0)
    x = own(0) + swap(own(1), 4) + swap(own(3), 12) + swap(own(2), 8)
    keep, send = halves(x, bit(1))
    x = keep + swap(send, 2)
    x = x + swap(x, 2, "col") + swap(x, 6, "col") + swap(x, 4, "col")
    x = x + swap(x, 1, "col")
    x = joined(x, swap(x, 2), bit(1))
    parts = [x, swap(x, 4), swap(x, 8), swap(x, 12)]
    parts = jnp.stack(parts)
    x = jnp.concatenate([lax.dynamic_index_in_dim(parts, y ^ m, 0, False) for m in range(4)], 0)
    return joined(x, swap(x, 1), bit(0))


def gram_kernel(inputs, product, out):
    a = inputs[...]
    b = product[...]
    at = 0
    for k in range(4):
        for i in range(k, 4):
            left = a[:, i * PANEL : (i + 1) * PANEL]
            right = b[:, k * PANEL : (k + 1) * PANEL]
            out[at] = lax.dot_general(left, right, TN, precision=HIGHEST_PRECISION, preferred_element_type=F32)
            at += 1


def gram_blocks(inputs, product):
    return pl.pallas_call(
        gram_kernel,
        out_shape=jax.ShapeDtypeStruct((10, PANEL, PANEL), F32),
        compiler_params=pltpu.CompilerParams(vmem_limit_bytes=VMEM_LIMIT),
    )(inputs, product)


def block_index(i, k):
    return k * 4 - (k * (k - 1)) // 2 + i - k


def series_inverse(a, eye, mask):
    picked = jnp.where(mask, a, 0.0)
    across = lax.rsqrt(jnp.sum(picked, axis=0, keepdims=True))
    down = lax.rsqrt(jnp.sum(picked, axis=1, keepdims=True))
    error = jnp.where(mask, 0.0, -(a * across * down))
    result = eye + error
    for _ in range(3):
        parts = split(error)
        error = dot3(parts, parts, NN)
        result = result + dot3(split(result), split(error), NN)
    short = error.astype(BF16)
    error = dot1(short, short, NN)
    result = result + dot1(result.astype(BF16), error.astype(BF16), NN)
    return result * across * down, jnp.sum(error * error, keepdims=True)


def pivot_inverse(a, work):
    size = a.shape[0]
    work[...] = a
    lanes = lax.broadcasted_iota(jnp.int32, (1, size), 1)
    rows = lax.broadcasted_iota(jnp.int32, (size, 1), 0)

    def step(p, carry):
        now = work[...]
        across = work[pl.ds(p, 1), :]
        down = jnp.sum(jnp.where(lanes == p, now, 0.0), axis=1, keepdims=True)
        inverse = 1.0 / jnp.sum(jnp.where(lanes == p, across, 0.0), axis=1, keepdims=True)
        new = now - down * (across * inverse)
        new = jnp.where(lanes == p, down * inverse, new)
        new = jnp.where(rows == p, across * inverse, new)
        work[...] = jnp.where((rows == p) & (lanes == p), -inverse, new)
        return carry

    lax.fori_loop(0, size, step, 0)
    return -work[...]


def solve_kernel(weight, gram, sides, out, factor, inverses, work, worst):
    size = PANEL
    mask = lax.broadcasted_iota(jnp.int32, (size, size), 0) == lax.broadcasted_iota(jnp.int32, (size, size), 1)
    eye = jnp.where(mask, 1.0, 0.0).astype(F32)
    at = lambda k: slice(k * size, (k + 1) * size)

    def run(robust):
        for k in range(4):
            for i in range(k, 4):
                here = gram[block_index(i, k)]
                factor[block_index(i, k)] = here + weight[0] * eye if i == k else here
        out[...] = sides[...]
        for k in range(4):
            here = factor[block_index(k, k)]
            if robust:
                inverse = pivot_inverse(here, work)
            else:
                inverse, off = series_inverse(here, eye, mask)
                worst[...] = off if k == 0 else jnp.where(off < worst[...], worst[...], off)
            inverses[k] = inverse
            parts = split(inverse)
            solved = split(out[:, at(k)])
            columns = [split(factor[block_index(i, k)]) for i in range(k + 1, 4)]
            lefts = []
            for i in range(k + 1, 4):
                left = dot3(columns[i - k - 1], parts, NN)
                factor[block_index(i, k)] = left
                lefts.append(split(left))
            for j in range(k + 1, 4):
                for i in range(j, 4):
                    factor[block_index(i, j)] -= dot3(lefts[i - k - 1], columns[j - k - 1], NT)
            for i in range(k + 1, 4):
                out[:, at(i)] -= dot3(solved, lefts[i - k - 1], NT)
        for k in range(3, -1, -1):
            total = dot3(split(out[:, at(k)]), split(inverses[k]), NN)
            for i in range(k + 1, 4):
                total = total - dot3(split(out[:, at(i)]), split(factor[block_index(i, k)]), NN)
            out[:, at(k)] = total

    run(False)

    @pl.when(jnp.logical_not(worst[0, 0] < 1e-6))
    def _():
        run(True)


def solve(weight, gram, sides):
    return pl.pallas_call(
        solve_kernel,
        out_shape=jax.ShapeDtypeStruct(sides.shape, F32),
        in_specs=[
            pl.BlockSpec(memory_space=pltpu.SMEM),
            pl.BlockSpec(memory_space=pltpu.VMEM),
            pl.BlockSpec(memory_space=pltpu.VMEM),
        ],
        out_specs=pl.BlockSpec(memory_space=pltpu.VMEM),
        scratch_shapes=[
            pltpu.VMEM((10, PANEL, PANEL), F32),
            pltpu.VMEM((4, PANEL, PANEL), F32),
            pltpu.VMEM((PANEL, PANEL), F32),
            pltpu.VMEM((1, 1), F32),
        ],
        compiler_params=pltpu.CompilerParams(vmem_limit_bytes=VMEM_LIMIT),
    )(weight, gram, sides)


def extended(cells, sides, width):
    for axis, dim in sides:
        count = lax.axis_size(axis)
        ends = count - 1
        head = lax.slice_in_dim(cells, 0, width, axis=dim)
        tail = lax.slice_in_dim(cells, cells.shape[dim] - width, cells.shape[dim], axis=dim)
        cells = jnp.concatenate(
            [
                lax.ppermute(tail, axis, [(i, (i + 1) % count) for i in range(ends)]),
                cells,
                lax.ppermute(head, axis, [((i + 1) % count, i) for i in range(ends)]),
            ],
            axis=dim,
        )
    return cells


def stencil_first(field, diagonal):
    centre = field[1:-1]
    side_padded = jnp.pad(centre, ((0, 0), (1, 1), (0, 0)))
    neighbours = field[:-2] + field[2:] + side_padded[:, :-2] + side_padded[:, 2:]
    return diagonal[:, :, None] * centre + COUPLING * neighbours


def stencil_last(field, diagonal):
    centre = field[:, 1:-1]
    side_padded = jnp.pad(centre, ((0, 0), (0, 0), (1, 1)))
    neighbours = field[:, :-2] + field[:, 2:] + side_padded[:, :, :-2] + side_padded[:, :, 2:]
    return diagonal[None] * centre + COUPLING * neighbours


def device_of(line):
    chip_row, core, col = line % 8, (line // 8) % 2, line // 16
    return (chip_row * 2 + core) * 8 + col


def local(value_matrix, inputs, plant_diag, state_cost, control_weight):
    row_index = lax.axis_index("row")
    col_index = lax.axis_index("col")
    both = ("row", "col")
    grid_side = plant_diag.shape[0]
    rows_block, cols_block = value_matrix.shape
    actuators = inputs.shape[1]
    lines_rows = rows_block // grid_side
    lines_cols = cols_block // grid_side
    diag_rows = lax.dynamic_slice_in_dim(plant_diag, row_index * lines_rows, lines_rows, 0)
    diag_cols = lax.dynamic_slice_in_dim(plant_diag, col_index * lines_cols, lines_cols, 0)
    me = row_index.astype(jnp.int32).reshape(1)
    trade = [((a * 2 + core) * 8 + b, (b * 2 + core) * 8 + a) for a in range(8) for b in range(8) for core in range(2)]
    mine_inputs = lax.dynamic_slice_in_dim(inputs, col_index * LINE, LINE, 0)
    mine_inputs = lax.ppermute(mine_inputs, both, trade)
    odd = product_lines(me, value_matrix, inputs, 1)
    even = product_lines(me, value_matrix, inputs, 0)
    product = scatter_lines(even, odd)

    gram = gram_blocks(mine_inputs, product)
    gram = sum_all(gram.reshape(10 * PANEL, PANEL), row_index, col_index).reshape(10, PANEL, PANEL)

    lines = STATES_LINES = 128
    above = lax.ppermute(product, both, [(device_of(i), device_of(i + 1)) for i in range(lines - 1)])
    below = lax.ppermute(product, both, [(device_of(i + 1), device_of(i)) for i in range(lines - 1)])
    line = col_index * 16 + line_of(row_index)
    diagonal = lax.dynamic_slice_in_dim(plant_diag, line, 1, 0)
    gain = stencil_first(jnp.stack([above, product, below]), diagonal)[0]
    gain_cols = lax.all_gather(gain, "row", axis=0)
    gain_cols = gain_cols.reshape(8, 2, LINE, actuators).swapaxes(0, 1).reshape(cols_block, actuators)
    gain_rows = lax.all_gather(lax.ppermute(gain, both, trade), "col", axis=0, tiled=True)

    padded_value = extended(value_matrix, (("col", 1),), grid_side)
    plant_cols = stencil_last(padded_value.reshape(rows_block, lines_cols + 2, grid_side), diag_cols)
    padded_product = extended(plant_cols.reshape(rows_block, cols_block), (("row", 0),), grid_side)
    propagated = stencil_first(padded_product.reshape(lines_rows + 2, grid_side, cols_block), diag_rows)
    propagated = propagated.reshape(rows_block, cols_block)
    row_states = row_index * rows_block + jnp.arange(rows_block, dtype=jnp.int32)
    col_states = col_index * cols_block + jnp.arange(cols_block, dtype=jnp.int32)
    diagonal_mask = row_states[:, None] == col_states[None, :]
    propagated = propagated + jnp.where(diagonal_mask, state_cost[:, None], jnp.float32(0.0))

    solved = solve(control_weight, gram, gain_rows)
    downdate = lax.dot_general(solved, gain_cols, NT, precision=lax.Precision.HIGH)
    return propagated - downdate


def solution(mesh):
    in_specs = (P("row", "col"), P("row", None), P(), P("row"), P())
    out_specs = P("row", "col")
    return jax.shard_map(local, mesh=mesh, in_specs=in_specs, out_specs=out_specs, check_vma=False)
```

time: 1250 us -> 593 us (0.47)
  waiting for transfers between devices: 628 us -> 72.1 us
  other arithmetic: 331 us -> 68.9 us
  Pallas kernels: 0 us -> 221 us
  matrix products: 137 us -> 19 us
  starting transfers between devices: 16.3 us -> 130 us
  local copies, waits for them, and re-layouts: 111 us -> 58.8 us
    psum x4 -> x0, waiting for transfers between devices: 567 us -> none  [the longest x2 256 us: broadcast(): return lax.psum(kept, axis)]
    another operation x33 -> x12, other arithmetic: 251 us -> 0.62 us  [the longest x6 0.19 us: reduce_y(): got = swap(jnp.stack([blocks[near], blocks[near ^ far]]), near * 4)]
    pallas_call x0 -> x4, Pallas kernels: none -> 221 us  [the longest x1 192 us: solve(): pl.pallas_call(solve_kernel, out_shape=jax.ShapeDtypeStruct(sides.shape,...]
    ppermute x0 -> x29, starting transfers between devices: none -> 113 us  [the longest x25 100 us: swap(): return lax.ppermute(x, axis, [(i, i ^ mask) for i in range(count)])]
    ppermute x0 -> x29, waiting for transfers between devices: none -> 71.3 us  [the longest x25 59.8 us: swap(): return lax.ppermute(x, axis, [(i, i ^ mask) for i in range(count)])]
    another operation x29 -> x0, matrix products: 66 us -> none  [the longest x15 40.1 us: local(): jax.scipy.linalg.solve_triangular(factor, gain_trans, lower=True)]
    dot_general x3 -> x1, matrix products: 71.4 us -> 19 us  [local(): lax.dot_general(solved, gain_cols, NT, precision=lax.Precision.HIGH)]
    ppermute x3 -> x2, waiting for transfers between devices: 39.5 us -> 0.01 us  [extended(): lax.ppermute(head, axis, [((i + 1) % count, i) for i in range(ends)])]
  transfers between devices with their start and end apart: 10 -> 35, of which waited for: 9 -> 14; matrix products, arithmetic and copies ran while one was open for 9% -> 20% of each run, Pallas kernels for 0% -> 36%
where the time goes in v1:
time: 593 us; the launch traced here: 585 us
  Pallas kernels  221 us (37%)
  starting transfers between devices  130 us (22%)
  waiting for transfers between devices  72.1 us (12%)
  other arithmetic  68.9 us (12%)
  local copies, waits for them, and re-layouts  58.8 us (10%)
  matrix products  19 us (3%)
  between operations  15 us (3%)
    pallas_call x1, Pallas kernels, solve(): pl.pallas_call(solve_kernel, out_shape=jax.ShapeDtypeStruct(sides.shape,...  192 us
    ppermute x25, starting transfers between devices, swap(): return lax.ppermute(x, axis, [(i, i ^ mask) for i in range(count)])  100 us
    ppermute x25, waiting for transfers between devices, swap(): return lax.ppermute(x, axis, [(i, i ^ mask) for i in range(count)])  59.8 us
    pallas_call x2, Pallas kernels, product_lines(): pl.pallas_call(product_kernel, grid_spec=pltpu.PrefetchScalarGridSpec(num...  23.3 us
    add x1, other arithmetic, stencil_last(): return diagonal[None] * centre + COUPLING * neighbours  20.3 us
    unnamed x20, local copies, waits for them, and re-layouts  20.1 us
    dot_general x1, matrix products, local(): lax.dot_general(solved, gain_cols, NT, precision=lax.Precision.HIGH)  19 us
    add x2, other arithmetic, stencil_first(): return diagonal[:, :, None] * centre + COUPLING * neighbours  18.2 us
  transfers between devices with their start and end apart: 35, of which 14 were waited for; matrix products, arithmetic and copies ran while one was open for 20% of the time, Pallas kernels for 36%

profile of v1, /device:TPU:1, one launch (start us, length us, event | category | flops | bytes accessed | tf_op | source)
XLA Modules:
  0.0 584.7 jit_solution(6228512397886962160)
XLA Ops:
  6.5 11.7 %shard_map.56 = f32[8,128,1024]{2,1,0:T(8,128)} custom-call(s32[1]{0:T(128)} %bitcast.6.me_ref, f32[1024,2048]{1,0:T(8,128)} %second.3, f32[1024,2048]{1,0:T(8,128)} %second.3, f32[1024,1024]{1,0:T(8,128)} %inputs.3), custom_call_target="tpu_custom_call" | custom-call | flops 6442450944 | bytes 12582912 | tf_op jit(solution)/shard_map/pallas_call | solution.py:51
  18.2 1.4 collective-permute-start.5
  19.6 11.6 %shard_map.55 = f32[8,128,1024]{2,1,0:T(8,128)} custom-call(s32[1]{0:T(128)} %bitcast.6.me_ref, f32[1024,2048]{1,0:T(8,128)} %second.3, f32[1024,2048]{1,0:T(8,128)} %second.3, f32[1024,1024]{1,0:T(8,128)} %inputs.3), custom_call_target="tpu_custom_call" | custom-call | flops 6442450944 | bytes 12582912 | tf_op jit(solution)/shard_map/pallas_call | solution.py:51
  31.3 1.7 fusion.45
  33.0 2.9 collective-permute-start.13
  38.2 9.9 %collective-permute-done.13 = f32[2,2,32,1024]{3,2,1,0:T(8,128)S(1)} collective-permute-done((f32[2,2,32,1024]{3,2,1,0:T(8,128)S(1)}, f32[2,2,32,1024]{3,2,1,0:T(8,128)S(1)}, u32[]{:S(2)}, u32[]{:S(2)}) %collective-permute-start.13) | collective-permute-done | bytes 524320 | tf_op jit(solution)/shard_map/ppermute | solution.py:72
  48.2 2.9 collective-permute-done.11
  52.3 4.4 collective-permute-done.14
  56.8 4.2 collective-permute-done.6
  61.4 6.6 %collective-permute-done.7 = f32[2,32,1024]{2,1,0:T(8,128)S(1)} collective-permute-done((f32[2,32,1024]{2,1,0:T(8,128)S(1)}, f32[2,32,1024]{2,1,0:T(8,128)S(1)}, u32[]{:S(2)}, u32[]{:S(2)}) %collective-permute-start.7) | collective-permute-done | bytes 262176 | tf_op jit(solution)/shard_map/ppermute | solution.py:72
  68.0 1.6 collective-permute-start.9
  72.2 2.9 collective-permute-done.9
  75.6 2.3 collective-permute-done.8
  79.5 3.2 collective-permute-start.30
  82.7 8.2 %collective-permute-start.31 = (f32[128,1024]{1,0:T(8,128)S(1)}, f32[128,1024]{1,0:T(8,128)S(1)}, u32[]{:S(2)}, u32[]{:S(2)}) collective-permute-start(f32[128,1024]{1,0:T(8,128)S(1)} %get-tuple-element.57.product), channel_id=1, source_target_pairs={{16,0},{32,16},{48,32},{64,48},{80,64},{96,80},{112,96},{8,112},{2... | collective-permute-start | bytes 1572872 | tf_op jit(solution)/shard_map/ppermute | solution.py:314
  90.9 8.4 %collective-permute-done.30 = f32[128,1024]{1,0:T(8,128)S(1)} collective-permute-done((f32[128,1024]{1,0:T(8,128)S(1)}, f32[128,1024]{1,0:T(8,128)S(1)}, u32[]{:S(2)}, u32[]{:S(2)}) %collective-permute-start.30) | collective-permute-done | bytes 524320 | tf_op jit(solution)/shard_map/ppermute | solution.py:313
  99.3 3.1 collective-permute-done.31
  107.8 4.9 shard_map.57
  112.7 2.0 slice_select_fusion.1
  114.7 4.4 collective-permute-start.16
  119.1 2.8 collective-permute-done.16
  124.3 43.5 %collective-permute-start.19 = (f32[320,256]{1,0:T(8,128)}, f32[320,256]{1,0:T(8,128)}, u32[]{:S(2)}, u32[]{:S(2)}) collective-permute-start(f32[320,256]{1,0:T(8,128)} %get-tuple-element.50), channel_id=1, source_target_pairs={{0,64},{8,72},{16,80},{24,88},{32,96},{40,104},{48,112},{56,120},{... | collective-permute-start | bytes 983048 | tf_op jit(solution)/shard_map/ppermute | solution.py:72
  167.8 9.4 %collective-permute-start.18 = (f32[320,256]{1,0:T(8,128)}, f32[320,256]{1,0:T(8,128)}, u32[]{:S(2)}, u32[]{:S(2)}) collective-permute-start(f32[320,256]{1,0:T(8,128)} %get-tuple-element.51), channel_id=1, source_target_pairs={{0,96},{8,104},{16,112},{24,120},{32,64},{40,72},{48,80},{56,88},{... | collective-permute-start | bytes 983048 | tf_op jit(solution)/shard_map/ppermute | solution.py:72
  177.8 9.3 %copy.19 = f32[1024,2048]{0,1:T(8,128)} copy(f32[1024,2048]{1,0:T(8,128)} %second.3) | data formatting | bytes 16777216 | tf_op args[0]
  187.1 2.1 fusion.50
  190.5 8.8 %collective-permute-start = (f32[1024,128]{0,1:T(8,128)S(1)}, f32[1024,128]{0,1:T(8,128)S(1)}, u32[]{:S(2)}, u32[]{:S(2)}) collective-permute-start(f32[1024,128]{0,1:T(8,128)S(1)} %get-tuple-element.39), channel_id=1, source_target_pairs={{0,1},{1,2},{2,3},{3,4},{4,5},{5,6},{6,7},{8,9},{9,10},{10,11},{11... | collective-permute-start | bytes 1572872 | tf_op jit(solution)/shard_map/ppermute | solution.py:262
  200.6 7.5 %collective-permute-start.20 = (f32[160,256]{1,0:T(8,128)S(1)}, f32[160,256]{1,0:T(8,128)S(1)}, u32[]{:S(2)}, u32[]{:S(2)}) collective-permute-start(f32[160,256]{1,0:T(8,128)S(1)} %slice_select_fusion.2), channel_id=1, source_target_pairs={{0,16},{8,24},{16,0},{24,8},{32,48},{40,56},{48,32},{56,40},{64,80... | collective-permute-start | bytes 491528 | tf_op jit(solution)/shard_map/ppermute | solution.py:72
  208.8 12.1 %collective-permute-done.20 = f32[160,256]{1,0:T(8,128)S(1)} collective-permute-done((f32[160,256]{1,0:T(8,128)S(1)}, f32[160,256]{1,0:T(8,128)S(1)}, u32[]{:S(2)}, u32[]{:S(2)}) %collective-permute-start.20) | collective-permute-done | bytes 163872 | tf_op jit(solution)/shard_map/ppermute | solution.py:72
  220.9 15.4 %collective-permute-start.23 = (f32[160,256]{1,0:T(8,128)S(1)}, f32[160,256]{1,0:T(8,128)S(1)}, u32[]{:S(2)}, u32[]{:S(2)}) collective-permute-start(f32[160,256]{1,0:T(8,128)S(1)} %select_add_fusion), channel_id=1, source_target_pairs={{0,4},{1,5},{2,6},{3,7},{4,0},{5,1},{6,2},{7,3},{8,12},{9,13},{10,... | collective-permute-start | bytes 491528 | tf_op jit(solution)/shard_map/ppermute | solution.py:72
  237.2 8.9 %pad_maximum_fusion = f32[1024,2304]{0,1:T(8,128)} fusion(f32[1024,128]{0,1:T(8,128)S(1)} %collective-permute-done.1, f32[1024,2048]{0,1:T(8,128)} %copy.19, f32[1024,128]{0,1:T(8,128)S(1)} %collective-permute-done), kind=kLoop, calls=%fused_computation | loop fusion | flops 4718592 | bytes 18874368 | tf_op jit(solution)/shard_map/concatenate | solution.py:260
  246.1 8.4 %slice.449 = f32[1024,16,128]{0,2,1:T(8,128)} slice(f32[1024,18,128]{0,2,1:T(8,128)} %bitcast.168), slice={[0:1024], [1:17], [0:128]} | slice | bytes 16777216 | tf_op jit(solution)/shard_map/slice | solution.py:279
  254.6 2.3 collective-permute-start.24
  256.9 20.3 %fusion.3 = f32[1024,16,128]{0,2,1:T(8,128)} fusion(f32[1024,16,128]{0,2,1:T(8,128)} %slice.449, f32[1024,18,128]{0,2,1:T(8,128)} %bitcast.169, f32[16,128]{1,0:T(8,128)S(1)} %constant_dynamic-slice_fusion.5), kind=kLoop, calls=%fused_computation.8 | loop fusion | flops 12582912 | bytes 33562624 | tf_op jit(solution)/shard_map/add | solution.py:282
  277.4 3.2 fusion.49
  280.6 3.7 collective-permute-start.3
  284.2 3.3 collective-permute-start.2
  287.7 3.0 collective-permute-start.28
  291.5 9.0 %copy.26 = f32[256,8,8,128]{3,2,1,0:T(8,128)} copy(f32[256,8,8,128]{3,1,2,0:T(8,128)} %bitcast.170) | data formatting | bytes 16777216
  300.5 9.3 %copy.22 = f32[8,128,2048]{2,1,0:T(8,128)} copy(f32[8,128,2048]{1,0,2:T(8,128)} %bitcast.173) | data formatting | bytes 16777216 | tf_op jit(solution)/shard_map/slice | solution.py:272
  309.8 10.0 %collective-permute-done.26 = f32[320,256]{1,0:T(8,128)S(1)} collective-permute-done((f32[320,256]{1,0:T(8,128)S(1)}, f32[320,256]{1,0:T(8,128)S(1)}, u32[]{:S(2)}, u32[]{:S(2)}) %collective-permute-start.26) | collective-permute-done | bytes 327712 | tf_op jit(solution)/shard_map/ppermute | solution.py:72
  320.9 10.0 %fusion.8 = f32[1024,2048]{0,1:T(8,128)} fusion(f32[128,2048]{0,1:T(8,128)} %collective-permute-done.3, f32[1024,2048]{0,1:T(8,128)} %bitcast.171, f32[128,2048]{0,1:T(8,128)} %collective-permute-done.2), kind=kLoop, calls=%fused_computation.14 | loop fusion | flops 6291456 | bytes 18874368 | tf_op jit(solution)/shard_map/add | solution.py:274
  331.0 9.2 %copy.23 = f32[1024,2048]{1,0:T(8,128)} copy(f32[1024,2048]{0,1:T(8,128)} %fusion.8) | data formatting | bytes 16777216 | tf_op jit(solution)/shard_map/add | solution.py:274
  340.1 18.0 %fusion.7 = f32[8,128,2048]{2,1,0:T(8,128)} fusion(f32[8,128,2048]{2,1,0:T(8,128)} %bitcast.172, f32[8,128,2048]{2,1,0:T(8,128)} %copy.22, f32[8,128]{1,0:T(8,128)S(1)} %constant_dynamic-slice_fusion.6), kind=kLoop, calls=%fused_computation.12 | loop fusion | flops 10485760 | bytes 25169920 | tf_op jit(solution)/shard_map/add | solution.py:275
  358.1 1.5 broadcast_select_fusion.1
  359.6 1.7 pad_maximum_fusion.3
  361.3 192.5 %shard_map.58 = f32[1024,1024]{1,0:T(8,128)} custom-call(f32[1]{0:T(128)S(6)} %copy.27.weight, f32[10,256,256]{2,1,0:T(8,128)} %bitcast.174, f32[1024,1024]{1,0:T(8,128)} %all-gather.3.cloned.1.call-done.sides), custom_call_target="tpu_custom_call" | custom-call | tf_op jit(solution)/shard_map/pallas_call | solution.py:235
  553.8 4.4 copy.25
  558.4 19.0 %fusion.9 = f32[1024,2048]{1,0:T(8,128)} fusion(f32[8,128,2048]{2,1,0:T(8,128)} %fusion.7, f32[1024]{0:T(1024)S(1)} %copy-done.8, s32[2048]{0:T(1024)S(1)} %iota_add_fusion, s32[1024]{0:T(1024)S(1)} %iota_add_fusion.1, f32[1024,1024]{1,0:T(8,128)S(1)} %copy-done.3, f32[2048,1024]{1,0:T(8,128)S(1)} %bitcast.176), kind=kOutput, calls=%fused_computation.18 | convolution fusion | flops 12893290496 | bytes 29376512 | tf_op jit(solution)/shard_map/dot_general | solution.py:333
  (109 shorter events, 22.9 us)
Async XLA Ops:
  6.5 84.4 %copy-start = (f32[128,128]{1,0:T(8,128)S(1)}, f32[128,128]{1,0:T(8,128)}, u32[]{:S(2)}) copy-start(f32[128,128]{1,0:T(8,128)} %param.7) | copy-start | bytes 196612
  6.5 354.8 %all-gather.3.cloned.1.call-start = ((), (), s32[]{:S(2)}) async-start(), calls=%async_computation | async-start | bytes 4718592 | tf_op jit(solution)/shard_map/all_gather | solution.py:320
  18.2 13.1 %collective-permute-start.5 = (f32[8,128,1024]{2,1,0:T(8,128)}, f32[8,128,1024]{2,1,0:T(8,128)S(1)}, u32[]{:S(2)}, u32[]{:S(2)}) collective-permute-start(f32[8,128,1024]{2,1,0:T(8,128)} %shard_map.56), channel_id=1, source_target_pairs={{0,8},{8,0},{16,24},{24,16},{32,40},{40,32},{48,56},{56,48},{64,72... | collective-permute-start | bytes 12582920 | tf_op jit(solution)/shard_map/ppermute | solution.py:72
  31.3 4.7 copy-start.2
  33.0 15.0 %collective-permute-start.13 = (f32[2,2,32,1024]{3,2,1,0:T(8,128)S(1)}, f32[2,2,32,1024]{3,2,1,0:T(8,128)S(1)}, u32[]{:S(2)}, u32[]{:S(2)}) collective-permute-start(f32[2,2,32,1024]{3,2,1,0:T(8,128)S(1)} %pad_maximum_fusion.8), channel_id=1, source_target_pairs={{0,96},{8,104},{16,112},{24,120},{32,64},{40,72},{48,80},{56,88},{... | collective-permute-start | bytes 1572872 | tf_op jit(solution)/shard_map/ppermute | solution.py:72
  36.5 24.5 %collective-permute-start.6 = (f32[4,64,1024]{2,1,0:T(8,128)S(1)}, f32[4,64,1024]{2,1,0:T(8,128)S(1)}, u32[]{:S(2)}, u32[]{:S(2)}) collective-permute-start(f32[4,64,1024]{2,1,0:T(8,128)S(1)} %pad_maximum_fusion.6), channel_id=1, source_target_pairs={{0,16},{8,24},{16,0},{24,8},{32,48},{40,56},{48,32},{56,40},{64,80... | collective-permute-start | bytes 3145736 | tf_op jit(solution)/shard_map/ppermute | solution.py:72
  38.1 13.0 %collective-permute-start.11 = (f32[2,2,32,1024]{3,2,1,0:T(8,128)S(1)}, f32[2,2,32,1024]{3,2,1,0:T(8,128)S(1)}, u32[]{:S(2)}, u32[]{:S(2)}) collective-permute-start(f32[2,2,32,1024]{3,2,1,0:T(8,128)S(1)} %pad_maximum_fusion.7), channel_id=1, source_target_pairs={{0,32},{8,40},{16,48},{24,56},{32,0},{40,8},{48,16},{56,24},{64,96... | collective-permute-start | bytes 1572872 | tf_op jit(solution)/shard_map/ppermute | solution.py:72
  48.1 8.6 %collective-permute-start.14 = (f32[2,32,1024]{2,1,0:T(8,128)S(1)}, f32[2,32,1024]{2,1,0:T(8,128)S(1)}, u32[]{:S(2)}, u32[]{:S(2)}) collective-permute-start(f32[2,32,1024]{2,1,0:T(8,128)S(1)} %fusion.14), channel_id=1, source_target_pairs={{0,32},{8,40},{16,48},{24,56},{32,0},{40,8},{48,16},{56,24},{64,96... | collective-permute-start | bytes 786440 | tf_op jit(solution)/shard_map/ppermute | solution.py:72
  51.1 10.2 %collective-permute-start.12 = (f32[2,32,1024]{2,1,0:T(8,128)S(1)}, f32[2,32,1024]{2,1,0:T(8,128)S(1)}, u32[]{:S(2)}, u32[]{:S(2)}) collective-permute-start(f32[2,32,1024]{2,1,0:T(8,128)S(1)} %fusion.17), channel_id=1, source_target_pairs={{0,96},{8,104},{16,112},{24,120},{32,64},{40,72},{48,80},{56,88},{... | collective-permute-start | bytes 786440 | tf_op jit(solution)/shard_map/ppermute | solution.py:72
  61.2 6.7 %collective-permute-start.7 = (f32[2,32,1024]{2,1,0:T(8,128)S(1)}, f32[2,32,1024]{2,1,0:T(8,128)S(1)}, u32[]{:S(2)}, u32[]{:S(2)}) collective-permute-start(f32[2,32,1024]{2,1,0:T(8,128)S(1)} %pad_maximum_fusion.11), channel_id=1, source_target_pairs={{0,32},{8,40},{16,48},{24,56},{32,0},{40,8},{48,16},{56,24},{64,96... | collective-permute-start | bytes 786440 | tf_op jit(solution)/shard_map/ppermute | solution.py:72
  68.0 7.0 %collective-permute-start.9 = (f32[2,32,1024]{2,1,0:T(8,128)S(1)}, f32[2,32,1024]{2,1,0:T(8,128)S(1)}, u32[]{:S(2)}, u32[]{:S(2)}) collective-permute-start(f32[2,32,1024]{2,1,0:T(8,128)S(1)} %pad_maximum_fusion.12), channel_id=1, source_target_pairs={{0,96},{8,104},{16,112},{24,120},{32,64},{40,72},{48,80},{56,88},{... | collective-permute-start | bytes 786440 | tf_op jit(solution)/shard_map/ppermute | solution.py:72
  69.6 5.9 %collective-permute-start.15 = (f32[64,1024]{1,0:T(8,128)S(1)}, f32[64,1024]{1,0:T(8,128)S(1)}, u32[]{:S(2)}, u32[]{:S(2)}) collective-permute-start(f32[64,1024]{1,0:T(8,128)S(1)} %pad_maximum_fusion.13), channel_id=1, source_target_pairs={{0,16},{8,24},{16,0},{24,8},{32,48},{40,56},{48,32},{56,40},{64,80... | collective-permute-start | bytes 786440 | tf_op jit(solution)/shard_map/ppermute | solution.py:72
  71.0 6.9 %collective-permute-start.8 = (f32[32,1024]{1,0:T(8,128)S(1)}, f32[32,1024]{1,0:T(8,128)S(1)}, u32[]{:S(2)}, u32[]{:S(2)}) collective-permute-start(f32[32,1024]{1,0:T(8,128)S(1)} %get-tuple-element.64), channel_id=1, source_target_pairs={{0,96},{8,104},{16,112},{24,120},{32,64},{40,72},{48,80},{56,88},{... | collective-permute-start | bytes 393224 | tf_op jit(solution)/shard_map/ppermute | solution.py:72
  75.1 4.2 collective-permute-start.10
  79.5 27.5 %copy-start.4 = (f32[128,1024]{1,0:T(8,128)}, f32[128,1024]{1,0:T(8,128)S(1)}, u32[]{:S(2)}) copy-start(f32[128,1024]{1,0:T(8,128)S(1)} %get-tuple-element.57.product) | copy-start | bytes 1572868
  79.5 19.8 %collective-permute-start.30 = (f32[128,1024]{1,0:T(8,128)S(1)}, f32[128,1024]{1,0:T(8,128)S(1)}, u32[]{:S(2)}, u32[]{:S(2)}) collective-permute-start(f32[128,1024]{1,0:T(8,128)S(1)} %get-tuple-element.57.product), channel_id=1, source_target_pairs={{0,16},{16,32},{32,48},{48,64},{64,80},{80,96},{96,112},{112,8},{8... | collective-permute-start | bytes 1572872 | tf_op jit(solution)/shard_map/ppermute | solution.py:313
  82.7 19.8 %collective-permute-start.31 = (f32[128,1024]{1,0:T(8,128)S(1)}, f32[128,1024]{1,0:T(8,128)S(1)}, u32[]{:S(2)}, u32[]{:S(2)}) collective-permute-start(f32[128,1024]{1,0:T(8,128)S(1)} %get-tuple-element.57.product), channel_id=1, source_target_pairs={{16,0},{32,16},{48,32},{64,48},{80,64},{96,80},{112,96},{8,112},{2... | collective-permute-start | bytes 1572872 | tf_op jit(solution)/shard_map/ppermute | solution.py:314
  102.7 1.6 copy-start.5
  102.7 0.7 collective-permute-start.32
  103.4 0.8 copy-start.7
  104.2 449.6 %all-gather.5.cloned.1.call-start = ((), (), s32[]{:S(2)}) async-start(), calls=%async_computation.1 | async-start | bytes 8912896 | tf_op jit(solution)/shard_map/all_gather | solution.py:318
  106.0 0.9 collective-permute-start.4
  107.0 0.8 copy-start.6
  114.7 7.2 %collective-permute-start.16 = (f32[1280,256]{1,0:T(8,128)S(1)}, f32[1280,256]{1,0:T(8,128)}, u32[]{:S(2)}, u32[]{:S(2)}) collective-permute-start(f32[1280,256]{1,0:T(8,128)S(1)} %bitcast.179), channel_id=1, source_target_pairs={{0,8},{8,0},{16,24},{24,16},{32,40},{40,32},{48,56},{56,48},{64,72... | collective-permute-start | bytes 3932168 | tf_op jit(solution)/shard_map/ppermute | solution.py:72
  124.3 75.0 %collective-permute-start.19 = (f32[320,256]{1,0:T(8,128)}, f32[320,256]{1,0:T(8,128)}, u32[]{:S(2)}, u32[]{:S(2)}) collective-permute-start(f32[320,256]{1,0:T(8,128)} %get-tuple-element.50), channel_id=1, source_target_pairs={{0,64},{8,72},{16,80},{24,88},{32,96},{40,104},{48,112},{56,120},{... | collective-permute-start | bytes 983048 | tf_op jit(solution)/shard_map/ppermute | solution.py:72
  167.8 31.5 %collective-permute-start.18 = (f32[320,256]{1,0:T(8,128)}, f32[320,256]{1,0:T(8,128)}, u32[]{:S(2)}, u32[]{:S(2)}) collective-permute-start(f32[320,256]{1,0:T(8,128)} %get-tuple-element.51), channel_id=1, source_target_pairs={{0,96},{8,104},{16,112},{24,120},{32,64},{40,72},{48,80},{56,88},{... | collective-permute-start | bytes 983048 | tf_op jit(solution)/shard_map/ppermute | solution.py:72
  177.2 22.1 %collective-permute-start.17 = (f32[320,256]{1,0:T(8,128)S(1)}, f32[320,256]{1,0:T(8,128)}, u32[]{:S(2)}, u32[]{:S(2)}) collective-permute-start(f32[320,256]{1,0:T(8,128)S(1)} %get-tuple-element.49), channel_id=1, source_target_pairs={{0,32},{8,40},{16,48},{24,56},{32,0},{40,8},{48,16},{56,24},{64,96... | collective-permute-start | bytes 983048 | tf_op jit(solution)/shard_map/ppermute | solution.py:72
  189.2 48.0 %collective-permute-start.1 = (f32[1024,128]{0,1:T(8,128)}, f32[1024,128]{0,1:T(8,128)S(1)}, u32[]{:S(2)}, u32[]{:S(2)}) collective-permute-start(f32[1024,128]{0,1:T(8,128)} %get-tuple-element.40), channel_id=1, source_target_pairs={{1,0},{2,1},{3,2},{4,3},{5,4},{6,5},{7,6},{9,8},{10,9},{11,10},{12... | collective-permute-start | bytes 1572872 | tf_op jit(solution)/shard_map/ppermute | solution.py:264
  190.5 46.8 %collective-permute-start = (f32[1024,128]{0,1:T(8,128)S(1)}, f32[1024,128]{0,1:T(8,128)S(1)}, u32[]{:S(2)}, u32[]{:S(2)}) collective-permute-start(f32[1024,128]{0,1:T(8,128)S(1)} %get-tuple-element.39), channel_id=1, source_target_pairs={{0,1},{1,2},{2,3},{3,4},{4,5},{5,6},{6,7},{8,9},{9,10},{10,11},{11... | collective-permute-start | bytes 1572872 | tf_op jit(solution)/shard_map/ppermute | solution.py:262
  200.6 20.3 %collective-permute-start.20 = (f32[160,256]{1,0:T(8,128)S(1)}, f32[160,256]{1,0:T(8,128)S(1)}, u32[]{:S(2)}, u32[]{:S(2)}) collective-permute-start(f32[160,256]{1,0:T(8,128)S(1)} %slice_select_fusion.2), channel_id=1, source_target_pairs={{0,16},{8,24},{16,0},{24,8},{32,48},{40,56},{48,32},{56,40},{64,80... | collective-permute-start | bytes 491528 | tf_op jit(solution)/shard_map/ppermute | solution.py:72
  220.9 33.7 %collective-permute-start.23 = (f32[160,256]{1,0:T(8,128)S(1)}, f32[160,256]{1,0:T(8,128)S(1)}, u32[]{:S(2)}, u32[]{:S(2)}) collective-permute-start(f32[160,256]{1,0:T(8,128)S(1)} %select_add_fusion), channel_id=1, source_target_pairs={{0,4},{1,5},{2,6},{3,7},{4,0},{5,1},{6,2},{7,3},{8,12},{9,13},{10,... | collective-permute-start | bytes 491528 | tf_op jit(solution)/shard_map/ppermute | solution.py:72
  236.3 18.3 %collective-permute-start.22 = (f32[160,256]{1,0:T(8,128)S(1)}, f32[160,256]{1,0:T(8,128)S(1)}, u32[]{:S(2)}, u32[]{:S(2)}) collective-permute-start(f32[160,256]{1,0:T(8,128)S(1)} %select_add_fusion), channel_id=1, source_target_pairs={{0,6},{1,7},{2,4},{3,5},{4,2},{5,3},{6,0},{7,1},{8,14},{9,15},{10,... | collective-permute-start | bytes 491528 | tf_op jit(solution)/shard_map/ppermute | solution.py:72
  237.2 17.4 %collective-permute-start.21 = (f32[160,256]{1,0:T(8,128)S(1)}, f32[160,256]{1,0:T(8,128)S(1)}, u32[]{:S(2)}, u32[]{:S(2)}) collective-permute-start(f32[160,256]{1,0:T(8,128)S(1)} %select_add_fusion), channel_id=1, source_target_pairs={{0,2},{1,3},{2,0},{3,1},{4,6},{5,7},{6,4},{7,5},{8,10},{9,11},{10,... | collective-permute-start | bytes 491528 | tf_op jit(solution)/shard_map/ppermute | solution.py:72
  254.6 22.6 %collective-permute-start.24 = (f32[160,256]{1,0:T(8,128)S(1)}, f32[160,256]{1,0:T(8,128)S(1)}, u32[]{:S(2)}, u32[]{:S(2)}) collective-permute-start(f32[160,256]{1,0:T(8,128)S(1)} %add_add_fusion.1), channel_id=1, source_target_pairs={{0,1},{1,0},{2,3},{3,2},{4,5},{5,4},{6,7},{7,6},{8,9},{9,8},{10,11... | collective-permute-start | bytes 491528 | tf_op jit(solution)/shard_map/ppermute | solution.py:72
  277.3 10.3 %collective-permute-start.25 = (f32[160,256]{1,0:T(8,128)S(1)}, f32[160,256]{1,0:T(8,128)S(1)}, u32[]{:S(2)}, u32[]{:S(2)}) collective-permute-start(f32[160,256]{1,0:T(8,128)S(1)} %add.446), channel_id=1, source_target_pairs={{0,16},{8,24},{16,0},{24,8},{32,48},{40,56},{48,32},{56,40},{64,80... | collective-permute-start | bytes 491528 | tf_op jit(solution)/shard_map/ppermute | solution.py:72
  280.6 40.4 %collective-permute-start.3 = (f32[128,2048]{0,1:T(8,128)}, f32[128,2048]{0,1:T(8,128)}, u32[]{:S(2)}, u32[]{:S(2)}) collective-permute-start(f32[128,2048]{0,1:T(8,128)} %bitcast.3), channel_id=1, source_target_pairs={{8,0},{16,8},{24,16},{32,24},{40,32},{48,40},{56,48},{64,56},{72,6... | collective-permute-start | bytes 3145736 | tf_op jit(solution)/shard_map/ppermute | solution.py:264
  284.2 36.7 %collective-permute-start.2 = (f32[128,2048]{0,1:T(8,128)}, f32[128,2048]{0,1:T(8,128)}, u32[]{:S(2)}, u32[]{:S(2)}) collective-permute-start(f32[128,2048]{0,1:T(8,128)} %bitcast.1), channel_id=1, source_target_pairs={{0,8},{8,16},{16,24},{24,32},{32,40},{40,48},{48,56},{56,64},{64,7... | collective-permute-start | bytes 3145736 | tf_op jit(solution)/shard_map/ppermute | solution.py:262
  287.7 22.1 %collective-permute-start.28 = (f32[320,256]{1,0:T(8,128)S(1)}, f32[320,256]{1,0:T(8,128)S(1)}, u32[]{:S(2)}, u32[]{:S(2)}) collective-permute-start(f32[320,256]{1,0:T(8,128)S(1)} %get-tuple-element.59), channel_id=1, source_target_pairs={{0,96},{8,104},{16,112},{24,120},{32,64},{40,72},{48,80},{56,88},{... | collective-permute-start | bytes 983048 | tf_op jit(solution)/shard_map/ppermute | solution.py:72
  290.7 19.1 %collective-permute-start.27 = (f32[320,256]{1,0:T(8,128)S(1)}, f32[320,256]{1,0:T(8,128)S(1)}, u32[]{:S(2)}, u32[]{:S(2)}) collective-permute-start(f32[320,256]{1,0:T(8,128)S(1)} %get-tuple-element.59), channel_id=1, source_target_pairs={{0,64},{8,72},{16,80},{24,88},{32,96},{40,104},{48,112},{56,120},{... | collective-permute-start | bytes 983048 | tf_op jit(solution)/shard_map/ppermute | solution.py:72
  291.4 28.3 %collective-permute-start.26 = (f32[320,256]{1,0:T(8,128)S(1)}, f32[320,256]{1,0:T(8,128)S(1)}, u32[]{:S(2)}, u32[]{:S(2)}) collective-permute-start(f32[320,256]{1,0:T(8,128)S(1)} %get-tuple-element.59), channel_id=1, source_target_pairs={{0,32},{8,40},{16,48},{24,56},{32,0},{40,8},{48,16},{56,24},{64,96... | collective-permute-start | bytes 983048 | tf_op jit(solution)/shard_map/ppermute | solution.py:72
  320.0 38.1 %collective-permute-start.29 = (f32[1280,256]{1,0:T(8,128)S(1)}, f32[1280,256]{1,0:T(8,128)}, u32[]{:S(2)}, u32[]{:S(2)}) collective-permute-start(f32[1280,256]{1,0:T(8,128)S(1)} %pad_maximum_fusion.5), channel_id=1, source_target_pairs={{0,8},{8,0},{16,24},{24,16},{32,40},{40,32},{48,56},{56,48},{64,72... | collective-permute-start | bytes 3932168 | tf_op jit(solution)/shard_map/ppermute | solution.py:72
  553.8 4.6 copy-start.3
  553.8 4.6 copy-start.8
  558.4 19.0 %copy-start.1 = (f32[128,128]{1,0:T(8,128)S(1)}, f32[128,128]{1,0:T(8,128)}, u32[]{:S(2)}) copy-start(f32[128,128]{1,0:T(8,128)} %param.7) | copy-start | bytes 196612
Sparse Core Ops, SparseCore 0:
  104.3 131.9 all-gather.2
  238.0 70.7 all-gather.4

commit v2 on v1

--- a/solution.py
+++ b/solution.py
@@ -8,7 +8,6 @@
 from jax.sharding import PartitionSpec as P
 
 COUPLING = 0.25
-HIGHEST_PRECISION = lax.Precision.HIGHEST
 F32 = jnp.float32
 BF16 = jnp.bfloat16
 NN = (((1,), (0,)), ((), ()))
@@ -67,31 +66,36 @@
     )(me, value_matrix, value_matrix, inputs)
 
 
-def swap(x, mask, axis="row"):
-    count = 16 if axis == "row" else 8
-    return lax.ppermute(x, axis, [(i, i ^ mask) for i in range(count)])
+def swap(x, mask):
+    return lax.ppermute(x, ("row", "col"), [(i, i ^ mask) for i in range(128)])
+
+
+CORE, X_LOW, X_HIGH = 8, 16, 1
+Y = (0, 32, 64, 96)
+Z = (0, 2, 4, 6)
+X = (0, 16, 1, 17)
 
 
 def reduce_y(near, far, blocks):
     kept = [blocks[0], blocks[far]]
-    got = swap(jnp.stack([blocks[near], blocks[near ^ far]]), near * 4)
+    got = swap(jnp.stack([blocks[near], blocks[near ^ far]]), Y[near])
     kept = [kept[0] + got[0], kept[1] + got[1]]
-    return kept[0] + swap(kept[1], far * 4)
+    return kept[0] + swap(kept[1], Y[far])
 
 
 def scatter_lines(even, odd):
-    got = swap(odd, 1)
+    got = swap(odd, CORE)
     quarter = LINE // 4
     cut = lambda i, q: even[i, q * quarter : (q + 1) * quarter] + got[i, q * quarter : (q + 1) * quarter]
     half = lambda i, q: jnp.concatenate([cut(i, q), cut(i, q + 1)], 0)
-    came = swap(jnp.stack([half(2 * m + 1, 0) for m in range(4)]), 2)
+    came = swap(jnp.stack([half(2 * m + 1, 0) for m in range(4)]), X_LOW)
     own = [half(2 * m, 0) + came[m] for m in range(4)]
     a = reduce_y(1, 3, [o[:quarter] for o in own])
     b = reduce_y(3, 1, [o[quarter:] for o in own])
     pair = lambda m, q: jnp.stack([cut(2 * m, q), cut(2 * m + 1, q)])
     c = reduce_y(1, 3, [pair(m, 2) for m in range(4)])
     d = reduce_y(3, 1, [pair(m, 3) for m in range(4)])
-    rest = jnp.concatenate([c[0], d[0]], 0) + swap(jnp.concatenate([c[1], d[1]], 0), 2)
+    rest = jnp.concatenate([c[0], d[0]], 0) + swap(jnp.concatenate([c[1], d[1]], 0), X_LOW)
     return jnp.concatenate([a, b, rest], 0)
 
 
@@ -105,34 +109,49 @@
     return jnp.concatenate([jnp.where(bit, got, mine), jnp.where(bit, mine, got)], 0)
 
 
+def scatter_four(x, place, masks):
+    count = x.shape[0] // 4
+    own = lambda m: lax.dynamic_slice_in_dim(x, (place ^ m) * count, count, 0)
+    return own(0) + swap(own(1), masks[1]) + swap(own(2), masks[2]) + swap(own(3), masks[3])
+
+
+def gather_four(x, place, masks):
+    parts = jnp.stack([x] + [swap(x, masks[m]) for m in range(1, 4)])
+    return jnp.concatenate([lax.dynamic_index_in_dim(parts, place ^ m, 0, False) for m in range(4)], 0)
+
+
 def sum_all(x, row_index, col_index):
-    bit = lambda k: (row_index >> k) & 1 == 1
-    keep, send = halves(x, bit(0))
-    x = keep + swap(send, 1)
-    y = row_index >> 2
-    count = x.shape[0] // 4
-    own = lambda m: lax.dynamic_slice_in_dim(x, (y ^ m) * count, count, 0)
-    x = own(0) + swap(own(1), 4) + swap(own(3), 12) + swap(own(2), 8)
-    keep, send = halves(x, bit(1))
-    x = keep + swap(send, 2)
-    x = x + swap(x, 2, "col") + swap(x, 6, "col") + swap(x, 4, "col")
-    x = x + swap(x, 1, "col")
-    x = joined(x, swap(x, 2), bit(1))
-    parts = [x, swap(x, 4), swap(x, 8), swap(x, 12)]
-    parts = jnp.stack(parts)
-    x = jnp.concatenate([lax.dynamic_index_in_dim(parts, y ^ m, 0, False) for m in range(4)], 0)
-    return joined(x, swap(x, 1), bit(0))
+    core, x_low, y = row_index & 1, (row_index >> 1) & 1, row_index >> 2
+    x_place = (col_index & 1) * 2 + x_low
+    keep, send = halves(x, core == 1)
+    x = keep + swap(send, CORE)
+    x = scatter_four(x, y, Y)
+    x = scatter_four(x, x_place, X)
+    x = x + swap(x, Z[1]) + swap(x, Z[2]) + swap(x, Z[3])
+    x = gather_four(x, x_place, X)
+    x = gather_four(x, y, Y)
+    return joined(x, swap(x, CORE), core == 1)
+
+
+def gather_rows(x, col_index):
+    pair = joined(x, swap(x, X_HIGH), (col_index & 1) == 1)
+    first, second = pair[:LINE], pair[LINE:]
+    first_near = swap(first, Z[1])
+    second_near = swap(second, Z[3])
+    first_far = swap(jnp.stack([first, first_near]), Z[3])
+    second_far = swap(jnp.stack([second, second_near]), Z[1])
+    return first, first_near, first_far, second, second_near, second_far
 
 
 def gram_kernel(inputs, product, out):
-    a = inputs[...]
-    b = product[...]
+    a = split(inputs[...])
+    b = split(product[...])
     at = 0
     for k in range(4):
         for i in range(k, 4):
-            left = a[:, i * PANEL : (i + 1) * PANEL]
-            right = b[:, k * PANEL : (k + 1) * PANEL]
-            out[at] = lax.dot_general(left, right, TN, precision=HIGHEST_PRECISION, preferred_element_type=F32)
+            left = [part[:, i * PANEL : (i + 1) * PANEL] for part in a]
+            right = [part[:, k * PANEL : (k + 1) * PANEL] for part in b]
+            out[at] = dot3(left, right, TN)
             at += 1
 
 
@@ -185,7 +204,7 @@
     return -work[...]
 
 
-def solve_kernel(weight, gram, sides, out, factor, inverses, work, worst):
+def solve_kernel(weight, z, gram, s0, s1, s2, t0, t1, t2, high, low, out, factor, inverses, work, worst):
     size = PANEL
     mask = lax.broadcasted_iota(jnp.int32, (size, size), 0) == lax.broadcasted_iota(jnp.int32, (size, size), 1)
     eye = jnp.where(mask, 1.0, 0.0).astype(F32)
@@ -196,7 +215,15 @@
             for i in range(k, 4):
                 here = gram[block_index(i, k)]
                 factor[block_index(i, k)] = here + weight[0] * eye if i == k else here
-        out[...] = sides[...]
+        rows = lambda step, h: pl.ds(pl.multiple_of(((z[0] ^ step) * 2 + h) * LINE, LINE), LINE)
+        out[rows(0, 0), :] = s0[...]
+        out[rows(1, 0), :] = s1[...]
+        out[rows(3, 0), :] = s2[0]
+        out[rows(2, 0), :] = s2[1]
+        out[rows(0, 1), :] = t0[...]
+        out[rows(3, 1), :] = t1[...]
+        out[rows(1, 1), :] = t2[0]
+        out[rows(2, 1), :] = t2[1]
         for k in range(4):
             here = factor[block_index(k, k)]
             if robust:
@@ -223,6 +250,7 @@
             for i in range(k + 1, 4):
                 total = total - dot3(split(out[:, at(i)]), split(factor[block_index(i, k)]), NN)
             out[:, at(k)] = total
+            high[:, at(k)], low[:, at(k)] = split(total)
 
     run(False)
 
@@ -231,41 +259,52 @@
         run(True)
 
 
-def solve(weight, gram, sides):
+def solve(weight, z, gram, sides):
+    scalar = pl.BlockSpec(memory_space=pltpu.SMEM)
+    array = pl.BlockSpec(memory_space=pltpu.VMEM)
+    size = 8 * LINE
     return pl.pallas_call(
         solve_kernel,
-        out_shape=jax.ShapeDtypeStruct(sides.shape, F32),
-        in_specs=[
-            pl.BlockSpec(memory_space=pltpu.SMEM),
-            pl.BlockSpec(memory_space=pltpu.VMEM),
-            pl.BlockSpec(memory_space=pltpu.VMEM),
-        ],
-        out_specs=pl.BlockSpec(memory_space=pltpu.VMEM),
+        out_shape=[jax.ShapeDtypeStruct((size, 4 * PANEL), BF16)] * 2,
+        in_specs=[scalar, scalar] + [array] * 7,
+        out_specs=[array, array],
         scratch_shapes=[
+            pltpu.VMEM((size, 4 * PANEL), F32),
             pltpu.VMEM((10, PANEL, PANEL), F32),
             pltpu.VMEM((4, PANEL, PANEL), F32),
             pltpu.VMEM((PANEL, PANEL), F32),
             pltpu.VMEM((1, 1), F32),
         ],
         compiler_params=pltpu.CompilerParams(vmem_limit_bytes=VMEM_LIMIT),
-    )(weight, gram, sides)
-
-
-def extended(cells, sides, width):
-    for axis, dim in sides:
-        count = lax.axis_size(axis)
-        ends = count - 1
-        head = lax.slice_in_dim(cells, 0, width, axis=dim)
-        tail = lax.slice_in_dim(cells, cells.shape[dim] - width, cells.shape[dim], axis=dim)
-        cells = jnp.concatenate(
-            [
-                lax.ppermute(tail, axis, [(i, (i + 1) % count) for i in range(ends)]),
-                cells,
-                lax.ppermute(head, axis, [((i + 1) % count, i) for i in range(ends)]),
-            ],
-            axis=dim,
-        )
-    return cells
+        cost_estimate=pl.CostEstimate(flops=9 << 30, bytes_accessed=12 << 20, transcendentals=0),
+    )(weight, z, gram, *sides)
+
+
+def downdate_kernel(high, low, first, second, base, out):
+    lines = split(jnp.concatenate([first[0], second[0]], 0))
+    out[...] = base[...] - dot3((high[...], low[...]), lines, NT)
+
+
+def downdate(solved, gain_cols, base):
+    rows, acts = solved[0].shape
+    whole = pl.BlockSpec((rows, acts), lambda b: (0, 0))
+    line = lambda b: (b % 8) * 2 + b // 8
+    block = pl.BlockSpec((rows, 2 * LINE), lambda b: (0, b))
+    return pl.pallas_call(
+        downdate_kernel,
+        grid=(8,),
+        in_specs=[
+            whole,
+            whole,
+            pl.BlockSpec((1, LINE, acts), lambda b: (line(2 * b), 0, 0)),
+            pl.BlockSpec((1, LINE, acts), lambda b: (line(2 * b + 1), 0, 0)),
+            block,
+        ],
+        out_specs=block,
+        out_shape=jax.ShapeDtypeStruct(base.shape, F32),
+        compiler_params=pltpu.CompilerParams(vmem_limit_bytes=VMEM_LIMIT),
+        cost_estimate=pl.CostEstimate(flops=12 << 30, bytes_accessed=28 << 20, transcendentals=0),
+    )(*solved, gain_cols, gain_cols, base)
 
 
 def stencil_first(field, diagonal):
@@ -275,11 +314,47 @@
     return diagonal[:, :, None] * centre + COUPLING * neighbours
 
 
-def stencil_last(field, diagonal):
-    centre = field[:, 1:-1]
-    side_padded = jnp.pad(centre, ((0, 0), (0, 0), (1, 1)))
-    neighbours = field[:, :-2] + field[:, 2:] + side_padded[:, :, :-2] + side_padded[:, :, 2:]
-    return diagonal[None] * centre + COUPLING * neighbours
+def plant_kernel(place, value, above, below, left, right, rows_diag, cols_diag, cost, out):
+    b = pl.program_id(0)
+    last = pl.num_programs(0) - 1
+    rows = value.shape[0]
+    lanes = lax.broadcasted_iota(jnp.int32, (1, LINE), 1)
+    inner = lax.broadcasted_iota(jnp.int32, (LINE, 1), 0)
+
+    def column(at):
+        cols = pl.ds(pl.multiple_of(at * LINE, LINE), LINE)
+        return jnp.concatenate([above[:, cols], value[:, cols], below[:, cols]], 0)
+
+    here = column(b)
+    before = jnp.where(b == 0, left[...], column(jnp.maximum(b - 1, 0)))
+    after = jnp.where(b == last, right[...], column(jnp.minimum(b + 1, last)))
+    sides = jnp.where(lanes == 0, 0.0, pltpu.roll(here, 1, 1)) + jnp.where(
+        lanes == LINE - 1, 0.0, pltpu.roll(here, LINE - 1, 1)
+    )
+    field = cols_diag[pl.ds(b, 1), :] * here + COUPLING * (before + after + sides)
+    for a in range(rows // LINE):
+        line = lambda k: field[(a + k) * LINE : (a + k + 1) * LINE]
+        centre = line(1)
+        sides = jnp.where(inner == 0, 0.0, pltpu.roll(centre, 1, 0)) + jnp.where(
+            inner == LINE - 1, 0.0, pltpu.roll(centre, LINE - 1, 0)
+        )
+        new = rows_diag[:, a : a + 1] * centre + COUPLING * (line(0) + line(2) + sides)
+        on_diagonal = (inner == lanes) & (place[0] + a == place[1] + b)
+        out[a * LINE : (a + 1) * LINE, :] = new + jnp.where(on_diagonal, cost[a : a + 1, :], 0.0)
+
+
+def plant_both(place, value, above, below, left, right, rows_diag, cols_diag, cost):
+    rows, cols = value.shape
+    array = pl.BlockSpec(memory_space=pltpu.VMEM)
+    return pl.pallas_call(
+        plant_kernel,
+        grid=(cols // LINE,),
+        in_specs=[pl.BlockSpec(memory_space=pltpu.SMEM)] + [array] * 8,
+        out_specs=pl.BlockSpec((rows, LINE), lambda b: (0, b)),
+        out_shape=jax.ShapeDtypeStruct(value.shape, F32),
+        compiler_params=pltpu.CompilerParams(vmem_limit_bytes=VMEM_LIMIT),
+        cost_estimate=pl.CostEstimate(flops=32 << 20, bytes_accessed=40 << 20, transcendentals=0),
+    )(place, value, above, below, left, right, rows_diag, cols_diag, cost)
 
 
 def device_of(line):
@@ -302,36 +377,62 @@
     trade = [((a * 2 + core) * 8 + b, (b * 2 + core) * 8 + a) for a in range(8) for b in range(8) for core in range(2)]
     mine_inputs = lax.dynamic_slice_in_dim(inputs, col_index * LINE, LINE, 0)
     mine_inputs = lax.ppermute(mine_inputs, both, trade)
+
+    def shifted(x, down, right):
+        pairs = [
+            (r * 8 + c, (r + down) * 8 + c + right)
+            for r in range(16)
+            for c in range(8)
+            if 0 <= r + down < 16 and 0 <= c + right < 8
+        ]
+        return lax.ppermute(x, both, pairs)
+
+    top, bottom = value_matrix[:LINE], value_matrix[-LINE:]
+    above, below = shifted(bottom, 1, 0), shifted(top, -1, 0)
+    left = [
+        shifted(bottom[:, -LINE:], 1, 1),
+        shifted(value_matrix[:, -LINE:], 0, 1),
+        shifted(top[:, -LINE:], -1, 1),
+    ]
+    right = [
+        shifted(bottom[:, :LINE], 1, -1),
+        shifted(value_matrix[:, :LINE], 0, -1),
+        shifted(top[:, :LINE], -1, -1),
+    ]
     odd = product_lines(me, value_matrix, inputs, 1)
-    even = product_lines(me, value_matrix, inputs, 0)
+    held = (value_matrix, inputs, mine_inputs, above, below, left, right)
+    value_here, inputs_here, mine_inputs, above, below, left, right = lax.optimization_barrier(held)
+    even = product_lines(me, value_here, inputs_here, 0)
     product = scatter_lines(even, odd)
 
     gram = gram_blocks(mine_inputs, product)
+    product, gram = lax.optimization_barrier((product, gram))
     gram = sum_all(gram.reshape(10 * PANEL, PANEL), row_index, col_index).reshape(10, PANEL, PANEL)
 
-    lines = STATES_LINES = 128
-    above = lax.ppermute(product, both, [(device_of(i), device_of(i + 1)) for i in range(lines - 1)])
-    below = lax.ppermute(product, both, [(device_of(i + 1), device_of(i)) for i in range(lines - 1)])
+    lines = 128
+    over = lax.ppermute(product, both, [(device_of(i), device_of(i + 1)) for i in range(lines - 1)])
+    under = lax.ppermute(product, both, [(device_of(i + 1), device_of(i)) for i in range(lines - 1)])
     line = col_index * 16 + line_of(row_index)
     diagonal = lax.dynamic_slice_in_dim(plant_diag, line, 1, 0)
-    gain = stencil_first(jnp.stack([above, product, below]), diagonal)[0]
+    gain = stencil_first(jnp.stack([over, product, under]), diagonal)[0]
     gain_cols = lax.all_gather(gain, "row", axis=0)
-    gain_cols = gain_cols.reshape(8, 2, LINE, actuators).swapaxes(0, 1).reshape(cols_block, actuators)
-    gain_rows = lax.all_gather(lax.ppermute(gain, both, trade), "col", axis=0, tiled=True)
-
-    padded_value = extended(value_matrix, (("col", 1),), grid_side)
-    plant_cols = stencil_last(padded_value.reshape(rows_block, lines_cols + 2, grid_side), diag_cols)
-    padded_product = extended(plant_cols.reshape(rows_block, cols_block), (("row", 0),), grid_side)
-    propagated = stencil_first(padded_product.reshape(lines_rows + 2, grid_side, cols_block), diag_rows)
-    propagated = propagated.reshape(rows_block, cols_block)
-    row_states = row_index * rows_block + jnp.arange(rows_block, dtype=jnp.int32)
-    col_states = col_index * cols_block + jnp.arange(cols_block, dtype=jnp.int32)
-    diagonal_mask = row_states[:, None] == col_states[None, :]
-    propagated = propagated + jnp.where(diagonal_mask, state_cost[:, None], jnp.float32(0.0))
-
-    solved = solve(control_weight, gram, gain_rows)
-    downdate = lax.dot_general(solved, gain_cols, NT, precision=lax.Precision.HIGH)
-    return propagated - downdate
+    gain_rows = gather_rows(lax.ppermute(gain, both, trade), col_index)
+
+    place = jnp.stack([row_index * lines_rows, col_index * lines_cols]).astype(jnp.int32)
+    base = plant_both(
+        place,
+        value_matrix,
+        above,
+        below,
+        jnp.concatenate(left, 0),
+        jnp.concatenate(right, 0),
+        diag_rows.T,
+        diag_cols,
+        state_cost.reshape(lines_rows, grid_side),
+    )
+    z = (col_index >> 1).astype(jnp.int32).reshape(1)
+    solved = solve(control_weight, z, gram, gain_rows)
+    return downdate(solved, gain_cols, base)
 
 
 def solution(mesh):

time: 593 us -> 594 us (level)
  the two profiles are of different devices: /device:TPU:1 before, /device:TPU:24 now
where the time goes in v2:
time: 594 us; the launch traced here: 584 us
  Pallas kernels  259 us (44%)
  waiting for transfers between devices  171 us (29%)
  starting transfers between devices  105 us (18%)
  other arithmetic  21.4 us (4%)
  between operations  15.3 us (3%)
  local copies, waits for them, and re-layouts  11.3 us (2%)
    pallas_call x1, Pallas kernels, solve(): pl.pallas_call(solve_kernel, out_shape=[jax.ShapeDtypeStruct((size, 4 * P...  193 us
    ppermute x33, waiting for transfers between devices, swap(): return lax.ppermute(x, ('row', 'col'), [(i, i ^ mask) for i in range(128)])  83.4 us
    ppermute x33, starting transfers between devices, swap(): return lax.ppermute(x, ('row', 'col'), [(i, i ^ mask) for i in range(128)])  66.8 us
    ppermute x8, waiting for transfers between devices, shifted(): return lax.ppermute(x, both, pairs)  42 us
    ppermute x1, waiting for transfers between devices, local(): gain_rows = gather_rows(lax.ppermute(gain, both, trade), col_index)  27.7 us
    ppermute x8, starting transfers between devices, shifted(): return lax.ppermute(x, both, pairs)  25.1 us
    pallas_call x2, Pallas kernels, product_lines(): pl.pallas_call(product_kernel, grid_spec=pltpu.PrefetchScalarGridSpec(num...  23.4 us
    pallas_call x1, Pallas kernels, plant_both(): pl.pallas_call(plant_kernel, grid=(cols // LINE,), in_specs=[pl.BlockSpec...  20.1 us
  transfers between devices with their start and end apart: 46, of which 24 were waited for; matrix products, arithmetic and copies ran while one was open for 4% of the time, Pallas kernels for 38%

profile of v2, /device:TPU:24, one launch (start us, length us, event | category | flops | bytes accessed | tf_op | source)
XLA Modules:
  0.0 583.8 jit_solution(4314720742767190113)
XLA Ops:
  6.5 11.7 %shard_map.56 = f32[8,128,1024]{2,1,0:T(8,128)} custom-call(s32[1]{0:T(128)} %bitcast.1.me_ref, f32[1024,2048]{1,0:T(8,128)} %value.1, f32[1024,2048]{1,0:T(8,128)} %value.1, f32[1024,1024]{1,0:T(8,128)} %inputs.2), custom_call_target="tpu_custom_call" | custom-call | flops 6442450944 | bytes 12582912 | tf_op jit(solution)/shard_map/pallas_call | solution.py:50
  19.3 5.6 collective-permute-start
  26.6 4.3 collective-permute-start.2
  30.9 1.9 collective-permute-start.1
  35.1 22.3 %collective-permute-done.8 = f32[128,128]{1,0:T(8,128)S(1)} collective-permute-done((f32[128,128]{1,0:T(8,128)S(1)}, f32[128,128]{1,0:T(8,128)S(1)}, u32[]{:S(2)}, u32[]{:S(2)}) %collective-permute-start.8) | collective-permute-done | bytes 65568 | tf_op jit(solution)/shard_map/ppermute | solution.py:388
  58.7 6.4 %collective-permute-done.6 = f32[128,128]{1,0:T(8,128)S(1)} collective-permute-done((f32[128,128]{1,0:T(8,128)S(1)}, f32[128,128]{1,0:T(8,128)S(1)}, u32[]{:S(2)}, u32[]{:S(2)}) %collective-permute-start.6) | collective-permute-done | bytes 65568 | tf_op jit(solution)/shard_map/ppermute | solution.py:388
  68.2 5.4 collective-permute-start.3
  76.8 8.3 %collective-permute-start.4 = (f32[1024,128]{1,0:T(8,128)S(1)}, f32[1024,128]{1,0:T(8,128)S(1)}, u32[]{:S(2)}, u32[]{:S(2)}) collective-permute-start(f32[1024,128]{1,0:T(8,128)S(1)} %get-tuple-element.72), channel_id=1, source_target_pairs={{0,1},{1,2},{2,3},{3,4},{4,5},{5,6},{6,7},{8,9},{9,10},{10,11},{11... | collective-permute-start | bytes 1572872 | tf_op jit(solution)/shard_map/ppermute | solution.py:388
  85.2 10.8 %collective-permute-done.7 = f32[1024,128]{1,0:T(8,128)S(1)} collective-permute-done((f32[1024,128]{1,0:T(8,128)S(1)}, f32[1024,128]{1,0:T(8,128)S(1)}, u32[]{:S(2)}, u32[]{:S(2)}) %collective-permute-start.7) | collective-permute-done | bytes 524320 | tf_op jit(solution)/shard_map/ppermute | solution.py:388
  97.0 11.7 %shard_map.55 = f32[8,128,1024]{2,1,0:T(8,128)} custom-call(s32[1]{0:T(128)} %bitcast.1.me_ref, f32[1024,2048]{1,0:T(8,128)} %value.1, f32[1024,2048]{1,0:T(8,128)} %value.1, f32[1024,1024]{1,0:T(8,128)} %inputs.2), custom_call_target="tpu_custom_call" | custom-call | flops 6442450944 | bytes 12582912 | tf_op jit(solution)/shard_map/pallas_call | solution.py:50
  110.2 2.0 fusion.25
  116.6 14.0 %collective-permute-start.15 = (f32[2,2,32,1024]{3,2,1,0:T(8,128)S(1)}, f32[2,2,32,1024]{3,2,1,0:T(8,128)S(1)}, u32[]{:S(2)}, u32[]{:S(2)}) collective-permute-start(f32[2,2,32,1024]{3,2,1,0:T(8,128)S(1)} %pad_maximum_fusion.8), channel_id=1, source_target_pairs={{0,32},{1,33},{2,34},{3,35},{4,36},{5,37},{6,38},{7,39},{8,40},{9,... | collective-permute-start | bytes 1572872 | tf_op jit(solution)/shard_map/ppermute | solution.py:70
  130.6 10.7 %collective-permute-start.18 = (f32[2,32,1024]{2,1,0:T(8,128)S(1)}, f32[2,32,1024]{2,1,0:T(8,128)S(1)}, u32[]{:S(2)}, u32[]{:S(2)}) collective-permute-start(f32[2,32,1024]{2,1,0:T(8,128)S(1)} %fusion.4), channel_id=1, source_target_pairs={{0,32},{1,33},{2,34},{3,35},{4,36},{5,37},{6,38},{7,39},{8,40},{9,... | collective-permute-start | bytes 786440 | tf_op jit(solution)/shard_map/ppermute | solution.py:70
  141.4 2.3 collective-permute-start.16
  143.6 4.2 collective-permute-done.18
  148.1 2.4 collective-permute-start.11
  150.6 7.1 %collective-permute-done.11 = f32[2,32,1024]{2,1,0:T(8,128)S(1)} collective-permute-done((f32[2,32,1024]{2,1,0:T(8,128)S(1)}, f32[2,32,1024]{2,1,0:T(8,128)S(1)}, u32[]{:S(2)}, u32[]{:S(2)}) %collective-permute-start.11) | collective-permute-done | bytes 262176 | tf_op jit(solution)/shard_map/ppermute | solution.py:70
  157.9 2.0 collective-permute-start.19
  159.9 2.6 collective-permute-start.12
  162.5 5.7 collective-permute-done.13
  170.2 3.1 collective-permute-done.14
  174.2 4.0 shard_map.57
  178.1 3.2 collective-permute-start.38
  181.3 2.6 collective-permute-start.37
  184.0 9.7 %collective-permute-done.38 = f32[128,1024]{1,0:T(8,128)S(1)} collective-permute-done((f32[128,1024]{1,0:T(8,128)S(1)}, f32[128,1024]{1,0:T(8,128)S(1)}, u32[]{:S(2)}, u32[]{:S(2)}) %collective-permute-start.38) | collective-permute-done | bytes 524320 | tf_op jit(solution)/shard_map/ppermute | solution.py:414
  193.7 8.4 %collective-permute-done.37 = f32[128,1024]{1,0:T(8,128)S(1)} collective-permute-done((f32[128,1024]{1,0:T(8,128)S(1)}, f32[128,1024]{1,0:T(8,128)S(1)}, u32[]{:S(2)}, u32[]{:S(2)}) %collective-permute-start.37) | collective-permute-done | bytes 524320 | tf_op jit(solution)/shard_map/ppermute | solution.py:413
  202.9 2.4 fusion.3
  207.2 3.2 collective-permute-done.20
  212.8 2.1 collective-permute-start.21
  214.8 2.8 collective-permute-start.23
  217.6 11.7 %collective-permute-done.21 = f32[320,256]{1,0:T(8,128)S(1)} collective-permute-done((f32[320,256]{1,0:T(8,128)}, f32[320,256]{1,0:T(8,128)S(1)}, u32[]{:S(2)}, u32[]{:S(2)}) %collective-permute-start.21) | collective-permute-done | bytes 327712 | tf_op jit(solution)/shard_map/ppermute | solution.py:70
  229.3 17.0 %collective-permute-done.22 = f32[320,256]{1,0:T(8,128)} collective-permute-done((f32[320,256]{1,0:T(8,128)S(1)}, f32[320,256]{1,0:T(8,128)}, u32[]{:S(2)}, u32[]{:S(2)}) %collective-permute-start.22) | collective-permute-done | bytes 327712 | tf_op jit(solution)/shard_map/ppermute | solution.py:70
  247.7 3.9 collective-permute-start.25
  251.6 2.9 collective-permute-done.24
  254.5 2.2 collective-permute-done.25
  256.8 9.9 %collective-permute-start.28 = (f32[80,256]{1,0:T(8,128)S(1)}, f32[80,256]{1,0:T(8,128)S(1)}, u32[]{:S(2)}, u32[]{:S(2)}) collective-permute-start(f32[80,256]{1,0:T(8,128)S(1)} %add_add_fusion.2), channel_id=1, source_target_pairs={{0,4},{1,5},{2,6},{3,7},{4,0},{5,1},{6,2},{7,3},{8,12},{9,13},{10,... | collective-permute-start | bytes 245768 | tf_op jit(solution)/shard_map/ppermute | solution.py:70
  266.8 2.5 collective-permute-done.28
  271.3 2.0 collective-permute-start.31
  273.4 2.0 collective-permute-start.30
  275.4 1.9 collective-permute-start.39
  279.3 3.6 collective-permute-start.35
  283.0 27.7 %collective-permute-done.39 = f32[128,1024]{1,0:T(8,128)S(1)} collective-permute-done((f32[128,1024]{1,0:T(8,128)S(1)}, f32[128,1024]{1,0:T(8,128)S(1)}, u32[]{:S(2)}, u32[]{:S(2)}) %collective-permute-start.39) | collective-permute-done | bytes 524320 | tf_op jit(solution)/shard_map/ppermute | solution.py:419
  312.1 10.6 %collective-permute-done.40 = f32[128,1024]{1,0:T(8,128)S(1)} collective-permute-done((f32[128,1024]{1,0:T(8,128)S(1)}, f32[128,1024]{1,0:T(8,128)S(1)}, u32[]{:S(2)}, u32[]{:S(2)}) %collective-permute-start.40) | collective-permute-done | bytes 524320 | tf_op jit(solution)/shard_map/ppermute | solution.py:70
  325.6 8.6 %collective-permute-done.43.t1 = f32[128,1024]{1,0:T(8,128)S(1)} collective-permute-done((f32[128,1024]{1,0:T(8,128)S(1)}, f32[128,1024]{1,0:T(8,128)S(1)}, u32[]{:S(2)}, u32[]{:S(2)}) %collective-permute-start.43) | collective-permute-done | bytes 524320 | tf_op jit(solution)/shard_map/ppermute | solution.py:70
  335.0 4.1 collective-permute-start.42
  340.3 20.1 %shard_map.59.base = f32[1024,2048]{1,0:T(8,128)} custom-call(s32[2]{0:T(128)} %pad_add_fusion.place, f32[1024,2048]{1,0:T(8,128)} %value.1, f32[128,2048]{1,0:T(8,128)} %collective-permute-done.1.above, f32[128,2048]{1,0:T(8,128)} %collective-permute-done.2.below, f32[1280,128]{1,0:T(8,128)} %get-tuple-element.111.left, ...), custom_call_target="tpu_custom_call" | custom-call | flops 33554432 | bytes 41943040 | tf_op jit(solution)/shard_map/pallas_call | solution.py:349
  364.6 192.7 %shard_map.58 = (bf16[1024,1024]{1,0:T(8,128)(2,1)}, bf16[1024,1024]{1,0:T(8,128)(2,1)}) custom-call(f32[1]{0:T(128)S(6)} %copy.9.weight, s32[1]{0:T(128)} %bitcast.z, f32[10,256,256]{2,1,0:T(8,128)} %bitcast.168, f32[128,1024]{1,0:T(8,128)} %copy-done.6, f32[128,1024]{1,0:T(8,128)} %copy-done.14, f32[2,128,1024]{2,1,0:T(8,128)} %collective-permute-done.42.s2, ...), custom_call_target="tpu_custom_call" | custom-call | flops 9663676416 | bytes 12582912 | tf_op jit(solution)/shard_map/pallas_call | solution.py:266
  557.3 19.2 %shard_map.60 = f32[1024,2048]{1,0:T(8,128)} custom-call(bf16[1024,1024]{1,0:T(8,128)(2,1)} %get-tuple-element.25.high, bf16[1024,1024]{1,0:T(8,128)(2,1)} %get-tuple-element.26.low, f32[16,128,1024]{2,1,0:T(8,128)} %all-gather.2.cloned.1.call-done.first.second, f32[16,128,1024]{2,1,0:T(8,128)} %all-gather.2.cloned.1.call-done.first.second, ...), custom_call_target="tpu_custom_call" | custom-call | flops 12884901888 | bytes 29360128 | tf_op jit(solution)/shard_map/pallas_call | solution.py:293
  (156 shorter events, 42.8 us)
Async XLA Ops:
  6.5 177.5 %copy-start = (f32[128,128]{1,0:T(8,128)S(1)}, f32[128,128]{1,0:T(8,128)}, u32[]{:S(2)}) copy-start(f32[128,128]{1,0:T(8,128)} %param.7) | copy-start | bytes 196612
  6.5 550.7 %all-gather.2.cloned.1.call-start = ((), (), s32[]{:S(2)}) async-start(), calls=%async_computation | async-start | bytes 8912896 | tf_op jit(solution)/shard_map/all_gather | solution.py:418
  18.2 90.5 %collective-permute-start.9 = (f32[8,128,1024]{2,1,0:T(8,128)}, f32[8,128,1024]{2,1,0:T(8,128)}, u32[]{:S(2)}, u32[]{:S(2)}) collective-permute-start(f32[8,128,1024]{2,1,0:T(8,128)} %shard_map.56), channel_id=1, source_target_pairs={{0,8},{1,9},{2,10},{3,11},{4,12},{5,13},{6,14},{7,15},{8,0},{9,1},... | collective-permute-start | bytes 12582920 | tf_op jit(solution)/shard_map/ppermute | solution.py:70
  19.3 57.5 %collective-permute-start = (f32[128,1024]{1,0:T(8,128)S(1)}, f32[128,1024]{1,0:T(8,128)S(1)}, u32[]{:S(2)}, u32[]{:S(2)}) collective-permute-start(f32[128,1024]{1,0:T(8,128)S(1)} %constant_dynamic-slice_fusion.9), channel_id=1, source_target_pairs={{0,0},{8,8},{1,16},{9,24},{2,32},{10,40},{3,48},{11,56},{4,64},{12... | collective-permute-start | bytes 1572872 | tf_op jit(solution)/shard_map/ppermute | solution.py:379
  26.6 69.4 %collective-permute-start.2 = (f32[128,2048]{1,0:T(8,128)S(1)}, f32[128,2048]{1,0:T(8,128)}, u32[]{:S(2)}, u32[]{:S(2)}) collective-permute-start(f32[128,2048]{1,0:T(8,128)S(1)} %get-tuple-element.73), channel_id=1, source_target_pairs={{8,0},{9,1},{10,2},{11,3},{12,4},{13,5},{14,6},{15,7},{16,8},{17,9... | collective-permute-start | bytes 3145736 | tf_op jit(solution)/shard_map/ppermute | solution.py:388
  30.9 66.1 %collective-permute-start.1 = (f32[128,2048]{1,0:T(8,128)S(1)}, f32[128,2048]{1,0:T(8,128)}, u32[]{:S(2)}, u32[]{:S(2)}) collective-permute-start(f32[128,2048]{1,0:T(8,128)S(1)} %get-tuple-element.74), channel_id=1, source_target_pairs={{0,8},{1,9},{2,10},{3,11},{4,12},{5,13},{6,14},{7,15},{8,16},{9,17... | collective-permute-start | bytes 3145736 | tf_op jit(solution)/shard_map/ppermute | solution.py:388
  33.8 23.6 %collective-permute-start.8 = (f32[128,128]{1,0:T(8,128)S(1)}, f32[128,128]{1,0:T(8,128)S(1)}, u32[]{:S(2)}, u32[]{:S(2)}) collective-permute-start(f32[128,128]{1,0:T(8,128)S(1)} %get-tuple-element.67), channel_id=1, source_target_pairs={{9,0},{10,1},{11,2},{12,3},{13,4},{14,5},{15,6},{17,8},{18,9},{19,... | collective-permute-start | bytes 196616 | tf_op jit(solution)/shard_map/ppermute | solution.py:388
  57.4 7.7 %collective-permute-start.6 = (f32[128,128]{1,0:T(8,128)S(1)}, f32[128,128]{1,0:T(8,128)S(1)}, u32[]{:S(2)}, u32[]{:S(2)}) collective-permute-start(f32[128,128]{1,0:T(8,128)S(1)} %get-tuple-element.68), channel_id=1, source_target_pairs={{1,8},{2,9},{3,10},{4,11},{5,12},{6,13},{7,14},{9,16},{10,17},{11,... | collective-permute-start | bytes 196616 | tf_op jit(solution)/shard_map/ppermute | solution.py:388
  65.1 3.2 collective-permute-start.5
  68.2 7.3 %collective-permute-start.3 = (f32[128,128]{1,0:T(8,128)S(1)}, f32[128,128]{1,0:T(8,128)S(1)}, u32[]{:S(2)}, u32[]{:S(2)}) collective-permute-start(f32[128,128]{1,0:T(8,128)S(1)} %get-tuple-element.70), channel_id=1, source_target_pairs={{0,9},{1,10},{2,11},{3,12},{4,13},{5,14},{6,15},{8,17},{9,18},{10,... | collective-permute-start | bytes 196616 | tf_op jit(solution)/shard_map/ppermute | solution.py:388
  75.5 20.5 %collective-permute-start.7 = (f32[1024,128]{1,0:T(8,128)S(1)}, f32[1024,128]{1,0:T(8,128)S(1)}, u32[]{:S(2)}, u32[]{:S(2)}) collective-permute-start(f32[1024,128]{1,0:T(8,128)S(1)} %get-tuple-element.71), channel_id=1, source_target_pairs={{1,0},{2,1},{3,2},{4,3},{5,4},{6,5},{7,6},{9,8},{10,9},{11,10},{12... | collective-permute-start | bytes 1572872 | tf_op jit(solution)/shard_map/ppermute | solution.py:388
  76.8 19.2 %collective-permute-start.4 = (f32[1024,128]{1,0:T(8,128)S(1)}, f32[1024,128]{1,0:T(8,128)S(1)}, u32[]{:S(2)}, u32[]{:S(2)}) collective-permute-start(f32[1024,128]{1,0:T(8,128)S(1)} %get-tuple-element.72), channel_id=1, source_target_pairs={{0,1},{1,2},{2,3},{3,4},{4,5},{5,6},{6,7},{8,9},{9,10},{10,11},{11... | collective-permute-start | bytes 1572872 | tf_op jit(solution)/shard_map/ppermute | solution.py:388
  112.4 35.4 %collective-permute-start.10 = (f32[4,64,1024]{2,1,0:T(8,128)S(1)}, f32[4,64,1024]{2,1,0:T(8,128)S(1)}, u32[]{:S(2)}, u32[]{:S(2)}) collective-permute-start(f32[4,64,1024]{2,1,0:T(8,128)S(1)} %pad_maximum_fusion.3), channel_id=1, source_target_pairs={{0,16},{1,17},{2,18},{3,19},{4,20},{5,21},{6,22},{7,23},{8,24},{9,... | collective-permute-start | bytes 3145736 | tf_op jit(solution)/shard_map/ppermute | solution.py:70
  114.8 15.7 %collective-permute-start.17 = (f32[2,2,32,1024]{3,2,1,0:T(8,128)S(1)}, f32[2,2,32,1024]{3,2,1,0:T(8,128)S(1)}, u32[]{:S(2)}, u32[]{:S(2)}) collective-permute-start(f32[2,2,32,1024]{3,2,1,0:T(8,128)S(1)} %pad_maximum_fusion.9), channel_id=1, source_target_pairs={{0,96},{1,97},{2,98},{3,99},{4,100},{5,101},{6,102},{7,103},{8,104... | collective-permute-start | bytes 1572872 | tf_op jit(solution)/shard_map/ppermute | solution.py:70
  116.6 24.8 %collective-permute-start.15 = (f32[2,2,32,1024]{3,2,1,0:T(8,128)S(1)}, f32[2,2,32,1024]{3,2,1,0:T(8,128)S(1)}, u32[]{:S(2)}, u32[]{:S(2)}) collective-permute-start(f32[2,2,32,1024]{3,2,1,0:T(8,128)S(1)} %pad_maximum_fusion.8), channel_id=1, source_target_pairs={{0,32},{1,33},{2,34},{3,35},{4,36},{5,37},{6,38},{7,39},{8,40},{9,... | collective-permute-start | bytes 1572872 | tf_op jit(solution)/shard_map/ppermute | solution.py:70
  130.6 17.2 %collective-permute-start.18 = (f32[2,32,1024]{2,1,0:T(8,128)S(1)}, f32[2,32,1024]{2,1,0:T(8,128)S(1)}, u32[]{:S(2)}, u32[]{:S(2)}) collective-permute-start(f32[2,32,1024]{2,1,0:T(8,128)S(1)} %fusion.4), channel_id=1, source_target_pairs={{0,32},{1,33},{2,34},{3,35},{4,36},{5,37},{6,38},{7,39},{8,40},{9,... | collective-permute-start | bytes 786440 | tf_op jit(solution)/shard_map/ppermute | solution.py:70
  141.4 9.2 %collective-permute-start.16 = (f32[2,32,1024]{2,1,0:T(8,128)S(1)}, f32[2,32,1024]{2,1,0:T(8,128)S(1)}, u32[]{:S(2)}, u32[]{:S(2)}) collective-permute-start(f32[2,32,1024]{2,1,0:T(8,128)S(1)} %fusion.7), channel_id=1, source_target_pairs={{0,96},{1,97},{2,98},{3,99},{4,100},{5,101},{6,102},{7,103},{8,104... | collective-permute-start | bytes 786440 | tf_op jit(solution)/shard_map/ppermute | solution.py:70
  148.1 9.6 %collective-permute-start.11 = (f32[2,32,1024]{2,1,0:T(8,128)S(1)}, f32[2,32,1024]{2,1,0:T(8,128)S(1)}, u32[]{:S(2)}, u32[]{:S(2)}) collective-permute-start(f32[2,32,1024]{2,1,0:T(8,128)S(1)} %pad_maximum_fusion.13), channel_id=1, source_target_pairs={{0,32},{1,33},{2,34},{3,35},{4,36},{5,37},{6,38},{7,39},{8,40},{9,... | collective-permute-start | bytes 786440 | tf_op jit(solution)/shard_map/ppermute | solution.py:70
  157.7 10.4 %collective-permute-start.13 = (f32[2,32,1024]{2,1,0:T(8,128)S(1)}, f32[2,32,1024]{2,1,0:T(8,128)S(1)}, u32[]{:S(2)}, u32[]{:S(2)}) collective-permute-start(f32[2,32,1024]{2,1,0:T(8,128)S(1)} %pad_maximum_fusion.14), channel_id=1, source_target_pairs={{0,96},{1,97},{2,98},{3,99},{4,100},{5,101},{6,102},{7,103},{8,104... | collective-permute-start | bytes 786440 | tf_op jit(solution)/shard_map/ppermute | solution.py:70
  157.9 11.0 %collective-permute-start.19 = (f32[64,1024]{1,0:T(8,128)S(1)}, f32[64,1024]{1,0:T(8,128)S(1)}, u32[]{:S(2)}, u32[]{:S(2)}) collective-permute-start(f32[64,1024]{1,0:T(8,128)S(1)} %pad_maximum_fusion.15), channel_id=1, source_target_pairs={{0,16},{1,17},{2,18},{3,19},{4,20},{5,21},{6,22},{7,23},{8,24},{9,... | collective-permute-start | bytes 786440 | tf_op jit(solution)/shard_map/ppermute | solution.py:70
  159.9 10.2 %collective-permute-start.12 = (f32[32,1024]{1,0:T(8,128)S(1)}, f32[32,1024]{1,0:T(8,128)S(1)}, u32[]{:S(2)}, u32[]{:S(2)}) collective-permute-start(f32[32,1024]{1,0:T(8,128)S(1)} %get-tuple-element.103), channel_id=1, source_target_pairs={{0,96},{1,97},{2,98},{3,99},{4,100},{5,101},{6,102},{7,103},{8,104... | collective-permute-start | bytes 393224 | tf_op jit(solution)/shard_map/ppermute | solution.py:70
  168.2 5.0 collective-permute-start.14
  178.1 15.6 %collective-permute-start.38 = (f32[128,1024]{1,0:T(8,128)S(1)}, f32[128,1024]{1,0:T(8,128)S(1)}, u32[]{:S(2)}, u32[]{:S(2)}) collective-permute-start(f32[128,1024]{1,0:T(8,128)S(1)} %copy-done.4), channel_id=1, source_target_pairs={{16,0},{32,16},{48,32},{64,48},{80,64},{96,80},{112,96},{8,112},{2... | collective-permute-start | bytes 1572872 | tf_op jit(solution)/shard_map/ppermute | solution.py:414
  181.3 20.8 %collective-permute-start.37 = (f32[128,1024]{1,0:T(8,128)S(1)}, f32[128,1024]{1,0:T(8,128)S(1)}, u32[]{:S(2)}, u32[]{:S(2)}) collective-permute-start(f32[128,1024]{1,0:T(8,128)S(1)} %copy-done.4), channel_id=1, source_target_pairs={{0,16},{16,32},{32,48},{48,64},{64,80},{80,96},{96,112},{112,8},{8... | collective-permute-start | bytes 1572872 | tf_op jit(solution)/shard_map/ppermute | solution.py:413
  207.1 3.4 collective-permute-start.20
  212.8 16.5 %collective-permute-start.21 = (f32[320,256]{1,0:T(8,128)}, f32[320,256]{1,0:T(8,128)S(1)}, u32[]{:S(2)}, u32[]{:S(2)}) collective-permute-start(f32[320,256]{1,0:T(8,128)} %get-tuple-element.83), channel_id=1, source_target_pairs={{0,32},{1,33},{2,34},{3,35},{4,36},{5,37},{6,38},{7,39},{8,40},{9,... | collective-permute-start | bytes 983048 | tf_op jit(solution)/shard_map/ppermute | solution.py:70
  214.8 14.5 %collective-permute-start.23 = (f32[320,256]{1,0:T(8,128)S(1)}, f32[320,256]{1,0:T(8,128)S(1)}, u32[]{:S(2)}, u32[]{:S(2)}) collective-permute-start(f32[320,256]{1,0:T(8,128)S(1)} %get-tuple-element.84), channel_id=1, source_target_pairs={{0,96},{1,97},{2,98},{3,99},{4,100},{5,101},{6,102},{7,103},{8,104... | collective-permute-start | bytes 983048 | tf_op jit(solution)/shard_map/ppermute | solution.py:70
  217.6 28.7 %collective-permute-start.22 = (f32[320,256]{1,0:T(8,128)S(1)}, f32[320,256]{1,0:T(8,128)}, u32[]{:S(2)}, u32[]{:S(2)}) collective-permute-start(f32[320,256]{1,0:T(8,128)S(1)} %get-tuple-element.85), channel_id=1, source_target_pairs={{0,64},{1,65},{2,66},{3,67},{4,68},{5,69},{6,70},{7,71},{8,72},{9,... | collective-permute-start | bytes 983048 | tf_op jit(solution)/shard_map/ppermute | solution.py:70
  217.6 57.8 %copy-start.7 = (f32[1,128,1024]{2,1,0:T(8,128)S(1)}, f32[1,128,1024]{2,1,0:T(8,128)}, u32[]{:S(2)}) copy-start(f32[1,128,1024]{2,1,0:T(8,128)} %fusion.3) | copy-start | bytes 1572868
  247.4 7.1 %collective-permute-start.24 = (f32[80,256]{1,0:T(8,128)S(1)}, f32[80,256]{1,0:T(8,128)S(1)}, u32[]{:S(2)}, u32[]{:S(2)}) collective-permute-start(f32[80,256]{1,0:T(8,128)S(1)} %get-tuple-element.98), channel_id=1, source_target_pairs={{0,16},{1,17},{2,18},{3,19},{4,20},{5,21},{6,22},{7,23},{8,24},{9,... | collective-permute-start | bytes 245768 | tf_op jit(solution)/shard_map/ppermute | solution.py:70
  247.5 7.0 %collective-permute-start.26 = (f32[80,256]{1,0:T(8,128)S(1)}, f32[80,256]{1,0:T(8,128)S(1)}, u32[]{:S(2)}, u32[]{:S(2)}) collective-permute-start(f32[80,256]{1,0:T(8,128)S(1)} %get-tuple-element.99), channel_id=1, source_target_pairs={{0,17},{1,16},{2,19},{3,18},{4,21},{5,20},{6,23},{7,22},{8,25},{9,... | collective-permute-start | bytes 245768 | tf_op jit(solution)/shard_map/ppermute | solution.py:70
  247.7 9.0 %collective-permute-start.25 = (f32[80,256]{1,0:T(8,128)S(1)}, f32[80,256]{1,0:T(8,128)S(1)}, u32[]{:S(2)}, u32[]{:S(2)}) collective-permute-start(f32[80,256]{1,0:T(8,128)S(1)} %get-tuple-element.100), channel_id=1, source_target_pairs={{0,1},{1,0},{2,3},{3,2},{4,5},{5,4},{6,7},{7,6},{8,9},{9,8},{10,11... | collective-permute-start | bytes 245768 | tf_op jit(solution)/shard_map/ppermute | solution.py:70
  256.7 10.0 %collective-permute-start.29 = (f32[80,256]{1,0:T(8,128)S(1)}, f32[80,256]{1,0:T(8,128)S(1)}, u32[]{:S(2)}, u32[]{:S(2)}) collective-permute-start(f32[80,256]{1,0:T(8,128)S(1)} %add_add_fusion.2), channel_id=1, source_target_pairs={{0,6},{1,7},{2,4},{3,5},{4,2},{5,3},{6,0},{7,1},{8,14},{9,15},{10,... | collective-permute-start | bytes 245768 | tf_op jit(solution)/shard_map/ppermute | solution.py:70
  256.8 12.5 %collective-permute-start.28 = (f32[80,256]{1,0:T(8,128)S(1)}, f32[80,256]{1,0:T(8,128)S(1)}, u32[]{:S(2)}, u32[]{:S(2)}) collective-permute-start(f32[80,256]{1,0:T(8,128)S(1)} %add_add_fusion.2), channel_id=1, source_target_pairs={{0,4},{1,5},{2,6},{3,7},{4,0},{5,1},{6,2},{7,3},{8,12},{9,13},{10,... | collective-permute-start | bytes 245768 | tf_op jit(solution)/shard_map/ppermute | solution.py:70
  266.8 4.4 collective-permute-start.27
  271.2 6.6 %collective-permute-start.32 = (f32[80,256]{1,0:T(8,128)S(1)}, f32[80,256]{1,0:T(8,128)S(1)}, u32[]{:S(2)}, u32[]{:S(2)}) collective-permute-start(f32[80,256]{1,0:T(8,128)S(1)} %add_add_fusion.1), channel_id=1, source_target_pairs={{0,17},{1,16},{2,19},{3,18},{4,21},{5,20},{6,23},{7,22},{8,25},{9,... | collective-permute-start | bytes 245768 | tf_op jit(solution)/shard_map/ppermute | solution.py:70
  271.3 6.5 %collective-permute-start.31 = (f32[80,256]{1,0:T(8,128)S(1)}, f32[80,256]{1,0:T(8,128)S(1)}, u32[]{:S(2)}, u32[]{:S(2)}) collective-permute-start(f32[80,256]{1,0:T(8,128)S(1)} %add_add_fusion.1), channel_id=1, source_target_pairs={{0,1},{1,0},{2,3},{3,2},{4,5},{5,4},{6,7},{7,6},{8,9},{9,8},{10,11... | collective-permute-start | bytes 245768 | tf_op jit(solution)/shard_map/ppermute | solution.py:70
  273.4 5.3 collective-permute-start.30
  275.4 35.3 %collective-permute-start.39 = (f32[128,1024]{1,0:T(8,128)S(1)}, f32[128,1024]{1,0:T(8,128)S(1)}, u32[]{:S(2)}, u32[]{:S(2)}) collective-permute-start(f32[128,1024]{1,0:T(8,128)S(1)} %bitcast.171), channel_id=1, source_target_pairs={{0,0},{8,8},{1,16},{9,24},{2,32},{10,40},{3,48},{11,56},{4,64},{12... | collective-permute-start | bytes 1572872 | tf_op jit(solution)/shard_map/ppermute | solution.py:419
  278.8 31.9 %collective-permute-start.34 = (f32[320,256]{1,0:T(8,128)S(1)}, f32[320,256]{1,0:T(8,128)S(1)}, u32[]{:S(2)}, u32[]{:S(2)}) collective-permute-start(f32[320,256]{1,0:T(8,128)S(1)} %get-tuple-element.93), channel_id=1, source_target_pairs={{0,64},{1,65},{2,66},{3,67},{4,68},{5,69},{6,70},{7,71},{8,72},{9,... | collective-permute-start | bytes 983048 | tf_op jit(solution)/shard_map/ppermute | solution.py:70
  278.9 31.8 %collective-permute-start.33 = (f32[320,256]{1,0:T(8,128)S(1)}, f32[320,256]{1,0:T(8,128)S(1)}, u32[]{:S(2)}, u32[]{:S(2)}) collective-permute-start(f32[320,256]{1,0:T(8,128)S(1)} %get-tuple-element.93), channel_id=1, source_target_pairs={{0,32},{1,33},{2,34},{3,35},{4,36},{5,37},{6,38},{7,39},{8,40},{9,... | collective-permute-start | bytes 983048 | tf_op jit(solution)/shard_map/ppermute | solution.py:70
  279.3 31.4 %collective-permute-start.35 = (f32[320,256]{1,0:T(8,128)S(1)}, f32[320,256]{1,0:T(8,128)S(1)}, u32[]{:S(2)}, u32[]{:S(2)}) collective-permute-start(f32[320,256]{1,0:T(8,128)S(1)} %get-tuple-element.93), channel_id=1, source_target_pairs={{0,96},{1,97},{2,98},{3,99},{4,100},{5,101},{6,102},{7,103},{8,104... | collective-permute-start | bytes 983048 | tf_op jit(solution)/shard_map/ppermute | solution.py:70
  310.7 12.0 %collective-permute-start.40 = (f32[128,1024]{1,0:T(8,128)S(1)}, f32[128,1024]{1,0:T(8,128)S(1)}, u32[]{:S(2)}, u32[]{:S(2)}) collective-permute-start(f32[128,1024]{1,0:T(8,128)S(1)} %collective-permute-done.39), channel_id=1, source_target_pairs={{0,1},{1,0},{2,3},{3,2},{4,5},{5,4},{6,7},{7,6},{8,9},{9,8},{10,11... | collective-permute-start | bytes 1572872 | tf_op jit(solution)/shard_map/ppermute | solution.py:70
  312.1 48.4 %collective-permute-start.36 = (f32[1280,256]{1,0:T(8,128)}, f32[1280,256]{1,0:T(8,128)}, u32[]{:S(2)}, u32[]{:S(2)}) collective-permute-start(f32[1280,256]{1,0:T(8,128)} %pad_maximum_fusion.2), channel_id=1, source_target_pairs={{0,8},{1,9},{2,10},{3,11},{4,12},{5,13},{6,14},{7,15},{8,0},{9,1},... | collective-permute-start | bytes 3932168 | tf_op jit(solution)/shard_map/ppermute | solution.py:70
  322.8 11.4 %collective-permute-start.43 = (f32[128,1024]{1,0:T(8,128)S(1)}, f32[128,1024]{1,0:T(8,128)S(1)}, u32[]{:S(2)}, u32[]{:S(2)}) collective-permute-start(f32[128,1024]{1,0:T(8,128)S(1)} %get-tuple-element.86.t0), channel_id=1, source_target_pairs={{0,6},{1,7},{2,4},{3,5},{4,2},{5,3},{6,0},{7,1},{8,14},{9,15},{10,... | collective-permute-start | bytes 1572872 | tf_op jit(solution)/shard_map/ppermute | solution.py:70
  322.9 11.5 %collective-permute-start.41 = (f32[128,1024]{1,0:T(8,128)S(1)}, f32[128,1024]{1,0:T(8,128)S(1)}, u32[]{:S(2)}, u32[]{:S(2)}) collective-permute-start(f32[128,1024]{1,0:T(8,128)S(1)} %get-tuple-element.87.s0), channel_id=1, source_target_pairs={{0,2},{1,3},{2,0},{3,1},{4,6},{5,7},{6,4},{7,5},{8,10},{9,11},{10,... | collective-permute-start | bytes 1572872 | tf_op jit(solution)/shard_map/ppermute | solution.py:70
  334.3 29.3 %collective-permute-start.44 = (f32[2,128,1024]{2,1,0:T(8,128)S(1)}, f32[2,128,1024]{2,1,0:T(8,128)S(1)}, u32[]{:S(2)}, u32[]{:S(2)}) collective-permute-start(f32[2,128,1024]{2,1,0:T(8,128)S(1)} %pad_maximum_fusion.5), channel_id=1, source_target_pairs={{0,2},{1,3},{2,0},{3,1},{4,6},{5,7},{6,4},{7,5},{8,10},{9,11},{10,... | collective-permute-start | bytes 3145736 | tf_op jit(solution)/shard_map/ppermute | solution.py:70
  335.0 28.6 %collective-permute-start.42 = (f32[2,128,1024]{2,1,0:T(8,128)S(1)}, f32[2,128,1024]{2,1,0:T(8,128)}, u32[]{:S(2)}, u32[]{:S(2)}) collective-permute-start(f32[2,128,1024]{2,1,0:T(8,128)S(1)} %pad_maximum_fusion.4), channel_id=1, source_target_pairs={{0,6},{1,7},{2,4},{3,5},{4,2},{5,3},{6,0},{7,1},{8,14},{9,15},{10,... | collective-permute-start | bytes 3145736 | tf_op jit(solution)/shard_map/ppermute | solution.py:70
  (22 other events, 231.2 us)
Sparse Core Ops, SparseCore 0:
  205.4 67.2 all-gather.1

commit v3 on v2

--- a/solution.py
+++ b/solution.py
@@ -62,7 +62,7 @@
         ),
         out_shape=jax.ShapeDtypeStruct((8, LINE, acts), F32),
         compiler_params=pltpu.CompilerParams(vmem_limit_bytes=VMEM_LIMIT),
-        cost_estimate=pl.CostEstimate(flops=6 * 1024 * rows * acts, bytes_accessed=12 << 20, transcendentals=0),
+        cost_estimate=pl.CostEstimate(flops=1 << 20, bytes_accessed=1 << 20, transcendentals=0),
     )(me, value_matrix, value_matrix, inputs)
 
 
@@ -76,25 +76,32 @@
 X = (0, 16, 1, 17)
 
 
-def reduce_y(near, far, blocks):
-    kept = [blocks[0], blocks[far]]
-    got = swap(jnp.stack([blocks[near], blocks[near ^ far]]), Y[near])
-    kept = [kept[0] + got[0], kept[1] + got[1]]
-    return kept[0] + swap(kept[1], Y[far])
-
-
-def scatter_lines(even, odd):
+def y_first(near, blocks):
+    return swap(jnp.stack([blocks[near], blocks[2]]), Y[near])
+
+
+def y_second(near, blocks, got):
+    far = 4 - near
+    kept = blocks[far] + got[1]
+    return blocks[0] + got[0] + swap(kept, Y[far])
+
+
+def scatter_lines(even, odd, first_wait, second_wait):
     got = swap(odd, CORE)
     quarter = LINE // 4
     cut = lambda i, q: even[i, q * quarter : (q + 1) * quarter] + got[i, q * quarter : (q + 1) * quarter]
     half = lambda i, q: jnp.concatenate([cut(i, q), cut(i, q + 1)], 0)
+    pair = lambda m, q: jnp.stack([cut(2 * m, q), cut(2 * m + 1, q)])
     came = swap(jnp.stack([half(2 * m + 1, 0) for m in range(4)]), X_LOW)
+    c = [pair(m, 2) for m in range(4)]
+    d = [pair(m, 3) for m in range(4)]
+    c_got, d_got = first_wait(y_first(1, c), y_first(3, d))
+    c, d = y_second(1, c, c_got), y_second(3, d, d_got)
+    came = second_wait(came)
     own = [half(2 * m, 0) + came[m] for m in range(4)]
-    a = reduce_y(1, 3, [o[:quarter] for o in own])
-    b = reduce_y(3, 1, [o[quarter:] for o in own])
-    pair = lambda m, q: jnp.stack([cut(2 * m, q), cut(2 * m + 1, q)])
-    c = reduce_y(1, 3, [pair(m, 2) for m in range(4)])
-    d = reduce_y(3, 1, [pair(m, 3) for m in range(4)])
+    a = [o[:quarter] for o in own]
+    b = [o[quarter:] for o in own]
+    a, b = y_second(1, a, y_first(1, a)), y_second(3, b, y_first(3, b))
     rest = jnp.concatenate([c[0], d[0]], 0) + swap(jnp.concatenate([c[1], d[1]], 0), X_LOW)
     return jnp.concatenate([a, b, rest], 0)
 
@@ -109,10 +116,11 @@
     return jnp.concatenate([jnp.where(bit, got, mine), jnp.where(bit, mine, got)], 0)
 
 
-def scatter_four(x, place, masks):
+def scatter_four(x, place, masks, wait=lambda *got: got):
     count = x.shape[0] // 4
     own = lambda m: lax.dynamic_slice_in_dim(x, (place ^ m) * count, count, 0)
-    return own(0) + swap(own(1), masks[1]) + swap(own(2), masks[2]) + swap(own(3), masks[3])
+    near, far, across = wait(swap(own(1), masks[1]), swap(own(2), masks[2]), swap(own(3), masks[3]))
+    return own(0) + near + far + across
 
 
 def gather_four(x, place, masks):
@@ -120,27 +128,34 @@
     return jnp.concatenate([lax.dynamic_index_in_dim(parts, place ^ m, 0, False) for m in range(4)], 0)
 
 
-def sum_all(x, row_index, col_index):
-    core, x_low, y = row_index & 1, (row_index >> 1) & 1, row_index >> 2
-    x_place = (col_index & 1) * 2 + x_low
+def tied(*values):
+    return lax.optimization_barrier(values)
+
+
+def sum_start(x, core, y, wait):
     keep, send = halves(x, core == 1)
     x = keep + swap(send, CORE)
-    x = scatter_four(x, y, Y)
+    return scatter_four(x, y, Y, wait)
+
+
+def sum_middle(x, x_place):
     x = scatter_four(x, x_place, X)
-    x = x + swap(x, Z[1]) + swap(x, Z[2]) + swap(x, Z[3])
-    x = gather_four(x, x_place, X)
-    x = gather_four(x, y, Y)
-    return joined(x, swap(x, CORE), core == 1)
-
-
-def gather_rows(x, col_index):
-    pair = joined(x, swap(x, X_HIGH), (col_index & 1) == 1)
-    first, second = pair[:LINE], pair[LINE:]
-    first_near = swap(first, Z[1])
-    second_near = swap(second, Z[3])
-    first_far = swap(jnp.stack([first, first_near]), Z[3])
-    second_far = swap(jnp.stack([second, second_near]), Z[1])
-    return first, first_near, first_far, second, second_near, second_far
+    return x + swap(x, Z[1]) + swap(x, Z[2]) + swap(x, Z[3])
+
+
+def sum_spread(x, x_place, y):
+    return gather_four(gather_four(x, x_place, X), y, Y)
+
+
+def gather_rows_start(line):
+    first, second = line[: LINE // 2], line[LINE // 2 :]
+    pair = jnp.stack([first, swap(first, X_HIGH)])
+    quad = jnp.stack([second] + [swap(second, Z[m]) for m in range(1, 4)])
+    return pair, quad
+
+
+def gather_rows_end(pair, quad):
+    return [pair] + [swap(pair, Z[m]) for m in range(1, 4)] + [quad, swap(quad, X_HIGH)]
 
 
 def gram_kernel(inputs, product, out):
@@ -204,26 +219,16 @@
     return -work[...]
 
 
-def solve_kernel(weight, z, gram, s0, s1, s2, t0, t1, t2, high, low, out, factor, inverses, work, worst):
+def factor_kernel(weight, gram, factor, inverses, work, worst):
     size = PANEL
     mask = lax.broadcasted_iota(jnp.int32, (size, size), 0) == lax.broadcasted_iota(jnp.int32, (size, size), 1)
     eye = jnp.where(mask, 1.0, 0.0).astype(F32)
-    at = lambda k: slice(k * size, (k + 1) * size)
 
     def run(robust):
         for k in range(4):
             for i in range(k, 4):
                 here = gram[block_index(i, k)]
                 factor[block_index(i, k)] = here + weight[0] * eye if i == k else here
-        rows = lambda step, h: pl.ds(pl.multiple_of(((z[0] ^ step) * 2 + h) * LINE, LINE), LINE)
-        out[rows(0, 0), :] = s0[...]
-        out[rows(1, 0), :] = s1[...]
-        out[rows(3, 0), :] = s2[0]
-        out[rows(2, 0), :] = s2[1]
-        out[rows(0, 1), :] = t0[...]
-        out[rows(3, 1), :] = t1[...]
-        out[rows(1, 1), :] = t2[0]
-        out[rows(2, 1), :] = t2[1]
         for k in range(4):
             here = factor[block_index(k, k)]
             if robust:
@@ -233,7 +238,6 @@
                 worst[...] = off if k == 0 else jnp.where(off < worst[...], worst[...], off)
             inverses[k] = inverse
             parts = split(inverse)
-            solved = split(out[:, at(k)])
             columns = [split(factor[block_index(i, k)]) for i in range(k + 1, 4)]
             lefts = []
             for i in range(k + 1, 4):
@@ -243,14 +247,6 @@
             for j in range(k + 1, 4):
                 for i in range(j, 4):
                     factor[block_index(i, j)] -= dot3(lefts[i - k - 1], columns[j - k - 1], NT)
-            for i in range(k + 1, 4):
-                out[:, at(i)] -= dot3(solved, lefts[i - k - 1], NT)
-        for k in range(3, -1, -1):
-            total = dot3(split(out[:, at(k)]), split(inverses[k]), NN)
-            for i in range(k + 1, 4):
-                total = total - dot3(split(out[:, at(i)]), split(factor[block_index(i, k)]), NN)
-            out[:, at(k)] = total
-            high[:, at(k)], low[:, at(k)] = split(total)
 
     run(False)
 
@@ -259,25 +255,62 @@
         run(True)
 
 
-def solve(weight, z, gram, sides):
+def factored(weight, gram):
+    scalar = pl.BlockSpec(memory_space=pltpu.SMEM)
+    array = pl.BlockSpec(memory_space=pltpu.VMEM)
+    return pl.pallas_call(
+        factor_kernel,
+        out_shape=[
+            jax.ShapeDtypeStruct((10, PANEL, PANEL), F32),
+            jax.ShapeDtypeStruct((4, PANEL, PANEL), F32),
+        ],
+        in_specs=[scalar, array],
+        out_specs=[array, array],
+        scratch_shapes=[pltpu.VMEM((PANEL, PANEL), F32), pltpu.VMEM((1, 1), F32)],
+        compiler_params=pltpu.CompilerParams(vmem_limit_bytes=VMEM_LIMIT),
+        cost_estimate=pl.CostEstimate(flops=9 << 30, bytes_accessed=12 << 20, transcendentals=0),
+    )(weight, gram)
+
+
+def solve_kernel(place, factor, inverses, own, near, across, far, quad, other, high, low, out):
+    size = PANEL
+    half = LINE // 2
+    at = lambda k: slice(k * size, (k + 1) * size)
+
+    def put(step, e, second, value):
+        line = (place[0] ^ step) * 2 + (place[1] ^ e)
+        out[pl.ds(pl.multiple_of(line * LINE + second * half, half), half), :] = value
+
+    for step, pair in enumerate((own, near, across, far)):
+        for e in range(2):
+            put(step, e, 0, pair[e])
+    for e, lines in enumerate((quad, other)):
+        for step in range(4):
+            put(step, e, 1, lines[step])
+    for k in range(4):
+        solved = split(out[:, at(k)])
+        for i in range(k + 1, 4):
+            out[:, at(i)] -= dot3(solved, split(factor[block_index(i, k)]), NT)
+    for k in range(3, -1, -1):
+        total = dot3(split(out[:, at(k)]), split(inverses[k]), NN)
+        for i in range(k + 1, 4):
+            total = total - dot3((high[:, at(i)], low[:, at(i)]), split(factor[block_index(i, k)]), NN)
+        high[:, at(k)], low[:, at(k)] = split(total)
+
+
+def solve(place, factors, sides):
     scalar = pl.BlockSpec(memory_space=pltpu.SMEM)
     array = pl.BlockSpec(memory_space=pltpu.VMEM)
     size = 8 * LINE
     return pl.pallas_call(
         solve_kernel,
         out_shape=[jax.ShapeDtypeStruct((size, 4 * PANEL), BF16)] * 2,
-        in_specs=[scalar, scalar] + [array] * 7,
+        in_specs=[scalar] + [array] * 8,
         out_specs=[array, array],
-        scratch_shapes=[
-            pltpu.VMEM((size, 4 * PANEL), F32),
-            pltpu.VMEM((10, PANEL, PANEL), F32),
-            pltpu.VMEM((4, PANEL, PANEL), F32),
-            pltpu.VMEM((PANEL, PANEL), F32),
-            pltpu.VMEM((1, 1), F32),
-        ],
+        scratch_shapes=[pltpu.VMEM((size, 4 * PANEL), F32)],
         compiler_params=pltpu.CompilerParams(vmem_limit_bytes=VMEM_LIMIT),
         cost_estimate=pl.CostEstimate(flops=9 << 30, bytes_accessed=12 << 20, transcendentals=0),
-    )(weight, z, gram, *sides)
+    )(place, *factors, *sides)
 
 
 def downdate_kernel(high, low, first, second, base, out):
@@ -314,20 +347,20 @@
     return diagonal[:, :, None] * centre + COUPLING * neighbours
 
 
-def plant_kernel(place, value, above, below, left, right, rows_diag, cols_diag, cost, out):
-    b = pl.program_id(0)
-    last = pl.num_programs(0) - 1
-    rows = value.shape[0]
+def plant_kernel(start, last, sides, place, *refs):
+    blocks, ends = refs[:9], refs[9 : 9 + sides]
+    rows_diag, cols_diag, cost = refs[9 + sides : 12 + sides]
+    out = refs[-1]
+    b = pl.program_id(0) + start
+    rows = out.shape[0]
     lanes = lax.broadcasted_iota(jnp.int32, (1, LINE), 1)
     inner = lax.broadcasted_iota(jnp.int32, (LINE, 1), 0)
-
-    def column(at):
-        cols = pl.ds(pl.multiple_of(at * LINE, LINE), LINE)
-        return jnp.concatenate([above[:, cols], value[:, cols], below[:, cols]], 0)
-
-    here = column(b)
-    before = jnp.where(b == 0, left[...], column(jnp.maximum(b - 1, 0)))
-    after = jnp.where(b == last, right[...], column(jnp.minimum(b + 1, last)))
+    column = lambda k: jnp.concatenate([blocks[3 * k][...], blocks[3 * k + 1][...], blocks[3 * k + 2][...]], 0)
+    here = column(1)
+    before, after = column(0), column(2)
+    if sides:
+        before = jnp.where(b == 0, ends[0][...], before)
+        after = jnp.where(b == last, ends[1][...], after)
     sides = jnp.where(lanes == 0, 0.0, pltpu.roll(here, 1, 1)) + jnp.where(
         lanes == LINE - 1, 0.0, pltpu.roll(here, LINE - 1, 1)
     )
@@ -343,18 +376,34 @@
         out[a * LINE : (a + 1) * LINE, :] = new + jnp.where(on_diagonal, cost[a : a + 1, :], 0.0)
 
 
-def plant_both(place, value, above, below, left, right, rows_diag, cols_diag, cost):
+def plant_part(start, count, place, value, above, below, left, right, rows_diag, cols_diag, cost, before):
     rows, cols = value.shape
+    last = cols // LINE - 1
     array = pl.BlockSpec(memory_space=pltpu.VMEM)
+    blocks, specs = [], []
+    for step in (-1, 0, 1):
+        index = lambda b, step=step: (0, jnp.clip(b + start + step, 0, last))
+        for x in (above, value, below):
+            blocks.append(x)
+            specs.append(pl.BlockSpec((x.shape[0], LINE), index))
+    sides = [] if left is None else [left, right]
+    operands = [place, *blocks, *sides, rows_diag, cols_diag, cost]
+    specs = [pl.BlockSpec(memory_space=pltpu.SMEM)] + specs + [array] * (3 + len(sides))
+    aliases = {}
+    if before is not None:
+        aliases = {len(operands): 0}
+        operands.append(before)
+        specs.append(pl.BlockSpec(memory_space=pl.ANY))
     return pl.pallas_call(
-        plant_kernel,
-        grid=(cols // LINE,),
-        in_specs=[pl.BlockSpec(memory_space=pltpu.SMEM)] + [array] * 8,
-        out_specs=pl.BlockSpec((rows, LINE), lambda b: (0, b)),
+        functools.partial(plant_kernel, start, last, len(sides)),
+        grid=(count,),
+        in_specs=specs,
+        out_specs=pl.BlockSpec((rows, LINE), lambda b: (0, b + start)),
         out_shape=jax.ShapeDtypeStruct(value.shape, F32),
+        input_output_aliases=aliases,
         compiler_params=pltpu.CompilerParams(vmem_limit_bytes=VMEM_LIMIT),
-        cost_estimate=pl.CostEstimate(flops=32 << 20, bytes_accessed=40 << 20, transcendentals=0),
-    )(place, value, above, below, left, right, rows_diag, cols_diag, cost)
+        cost_estimate=pl.CostEstimate(flops=32 << 20, bytes_accessed=16 << 20, transcendentals=0),
+    )(*operands)
 
 
 def device_of(line):
@@ -378,60 +427,80 @@
     mine_inputs = lax.dynamic_slice_in_dim(inputs, col_index * LINE, LINE, 0)
     mine_inputs = lax.ppermute(mine_inputs, both, trade)
 
-    def shifted(x, down, right):
-        pairs = [
-            (r * 8 + c, (r + down) * 8 + c + right)
-            for r in range(16)
-            for c in range(8)
-            if 0 <= r + down < 16 and 0 <= c + right < 8
-        ]
-        return lax.ppermute(x, both, pairs)
-
-    top, bottom = value_matrix[:LINE], value_matrix[-LINE:]
-    above, below = shifted(bottom, 1, 0), shifted(top, -1, 0)
-    left = [
-        shifted(bottom[:, -LINE:], 1, 1),
-        shifted(value_matrix[:, -LINE:], 0, 1),
-        shifted(top[:, -LINE:], -1, 1),
-    ]
-    right = [
-        shifted(bottom[:, :LINE], 1, -1),
-        shifted(value_matrix[:, :LINE], 0, -1),
-        shifted(top[:, :LINE], -1, -1),
-    ]
-    odd = product_lines(me, value_matrix, inputs, 1)
-    held = (value_matrix, inputs, mine_inputs, above, below, left, right)
-    value_here, inputs_here, mine_inputs, above, below, left, right = lax.optimization_barrier(held)
-    even = product_lines(me, value_here, inputs_here, 0)
-    product = scatter_lines(even, odd)
-
-    gram = gram_blocks(mine_inputs, product)
-    product, gram = lax.optimization_barrier((product, gram))
-    gram = sum_all(gram.reshape(10 * PANEL, PANEL), row_index, col_index).reshape(10, PANEL, PANEL)
-
-    lines = 128
-    over = lax.ppermute(product, both, [(device_of(i), device_of(i + 1)) for i in range(lines - 1)])
-    under = lax.ppermute(product, both, [(device_of(i + 1), device_of(i)) for i in range(lines - 1)])
-    line = col_index * 16 + line_of(row_index)
-    diagonal = lax.dynamic_slice_in_dim(plant_diag, line, 1, 0)
-    gain = stencil_first(jnp.stack([over, product, under]), diagonal)[0]
-    gain_cols = lax.all_gather(gain, "row", axis=0)
-    gain_rows = gather_rows(lax.ppermute(gain, both, trade), col_index)
-
-    place = jnp.stack([row_index * lines_rows, col_index * lines_cols]).astype(jnp.int32)
-    base = plant_both(
-        place,
+    def shifted(x, axis, by):
+        count = lax.axis_size(axis)
+        return lax.ppermute(x, axis, [(i, i + by) for i in range(count) if 0 <= i + by < count])
+
+    above = shifted(value_matrix[-LINE:], "row", 1)
+    below = shifted(value_matrix[:LINE], "row", -1)
+    tall = lambda cols: jnp.concatenate([above[:, cols], value_matrix[:, cols], below[:, cols]], 0)
+    left = shifted(tall(slice(-LINE, None)), "col", 1)
+    right = shifted(tall(slice(None, LINE)), "col", -1)
+    operands = (
+        jnp.stack([row_index * lines_rows, col_index * lines_cols]).astype(jnp.int32),
         value_matrix,
         above,
         below,
-        jnp.concatenate(left, 0),
-        jnp.concatenate(right, 0),
+        left,
+        right,
         diag_rows.T,
         diag_cols,
         state_cost.reshape(lines_rows, grid_side),
     )
-    z = (col_index >> 1).astype(jnp.int32).reshape(1)
-    solved = solve(control_weight, z, gram, gain_rows)
+    odd = product_lines(me, value_matrix, inputs, 1)
+    even = product_lines(me, value_matrix, inputs, 0)
+    held = {}
+
+    def first_wait(c_got, d_got):
+        base = plant_part(4, 4, *operands[:4], None, None, *operands[6:], None)
+        base = plant_part(8, 4, *operands[:4], None, None, *operands[6:], base)
+        c_got, d_got, held["base"] = tied(c_got, d_got, base)
+        return c_got, d_got
+
+    def second_wait(came):
+        came, held["inputs"], held["left"], held["right"] = tied(came, mine_inputs, left, right)
+        return came
+
+    product = scatter_lines(even, odd, first_wait, second_wait)
+    mine_inputs = held["inputs"]
+    operands = (*operands[:4], held["left"], held["right"], *operands[6:])
+
+    gram = gram_blocks(mine_inputs, product)
+    product, gram = tied(product, gram)
+    core, x_low, y = row_index & 1, (row_index >> 1) & 1, row_index >> 2
+    x_high, z = col_index & 1, col_index >> 1
+    x_place = x_high * 2 + x_low
+
+    lines = grid_side
+    over = lax.ppermute(product, both, [(device_of(i), device_of(i + 1)) for i in range(lines - 1)])
+    under = lax.ppermute(product, both, [(device_of(i + 1), device_of(i)) for i in range(lines - 1)])
+
+    def third_wait(*got):
+        base = plant_part(0, 4, *operands, held["base"])
+        *got, held["base"] = tied(*got, base)
+        return got
+
+    total = sum_start(gram.reshape(10 * PANEL, PANEL), core, y, third_wait)
+    line = col_index * 16 + line_of(row_index)
+    diagonal = lax.dynamic_slice_in_dim(plant_diag, line, 1, 0)
+    gain = stencil_first(jnp.stack([over, product, under]), diagonal)[0]
+    gain, total = tied(gain, total)
+
+    gain_cols = lax.all_gather(gain, "row", axis=0)
+    traded = lax.ppermute(gain, both, trade)
+    total = sum_middle(total, x_place)
+    traded, total = tied(traded, total)
+
+    pair, quad = gather_rows_start(traded)
+    total = sum_spread(total, x_place, y)
+    pair, quad, total = tied(pair, quad, total)
+
+    sides = gather_rows_end(pair, quad)
+    base = plant_part(12, 4, *operands, held["base"])
+    total = joined(total, swap(total, CORE), core == 1)
+    total, base = tied(total, base)
+    factors = factored(control_weight, total.reshape(10, PANEL, PANEL))
+    solved = solve(jnp.stack([z, x_high]).astype(jnp.int32), factors, sides)
     return downdate(solved, gain_cols, base)
 
 

time: 594 us -> 518 us (0.87)
  the two profiles are of different devices: /device:TPU:24 before, /device:TPU:1 now
where the time goes in v3:
time: 518 us; the launch traced here: 509 us
  Pallas kernels  263 us (51%)
  waiting for transfers between devices  103 us (20%)
  starting transfers between devices  94.2 us (18%)
  other arithmetic  22.4 us (4%)
  between operations  15.1 us (3%)
  local copies, waits for them, and re-layouts  10.5 us (2%)
    pallas_call x1, Pallas kernels, factored(): pl.pallas_call(factor_kernel, out_shape=[jax.ShapeDtypeStruct((10, PANEL,...  176 us
    ppermute x36, waiting for transfers between devices, swap(): return lax.ppermute(x, ('row', 'col'), [(i, i ^ mask) for i in range(128)])  71.1 us
    ppermute x36, starting transfers between devices, swap(): return lax.ppermute(x, ('row', 'col'), [(i, i ^ mask) for i in range(128)])  68.6 us
    pallas_call x4, Pallas kernels, plant_part(): pl.pallas_call(functools.partial(plant_kernel, start, last, len(sides)),...  27.9 us
    ppermute x4, waiting for transfers between devices, shifted(): lax.ppermute(x, axis, [(i, i + by) for i in range(count) if 0 <= i + by <...  26.8 us
    pallas_call x2, Pallas kernels, product_lines(): pl.pallas_call(product_kernel, grid_spec=pltpu.PrefetchScalarGridSpec(num...  23.4 us
    pallas_call x1, Pallas kernels, downdate(): pl.pallas_call(downdate_kernel, grid=(8,), in_specs=[whole, whole, pl.Blo...  19.2 us
    pallas_call x1, Pallas kernels, solve(): pl.pallas_call(solve_kernel, out_shape=[jax.ShapeDtypeStruct((size, 4 * P...  12.6 us
  transfers between devices with their start and end apart: 45, of which 19 were waited for; matrix products, arithmetic and copies ran while one was open for 5% of the time, Pallas kernels for 45%

profile of v3, /device:TPU:1, one launch (start us, length us, event | category | flops | bytes accessed | tf_op | source)
XLA Modules:
  0.0 508.8 jit_solution(13411469818315641508)
XLA Ops:
  6.5 11.7 %shard_map.56 = f32[8,128,1024]{2,1,0:T(8,128)} custom-call(s32[1]{0:T(128)} %bitcast.3.me_ref, f32[1024,2048]{1,0:T(8,128)} %refs_7_.7, f32[1024,2048]{1,0:T(8,128)} %refs_7_.7, f32[1024,1024]{1,0:T(8,128)} %inputs.3), custom_call_target="tpu_custom_call" | custom-call | flops 1048576 | bytes 1048576 | tf_op jit(solution)/shard_map/pallas_call | solution.py:50
  19.7 2.7 fusion.32
  24.3 3.6 collective-permute-start.3
  29.8 5.3 %collective-permute-start.2 = (f32[128,1024]{1,0:T(8,128)}, f32[128,1024]{1,0:T(8,128)}, u32[]{:S(2)}, u32[]{:S(2)}) collective-permute-start(f32[128,1024]{1,0:T(8,128)} %constant_dynamic-slice_fusion.8), channel_id=1, source_target_pairs={{0,0},{8,8},{1,16},{9,24},{2,32},{10,40},{3,48},{11,56},{4,64},{12... | collective-permute-start | bytes 1572872 | tf_op jit(solution)/shard_map/ppermute | solution.py:428
  35.9 11.8 %shard_map.55 = f32[8,128,1024]{2,1,0:T(8,128)} custom-call(s32[1]{0:T(128)} %bitcast.3.me_ref, f32[1024,2048]{1,0:T(8,128)} %refs_7_.7, f32[1024,2048]{1,0:T(8,128)} %refs_7_.7, f32[1024,1024]{1,0:T(8,128)} %inputs.3), custom_call_target="tpu_custom_call" | custom-call | flops 1048576 | bytes 1048576 | tf_op jit(solution)/shard_map/pallas_call | solution.py:50
  56.5 3.0 collective-permute-start.12
  62.5 2.2 collective-permute-start.1
  64.8 5.1 collective-permute-start.5
  69.9 6.8 %shard_map.57.refs_12_ = f32[1024,2048]{1,0:T(8,128)} custom-call(s32[2]{0:T(128)} %pad_add_fusion.1.place, f32[128,2048]{1,0:T(8,128)} %copy-done.3, f32[1024,2048]{1,0:T(8,128)} %refs_7_.7, f32[128,2048]{1,0:T(8,128)} %copy-done.2, f32[128,2048]{1,0:T(8,128)} %copy-done.3, f32[1024,2048]{1,0:T(8,128)} %refs_7_.7, f32[128,2048]{1,0:T(8,128)} %copy-done.2, ...), custom_call_target="tpu_custom_call" | custom-call | flops 33554432 | bytes 16777216 | tf_op jit(solution)/shard_map/pallas_call | solution.py:397
  76.7 6.7 %shard_map.58.refs_14_ = f32[1024,2048]{1,0:T(8,128)} custom-call(s32[2]{0:T(128)} %pad_add_fusion.1.place, f32[128,2048]{1,0:T(8,128)} %copy-done.3, f32[1024,2048]{1,0:T(8,128)} %refs_7_.7, f32[128,2048]{1,0:T(8,128)} %copy-done.2, f32[128,2048]{1,0:T(8,128)} %copy-done.3, f32[1024,2048]{1,0:T(8,128)} %refs_7_.7, ...), custom_call_target="tpu_custom_call", output_to_operand_aliasing={{}: (13, {})} | custom-call | flops 33554432 | bytes 16777216 | tf_op jit(solution)/shard_map/pallas_call | solution.py:397
  85.0 5.2 %collective-permute-done.14 = f32[2,32,1024]{2,1,0:T(8,128)S(1)} collective-permute-done((f32[2,32,1024]{2,1,0:T(8,128)S(1)}, f32[2,32,1024]{2,1,0:T(8,128)S(1)}, u32[]{:S(2)}, u32[]{:S(2)}) %collective-permute-start.14) | collective-permute-done | bytes 262176 | tf_op jit(solution)/shard_map/ppermute | solution.py:70
  90.5 10.9 %collective-permute-done.5.refs_9_ = f32[1280,128]{1,0:T(8,128)S(1)} collective-permute-done((f32[1280,128]{1,0:T(8,128)S(1)}, f32[1280,128]{1,0:T(8,128)S(1)}, u32[]{:S(2)}, u32[]{:S(2)}) %collective-permute-start.5) | collective-permute-done | bytes 655392 | tf_op jit(solution)/shard_map/ppermute | solution.py:432
  101.4 15.9 %collective-permute-done.6.refs_10_ = f32[1280,128]{1,0:T(8,128)} collective-permute-done((f32[1280,128]{1,0:T(8,128)S(1)}, f32[1280,128]{1,0:T(8,128)}, u32[]{:S(2)}, u32[]{:S(2)}) %collective-permute-start.6) | collective-permute-done | bytes 655392 | tf_op jit(solution)/shard_map/ppermute | solution.py:432
  117.7 5.1 %collective-permute-done.7 = f32[2,32,1024]{2,1,0:T(8,128)S(1)} collective-permute-done((f32[2,32,1024]{2,1,0:T(8,128)S(1)}, f32[2,32,1024]{2,1,0:T(8,128)S(1)}, u32[]{:S(2)}, u32[]{:S(2)}) %collective-permute-start.7) | collective-permute-done | bytes 262176 | tf_op jit(solution)/shard_map/ppermute | solution.py:70
  123.4 2.5 collective-permute-start.8
  125.9 3.5 collective-permute-done.9
  130.8 3.0 collective-permute-done.10
  134.7 3.9 shard_map.59
  138.6 2.0 slice_select_fusion.1
  140.7 6.1 %collective-permute-start.18 = (f32[1280,256]{1,0:T(8,128)S(1)}, f32[1280,256]{1,0:T(8,128)}, u32[]{:S(2)}, u32[]{:S(2)}) collective-permute-start(f32[1280,256]{1,0:T(8,128)S(1)} %bitcast.160), channel_id=1, source_target_pairs={{0,8},{1,9},{2,10},{3,11},{4,12},{5,13},{6,14},{7,15},{8,0},{9,1},... | collective-permute-start | bytes 3932168 | tf_op jit(solution)/shard_map/ppermute | solution.py:70
  148.6 5.8 %collective-permute-start.17 = (f32[128,1024]{1,0:T(8,128)S(1)}, f32[128,1024]{1,0:T(8,128)}, u32[]{:S(2)}, u32[]{:S(2)}) collective-permute-start(f32[128,1024]{1,0:T(8,128)S(1)} %copy-done.5), channel_id=1, source_target_pairs={{16,0},{32,16},{48,32},{64,48},{80,64},{96,80},{112,96},{8,112},{2... | collective-permute-start | bytes 1572872 | tf_op jit(solution)/shard_map/ppermute | solution.py:476
  156.7 3.9 collective-permute-start.21
  160.5 7.1 %shard_map.60.refs_14_ = f32[1024,2048]{1,0:T(8,128)} custom-call(s32[2]{0:T(128)} %pad_add_fusion.1.place, f32[128,2048]{1,0:T(8,128)} %copy-done.3, f32[1024,2048]{1,0:T(8,128)} %refs_7_.7, f32[128,2048]{1,0:T(8,128)} %copy-done.2, f32[128,2048]{1,0:T(8,128)} %copy-done.3, f32[1024,2048]{1,0:T(8,128)} %refs_7_.7, ...), custom_call_target="tpu_custom_call", output_to_operand_aliasing={{}: (15, {})} | custom-call | flops 33554432 | bytes 16777216 | tf_op jit(solution)/shard_map/pallas_call | solution.py:397
  167.6 5.3 %collective-permute-done.17 = f32[128,1024]{1,0:T(8,128)} collective-permute-done((f32[128,1024]{1,0:T(8,128)S(1)}, f32[128,1024]{1,0:T(8,128)}, u32[]{:S(2)}, u32[]{:S(2)}) %collective-permute-start.17) | collective-permute-done | bytes 524320 | tf_op jit(solution)/shard_map/ppermute | solution.py:476
  172.9 2.2 fusion.4
  175.1 2.2 collective-permute-done.20
  177.3 2.4 collective-permute-done.21
  180.9 3.0 collective-permute-start.25
  183.9 6.0 %collective-permute-start.24 = (f32[80,256]{1,0:T(8,128)S(1)}, f32[80,256]{1,0:T(8,128)S(1)}, u32[]{:S(2)}, u32[]{:S(2)}) collective-permute-start(f32[80,256]{1,0:T(8,128)S(1)} %get-tuple-element.124), channel_id=1, source_target_pairs={{0,1},{1,0},{2,3},{3,2},{4,5},{5,4},{6,7},{7,6},{8,9},{9,8},{10,11... | collective-permute-start | bytes 245768 | tf_op jit(solution)/shard_map/ppermute | solution.py:70
  193.2 4.6 collective-permute-start.28
  199.7 5.5 %collective-permute-done.28 = f32[80,256]{1,0:T(8,128)S(1)} collective-permute-done((f32[80,256]{1,0:T(8,128)S(1)}, f32[80,256]{1,0:T(8,128)S(1)}, u32[]{:S(2)}, u32[]{:S(2)}) %collective-permute-start.28) | collective-permute-done | bytes 81952 | tf_op jit(solution)/shard_map/ppermute | solution.py:70
  205.2 14.0 %collective-permute-done.27 = f32[80,256]{1,0:T(8,128)S(1)} collective-permute-done((f32[80,256]{1,0:T(8,128)S(1)}, f32[80,256]{1,0:T(8,128)S(1)}, u32[]{:S(2)}, u32[]{:S(2)}) %collective-permute-start.27) | collective-permute-done | bytes 81952 | tf_op jit(solution)/shard_map/ppermute | solution.py:70
  219.2 2.6 collective-permute-done.26
  221.9 2.6 collective-permute-start.35
  226.0 4.0 collective-permute-start.31
  233.3 3.5 collective-permute-start.38
  236.8 9.5 %collective-permute-done.29 = f32[64,1024]{1,0:T(8,128)S(1)} collective-permute-done((f32[64,1024]{1,0:T(8,128)S(1)}, f32[64,1024]{1,0:T(8,128)S(1)}, u32[]{:S(2)}, u32[]{:S(2)}) %collective-permute-start.29) | collective-permute-done | bytes 262176 | tf_op jit(solution)/shard_map/ppermute | solution.py:70
  246.3 3.1 collective-permute-start.36
  249.5 2.5 pad_maximum_fusion.4.quad
  252.0 7.6 %collective-permute-done.37 = f32[320,256]{1,0:T(8,128)S(1)} collective-permute-done((f32[320,256]{1,0:T(8,128)S(1)}, f32[320,256]{1,0:T(8,128)S(1)}, u32[]{:S(2)}, u32[]{:S(2)}) %collective-permute-start.37) | collective-permute-done | bytes 327712 | tf_op jit(solution)/shard_map/ppermute | solution.py:70
  259.6 5.2 %collective-permute-done.36 = f32[320,256]{1,0:T(8,128)S(1)} collective-permute-done((f32[320,256]{1,0:T(8,128)S(1)}, f32[320,256]{1,0:T(8,128)S(1)}, u32[]{:S(2)}, u32[]{:S(2)}) %collective-permute-start.36) | collective-permute-done | bytes 327712 | tf_op jit(solution)/shard_map/ppermute | solution.py:70
  265.1 2.2 collective-permute-start.39
  268.5 7.2 %shard_map.61.base = f32[1024,2048]{1,0:T(8,128)} custom-call(s32[2]{0:T(128)} %pad_add_fusion.1.place, f32[128,2048]{1,0:T(8,128)} %copy-done.3, f32[1024,2048]{1,0:T(8,128)} %refs_7_.7, f32[128,2048]{1,0:T(8,128)} %copy-done.2, f32[128,2048]{1,0:T(8,128)} %copy-done.3, f32[1024,2048]{1,0:T(8,128)} %refs_7_.7, ...), custom_call_target="tpu_custom_call", output_to_operand_aliasing={{}: (15, {})} | custom-call | flops 33554432 | bytes 16777216 | tf_op jit(solution)/shard_map/pallas_call | solution.py:397
  275.7 10.2 %collective-permute-start.40 = (f32[2,64,1024]{2,1,0:T(8,128)S(1)}, f32[2,64,1024]{2,1,0:T(8,128)S(1)}, u32[]{:S(2)}, u32[]{:S(2)}) collective-permute-start(f32[2,64,1024]{2,1,0:T(8,128)S(1)} %pad_maximum_fusion.10.own), channel_id=1, source_target_pairs={{0,2},{1,3},{2,0},{3,1},{4,6},{5,7},{6,4},{7,5},{8,10},{9,11},{10,... | collective-permute-start | bytes 1572872 | tf_op jit(solution)/shard_map/ppermute | solution.py:70
  285.9 2.5 collective-permute-start.42
  291.8 176.4 %shard_map.62 = (f32[10,256,256]{2,1,0:T(8,128)}, f32[4,256,256]{2,1,0:T(8,128)}) custom-call(f32[1]{0:T(128)S(6)} %copy.14.weight, f32[10,256,256]{2,1,0:T(8,128)} %bitcast.155), custom_call_target="tpu_custom_call" | custom-call | flops 9663676416 | bytes 12582912 | tf_op jit(solution)/shard_map/pallas_call | solution.py:261
  469.7 12.6 %shard_map.63 = (bf16[1024,1024]{1,0:T(8,128)(2,1)}, bf16[1024,1024]{1,0:T(8,128)(2,1)}) custom-call(s32[2]{0:T(128)} %pad_add_fusion.place, f32[10,256,256]{2,1,0:T(8,128)} %get-tuple-element.50.factor, f32[4,256,256]{2,1,0:T(8,128)} %get-tuple-element.51.inverses, f32[2,64,1024]{2,1,0:T(8,128)} %copy-done.9, f32[2,64,1024]{2,1,0:T(8,128)} %copy-done.13, ...), custom_call_target="tpu_custom_call" | custom-call | flops 9663676416 | bytes 12582912 | tf_op jit(solution)/shard_map/pallas_call | solution.py:305
  482.2 19.2 %shard_map.64 = f32[1024,2048]{1,0:T(8,128)} custom-call(bf16[1024,1024]{1,0:T(8,128)(2,1)} %get-tuple-element.54.high, bf16[1024,1024]{1,0:T(8,128)(2,1)} %get-tuple-element.55.low, f32[16,128,1024]{2,1,0:T(8,128)} %bitcast.174, f32[16,128,1024]{2,1,0:T(8,128)} %bitcast.175, f32[1024,2048]{1,0:T(8,128)} %shard_map.61.base), custom_call_target="tpu_custom_call" | custom-call | flops 12884901888 | bytes 29360128 | tf_op jit(solution)/shard_map/pallas_call | solution.py:326
  (146 shorter events, 43.9 us)
Async XLA Ops:
  6.5 28.6 %copy-start = (f32[128,128]{1,0:T(8,128)S(1)}, f32[128,128]{1,0:T(8,128)}, u32[]{:S(2)}) copy-start(f32[128,128]{1,0:T(8,128)} %param.7) | copy-start | bytes 196612
  6.5 475.7 %all-gather.3.cloned.1.call-start = ((), (), s32[]{:S(2)}) async-start(), calls=%async_computation | async-start | bytes 8912896 | tf_op jit(solution)/shard_map/all_gather | solution.py:489
  18.2 32.7 %collective-permute-start = (f32[8,128,1024]{2,1,0:T(8,128)}, f32[8,128,1024]{2,1,0:T(8,128)}, u32[]{:S(2)}, u32[]{:S(2)}) collective-permute-start(f32[8,128,1024]{2,1,0:T(8,128)} %shard_map.56), channel_id=1, source_target_pairs={{0,8},{1,9},{2,10},{3,11},{4,12},{5,13},{6,14},{7,15},{8,0},{9,1},... | collective-permute-start | bytes 12582920 | tf_op jit(solution)/shard_map/ppermute | solution.py:70
  22.4 27.8 %collective-permute-start.4 = (f32[128,2048]{1,0:T(8,128)}, f32[128,2048]{1,0:T(8,128)S(1)}, u32[]{:S(2)}, u32[]{:S(2)}) collective-permute-start(f32[128,2048]{1,0:T(8,128)} %get-tuple-element.91), channel_id=1, source_target_pairs={{8,0},{16,8},{24,16},{32,24},{40,32},{48,40},{56,48},{64,56},{72,6... | collective-permute-start | bytes 3145736 | tf_op jit(solution)/shard_map/ppermute | solution.py:432
  24.3 25.9 %collective-permute-start.3 = (f32[128,2048]{1,0:T(8,128)S(1)}, f32[128,2048]{1,0:T(8,128)S(1)}, u32[]{:S(2)}, u32[]{:S(2)}) collective-permute-start(f32[128,2048]{1,0:T(8,128)S(1)} %get-tuple-element.92), channel_id=1, source_target_pairs={{0,8},{8,16},{16,24},{24,32},{32,40},{40,48},{48,56},{56,64},{64,7... | collective-permute-start | bytes 3145736 | tf_op jit(solution)/shard_map/ppermute | solution.py:432
  29.8 60.7 %collective-permute-start.2 = (f32[128,1024]{1,0:T(8,128)}, f32[128,1024]{1,0:T(8,128)}, u32[]{:S(2)}, u32[]{:S(2)}) collective-permute-start(f32[128,1024]{1,0:T(8,128)} %constant_dynamic-slice_fusion.8), channel_id=1, source_target_pairs={{0,0},{8,8},{1,16},{9,24},{2,32},{10,40},{3,48},{11,56},{4,64},{12... | collective-permute-start | bytes 1572872 | tf_op jit(solution)/shard_map/ppermute | solution.py:428
  53.9 29.6 %collective-permute-start.11 = (f32[2,2,32,1024]{3,2,1,0:T(8,128)}, f32[2,2,32,1024]{3,2,1,0:T(8,128)S(1)}, u32[]{:S(2)}, u32[]{:S(2)}) collective-permute-start(f32[2,2,32,1024]{3,2,1,0:T(8,128)} %pad_maximum_fusion.7), channel_id=1, source_target_pairs={{0,32},{1,33},{2,34},{3,35},{4,36},{5,37},{6,38},{7,39},{8,40},{9,... | collective-permute-start | bytes 1572872 | tf_op jit(solution)/shard_map/ppermute | solution.py:70
  56.5 28.3 %collective-permute-start.12 = (f32[2,2,32,1024]{3,2,1,0:T(8,128)}, f32[2,2,32,1024]{3,2,1,0:T(8,128)S(1)}, u32[]{:S(2)}, u32[]{:S(2)}) collective-permute-start(f32[2,2,32,1024]{3,2,1,0:T(8,128)} %pad_maximum_fusion.8), channel_id=1, source_target_pairs={{0,96},{1,97},{2,98},{3,99},{4,100},{5,101},{6,102},{7,103},{8,104... | collective-permute-start | bytes 1572872 | tf_op jit(solution)/shard_map/ppermute | solution.py:70
  62.5 54.8 %collective-permute-start.1 = (f32[4,64,1024]{2,1,0:T(8,128)S(1)}, f32[4,64,1024]{2,1,0:T(8,128)S(1)}, u32[]{:S(2)}, u32[]{:S(2)}) collective-permute-start(f32[4,64,1024]{2,1,0:T(8,128)S(1)} %pad_maximum_fusion.3), channel_id=1, source_target_pairs={{0,16},{1,17},{2,18},{3,19},{4,20},{5,21},{6,22},{7,23},{8,24},{9,... | collective-permute-start | bytes 3145736 | tf_op jit(solution)/shard_map/ppermute | solution.py:70
  64.8 36.7 %collective-permute-start.5 = (f32[1280,128]{1,0:T(8,128)S(1)}, f32[1280,128]{1,0:T(8,128)S(1)}, u32[]{:S(2)}, u32[]{:S(2)}) collective-permute-start(f32[1280,128]{1,0:T(8,128)S(1)} %pad_maximum_fusion.5), channel_id=1, source_target_pairs={{0,1},{1,2},{2,3},{3,4},{4,5},{5,6},{6,7},{8,9},{9,10},{10,11},{11... | collective-permute-start | bytes 1966088 | tf_op jit(solution)/shard_map/ppermute | solution.py:432
  83.5 33.8 %collective-permute-start.6 = (f32[1280,128]{1,0:T(8,128)S(1)}, f32[1280,128]{1,0:T(8,128)}, u32[]{:S(2)}, u32[]{:S(2)}) collective-permute-start(f32[1280,128]{1,0:T(8,128)S(1)} %pad_maximum_fusion.6), channel_id=1, source_target_pairs={{1,0},{2,1},{3,2},{4,3},{5,4},{6,5},{7,6},{9,8},{10,9},{11,10},{12... | collective-permute-start | bytes 1966088 | tf_op jit(solution)/shard_map/ppermute | solution.py:432
  84.8 5.3 %collective-permute-start.14 = (f32[2,32,1024]{2,1,0:T(8,128)S(1)}, f32[2,32,1024]{2,1,0:T(8,128)S(1)}, u32[]{:S(2)}, u32[]{:S(2)}) collective-permute-start(f32[2,32,1024]{2,1,0:T(8,128)S(1)} %maximum_add_fusion.7), channel_id=1, source_target_pairs={{0,32},{1,33},{2,34},{3,35},{4,36},{5,37},{6,38},{7,39},{8,40},{9,... | collective-permute-start | bytes 786440 | tf_op jit(solution)/shard_map/ppermute | solution.py:70
  90.1 27.5 %collective-permute-start.13 = (f32[2,32,1024]{2,1,0:T(8,128)S(1)}, f32[2,32,1024]{2,1,0:T(8,128)S(1)}, u32[]{:S(2)}, u32[]{:S(2)}) collective-permute-start(f32[2,32,1024]{2,1,0:T(8,128)S(1)} %maximum_add_fusion.5), channel_id=1, source_target_pairs={{0,96},{1,97},{2,98},{3,99},{4,100},{5,101},{6,102},{7,103},{8,104... | collective-permute-start | bytes 786440 | tf_op jit(solution)/shard_map/ppermute | solution.py:70
  117.5 5.3 %collective-permute-start.7 = (f32[2,32,1024]{2,1,0:T(8,128)S(1)}, f32[2,32,1024]{2,1,0:T(8,128)S(1)}, u32[]{:S(2)}, u32[]{:S(2)}) collective-permute-start(f32[2,32,1024]{2,1,0:T(8,128)S(1)} %pad_maximum_fusion.13), channel_id=1, source_target_pairs={{0,32},{1,33},{2,34},{3,35},{4,36},{5,37},{6,38},{7,39},{8,40},{9,... | collective-permute-start | bytes 786440 | tf_op jit(solution)/shard_map/ppermute | solution.py:70
  122.9 6.5 %collective-permute-start.9 = (f32[2,32,1024]{2,1,0:T(8,128)S(1)}, f32[2,32,1024]{2,1,0:T(8,128)S(1)}, u32[]{:S(2)}, u32[]{:S(2)}) collective-permute-start(f32[2,32,1024]{2,1,0:T(8,128)S(1)} %pad_maximum_fusion.14), channel_id=1, source_target_pairs={{0,96},{1,97},{2,98},{3,99},{4,100},{5,101},{6,102},{7,103},{8,104... | collective-permute-start | bytes 786440 | tf_op jit(solution)/shard_map/ppermute | solution.py:70
  123.3 6.4 %collective-permute-start.15 = (f32[64,1024]{1,0:T(8,128)S(1)}, f32[64,1024]{1,0:T(8,128)S(1)}, u32[]{:S(2)}, u32[]{:S(2)}) collective-permute-start(f32[64,1024]{1,0:T(8,128)S(1)} %pad_maximum_fusion.15), channel_id=1, source_target_pairs={{0,16},{1,17},{2,18},{3,19},{4,20},{5,21},{6,22},{7,23},{8,24},{9,... | collective-permute-start | bytes 786440 | tf_op jit(solution)/shard_map/ppermute | solution.py:70
  123.4 7.4 %collective-permute-start.8 = (f32[32,1024]{1,0:T(8,128)S(1)}, f32[32,1024]{1,0:T(8,128)S(1)}, u32[]{:S(2)}, u32[]{:S(2)}) collective-permute-start(f32[32,1024]{1,0:T(8,128)S(1)} %get-tuple-element.127), channel_id=1, source_target_pairs={{0,96},{1,97},{2,98},{3,99},{4,100},{5,101},{6,102},{7,103},{8,104... | collective-permute-start | bytes 393224 | tf_op jit(solution)/shard_map/ppermute | solution.py:70
  129.4 4.4 collective-permute-start.10
  140.7 13.8 %collective-permute-start.18 = (f32[1280,256]{1,0:T(8,128)S(1)}, f32[1280,256]{1,0:T(8,128)}, u32[]{:S(2)}, u32[]{:S(2)}) collective-permute-start(f32[1280,256]{1,0:T(8,128)S(1)} %bitcast.160), channel_id=1, source_target_pairs={{0,8},{1,9},{2,10},{3,11},{4,12},{5,13},{6,14},{7,15},{8,0},{9,1},... | collective-permute-start | bytes 3932168 | tf_op jit(solution)/shard_map/ppermute | solution.py:70
  146.7 20.9 %collective-permute-start.16 = (f32[128,1024]{1,0:T(8,128)S(1)}, f32[128,1024]{1,0:T(8,128)}, u32[]{:S(2)}, u32[]{:S(2)}) collective-permute-start(f32[128,1024]{1,0:T(8,128)S(1)} %copy-done.5), channel_id=1, source_target_pairs={{0,16},{16,32},{32,48},{48,64},{64,80},{80,96},{96,112},{112,8},{8... | collective-permute-start | bytes 1572872 | tf_op jit(solution)/shard_map/ppermute | solution.py:475
  148.6 24.3 %collective-permute-start.17 = (f32[128,1024]{1,0:T(8,128)S(1)}, f32[128,1024]{1,0:T(8,128)}, u32[]{:S(2)}, u32[]{:S(2)}) collective-permute-start(f32[128,1024]{1,0:T(8,128)S(1)} %copy-done.5), channel_id=1, source_target_pairs={{16,0},{32,16},{48,32},{64,48},{80,64},{96,80},{112,96},{8,112},{2... | collective-permute-start | bytes 1572872 | tf_op jit(solution)/shard_map/ppermute | solution.py:476
  156.7 18.5 %collective-permute-start.19 = (f32[320,256]{1,0:T(8,128)}, f32[320,256]{1,0:T(8,128)S(1)}, u32[]{:S(2)}, u32[]{:S(2)}) collective-permute-start(f32[320,256]{1,0:T(8,128)} %get-tuple-element.103), channel_id=1, source_target_pairs={{0,32},{1,33},{2,34},{3,35},{4,36},{5,37},{6,38},{7,39},{8,40},{9,... | collective-permute-start | bytes 983048 | tf_op jit(solution)/shard_map/ppermute | solution.py:70
  156.7 20.6 %collective-permute-start.20 = (f32[320,256]{1,0:T(8,128)S(1)}, f32[320,256]{1,0:T(8,128)}, u32[]{:S(2)}, u32[]{:S(2)}) collective-permute-start(f32[320,256]{1,0:T(8,128)S(1)} %get-tuple-element.102), channel_id=1, source_target_pairs={{0,64},{1,65},{2,66},{3,67},{4,68},{5,69},{6,70},{7,71},{8,72},{9,... | collective-permute-start | bytes 983048 | tf_op jit(solution)/shard_map/ppermute | solution.py:70
  156.7 23.0 %collective-permute-start.21 = (f32[320,256]{1,0:T(8,128)S(1)}, f32[320,256]{1,0:T(8,128)}, u32[]{:S(2)}, u32[]{:S(2)}) collective-permute-start(f32[320,256]{1,0:T(8,128)S(1)} %get-tuple-element.101), channel_id=1, source_target_pairs={{0,96},{1,97},{2,98},{3,99},{4,100},{5,101},{6,102},{7,103},{8,104... | collective-permute-start | bytes 983048 | tf_op jit(solution)/shard_map/ppermute | solution.py:70
  180.9 9.6 %collective-permute-start.25 = (f32[80,256]{1,0:T(8,128)S(1)}, f32[80,256]{1,0:T(8,128)S(1)}, u32[]{:S(2)}, u32[]{:S(2)}) collective-permute-start(f32[80,256]{1,0:T(8,128)S(1)} %get-tuple-element.123), channel_id=1, source_target_pairs={{0,17},{1,16},{2,19},{3,18},{4,21},{5,20},{6,23},{7,22},{8,25},{9,... | collective-permute-start | bytes 245768 | tf_op jit(solution)/shard_map/ppermute | solution.py:70
  183.9 8.4 %collective-permute-start.24 = (f32[80,256]{1,0:T(8,128)S(1)}, f32[80,256]{1,0:T(8,128)S(1)}, u32[]{:S(2)}, u32[]{:S(2)}) collective-permute-start(f32[80,256]{1,0:T(8,128)S(1)} %get-tuple-element.124), channel_id=1, source_target_pairs={{0,1},{1,0},{2,3},{3,2},{4,5},{5,4},{6,7},{7,6},{8,9},{9,8},{10,11... | collective-permute-start | bytes 245768 | tf_op jit(solution)/shard_map/ppermute | solution.py:70
  189.9 3.3 collective-permute-start.23
  189.9 32.0 %collective-permute-start.22 = (f32[128,1024]{1,0:T(8,128)S(1)}, f32[128,1024]{1,0:T(8,128)S(1)}, u32[]{:S(2)}, u32[]{:S(2)}) collective-permute-start(f32[128,1024]{1,0:T(8,128)S(1)} %copy-done.7), channel_id=1, source_target_pairs={{0,0},{8,8},{1,16},{9,24},{2,32},{10,40},{3,48},{11,56},{4,64},{12... | collective-permute-start | bytes 1572872 | tf_op jit(solution)/shard_map/ppermute | solution.py:490
  193.2 12.0 %collective-permute-start.28 = (f32[80,256]{1,0:T(8,128)S(1)}, f32[80,256]{1,0:T(8,128)S(1)}, u32[]{:S(2)}, u32[]{:S(2)}) collective-permute-start(f32[80,256]{1,0:T(8,128)S(1)} %add_add_fusion.2), channel_id=1, source_target_pairs={{0,6},{1,7},{2,4},{3,5},{4,2},{5,3},{6,0},{7,1},{8,14},{9,15},{10,... | collective-permute-start | bytes 245768 | tf_op jit(solution)/shard_map/ppermute | solution.py:70
  197.8 21.4 %collective-permute-start.27 = (f32[80,256]{1,0:T(8,128)S(1)}, f32[80,256]{1,0:T(8,128)S(1)}, u32[]{:S(2)}, u32[]{:S(2)}) collective-permute-start(f32[80,256]{1,0:T(8,128)S(1)} %add_add_fusion.2), channel_id=1, source_target_pairs={{0,4},{1,5},{2,6},{3,7},{4,0},{5,1},{6,2},{7,3},{8,12},{9,13},{10,... | collective-permute-start | bytes 245768 | tf_op jit(solution)/shard_map/ppermute | solution.py:70
  199.7 22.1 %collective-permute-start.26 = (f32[80,256]{1,0:T(8,128)S(1)}, f32[80,256]{1,0:T(8,128)S(1)}, u32[]{:S(2)}, u32[]{:S(2)}) collective-permute-start(f32[80,256]{1,0:T(8,128)S(1)} %add_add_fusion.2), channel_id=1, source_target_pairs={{0,2},{1,3},{2,0},{3,1},{4,6},{5,7},{6,4},{7,5},{8,10},{9,11},{10,... | collective-permute-start | bytes 245768 | tf_op jit(solution)/shard_map/ppermute | solution.py:70
  221.9 8.1 %collective-permute-start.35 = (f32[80,256]{1,0:T(8,128)S(1)}, f32[80,256]{1,0:T(8,128)S(1)}, u32[]{:S(2)}, u32[]{:S(2)}) collective-permute-start(f32[80,256]{1,0:T(8,128)S(1)} %add_add_fusion.1), channel_id=1, source_target_pairs={{0,17},{1,16},{2,19},{3,18},{4,21},{5,20},{6,23},{7,22},{8,25},{9,... | collective-permute-start | bytes 245768 | tf_op jit(solution)/shard_map/ppermute | solution.py:70
  224.5 7.0 %collective-permute-start.34 = (f32[80,256]{1,0:T(8,128)S(1)}, f32[80,256]{1,0:T(8,128)S(1)}, u32[]{:S(2)}, u32[]{:S(2)}) collective-permute-start(f32[80,256]{1,0:T(8,128)S(1)} %add_add_fusion.1), channel_id=1, source_target_pairs={{0,1},{1,0},{2,3},{3,2},{4,5},{5,4},{6,7},{7,6},{8,9},{9,8},{10,11... | collective-permute-start | bytes 245768 | tf_op jit(solution)/shard_map/ppermute | solution.py:70
  225.8 7.3 %collective-permute-start.33 = (f32[80,256]{1,0:T(8,128)S(1)}, f32[80,256]{1,0:T(8,128)S(1)}, u32[]{:S(2)}, u32[]{:S(2)}) collective-permute-start(f32[80,256]{1,0:T(8,128)S(1)} %add_add_fusion.1), channel_id=1, source_target_pairs={{0,16},{1,17},{2,18},{3,19},{4,20},{5,21},{6,22},{7,23},{8,24},{9,... | collective-permute-start | bytes 245768 | tf_op jit(solution)/shard_map/ppermute | solution.py:70
  225.9 20.4 %collective-permute-start.32 = (f32[64,1024]{1,0:T(8,128)S(1)}, f32[64,1024]{1,0:T(8,128)S(1)}, u32[]{:S(2)}, u32[]{:S(2)}) collective-permute-start(f32[64,1024]{1,0:T(8,128)S(1)} %get-tuple-element.114), channel_id=1, source_target_pairs={{0,6},{1,7},{2,4},{3,5},{4,2},{5,3},{6,0},{7,1},{8,14},{9,15},{10,... | collective-permute-start | bytes 786440 | tf_op jit(solution)/shard_map/ppermute | solution.py:70
  226.0 23.5 %collective-permute-start.31 = (f32[64,1024]{1,0:T(8,128)S(1)}, f32[64,1024]{1,0:T(8,128)}, u32[]{:S(2)}, u32[]{:S(2)}) collective-permute-start(f32[64,1024]{1,0:T(8,128)S(1)} %get-tuple-element.114), channel_id=1, source_target_pairs={{0,4},{1,5},{2,6},{3,7},{4,0},{5,1},{6,2},{7,3},{8,12},{9,13},{10,... | collective-permute-start | bytes 786440 | tf_op jit(solution)/shard_map/ppermute | solution.py:70
  230.0 19.5 %collective-permute-start.30 = (f32[64,1024]{1,0:T(8,128)S(1)}, f32[64,1024]{1,0:T(8,128)}, u32[]{:S(2)}, u32[]{:S(2)}) collective-permute-start(f32[64,1024]{1,0:T(8,128)S(1)} %get-tuple-element.114), channel_id=1, source_target_pairs={{0,2},{1,3},{2,0},{3,1},{4,6},{5,7},{6,4},{7,5},{8,10},{9,11},{10,... | collective-permute-start | bytes 786440 | tf_op jit(solution)/shard_map/ppermute | solution.py:70
  231.5 14.8 %collective-permute-start.29 = (f32[64,1024]{1,0:T(8,128)S(1)}, f32[64,1024]{1,0:T(8,128)S(1)}, u32[]{:S(2)}, u32[]{:S(2)}) collective-permute-start(f32[64,1024]{1,0:T(8,128)S(1)} %get-tuple-element.115), channel_id=1, source_target_pairs={{0,1},{1,0},{2,3},{3,2},{4,5},{5,4},{6,7},{7,6},{8,9},{9,8},{10,11... | collective-permute-start | bytes 786440 | tf_op jit(solution)/shard_map/ppermute | solution.py:70
  233.3 18.7 %collective-permute-start.38 = (f32[320,256]{1,0:T(8,128)S(1)}, f32[320,256]{1,0:T(8,128)S(1)}, u32[]{:S(2)}, u32[]{:S(2)}) collective-permute-start(f32[320,256]{1,0:T(8,128)S(1)} %get-tuple-element.117), channel_id=1, source_target_pairs={{0,96},{1,97},{2,98},{3,99},{4,100},{5,101},{6,102},{7,103},{8,104... | collective-permute-start | bytes 983048 | tf_op jit(solution)/shard_map/ppermute | solution.py:70
  246.3 13.3 %collective-permute-start.37 = (f32[320,256]{1,0:T(8,128)S(1)}, f32[320,256]{1,0:T(8,128)S(1)}, u32[]{:S(2)}, u32[]{:S(2)}) collective-permute-start(f32[320,256]{1,0:T(8,128)S(1)} %get-tuple-element.117), channel_id=1, source_target_pairs={{0,64},{1,65},{2,66},{3,67},{4,68},{5,69},{6,70},{7,71},{8,72},{9,... | collective-permute-start | bytes 983048 | tf_op jit(solution)/shard_map/ppermute | solution.py:70
  246.3 18.5 %collective-permute-start.36 = (f32[320,256]{1,0:T(8,128)S(1)}, f32[320,256]{1,0:T(8,128)S(1)}, u32[]{:S(2)}, u32[]{:S(2)}) collective-permute-start(f32[320,256]{1,0:T(8,128)S(1)} %get-tuple-element.117), channel_id=1, source_target_pairs={{0,32},{1,33},{2,34},{3,35},{4,36},{5,37},{6,38},{7,39},{8,40},{9,... | collective-permute-start | bytes 983048 | tf_op jit(solution)/shard_map/ppermute | solution.py:70
  249.5 36.4 %copy-start.9 = (f32[2,64,1024]{2,1,0:T(8,128)}, f32[2,64,1024]{2,1,0:T(8,128)S(1)}, u32[]{:S(2)}) copy-start(f32[2,64,1024]{2,1,0:T(8,128)S(1)} %pad_maximum_fusion.10.own) | copy-start | bytes 1572868
  265.1 24.8 %collective-permute-start.39 = (f32[1280,256]{1,0:T(8,128)S(1)}, f32[1280,256]{1,0:T(8,128)S(1)}, u32[]{:S(2)}, u32[]{:S(2)}) collective-permute-start(f32[1280,256]{1,0:T(8,128)S(1)} %pad_maximum_fusion.2), channel_id=1, source_target_pairs={{0,8},{1,9},{2,10},{3,11},{4,12},{5,13},{6,14},{7,15},{8,0},{9,1},... | collective-permute-start | bytes 3932168 | tf_op jit(solution)/shard_map/ppermute | solution.py:70
  268.5 19.9 %copy-start.8 = (f32[4,64,1024]{2,1,0:T(8,128)S(1)}, f32[4,64,1024]{2,1,0:T(8,128)}, u32[]{:S(2)}) copy-start(f32[4,64,1024]{2,1,0:T(8,128)} %pad_maximum_fusion.4.quad) | copy-start | bytes 3145732
  275.7 192.4 %collective-permute-start.40 = (f32[2,64,1024]{2,1,0:T(8,128)S(1)}, f32[2,64,1024]{2,1,0:T(8,128)S(1)}, u32[]{:S(2)}, u32[]{:S(2)}) collective-permute-start(f32[2,64,1024]{2,1,0:T(8,128)S(1)} %pad_maximum_fusion.10.own), channel_id=1, source_target_pairs={{0,2},{1,3},{2,0},{3,1},{4,6},{5,7},{6,4},{7,5},{8,10},{9,11},{10,... | collective-permute-start | bytes 1572872 | tf_op jit(solution)/shard_map/ppermute | solution.py:70
  285.9 182.3 %collective-permute-start.41 = (f32[2,64,1024]{2,1,0:T(8,128)S(1)}, f32[2,64,1024]{2,1,0:T(8,128)S(1)}, u32[]{:S(2)}, u32[]{:S(2)}) collective-permute-start(f32[2,64,1024]{2,1,0:T(8,128)S(1)} %pad_maximum_fusion.10.own), channel_id=1, source_target_pairs={{0,4},{1,5},{2,6},{3,7},{4,0},{5,1},{6,2},{7,3},{8,12},{9,13},{10,... | collective-permute-start | bytes 1572872 | tf_op jit(solution)/shard_map/ppermute | solution.py:70
  285.9 182.3 %collective-permute-start.42 = (f32[2,64,1024]{2,1,0:T(8,128)S(1)}, f32[2,64,1024]{2,1,0:T(8,128)S(1)}, u32[]{:S(2)}, u32[]{:S(2)}) collective-permute-start(f32[2,64,1024]{2,1,0:T(8,128)S(1)} %pad_maximum_fusion.10.own), channel_id=1, source_target_pairs={{0,6},{1,7},{2,4},{3,5},{4,2},{5,3},{6,0},{7,1},{8,14},{9,15},{10,... | collective-permute-start | bytes 1572872 | tf_op jit(solution)/shard_map/ppermute | solution.py:70
  288.4 179.8 %collective-permute-start.43 = (f32[4,64,1024]{2,1,0:T(8,128)S(1)}, f32[4,64,1024]{2,1,0:T(8,128)S(1)}, u32[]{:S(2)}, u32[]{:S(2)}) collective-permute-start(f32[4,64,1024]{2,1,0:T(8,128)S(1)} %copy-done.8), channel_id=1, source_target_pairs={{0,1},{1,0},{2,3},{3,2},{4,5},{5,4},{6,7},{7,6},{8,9},{9,8},{10,11... | collective-permute-start | bytes 3145736 | tf_op jit(solution)/shard_map/ppermute | solution.py:70
  (13 other events, 81.1 us)
Sparse Core Ops, SparseCore 0:
  181.0 77.3 all-gather.2

commit v4 on v3

--- a/solution.py
+++ b/solution.py
@@ -86,8 +86,8 @@
     return blocks[0] + got[0] + swap(kept, Y[far])
 
 
-def scatter_lines(even, odd, first_wait, second_wait):
-    got = swap(odd, CORE)
+def scatter_lines(even, odd, begun, first_wait, second_wait, third_wait):
+    got = begun(swap(odd, CORE))
     quarter = LINE // 4
     cut = lambda i, q: even[i, q * quarter : (q + 1) * quarter] + got[i, q * quarter : (q + 1) * quarter]
     half = lambda i, q: jnp.concatenate([cut(i, q), cut(i, q + 1)], 0)
@@ -101,7 +101,8 @@
     own = [half(2 * m, 0) + came[m] for m in range(4)]
     a = [o[:quarter] for o in own]
     b = [o[quarter:] for o in own]
-    a, b = y_second(1, a, y_first(1, a)), y_second(3, b, y_first(3, b))
+    a_got, b_got = third_wait(y_first(1, a), y_first(3, b))
+    a, b = y_second(1, a, a_got), y_second(3, b, b_got)
     rest = jnp.concatenate([c[0], d[0]], 0) + swap(jnp.concatenate([c[1], d[1]], 0), X_LOW)
     return jnp.concatenate([a, b, rest], 0)
 
@@ -116,11 +117,10 @@
     return jnp.concatenate([jnp.where(bit, got, mine), jnp.where(bit, mine, got)], 0)
 
 
-def scatter_four(x, place, masks, wait=lambda *got: got):
+def scatter_four(x, place, masks):
     count = x.shape[0] // 4
     own = lambda m: lax.dynamic_slice_in_dim(x, (place ^ m) * count, count, 0)
-    near, far, across = wait(swap(own(1), masks[1]), swap(own(2), masks[2]), swap(own(3), masks[3]))
-    return own(0) + near + far + across
+    return own(0) + swap(own(1), masks[1]) + swap(own(2), masks[2]) + swap(own(3), masks[3])
 
 
 def gather_four(x, place, masks):
@@ -132,19 +132,18 @@
     return lax.optimization_barrier(values)
 
 
-def sum_start(x, core, y, wait):
+def sum_start(x, core, z, x_place):
     keep, send = halves(x, core == 1)
     x = keep + swap(send, CORE)
-    return scatter_four(x, y, Y, wait)
-
-
-def sum_middle(x, x_place):
-    x = scatter_four(x, x_place, X)
-    return x + swap(x, Z[1]) + swap(x, Z[2]) + swap(x, Z[3])
-
-
-def sum_spread(x, x_place, y):
-    return gather_four(gather_four(x, x_place, X), y, Y)
+    return scatter_four(scatter_four(x, z, Z), x_place, X)
+
+
+def sum_middle(x):
+    return x + swap(x, Y[1]) + swap(x, Y[2]) + swap(x, Y[3])
+
+
+def sum_spread(x, x_place, z):
+    return gather_four(gather_four(x, x_place, X), z, Z)
 
 
 def gather_rows_start(line):
@@ -451,19 +450,28 @@
     even = product_lines(me, value_matrix, inputs, 0)
     held = {}
 
+    def begun(got):
+        got, held["above"], held["below"] = tied(got, above, below)
+        return got
+
     def first_wait(c_got, d_got):
-        base = plant_part(4, 4, *operands[:4], None, None, *operands[6:], None)
-        base = plant_part(8, 4, *operands[:4], None, None, *operands[6:], base)
+        middle = (*operands[:2], held["above"], held["below"], None, None, *operands[6:])
+        base = plant_part(4, 4, *middle, None)
+        base = plant_part(8, 4, *middle, base)
         c_got, d_got, held["base"] = tied(c_got, d_got, base)
         return c_got, d_got
 
     def second_wait(came):
-        came, held["inputs"], held["left"], held["right"] = tied(came, mine_inputs, left, right)
+        came, held["inputs"] = tied(came, mine_inputs)
         return came
 
-    product = scatter_lines(even, odd, first_wait, second_wait)
+    def third_wait(a_got, b_got):
+        a_got, b_got, held["left"], held["right"] = tied(a_got, b_got, left, right)
+        return a_got, b_got
+
+    product = scatter_lines(even, odd, begun, first_wait, second_wait, third_wait)
     mine_inputs = held["inputs"]
-    operands = (*operands[:4], held["left"], held["right"], *operands[6:])
+    operands = (*operands[:2], held["above"], held["below"], held["left"], held["right"], *operands[6:])
 
     gram = gram_blocks(mine_inputs, product)
     product, gram = tied(product, gram)
@@ -474,32 +482,27 @@
     lines = grid_side
     over = lax.ppermute(product, both, [(device_of(i), device_of(i + 1)) for i in range(lines - 1)])
     under = lax.ppermute(product, both, [(device_of(i + 1), device_of(i)) for i in range(lines - 1)])
-
-    def third_wait(*got):
-        base = plant_part(0, 4, *operands, held["base"])
-        *got, held["base"] = tied(*got, base)
-        return got
-
-    total = sum_start(gram.reshape(10 * PANEL, PANEL), core, y, third_wait)
+    total = sum_start(gram.reshape(10 * PANEL, PANEL), core, z, x_place)
     line = col_index * 16 + line_of(row_index)
     diagonal = lax.dynamic_slice_in_dim(plant_diag, line, 1, 0)
     gain = stencil_first(jnp.stack([over, product, under]), diagonal)[0]
     gain, total = tied(gain, total)
+    total = sum_middle(total)
+    gain, total = tied(gain, total)
+    traded = lax.ppermute(gain, both, trade)
+    total = sum_spread(total, x_place, z)
+    traded, gain, total = tied(traded, gain, total)
 
     gain_cols = lax.all_gather(gain, "row", axis=0)
-    traded = lax.ppermute(gain, both, trade)
-    total = sum_middle(total, x_place)
-    traded, total = tied(traded, total)
-
     pair, quad = gather_rows_start(traded)
-    total = sum_spread(total, x_place, y)
-    pair, quad, total = tied(pair, quad, total)
-
+    total = joined(total, swap(total, CORE), core == 1)
+    base = plant_part(0, 4, *operands, held["base"])
+    pair, quad, total, base = tied(pair, quad, total, base)
     sides = gather_rows_end(pair, quad)
-    base = plant_part(12, 4, *operands, held["base"])
-    total = joined(total, swap(total, CORE), core == 1)
-    total, base = tied(total, base)
     factors = factored(control_weight, total.reshape(10, PANEL, PANEL))
+    *factors, base = tied(*factors, base)
+    base = plant_part(12, 4, *operands, base)
+    *sides, base = tied(*sides, base)
     solved = solve(jnp.stack([z, x_high]).astype(jnp.int32), factors, sides)
     return downdate(solved, gain_cols, base)
 

time: 518 us -> 488 us (0.942)
  the two profiles are of different devices: /device:TPU:1 before, /device:TPU:8 now
where the time goes in v4:
time: 488 us; the launch traced here: 479 us
  Pallas kernels  264 us (54%)
  waiting for transfers between devices  94 us (19%)
  starting transfers between devices  77.1 us (16%)
  other arithmetic  17.9 us (4%)
  between operations  15.2 us (3%)
  local copies, waits for them, and re-layouts  10.7 us (2%)
    pallas_call x1, Pallas kernels, factored(): pl.pallas_call(factor_kernel, out_shape=[jax.ShapeDtypeStruct((10, PANEL,...  176 us
    ppermute x36, waiting for transfers between devices, swap(): return lax.ppermute(x, ('row', 'col'), [(i, i ^ mask) for i in range(128)])  70.6 us
    ppermute x36, starting transfers between devices, swap(): return lax.ppermute(x, ('row', 'col'), [(i, i ^ mask) for i in range(128)])  57.2 us
    pallas_call x4, Pallas kernels, plant_part(): pl.pallas_call(functools.partial(plant_kernel, start, last, len(sides)),...  28.2 us
    pallas_call x2, Pallas kernels, product_lines(): pl.pallas_call(product_kernel, grid_spec=pltpu.PrefetchScalarGridSpec(num...  23.4 us
    pallas_call x1, Pallas kernels, downdate(): pl.pallas_call(downdate_kernel, grid=(8,), in_specs=[whole, whole, pl.Blo...  19.2 us
    ppermute x4, waiting for transfers between devices, shifted(): lax.ppermute(x, axis, [(i, i + by) for i in range(count) if 0 <= i + by <...  16.4 us
    pallas_call x1, Pallas kernels, solve(): pl.pallas_call(solve_kernel, out_shape=[jax.ShapeDtypeStruct((size, 4 * P...  12.6 us
  transfers between devices with their start and end apart: 45, of which 21 were waited for; matrix products, arithmetic and copies ran while one was open for 4% of the time, Pallas kernels for 48%

profile of v4, /device:TPU:8, one launch (start us, length us, event | category | flops | bytes accessed | tf_op | source)
XLA Modules:
  0.0 478.7 jit_solution(8972623597114161953)
XLA Ops:
  6.5 11.8 %shard_map.56 = f32[8,128,1024]{2,1,0:T(8,128)} custom-call(s32[1]{0:T(128)} %bitcast.3.me_ref, f32[1024,2048]{1,0:T(8,128)} %refs_7_.7, f32[1024,2048]{1,0:T(8,128)} %refs_7_.7, f32[1024,1024]{1,0:T(8,128)} %inputs.3), custom_call_target="tpu_custom_call" | custom-call | flops 1048576 | bytes 1048576 | tf_op jit(solution)/shard_map/pallas_call | solution.py:50
  18.3 2.7 fusion.28
  21.0 2.4 collective-permute-start.1
  23.5 4.0 collective-permute-start.2
  29.4 1.9 collective-permute-start.4
  32.1 11.6 %shard_map.55 = f32[8,128,1024]{2,1,0:T(8,128)} custom-call(s32[1]{0:T(128)} %bitcast.3.me_ref, f32[1024,2048]{1,0:T(8,128)} %refs_7_.7, f32[1024,2048]{1,0:T(8,128)} %refs_7_.7, f32[1024,1024]{1,0:T(8,128)} %inputs.3), custom_call_target="tpu_custom_call" | custom-call | flops 1048576 | bytes 1048576 | tf_op jit(solution)/shard_map/pallas_call | solution.py:50
  47.0 4.1 collective-permute-done.2.refs_2_.refs_5_.refs_8_
  52.8 1.9 fusion.9
  59.6 4.3 collective-permute-start.12
  66.1 6.9 %shard_map.57.refs_12_ = f32[1024,2048]{1,0:T(8,128)} custom-call(s32[2]{0:T(128)} %pad_add_fusion.1.place, f32[128,2048]{1,0:T(8,128)} %copy-done.2, f32[1024,2048]{1,0:T(8,128)} %refs_7_.7, f32[128,2048]{1,0:T(8,128)} %copy-done.3, f32[128,2048]{1,0:T(8,128)} %copy-done.2, f32[1024,2048]{1,0:T(8,128)} %refs_7_.7, f32[128,2048]{1,0:T(8,128)} %copy-done.3, ...), custom_call_target="tpu_custom_call" | custom-call | flops 33554432 | bytes 16777216 | tf_op jit(solution)/shard_map/pallas_call | solution.py:396
  72.9 6.7 %shard_map.58.refs_14_ = f32[1024,2048]{1,0:T(8,128)} custom-call(s32[2]{0:T(128)} %pad_add_fusion.1.place, f32[128,2048]{1,0:T(8,128)} %copy-done.2, f32[1024,2048]{1,0:T(8,128)} %refs_7_.7, f32[128,2048]{1,0:T(8,128)} %copy-done.3, f32[128,2048]{1,0:T(8,128)} %copy-done.2, f32[1024,2048]{1,0:T(8,128)} %refs_7_.7, ...), custom_call_target="tpu_custom_call", output_to_operand_aliasing={{}: (13, {})} | custom-call | flops 33554432 | bytes 16777216 | tf_op jit(solution)/shard_map/pallas_call | solution.py:396
  81.2 6.1 %collective-permute-done.13 = f32[2,32,1024]{2,1,0:T(8,128)S(1)} collective-permute-done((f32[2,32,1024]{2,1,0:T(8,128)S(1)}, f32[2,32,1024]{2,1,0:T(8,128)S(1)}, u32[]{:S(2)}, u32[]{:S(2)}) %collective-permute-start.13) | collective-permute-done | bytes 262176 | tf_op jit(solution)/shard_map/ppermute | solution.py:70
  87.3 2.7 collective-permute-start.14
  90.1 5.0 %collective-permute-done.14 = f32[2,32,1024]{2,1,0:T(8,128)S(1)} collective-permute-done((f32[2,32,1024]{2,1,0:T(8,128)S(1)}, f32[2,32,1024]{2,1,0:T(8,128)S(1)}, u32[]{:S(2)}, u32[]{:S(2)}) %collective-permute-start.14) | collective-permute-done | bytes 262176 | tf_op jit(solution)/shard_map/ppermute | solution.py:70
  95.3 2.5 collective-permute-start.6
  97.9 2.4 collective-permute-start.5
  101.7 11.4 %collective-permute-done.8.refs_10_ = f32[1280,128]{1,0:T(8,128)S(1)} collective-permute-done((f32[1280,128]{1,0:T(8,128)S(1)}, f32[1280,128]{1,0:T(8,128)S(1)}, u32[]{:S(2)}, u32[]{:S(2)}) %collective-permute-start.8) | collective-permute-done | bytes 655392 | tf_op jit(solution)/shard_map/ppermute | solution.py:431
  113.1 3.7 collective-permute-start.10
  117.2 4.0 collective-permute-done.10
  123.9 3.9 shard_map.59
  127.8 2.0 slice_select_fusion.1
  129.9 3.1 collective-permute-done.18
  135.4 4.7 collective-permute-start.21
  140.1 2.9 collective-permute-start.16
  143.0 3.8 collective-permute-start.17
  146.9 3.4 collective-permute-done.20
  150.3 4.3 collective-permute-done.21
  157.1 2.9 collective-permute-start.23
  160.7 7.0 %collective-permute-done.17 = f32[128,1024]{1,0:T(8,128)S(1)} collective-permute-done((f32[128,1024]{1,0:T(8,128)S(1)}, f32[128,1024]{1,0:T(8,128)S(1)}, u32[]{:S(2)}, u32[]{:S(2)}) %collective-permute-start.17) | collective-permute-done | bytes 524320 | tf_op jit(solution)/shard_map/ppermute | solution.py:484
  168.7 3.0 collective-permute-done.23
  171.8 2.4 collective-permute-start.26
  178.7 2.3 collective-permute-start.29
  181.9 1.9 collective-permute-start.31
  183.8 3.2 collective-permute-done.30
  189.8 3.0 collective-permute-start.34
  192.8 1.9 collective-permute-start.28
  194.7 24.5 %collective-permute-done.32 = f32[320,256]{1,0:T(8,128)S(1)} collective-permute-done((f32[320,256]{1,0:T(8,128)S(1)}, f32[320,256]{1,0:T(8,128)S(1)}, u32[]{:S(2)}, u32[]{:S(2)}) %collective-permute-start.32) | collective-permute-done | bytes 327712 | tf_op jit(solution)/shard_map/ppermute | solution.py:70
  221.3 3.1 collective-permute-start.36
  224.3 4.6 collective-permute-start.37
  228.9 7.4 %shard_map.60.refs_14_ = f32[1024,2048]{1,0:T(8,128)} custom-call(s32[2]{0:T(128)} %pad_add_fusion.1.place, f32[128,2048]{1,0:T(8,128)} %copy-done.2, f32[1024,2048]{1,0:T(8,128)} %refs_7_.7, f32[128,2048]{1,0:T(8,128)} %copy-done.3, f32[128,2048]{1,0:T(8,128)} %copy-done.2, f32[1024,2048]{1,0:T(8,128)} %refs_7_.7, ...), custom_call_target="tpu_custom_call", output_to_operand_aliasing={{}: (15, {})} | custom-call | flops 33554432 | bytes 16777216 | tf_op jit(solution)/shard_map/pallas_call | solution.py:396
  236.4 4.6 collective-permute-done.37
  241.1 2.6 collective-permute-done.38
  245.6 2.1 collective-permute-start.43
  250.7 3.1 collective-permute-start.42
  253.9 176.5 %shard_map.61 = (f32[10,256,256]{2,1,0:T(8,128)}, f32[4,256,256]{2,1,0:T(8,128)}) custom-call(f32[1]{0:T(128)S(6)} %copy.14.weight, f32[10,256,256]{2,1,0:T(8,128)} %bitcast.143), custom_call_target="tpu_custom_call" | custom-call | flops 9663676416 | bytes 12582912 | tf_op jit(solution)/shard_map/pallas_call | solution.py:260
  430.4 7.2 %shard_map.62.base = f32[1024,2048]{1,0:T(8,128)} custom-call(s32[2]{0:T(128)} %pad_add_fusion.1.place, f32[128,2048]{1,0:T(8,128)} %copy-done.2, f32[1024,2048]{1,0:T(8,128)} %refs_7_.7, f32[128,2048]{1,0:T(8,128)} %copy-done.3, f32[128,2048]{1,0:T(8,128)} %copy-done.2, f32[1024,2048]{1,0:T(8,128)} %refs_7_.7, ...), custom_call_target="tpu_custom_call", output_to_operand_aliasing={{}: (15, {})} | custom-call | flops 33554432 | bytes 16777216 | tf_op jit(solution)/shard_map/pallas_call | solution.py:396
  439.7 12.6 %shard_map.63 = (bf16[1024,1024]{1,0:T(8,128)(2,1)}, bf16[1024,1024]{1,0:T(8,128)(2,1)}) custom-call(s32[2]{0:T(128)} %pad_add_fusion.place, f32[10,256,256]{2,1,0:T(8,128)} %get-tuple-element.68.factor, f32[4,256,256]{2,1,0:T(8,128)} %get-tuple-element.69.inverses, f32[2,64,1024]{2,1,0:T(8,128)} %copy-done.10, f32[2,64,1024]{2,1,0:T(8,128)} %copy-done.12, ...), custom_call_target="tpu_custom_call" | custom-call | flops 9663676416 | bytes 12582912 | tf_op jit(solution)/shard_map/pallas_call | solution.py:304
  452.2 19.2 %shard_map.64 = f32[1024,2048]{1,0:T(8,128)} custom-call(bf16[1024,1024]{1,0:T(8,128)(2,1)} %get-tuple-element.79.high, bf16[1024,1024]{1,0:T(8,128)(2,1)} %get-tuple-element.80.low, f32[16,128,1024]{2,1,0:T(8,128)} %bitcast.164, f32[16,128,1024]{2,1,0:T(8,128)} %bitcast.165, f32[1024,2048]{1,0:T(8,128)} %shard_map.62.base), custom_call_target="tpu_custom_call" | custom-call | flops 12884901888 | bytes 29360128 | tf_op jit(solution)/shard_map/pallas_call | solution.py:325
  (145 shorter events, 44.0 us)
Async XLA Ops:
  6.5 24.8 %copy-start = (f32[128,128]{1,0:T(8,128)S(1)}, f32[128,128]{1,0:T(8,128)}, u32[]{:S(2)}) copy-start(f32[128,128]{1,0:T(8,128)} %param.7) | copy-start | bytes 196612
  6.5 445.7 %all-gather.3.cloned.1.call-start = ((), (), s32[]{:S(2)}) async-start(), calls=%async_computation | async-start | bytes 8912896 | tf_op jit(solution)/shard_map/all_gather | solution.py:496
  18.3 34.5 %collective-permute-start = (f32[8,128,1024]{2,1,0:T(8,128)}, f32[8,128,1024]{2,1,0:T(8,128)}, u32[]{:S(2)}, u32[]{:S(2)}) collective-permute-start(f32[8,128,1024]{2,1,0:T(8,128)} %shard_map.56), channel_id=1, source_target_pairs={{0,8},{1,9},{2,10},{3,11},{4,12},{5,13},{6,14},{7,15},{8,0},{9,1},... | collective-permute-start | bytes 12582920 | tf_op jit(solution)/shard_map/ppermute | solution.py:70
  21.0 25.9 %collective-permute-start.1 = (f32[128,2048]{1,0:T(8,128)}, f32[128,2048]{1,0:T(8,128)S(1)}, u32[]{:S(2)}, u32[]{:S(2)}) collective-permute-start(f32[128,2048]{1,0:T(8,128)} %get-tuple-element.118), channel_id=1, source_target_pairs={{0,8},{8,16},{16,24},{24,32},{32,40},{40,48},{48,56},{56,64},{64,7... | collective-permute-start | bytes 3145736 | tf_op jit(solution)/shard_map/ppermute | solution.py:431
  23.5 27.6 %collective-permute-start.2 = (f32[128,2048]{1,0:T(8,128)S(1)}, f32[128,2048]{1,0:T(8,128)S(1)}, u32[]{:S(2)}, u32[]{:S(2)}) collective-permute-start(f32[128,2048]{1,0:T(8,128)S(1)} %get-tuple-element.117), channel_id=1, source_target_pairs={{8,0},{16,8},{24,16},{32,24},{40,32},{48,40},{56,48},{64,56},{72,6... | collective-permute-start | bytes 3145736 | tf_op jit(solution)/shard_map/ppermute | solution.py:431
  29.4 65.7 %collective-permute-start.4 = (f32[128,1024]{1,0:T(8,128)}, f32[128,1024]{1,0:T(8,128)}, u32[]{:S(2)}, u32[]{:S(2)}) collective-permute-start(f32[128,1024]{1,0:T(8,128)} %constant_dynamic-slice_fusion.8), channel_id=1, source_target_pairs={{0,0},{8,8},{1,16},{9,24},{2,32},{10,40},{3,48},{11,56},{4,64},{12... | collective-permute-start | bytes 1572872 | tf_op jit(solution)/shard_map/ppermute | solution.py:427
  51.2 50.5 %collective-permute-start.7 = (f32[1280,128]{1,0:T(8,128)S(1)}, f32[1280,128]{1,0:T(8,128)S(1)}, u32[]{:S(2)}, u32[]{:S(2)}) collective-permute-start(f32[1280,128]{1,0:T(8,128)S(1)} %pad_maximum_fusion.5), channel_id=1, source_target_pairs={{0,1},{1,2},{2,3},{3,4},{4,5},{5,6},{6,7},{8,9},{9,10},{10,11},{11... | collective-permute-start | bytes 1966088 | tf_op jit(solution)/shard_map/ppermute | solution.py:431
  58.7 21.0 %collective-permute-start.11 = (f32[2,2,32,1024]{3,2,1,0:T(8,128)}, f32[2,2,32,1024]{3,2,1,0:T(8,128)S(1)}, u32[]{:S(2)}, u32[]{:S(2)}) collective-permute-start(f32[2,2,32,1024]{3,2,1,0:T(8,128)} %pad_maximum_fusion.7), channel_id=1, source_target_pairs={{0,32},{1,33},{2,34},{3,35},{4,36},{5,37},{6,38},{7,39},{8,40},{9,... | collective-permute-start | bytes 1572872 | tf_op jit(solution)/shard_map/ppermute | solution.py:70
  59.6 20.1 %collective-permute-start.12 = (f32[2,2,32,1024]{3,2,1,0:T(8,128)}, f32[2,2,32,1024]{3,2,1,0:T(8,128)S(1)}, u32[]{:S(2)}, u32[]{:S(2)}) collective-permute-start(f32[2,2,32,1024]{3,2,1,0:T(8,128)} %pad_maximum_fusion.8), channel_id=1, source_target_pairs={{0,96},{1,97},{2,98},{3,99},{4,100},{5,101},{6,102},{7,103},{8,104... | collective-permute-start | bytes 1572872 | tf_op jit(solution)/shard_map/ppermute | solution.py:70
  65.4 29.7 %collective-permute-start.3 = (f32[4,64,1024]{2,1,0:T(8,128)S(1)}, f32[4,64,1024]{2,1,0:T(8,128)S(1)}, u32[]{:S(2)}, u32[]{:S(2)}) collective-permute-start(f32[4,64,1024]{2,1,0:T(8,128)S(1)} %pad_maximum_fusion.3), channel_id=1, source_target_pairs={{0,16},{1,17},{2,18},{3,19},{4,20},{5,21},{6,22},{7,23},{8,24},{9,... | collective-permute-start | bytes 3145736 | tf_op jit(solution)/shard_map/ppermute | solution.py:70
  79.7 7.5 %collective-permute-start.13 = (f32[2,32,1024]{2,1,0:T(8,128)S(1)}, f32[2,32,1024]{2,1,0:T(8,128)S(1)}, u32[]{:S(2)}, u32[]{:S(2)}) collective-permute-start(f32[2,32,1024]{2,1,0:T(8,128)S(1)} %maximum_add_fusion.5), channel_id=1, source_target_pairs={{0,96},{1,97},{2,98},{3,99},{4,100},{5,101},{6,102},{7,103},{8,104... | collective-permute-start | bytes 786440 | tf_op jit(solution)/shard_map/ppermute | solution.py:70
  79.9 33.2 %collective-permute-start.8 = (f32[1280,128]{1,0:T(8,128)S(1)}, f32[1280,128]{1,0:T(8,128)S(1)}, u32[]{:S(2)}, u32[]{:S(2)}) collective-permute-start(f32[1280,128]{1,0:T(8,128)S(1)} %pad_maximum_fusion.6), channel_id=1, source_target_pairs={{1,0},{2,1},{3,2},{4,3},{5,4},{6,5},{7,6},{9,8},{10,9},{11,10},{12... | collective-permute-start | bytes 1966088 | tf_op jit(solution)/shard_map/ppermute | solution.py:431
  87.3 7.8 %collective-permute-start.14 = (f32[2,32,1024]{2,1,0:T(8,128)S(1)}, f32[2,32,1024]{2,1,0:T(8,128)S(1)}, u32[]{:S(2)}, u32[]{:S(2)}) collective-permute-start(f32[2,32,1024]{2,1,0:T(8,128)S(1)} %maximum_add_fusion.7), channel_id=1, source_target_pairs={{0,32},{1,33},{2,34},{3,35},{4,36},{5,37},{6,38},{7,39},{8,40},{9,... | collective-permute-start | bytes 786440 | tf_op jit(solution)/shard_map/ppermute | solution.py:70
  95.3 17.8 %collective-permute-start.6 = (f32[2,32,1024]{2,1,0:T(8,128)S(1)}, f32[2,32,1024]{2,1,0:T(8,128)S(1)}, u32[]{:S(2)}, u32[]{:S(2)}) collective-permute-start(f32[2,32,1024]{2,1,0:T(8,128)S(1)} %pad_maximum_fusion.14), channel_id=1, source_target_pairs={{0,96},{1,97},{2,98},{3,99},{4,100},{5,101},{6,102},{7,103},{8,104... | collective-permute-start | bytes 786440 | tf_op jit(solution)/shard_map/ppermute | solution.py:70
  97.9 15.2 %collective-permute-start.5 = (f32[2,32,1024]{2,1,0:T(8,128)S(1)}, f32[2,32,1024]{2,1,0:T(8,128)S(1)}, u32[]{:S(2)}, u32[]{:S(2)}) collective-permute-start(f32[2,32,1024]{2,1,0:T(8,128)S(1)} %pad_maximum_fusion.13), channel_id=1, source_target_pairs={{0,32},{1,33},{2,34},{3,35},{4,36},{5,37},{6,38},{7,39},{8,40},{9,... | collective-permute-start | bytes 786440 | tf_op jit(solution)/shard_map/ppermute | solution.py:70
  100.3 16.8 %collective-permute-start.15 = (f32[64,1024]{1,0:T(8,128)S(1)}, f32[64,1024]{1,0:T(8,128)S(1)}, u32[]{:S(2)}, u32[]{:S(2)}) collective-permute-start(f32[64,1024]{1,0:T(8,128)S(1)} %pad_maximum_fusion.15), channel_id=1, source_target_pairs={{0,16},{1,17},{2,18},{3,19},{4,20},{5,21},{6,22},{7,23},{8,24},{9,... | collective-permute-start | bytes 786440 | tf_op jit(solution)/shard_map/ppermute | solution.py:70
  101.6 21.4 %copy-start.6 = (f32[1280,128]{1,0:T(8,128)}, f32[1280,128]{1,0:T(8,128)S(1)}, u32[]{:S(2)}) copy-start(f32[1280,128]{1,0:T(8,128)S(1)} %collective-permute-done.7.refs_9_) | copy-start | bytes 1966084
  113.1 8.1 %collective-permute-start.10 = (f32[32,1024]{1,0:T(8,128)S(1)}, f32[32,1024]{1,0:T(8,128)S(1)}, u32[]{:S(2)}, u32[]{:S(2)}) collective-permute-start(f32[32,1024]{1,0:T(8,128)S(1)} %slice_add_fusion.16), channel_id=1, source_target_pairs={{0,32},{1,33},{2,34},{3,35},{4,36},{5,37},{6,38},{7,39},{8,40},{9,... | collective-permute-start | bytes 393224 | tf_op jit(solution)/shard_map/ppermute | solution.py:70
  116.9 6.1 %collective-permute-start.9 = (f32[32,1024]{1,0:T(8,128)S(1)}, f32[32,1024]{1,0:T(8,128)S(1)}, u32[]{:S(2)}, u32[]{:S(2)}) collective-permute-start(f32[32,1024]{1,0:T(8,128)S(1)} %slice_add_fusion.18), channel_id=1, source_target_pairs={{0,96},{1,97},{2,98},{3,99},{4,100},{5,101},{6,102},{7,103},{8,104... | collective-permute-start | bytes 393224 | tf_op jit(solution)/shard_map/ppermute | solution.py:70
  129.8 3.2 collective-permute-start.18
  135.4 11.5 %collective-permute-start.19 = (f32[320,256]{1,0:T(8,128)}, f32[320,256]{1,0:T(8,128)}, u32[]{:S(2)}, u32[]{:S(2)}) collective-permute-start(f32[320,256]{1,0:T(8,128)} %get-tuple-element.127), channel_id=1, source_target_pairs={{0,2},{1,3},{2,0},{3,1},{4,6},{5,7},{6,4},{7,5},{8,10},{9,11},{10,... | collective-permute-start | bytes 983048 | tf_op jit(solution)/shard_map/ppermute | solution.py:70
  135.4 14.9 %collective-permute-start.20 = (f32[320,256]{1,0:T(8,128)}, f32[320,256]{1,0:T(8,128)}, u32[]{:S(2)}, u32[]{:S(2)}) collective-permute-start(f32[320,256]{1,0:T(8,128)} %get-tuple-element.129), channel_id=1, source_target_pairs={{0,4},{1,5},{2,6},{3,7},{4,0},{5,1},{6,2},{7,3},{8,12},{9,13},{10,... | collective-permute-start | bytes 983048 | tf_op jit(solution)/shard_map/ppermute | solution.py:70
  135.4 19.3 %collective-permute-start.21 = (f32[320,256]{1,0:T(8,128)S(1)}, f32[320,256]{1,0:T(8,128)}, u32[]{:S(2)}, u32[]{:S(2)}) collective-permute-start(f32[320,256]{1,0:T(8,128)S(1)} %get-tuple-element.128), channel_id=1, source_target_pairs={{0,6},{1,7},{2,4},{3,5},{4,2},{5,3},{6,0},{7,1},{8,14},{9,15},{10,... | collective-permute-start | bytes 983048 | tf_op jit(solution)/shard_map/ppermute | solution.py:70
  140.1 20.6 %collective-permute-start.16 = (f32[128,1024]{1,0:T(8,128)S(1)}, f32[128,1024]{1,0:T(8,128)S(1)}, u32[]{:S(2)}, u32[]{:S(2)}) collective-permute-start(f32[128,1024]{1,0:T(8,128)S(1)} %copy-done.5), channel_id=1, source_target_pairs={{0,16},{16,32},{32,48},{48,64},{64,80},{80,96},{96,112},{112,8},{8... | collective-permute-start | bytes 1572872 | tf_op jit(solution)/shard_map/ppermute | solution.py:483
  143.0 24.8 %collective-permute-start.17 = (f32[128,1024]{1,0:T(8,128)S(1)}, f32[128,1024]{1,0:T(8,128)S(1)}, u32[]{:S(2)}, u32[]{:S(2)}) collective-permute-start(f32[128,1024]{1,0:T(8,128)S(1)} %copy-done.5), channel_id=1, source_target_pairs={{16,0},{32,16},{48,32},{64,48},{80,64},{96,80},{112,96},{8,112},{2... | collective-permute-start | bytes 1572872 | tf_op jit(solution)/shard_map/ppermute | solution.py:484
  156.0 12.7 %collective-permute-start.22 = (f32[80,256]{1,0:T(8,128)S(1)}, f32[80,256]{1,0:T(8,128)S(1)}, u32[]{:S(2)}, u32[]{:S(2)}) collective-permute-start(f32[80,256]{1,0:T(8,128)S(1)} %get-tuple-element.148), channel_id=1, source_target_pairs={{0,16},{1,17},{2,18},{3,19},{4,20},{5,21},{6,22},{7,23},{8,24},{9,... | collective-permute-start | bytes 245768 | tf_op jit(solution)/shard_map/ppermute | solution.py:70
  157.1 14.6 %collective-permute-start.23 = (f32[80,256]{1,0:T(8,128)S(1)}, f32[80,256]{1,0:T(8,128)S(1)}, u32[]{:S(2)}, u32[]{:S(2)}) collective-permute-start(f32[80,256]{1,0:T(8,128)S(1)} %get-tuple-element.150), channel_id=1, source_target_pairs={{0,1},{1,0},{2,3},{3,2},{4,5},{5,4},{6,7},{7,6},{8,9},{9,8},{10,11... | collective-permute-start | bytes 245768 | tf_op jit(solution)/shard_map/ppermute | solution.py:70
  159.9 11.8 %collective-permute-start.24 = (f32[80,256]{1,0:T(8,128)S(1)}, f32[80,256]{1,0:T(8,128)S(1)}, u32[]{:S(2)}, u32[]{:S(2)}) collective-permute-start(f32[80,256]{1,0:T(8,128)S(1)} %get-tuple-element.149), channel_id=1, source_target_pairs={{0,17},{1,16},{2,19},{3,18},{4,21},{5,20},{6,23},{7,22},{8,25},{9,... | collective-permute-start | bytes 245768 | tf_op jit(solution)/shard_map/ppermute | solution.py:70
  168.0 24.8 %copy-start.8 = (f32[128,1024]{1,0:T(8,128)}, f32[128,1024]{1,0:T(8,128)S(1)}, u32[]{:S(2)}) copy-start(f32[128,1024]{1,0:T(8,128)S(1)} %fusion.4) | copy-start | bytes 1572868
  171.7 5.0 %collective-permute-start.25 = (f32[80,256]{1,0:T(8,128)S(1)}, f32[80,256]{1,0:T(8,128)S(1)}, u32[]{:S(2)}, u32[]{:S(2)}) collective-permute-start(f32[80,256]{1,0:T(8,128)S(1)} %add_add_fusion.2), channel_id=1, source_target_pairs={{0,32},{1,33},{2,34},{3,35},{4,36},{5,37},{6,38},{7,39},{8,40},{9,... | collective-permute-start | bytes 245768 | tf_op jit(solution)/shard_map/ppermute | solution.py:70
  171.8 6.0 %collective-permute-start.26 = (f32[80,256]{1,0:T(8,128)S(1)}, f32[80,256]{1,0:T(8,128)S(1)}, u32[]{:S(2)}, u32[]{:S(2)}) collective-permute-start(f32[80,256]{1,0:T(8,128)S(1)} %add_add_fusion.2), channel_id=1, source_target_pairs={{0,64},{1,65},{2,66},{3,67},{4,68},{5,69},{6,70},{7,71},{8,72},{9,... | collective-permute-start | bytes 245768 | tf_op jit(solution)/shard_map/ppermute | solution.py:70
  174.2 4.5 collective-permute-start.27
  178.7 5.1 %collective-permute-start.29 = (f32[80,256]{1,0:T(8,128)S(1)}, f32[80,256]{1,0:T(8,128)S(1)}, u32[]{:S(2)}, u32[]{:S(2)}) collective-permute-start(f32[80,256]{1,0:T(8,128)S(1)} %add_add_fusion.1), channel_id=1, source_target_pairs={{0,16},{1,17},{2,18},{3,19},{4,20},{5,21},{6,22},{7,23},{8,24},{9,... | collective-permute-start | bytes 245768 | tf_op jit(solution)/shard_map/ppermute | solution.py:70
  181.0 6.0 %collective-permute-start.30 = (f32[80,256]{1,0:T(8,128)S(1)}, f32[80,256]{1,0:T(8,128)S(1)}, u32[]{:S(2)}, u32[]{:S(2)}) collective-permute-start(f32[80,256]{1,0:T(8,128)S(1)} %add_add_fusion.1), channel_id=1, source_target_pairs={{0,1},{1,0},{2,3},{3,2},{4,5},{5,4},{6,7},{7,6},{8,9},{9,8},{10,11... | collective-permute-start | bytes 245768 | tf_op jit(solution)/shard_map/ppermute | solution.py:70
  181.9 6.0 %collective-permute-start.31 = (f32[80,256]{1,0:T(8,128)S(1)}, f32[80,256]{1,0:T(8,128)S(1)}, u32[]{:S(2)}, u32[]{:S(2)}) collective-permute-start(f32[80,256]{1,0:T(8,128)S(1)} %add_add_fusion.1), channel_id=1, source_target_pairs={{0,17},{1,16},{2,19},{3,18},{4,21},{5,20},{6,23},{7,22},{8,25},{9,... | collective-permute-start | bytes 245768 | tf_op jit(solution)/shard_map/ppermute | solution.py:70
  188.0 31.2 %collective-permute-start.32 = (f32[320,256]{1,0:T(8,128)S(1)}, f32[320,256]{1,0:T(8,128)S(1)}, u32[]{:S(2)}, u32[]{:S(2)}) collective-permute-start(f32[320,256]{1,0:T(8,128)S(1)} %get-tuple-element.143), channel_id=1, source_target_pairs={{0,2},{1,3},{2,0},{3,1},{4,6},{5,7},{6,4},{7,5},{8,10},{9,11},{10,... | collective-permute-start | bytes 983048 | tf_op jit(solution)/shard_map/ppermute | solution.py:70
  188.1 31.1 %collective-permute-start.33 = (f32[320,256]{1,0:T(8,128)S(1)}, f32[320,256]{1,0:T(8,128)S(1)}, u32[]{:S(2)}, u32[]{:S(2)}) collective-permute-start(f32[320,256]{1,0:T(8,128)S(1)} %get-tuple-element.143), channel_id=1, source_target_pairs={{0,4},{1,5},{2,6},{3,7},{4,0},{5,1},{6,2},{7,3},{8,12},{9,13},{10,... | collective-permute-start | bytes 983048 | tf_op jit(solution)/shard_map/ppermute | solution.py:70
  189.8 29.4 %collective-permute-start.34 = (f32[320,256]{1,0:T(8,128)S(1)}, f32[320,256]{1,0:T(8,128)S(1)}, u32[]{:S(2)}, u32[]{:S(2)}) collective-permute-start(f32[320,256]{1,0:T(8,128)S(1)} %get-tuple-element.143), channel_id=1, source_target_pairs={{0,6},{1,7},{2,4},{3,5},{4,2},{5,3},{6,0},{7,1},{8,14},{9,15},{10,... | collective-permute-start | bytes 983048 | tf_op jit(solution)/shard_map/ppermute | solution.py:70
  192.8 26.8 %collective-permute-start.28 = (f32[128,1024]{1,0:T(8,128)S(1)}, f32[128,1024]{1,0:T(8,128)S(1)}, u32[]{:S(2)}, u32[]{:S(2)}) collective-permute-start(f32[128,1024]{1,0:T(8,128)S(1)} %fusion.4), channel_id=1, source_target_pairs={{0,0},{8,8},{1,16},{9,24},{2,32},{10,40},{3,48},{11,56},{4,64},{12... | collective-permute-start | bytes 1572872 | tf_op jit(solution)/shard_map/ppermute | solution.py:492
  219.5 24.2 %collective-permute-start.39 = (f32[1280,256]{1,0:T(8,128)S(1)}, f32[1280,256]{1,0:T(8,128)S(1)}, u32[]{:S(2)}, u32[]{:S(2)}) collective-permute-start(f32[1280,256]{1,0:T(8,128)S(1)} %pad_maximum_fusion.2), channel_id=1, source_target_pairs={{0,8},{1,9},{2,10},{3,11},{4,12},{5,13},{6,14},{7,15},{8,0},{9,1},... | collective-permute-start | bytes 3932168 | tf_op jit(solution)/shard_map/ppermute | solution.py:70
  219.8 16.6 %collective-permute-start.35 = (f32[64,1024]{1,0:T(8,128)S(1)}, f32[64,1024]{1,0:T(8,128)S(1)}, u32[]{:S(2)}, u32[]{:S(2)}) collective-permute-start(f32[64,1024]{1,0:T(8,128)S(1)} %get-tuple-element.141), channel_id=1, source_target_pairs={{0,1},{1,0},{2,3},{3,2},{4,5},{5,4},{6,7},{7,6},{8,9},{9,8},{10,11... | collective-permute-start | bytes 786440 | tf_op jit(solution)/shard_map/ppermute | solution.py:70
  221.3 15.1 %collective-permute-start.36 = (f32[64,1024]{1,0:T(8,128)S(1)}, f32[64,1024]{1,0:T(8,128)S(1)}, u32[]{:S(2)}, u32[]{:S(2)}) collective-permute-start(f32[64,1024]{1,0:T(8,128)S(1)} %get-tuple-element.140), channel_id=1, source_target_pairs={{0,2},{1,3},{2,0},{3,1},{4,6},{5,7},{6,4},{7,5},{8,10},{9,11},{10,... | collective-permute-start | bytes 786440 | tf_op jit(solution)/shard_map/ppermute | solution.py:70
  224.3 16.7 %collective-permute-start.37 = (f32[64,1024]{1,0:T(8,128)S(1)}, f32[64,1024]{1,0:T(8,128)S(1)}, u32[]{:S(2)}, u32[]{:S(2)}) collective-permute-start(f32[64,1024]{1,0:T(8,128)S(1)} %get-tuple-element.140), channel_id=1, source_target_pairs={{0,4},{1,5},{2,6},{3,7},{4,0},{5,1},{6,2},{7,3},{8,12},{9,13},{10,... | collective-permute-start | bytes 786440 | tf_op jit(solution)/shard_map/ppermute | solution.py:70
  228.9 14.7 %collective-permute-start.38 = (f32[64,1024]{1,0:T(8,128)S(1)}, f32[64,1024]{1,0:T(8,128)S(1)}, u32[]{:S(2)}, u32[]{:S(2)}) collective-permute-start(f32[64,1024]{1,0:T(8,128)S(1)} %get-tuple-element.140), channel_id=1, source_target_pairs={{0,6},{1,7},{2,4},{3,5},{4,2},{5,3},{6,0},{7,1},{8,14},{9,15},{10,... | collective-permute-start | bytes 786440 | tf_op jit(solution)/shard_map/ppermute | solution.py:70
  245.6 192.0 %collective-permute-start.43 = (f32[4,64,1024]{2,1,0:T(8,128)S(1)}, f32[4,64,1024]{2,1,0:T(8,128)S(1)}, u32[]{:S(2)}, u32[]{:S(2)}) collective-permute-start(f32[4,64,1024]{2,1,0:T(8,128)S(1)} %pad_maximum_fusion.4.quad), channel_id=1, source_target_pairs={{0,1},{1,0},{2,3},{3,2},{4,5},{5,4},{6,7},{7,6},{8,9},{9,8},{10,11... | collective-permute-start | bytes 3145736 | tf_op jit(solution)/shard_map/ppermute | solution.py:70
  249.0 188.5 %collective-permute-start.40 = (f32[2,64,1024]{2,1,0:T(8,128)S(1)}, f32[2,64,1024]{2,1,0:T(8,128)S(1)}, u32[]{:S(2)}, u32[]{:S(2)}) collective-permute-start(f32[2,64,1024]{2,1,0:T(8,128)S(1)} %pad_maximum_fusion.10.own), channel_id=1, source_target_pairs={{0,2},{1,3},{2,0},{3,1},{4,6},{5,7},{6,4},{7,5},{8,10},{9,11},{10,... | collective-permute-start | bytes 1572872 | tf_op jit(solution)/shard_map/ppermute | solution.py:70
  249.0 188.6 %collective-permute-start.41 = (f32[2,64,1024]{2,1,0:T(8,128)S(1)}, f32[2,64,1024]{2,1,0:T(8,128)S(1)}, u32[]{:S(2)}, u32[]{:S(2)}) collective-permute-start(f32[2,64,1024]{2,1,0:T(8,128)S(1)} %pad_maximum_fusion.10.own), channel_id=1, source_target_pairs={{0,4},{1,5},{2,6},{3,7},{4,0},{5,1},{6,2},{7,3},{8,12},{9,13},{10,... | collective-permute-start | bytes 1572872 | tf_op jit(solution)/shard_map/ppermute | solution.py:70
  250.7 186.8 %collective-permute-start.42 = (f32[2,64,1024]{2,1,0:T(8,128)S(1)}, f32[2,64,1024]{2,1,0:T(8,128)S(1)}, u32[]{:S(2)}, u32[]{:S(2)}) collective-permute-start(f32[2,64,1024]{2,1,0:T(8,128)S(1)} %pad_maximum_fusion.10.own), channel_id=1, source_target_pairs={{0,6},{1,7},{2,4},{3,5},{4,2},{5,3},{6,0},{7,1},{8,14},{9,15},{10,... | collective-permute-start | bytes 1572872 | tf_op jit(solution)/shard_map/ppermute | solution.py:70
  (12 other events, 69.8 us)
Sparse Core Ops, SparseCore 0:
  219.7 69.6 all-gather.2

commit v5 on v4

--- a/solution.py
+++ b/solution.py
@@ -132,17 +132,13 @@
     return lax.optimization_barrier(values)
 
 
-def sum_start(x, core, z, x_place):
+def sum_cores(x, core):
     keep, send = halves(x, core == 1)
-    x = keep + swap(send, CORE)
-    return scatter_four(scatter_four(x, z, Z), x_place, X)
-
-
-def sum_middle(x):
-    return x + swap(x, Y[1]) + swap(x, Y[2]) + swap(x, Y[3])
-
-
-def sum_spread(x, x_place, z):
+    return keep + swap(send, CORE)
+
+
+def sum_rest(x, x_place, z):
+    x = x + swap(x, Y[1]) + swap(x, Y[2]) + swap(x, Y[3])
     return gather_four(gather_four(x, x_place, X), z, Z)
 
 
@@ -174,6 +170,7 @@
         gram_kernel,
         out_shape=jax.ShapeDtypeStruct((10, PANEL, PANEL), F32),
         compiler_params=pltpu.CompilerParams(vmem_limit_bytes=VMEM_LIMIT),
+        cost_estimate=pl.CostEstimate(flops=1 << 20, bytes_accessed=1 << 20, transcendentals=0),
     )(inputs, product)
 
 
@@ -346,59 +343,83 @@
     return diagonal[:, :, None] * centre + COUPLING * neighbours
 
 
-def plant_kernel(start, last, sides, place, *refs):
-    blocks, ends = refs[:9], refs[9 : 9 + sides]
-    rows_diag, cols_diag, cost = refs[9 + sides : 12 + sides]
-    out = refs[-1]
-    b = pl.program_id(0) + start
+def plant_kernel(start, sizes, place, *refs):
+    columns, at = [], 0
+    for size in sizes:
+        columns.append(refs[at : at + size])
+        at += size
+    rows_diag, cols_diag, cost = refs[at : at + 3]
+    out, window = refs[-2:]
+    step = pl.program_id(0)
+    b = step + start
     rows = out.shape[0]
     lanes = lax.broadcasted_iota(jnp.int32, (1, LINE), 1)
     inner = lax.broadcasted_iota(jnp.int32, (LINE, 1), 0)
-    column = lambda k: jnp.concatenate([blocks[3 * k][...], blocks[3 * k + 1][...], blocks[3 * k + 2][...]], 0)
-    here = column(1)
-    before, after = column(0), column(2)
-    if sides:
-        before = jnp.where(b == 0, ends[0][...], before)
-        after = jnp.where(b == last, ends[1][...], after)
+    column = lambda k: jnp.concatenate([ref[...] for ref in columns[k]], 0)
+
+    @pl.when(step == 0)
+    def _():
+        window[0] = column(0)
+        window[1] = column(1)
+
+    here = window[1]
+    after = column(2)
     sides = jnp.where(lanes == 0, 0.0, pltpu.roll(here, 1, 1)) + jnp.where(
         lanes == LINE - 1, 0.0, pltpu.roll(here, LINE - 1, 1)
     )
-    field = cols_diag[pl.ds(b, 1), :] * here + COUPLING * (before + after + sides)
+    field = cols_diag[pl.ds(b, 1), :] * here + COUPLING * (window[0] + after + sides)
+    window[0] = here
+    window[1] = after
     for a in range(rows // LINE):
         line = lambda k: field[(a + k) * LINE : (a + k + 1) * LINE]
         centre = line(1)
         sides = jnp.where(inner == 0, 0.0, pltpu.roll(centre, 1, 0)) + jnp.where(
             inner == LINE - 1, 0.0, pltpu.roll(centre, LINE - 1, 0)
         )
-        new = rows_diag[:, a : a + 1] * centre + COUPLING * (line(0) + line(2) + sides)
-        on_diagonal = (inner == lanes) & (place[0] + a == place[1] + b)
-        out[a * LINE : (a + 1) * LINE, :] = new + jnp.where(on_diagonal, cost[a : a + 1, :], 0.0)
+        here = slice(a * LINE, (a + 1) * LINE)
+        out[here, :] = rows_diag[here, :] * centre + COUPLING * (line(0) + line(2) + sides)
+    mine = place[1] + b - place[0]
+
+    @pl.when((mine >= 0) & (mine < rows // LINE))
+    def _():
+        here = pl.ds(pl.multiple_of(mine * LINE, LINE), LINE)
+        out[here, :] += jnp.where(inner == lanes, cost[pl.ds(mine, 1), :], 0.0)
 
 
 def plant_part(start, count, place, value, above, below, left, right, rows_diag, cols_diag, cost, before):
     rows, cols = value.shape
     last = cols // LINE - 1
     array = pl.BlockSpec(memory_space=pltpu.VMEM)
-    blocks, specs = [], []
-    for step in (-1, 0, 1):
-        index = lambda b, step=step: (0, jnp.clip(b + start + step, 0, last))
-        for x in (above, value, below):
-            blocks.append(x)
-            specs.append(pl.BlockSpec((x.shape[0], LINE), index))
-    sides = [] if left is None else [left, right]
-    operands = [place, *blocks, *sides, rows_diag, cols_diag, cost]
-    specs = [pl.BlockSpec(memory_space=pltpu.SMEM)] + specs + [array] * (3 + len(sides))
+    tall = rows + 2 * LINE
+
+    def column(index):
+        blocks = (above, value, below)
+        return list(blocks), [pl.BlockSpec((x.shape[0], LINE), index) for x in blocks]
+
+    whole = lambda x: ([x], [pl.BlockSpec((tall, LINE), lambda b: (0, 0))])
+    columns = [
+        whole(left) if start == 0 else column(lambda b: (0, start - 1)),
+        column(lambda b: (0, start)),
+        whole(right) if start == last else column(lambda b: (0, b + start + 1)),
+    ]
+    operands, specs = [place], [pl.BlockSpec(memory_space=pltpu.SMEM)]
+    for blocks, block_specs in columns:
+        operands += blocks
+        specs += block_specs
+    operands += [rows_diag, cols_diag, cost]
+    specs += [array] * 3
     aliases = {}
     if before is not None:
         aliases = {len(operands): 0}
         operands.append(before)
         specs.append(pl.BlockSpec(memory_space=pl.ANY))
     return pl.pallas_call(
-        functools.partial(plant_kernel, start, last, len(sides)),
+        functools.partial(plant_kernel, start, [len(blocks) for blocks, _ in columns]),
         grid=(count,),
         in_specs=specs,
         out_specs=pl.BlockSpec((rows, LINE), lambda b: (0, b + start)),
         out_shape=jax.ShapeDtypeStruct(value.shape, F32),
+        scratch_shapes=[pltpu.VMEM((2, tall, LINE), F32)],
         input_output_aliases=aliases,
         compiler_params=pltpu.CompilerParams(vmem_limit_bytes=VMEM_LIMIT),
         cost_estimate=pl.CostEstimate(flops=32 << 20, bytes_accessed=16 << 20, transcendentals=0),
@@ -442,7 +463,7 @@
         below,
         left,
         right,
-        diag_rows.T,
+        jnp.broadcast_to(diag_rows.reshape(rows_block, 1), (rows_block, LINE)),
         diag_cols,
         state_cost.reshape(lines_rows, grid_side),
     )
@@ -456,8 +477,8 @@
 
     def first_wait(c_got, d_got):
         middle = (*operands[:2], held["above"], held["below"], None, None, *operands[6:])
-        base = plant_part(4, 4, *middle, None)
-        base = plant_part(8, 4, *middle, base)
+        base = plant_part(1, 7, *middle, None)
+        base = plant_part(8, 7, *middle, base)
         c_got, d_got, held["base"] = tied(c_got, d_got, base)
         return c_got, d_got
 
@@ -473,8 +494,6 @@
     mine_inputs = held["inputs"]
     operands = (*operands[:2], held["above"], held["below"], held["left"], held["right"], *operands[6:])
 
-    gram = gram_blocks(mine_inputs, product)
-    product, gram = tied(product, gram)
     core, x_low, y = row_index & 1, (row_index >> 1) & 1, row_index >> 2
     x_high, z = col_index & 1, col_index >> 1
     x_place = x_high * 2 + x_low
@@ -482,27 +501,31 @@
     lines = grid_side
     over = lax.ppermute(product, both, [(device_of(i), device_of(i + 1)) for i in range(lines - 1)])
     under = lax.ppermute(product, both, [(device_of(i + 1), device_of(i)) for i in range(lines - 1)])
-    total = sum_start(gram.reshape(10 * PANEL, PANEL), core, z, x_place)
+    gram = gram_blocks(mine_inputs, product)
+    total = sum_cores(gram.reshape(10 * PANEL, PANEL), core)
     line = col_index * 16 + line_of(row_index)
     diagonal = lax.dynamic_slice_in_dim(plant_diag, line, 1, 0)
+    over, under, total = tied(over, under, total)
     gain = stencil_first(jnp.stack([over, product, under]), diagonal)[0]
     gain, total = tied(gain, total)
-    total = sum_middle(total)
-    gain, total = tied(gain, total)
+
+    gain_cols = lax.all_gather(gain, "row", axis=0)
     traded = lax.ppermute(gain, both, trade)
-    total = sum_spread(total, x_place, z)
-    traded, gain, total = tied(traded, gain, total)
-
-    gain_cols = lax.all_gather(gain, "row", axis=0)
+    total = scatter_four(total, z, Z)
+    traded, total = tied(traded, total)
+
     pair, quad = gather_rows_start(traded)
+    total = scatter_four(total, x_place, X)
+    pair, quad, total = tied(pair, quad, total)
+
+    sides = gather_rows_end(pair, quad)
+    total = sum_rest(total, x_place, z)
+    *sides, total = tied(*sides, total)
+    base = plant_part(0, 1, *operands, held["base"])
+    base = plant_part(lines_cols - 1, 1, *operands, base)
     total = joined(total, swap(total, CORE), core == 1)
-    base = plant_part(0, 4, *operands, held["base"])
-    pair, quad, total, base = tied(pair, quad, total, base)
-    sides = gather_rows_end(pair, quad)
+    total, base = tied(total, base)
     factors = factored(control_weight, total.reshape(10, PANEL, PANEL))
-    *factors, base = tied(*factors, base)
-    base = plant_part(12, 4, *operands, base)
-    *sides, base = tied(*sides, base)
     solved = solve(jnp.stack([z, x_high]).astype(jnp.int32), factors, sides)
     return downdate(solved, gain_cols, base)
 

time: 488 us -> 519 us (1.064)
  the two profiles are of different devices: /device:TPU:8 before, /device:TPU:33 now
where the time goes in v5:
time: 519 us; the launch traced here: 508 us
  Pallas kernels  260 us (50%)
  waiting for transfers between devices  104 us (20%)
  starting transfers between devices  101 us (19%)
  other arithmetic  18.2 us (4%)
  between operations  15.3 us (3%)
  local copies, waits for them, and re-layouts  10.2 us (2%)
    pallas_call x1, Pallas kernels, factored(): pl.pallas_call(factor_kernel, out_shape=[jax.ShapeDtypeStruct((10, PANEL,...  176 us
    ppermute x36, waiting for transfers between devices, swap(): return lax.ppermute(x, ('row', 'col'), [(i, i ^ mask) for i in range(128)])  71.2 us
    ppermute x36, starting transfers between devices, swap(): return lax.ppermute(x, ('row', 'col'), [(i, i ^ mask) for i in range(128)])  69.7 us
    pallas_call x4, Pallas kernels, plant_part(): pl.pallas_call(functools.partial(plant_kernel, start, [len(blocks) for bl...  24.8 us
    pallas_call x2, Pallas kernels, product_lines(): pl.pallas_call(product_kernel, grid_spec=pltpu.PrefetchScalarGridSpec(num...  23.4 us
    pallas_call x1, Pallas kernels, downdate(): pl.pallas_call(downdate_kernel, grid=(8,), in_specs=[whole, whole, pl.Blo...  19.3 us
    ppermute x4, starting transfers between devices, shifted(): lax.ppermute(x, axis, [(i, i + by) for i in range(count) if 0 <= i + by <...  17.4 us
    pallas_call x1, Pallas kernels, solve(): pl.pallas_call(solve_kernel, out_shape=[jax.ShapeDtypeStruct((size, 4 * P...  12.6 us
  transfers between devices with their start and end apart: 45, of which 19 were waited for; matrix products, arithmetic and copies ran while one was open for 5% of the time, Pallas kernels for 44%

profile of v5, /device:TPU:33, one launch (start us, length us, event | category | flops | bytes accessed | tf_op | source)
XLA Modules:
  0.0 508.4 jit_solution(14706279724182340433)
XLA Ops:
  6.5 11.7 %shard_map.56 = f32[8,128,1024]{2,1,0:T(8,128)} custom-call(s32[1]{0:T(128)} %bitcast.3.me_ref, f32[1024,2048]{1,0:T(8,128)} %refs_4_.5, f32[1024,2048]{1,0:T(8,128)} %refs_4_.5, f32[1024,1024]{1,0:T(8,128)} %inputs.3), custom_call_target="tpu_custom_call" | custom-call | flops 1048576 | bytes 1048576 | tf_op jit(solution)/shard_map/pallas_call | solution.py:50
  18.9 2.7 fusion.30
  21.7 1.9 collective-permute-start.2
  23.6 3.6 collective-permute-start.1
  27.2 1.9 constant_dynamic-slice_fusion.8
  29.2 2.7 collective-permute-start.4
  31.9 11.7 %shard_map.55 = f32[8,128,1024]{2,1,0:T(8,128)} custom-call(s32[1]{0:T(128)} %bitcast.3.me_ref, f32[1024,2048]{1,0:T(8,128)} %refs_4_.5, f32[1024,2048]{1,0:T(8,128)} %refs_4_.5, f32[1024,1024]{1,0:T(8,128)} %inputs.3), custom_call_target="tpu_custom_call" | custom-call | flops 1048576 | bytes 1048576 | tf_op jit(solution)/shard_map/pallas_call | solution.py:50
  47.0 5.5 %collective-permute-start.7 = (f32[1280,128]{1,0:T(8,128)S(1)}, f32[1280,128]{1,0:T(8,128)S(1)}, u32[]{:S(2)}, u32[]{:S(2)}) collective-permute-start(f32[1280,128]{1,0:T(8,128)S(1)} %pad_maximum_fusion.5), channel_id=1, source_target_pairs={{0,1},{1,2},{2,3},{3,4},{4,5},{5,6},{6,7},{8,9},{9,10},{10,11},{11... | collective-permute-start | bytes 1966088 | tf_op jit(solution)/shard_map/ppermute | solution.py:452
  57.2 2.4 collective-permute-start.11
  59.7 5.0 collective-permute-start.12
  69.0 9.2 %shard_map.57.refs_12_ = f32[1024,2048]{1,0:T(8,128)} custom-call(s32[2]{0:T(128)} %pad_add_fusion.1.place, f32[128,2048]{1,0:T(8,128)} %copy-done.3, f32[1024,2048]{1,0:T(8,128)} %refs_4_.5, f32[128,2048]{1,0:T(8,128)} %copy-done.2, f32[128,2048]{1,0:T(8,128)} %copy-done.3, f32[1024,2048]{1,0:T(8,128)} %refs_4_.5, f32[128,2048]{1,0:T(8,128)} %copy-done.2, ...), custom_call_target="tpu_custom_call" | custom-call | flops 33554432 | bytes 16777216 | tf_op jit(solution)/shard_map/pallas_call | solution.py:416
  78.1 9.2 %shard_map.58.refs_10_ = f32[1024,2048]{1,0:T(8,128)} custom-call(s32[2]{0:T(128)} %pad_add_fusion.1.place, f32[128,2048]{1,0:T(8,128)} %copy-done.3, f32[1024,2048]{1,0:T(8,128)} %refs_4_.5, f32[128,2048]{1,0:T(8,128)} %copy-done.2, f32[128,2048]{1,0:T(8,128)} %copy-done.3, f32[1024,2048]{1,0:T(8,128)} %refs_4_.5, ...), custom_call_target="tpu_custom_call", output_to_operand_aliasing={{}: (13, {})} | custom-call | flops 33554432 | bytes 16777216 | tf_op jit(solution)/shard_map/pallas_call | solution.py:416
  88.4 6.3 %collective-permute-start.8 = (f32[1280,128]{1,0:T(8,128)S(1)}, f32[1280,128]{1,0:T(8,128)S(1)}, u32[]{:S(2)}, u32[]{:S(2)}) collective-permute-start(f32[1280,128]{1,0:T(8,128)S(1)} %pad_maximum_fusion.6), channel_id=1, source_target_pairs={{1,0},{2,1},{3,2},{4,3},{5,4},{6,5},{7,6},{9,8},{10,9},{11,10},{12... | collective-permute-start | bytes 1966088 | tf_op jit(solution)/shard_map/ppermute | solution.py:452
  94.8 2.8 collective-permute-start.13
  97.6 4.2 collective-permute-done.13
  102.1 1.8 collective-permute-start.5
  104.0 2.9 collective-permute-start.6
  108.0 3.0 collective-permute-done.6
  111.1 3.4 collective-permute-start.9
  114.8 2.0 collective-permute-done.9
  116.8 2.0 collective-permute-done.10
  120.7 3.9 shard_map.59
  124.6 2.0 slice_select_fusion.1
  126.7 3.7 collective-permute-start.18
  130.4 1.9 collective-permute-start.17
  132.3 3.4 collective-permute-start.16
  137.2 8.5 %collective-permute-done.17 = f32[128,1024]{1,0:T(8,128)S(1)} collective-permute-done((f32[128,1024]{1,0:T(8,128)S(1)}, f32[128,1024]{1,0:T(8,128)S(1)}, u32[]{:S(2)}, u32[]{:S(2)}) %collective-permute-start.17) | collective-permute-done | bytes 524320 | tf_op jit(solution)/shard_map/ppermute | solution.py:503
  145.8 11.4 %collective-permute-done.16 = f32[128,1024]{1,0:T(8,128)S(1)} collective-permute-done((f32[128,1024]{1,0:T(8,128)S(1)}, f32[128,1024]{1,0:T(8,128)S(1)}, u32[]{:S(2)}, u32[]{:S(2)}) %collective-permute-start.16) | collective-permute-done | bytes 524320 | tf_op jit(solution)/shard_map/ppermute | solution.py:502
  159.0 5.3 %collective-permute-start.22 = (f32[320,256]{1,0:T(8,128)S(1)}, f32[320,256]{1,0:T(8,128)}, u32[]{:S(2)}, u32[]{:S(2)}) collective-permute-start(f32[320,256]{1,0:T(8,128)S(1)} %get-tuple-element.120), channel_id=1, source_target_pairs={{0,6},{1,7},{2,4},{3,5},{4,2},{5,3},{6,0},{7,1},{8,14},{9,15},{10,... | collective-permute-start | bytes 983048 | tf_op jit(solution)/shard_map/ppermute | solution.py:70
  165.5 5.6 %collective-permute-start.19 = (f32[128,1024]{1,0:T(8,128)S(1)}, f32[128,1024]{1,0:T(8,128)S(1)}, u32[]{:S(2)}, u32[]{:S(2)}) collective-permute-start(f32[128,1024]{1,0:T(8,128)S(1)} %copy-done.7), channel_id=1, source_target_pairs={{0,0},{8,8},{1,16},{9,24},{2,32},{10,40},{3,48},{11,56},{4,64},{12... | collective-permute-start | bytes 1572872 | tf_op jit(solution)/shard_map/ppermute | solution.py:513
  171.2 7.1 %collective-permute-done.22 = f32[320,256]{1,0:T(8,128)} collective-permute-done((f32[320,256]{1,0:T(8,128)S(1)}, f32[320,256]{1,0:T(8,128)}, u32[]{:S(2)}, u32[]{:S(2)}) %collective-permute-start.22) | collective-permute-done | bytes 327712 | tf_op jit(solution)/shard_map/ppermute | solution.py:70
  179.4 12.5 %collective-permute-done.19 = f32[128,1024]{1,0:T(8,128)S(1)} collective-permute-done((f32[128,1024]{1,0:T(8,128)S(1)}, f32[128,1024]{1,0:T(8,128)S(1)}, u32[]{:S(2)}, u32[]{:S(2)}) %collective-permute-start.19) | collective-permute-done | bytes 524320 | tf_op jit(solution)/shard_map/ppermute | solution.py:513
  197.0 4.0 collective-permute-start.25
  201.0 6.1 %collective-permute-start.24 = (f32[64,1024]{1,0:T(8,128)S(1)}, f32[64,1024]{1,0:T(8,128)S(1)}, u32[]{:S(2)}, u32[]{:S(2)}) collective-permute-start(f32[64,1024]{1,0:T(8,128)S(1)} %get-tuple-element.132), channel_id=1, source_target_pairs={{0,2},{1,3},{2,0},{3,1},{4,6},{5,7},{6,4},{7,5},{8,10},{9,11},{10,... | collective-permute-start | bytes 786440 | tf_op jit(solution)/shard_map/ppermute | solution.py:70
  207.2 9.8 %collective-permute-done.24 = f32[64,1024]{1,0:T(8,128)S(1)} collective-permute-done((f32[64,1024]{1,0:T(8,128)S(1)}, f32[64,1024]{1,0:T(8,128)S(1)}, u32[]{:S(2)}, u32[]{:S(2)}) %collective-permute-start.24) | collective-permute-done | bytes 262176 | tf_op jit(solution)/shard_map/ppermute | solution.py:70
  218.5 9.0 %collective-permute-start.36 = (f32[80,256]{1,0:T(8,128)S(1)}, f32[80,256]{1,0:T(8,128)S(1)}, u32[]{:S(2)}, u32[]{:S(2)}) collective-permute-start(f32[80,256]{1,0:T(8,128)S(1)} %add_add_fusion.2), channel_id=1, source_target_pairs={{0,96},{1,97},{2,98},{3,99},{4,100},{5,101},{6,102},{7,103},{8,104... | collective-permute-start | bytes 245768 | tf_op jit(solution)/shard_map/ppermute | solution.py:70
  229.3 4.2 collective-permute-done.35
  235.2 1.9 collective-permute-start.39
  240.0 1.8 collective-permute-done.38
  242.3 3.0 collective-permute-start.42
  245.4 4.6 collective-permute-done.41
  253.7 25.1 %collective-permute-done.32.far = f32[2,64,1024]{2,1,0:T(8,128)S(1)} collective-permute-done((f32[2,64,1024]{2,1,0:T(8,128)S(1)}, f32[2,64,1024]{2,1,0:T(8,128)S(1)}, u32[]{:S(2)}, u32[]{:S(2)}) %collective-permute-start.32) | collective-permute-done | bytes 524320 | tf_op jit(solution)/shard_map/ppermute | solution.py:70
  278.8 4.5 collective-permute-start.43
  284.6 3.1 shard_map.60.refs_10_
  287.8 3.3 shard_map.61.base
  292.9 176.4 %shard_map.62 = (f32[10,256,256]{2,1,0:T(8,128)}, f32[4,256,256]{2,1,0:T(8,128)}) custom-call(f32[1]{0:T(128)S(6)} %copy.12.weight, f32[10,256,256]{2,1,0:T(8,128)} %bitcast.145), custom_call_target="tpu_custom_call" | custom-call | flops 9663676416 | bytes 12582912 | tf_op jit(solution)/shard_map/pallas_call | solution.py:257
  469.3 12.6 %shard_map.63 = (bf16[1024,1024]{1,0:T(8,128)(2,1)}, bf16[1024,1024]{1,0:T(8,128)(2,1)}) custom-call(s32[2]{0:T(128)} %pad_add_fusion.place, f32[10,256,256]{2,1,0:T(8,128)} %get-tuple-element.64.factor, f32[4,256,256]{2,1,0:T(8,128)} %get-tuple-element.65.inverses, f32[2,64,1024]{2,1,0:T(8,128)} %copy-done.15, f32[2,64,1024]{2,1,0:T(8,128)} %copy-done.18, ...), custom_call_target="tpu_custom_call" | custom-call | flops 9663676416 | bytes 12582912 | tf_op jit(solution)/shard_map/pallas_call | solution.py:301
  481.9 19.3 %shard_map.64 = f32[1024,2048]{1,0:T(8,128)} custom-call(bf16[1024,1024]{1,0:T(8,128)(2,1)} %get-tuple-element.72.high, bf16[1024,1024]{1,0:T(8,128)(2,1)} %get-tuple-element.73.low, f32[16,128,1024]{2,1,0:T(8,128)} %bitcast.165, f32[16,128,1024]{2,1,0:T(8,128)} %bitcast.166, f32[1024,2048]{1,0:T(8,128)} %shard_map.61.base), custom_call_target="tpu_custom_call" | custom-call | flops 12884901888 | bytes 29360128 | tf_op jit(solution)/shard_map/pallas_call | solution.py:322
  (153 shorter events, 43.2 us)
Async XLA Ops:
  6.5 37.7 %copy-start = (f32[128,128]{1,0:T(8,128)S(1)}, f32[128,128]{1,0:T(8,128)}, u32[]{:S(2)}) copy-start(f32[128,128]{1,0:T(8,128)} %param.7) | copy-start | bytes 196612
  6.5 475.4 %all-gather.3.cloned.1.call-start = ((), (), s32[]{:S(2)}) async-start(), calls=%async_computation | async-start | bytes 8912896 | tf_op jit(solution)/shard_map/all_gather | solution.py:512
  18.3 34.3 %collective-permute-start = (f32[8,128,1024]{2,1,0:T(8,128)}, f32[8,128,1024]{2,1,0:T(8,128)}, u32[]{:S(2)}, u32[]{:S(2)}) collective-permute-start(f32[8,128,1024]{2,1,0:T(8,128)} %shard_map.56), channel_id=1, source_target_pairs={{0,8},{1,9},{2,10},{3,11},{4,12},{5,13},{6,14},{7,15},{8,0},{9,1},... | collective-permute-start | bytes 12582920 | tf_op jit(solution)/shard_map/ppermute | solution.py:70
  21.7 24.6 %collective-permute-start.2 = (f32[128,2048]{1,0:T(8,128)}, f32[128,2048]{1,0:T(8,128)S(1)}, u32[]{:S(2)}, u32[]{:S(2)}) collective-permute-start(f32[128,2048]{1,0:T(8,128)} %get-tuple-element.109), channel_id=1, source_target_pairs={{8,0},{16,8},{24,16},{32,24},{40,32},{48,40},{56,48},{64,56},{72,6... | collective-permute-start | bytes 3145736 | tf_op jit(solution)/shard_map/ppermute | solution.py:452
  23.6 22.7 %collective-permute-start.1 = (f32[128,2048]{1,0:T(8,128)S(1)}, f32[128,2048]{1,0:T(8,128)S(1)}, u32[]{:S(2)}, u32[]{:S(2)}) collective-permute-start(f32[128,2048]{1,0:T(8,128)S(1)} %get-tuple-element.110), channel_id=1, source_target_pairs={{0,8},{8,16},{16,24},{24,32},{32,40},{40,48},{48,56},{56,64},{64,7... | collective-permute-start | bytes 3145736 | tf_op jit(solution)/shard_map/ppermute | solution.py:452
  29.2 72.7 %collective-permute-start.4 = (f32[128,1024]{1,0:T(8,128)}, f32[128,1024]{1,0:T(8,128)}, u32[]{:S(2)}, u32[]{:S(2)}) collective-permute-start(f32[128,1024]{1,0:T(8,128)} %constant_dynamic-slice_fusion.8), channel_id=1, source_target_pairs={{0,0},{8,8},{1,16},{9,24},{2,32},{10,40},{3,48},{11,56},{4,64},{12... | collective-permute-start | bytes 1572872 | tf_op jit(solution)/shard_map/ppermute | solution.py:448
  47.0 60.0 %collective-permute-start.7 = (f32[1280,128]{1,0:T(8,128)S(1)}, f32[1280,128]{1,0:T(8,128)S(1)}, u32[]{:S(2)}, u32[]{:S(2)}) collective-permute-start(f32[1280,128]{1,0:T(8,128)S(1)} %pad_maximum_fusion.5), channel_id=1, source_target_pairs={{0,1},{1,2},{2,3},{3,4},{4,5},{5,6},{6,7},{8,9},{9,10},{10,11},{11... | collective-permute-start | bytes 1966088 | tf_op jit(solution)/shard_map/ppermute | solution.py:452
  57.2 30.1 %collective-permute-start.11 = (f32[2,2,32,1024]{3,2,1,0:T(8,128)S(1)}, f32[2,2,32,1024]{3,2,1,0:T(8,128)S(1)}, u32[]{:S(2)}, u32[]{:S(2)}) collective-permute-start(f32[2,2,32,1024]{3,2,1,0:T(8,128)S(1)} %pad_maximum_fusion.7), channel_id=1, source_target_pairs={{0,32},{1,33},{2,34},{3,35},{4,36},{5,37},{6,38},{7,39},{8,40},{9,... | collective-permute-start | bytes 1572872 | tf_op jit(solution)/shard_map/ppermute | solution.py:70
  59.7 27.7 %collective-permute-start.12 = (f32[2,2,32,1024]{3,2,1,0:T(8,128)S(1)}, f32[2,2,32,1024]{3,2,1,0:T(8,128)S(1)}, u32[]{:S(2)}, u32[]{:S(2)}) collective-permute-start(f32[2,2,32,1024]{3,2,1,0:T(8,128)S(1)} %pad_maximum_fusion.8), channel_id=1, source_target_pairs={{0,96},{1,97},{2,98},{3,99},{4,100},{5,101},{6,102},{7,103},{8,104... | collective-permute-start | bytes 1572872 | tf_op jit(solution)/shard_map/ppermute | solution.py:70
  66.4 35.5 %collective-permute-start.3 = (f32[4,64,1024]{2,1,0:T(8,128)S(1)}, f32[4,64,1024]{2,1,0:T(8,128)S(1)}, u32[]{:S(2)}, u32[]{:S(2)}) collective-permute-start(f32[4,64,1024]{2,1,0:T(8,128)S(1)} %pad_maximum_fusion.3), channel_id=1, source_target_pairs={{0,16},{1,17},{2,18},{3,19},{4,20},{5,21},{6,22},{7,23},{8,24},{9,... | collective-permute-start | bytes 3145736 | tf_op jit(solution)/shard_map/ppermute | solution.py:70
  87.4 7.4 %collective-permute-start.14 = (f32[2,32,1024]{2,1,0:T(8,128)S(1)}, f32[2,32,1024]{2,1,0:T(8,128)S(1)}, u32[]{:S(2)}, u32[]{:S(2)}) collective-permute-start(f32[2,32,1024]{2,1,0:T(8,128)S(1)} %maximum_add_fusion.7), channel_id=1, source_target_pairs={{0,32},{1,33},{2,34},{3,35},{4,36},{5,37},{6,38},{7,39},{8,40},{9,... | collective-permute-start | bytes 786440 | tf_op jit(solution)/shard_map/ppermute | solution.py:70
  88.4 18.7 %collective-permute-start.8 = (f32[1280,128]{1,0:T(8,128)S(1)}, f32[1280,128]{1,0:T(8,128)S(1)}, u32[]{:S(2)}, u32[]{:S(2)}) collective-permute-start(f32[1280,128]{1,0:T(8,128)S(1)} %pad_maximum_fusion.6), channel_id=1, source_target_pairs={{1,0},{2,1},{3,2},{4,3},{5,4},{6,5},{7,6},{9,8},{10,9},{11,10},{12... | collective-permute-start | bytes 1966088 | tf_op jit(solution)/shard_map/ppermute | solution.py:452
  94.8 7.1 %collective-permute-start.13 = (f32[2,32,1024]{2,1,0:T(8,128)S(1)}, f32[2,32,1024]{2,1,0:T(8,128)S(1)}, u32[]{:S(2)}, u32[]{:S(2)}) collective-permute-start(f32[2,32,1024]{2,1,0:T(8,128)S(1)} %maximum_add_fusion.5), channel_id=1, source_target_pairs={{0,96},{1,97},{2,98},{3,99},{4,100},{5,101},{6,102},{7,103},{8,104... | collective-permute-start | bytes 786440 | tf_op jit(solution)/shard_map/ppermute | solution.py:70
  102.1 5.9 %collective-permute-start.5 = (f32[2,32,1024]{2,1,0:T(8,128)S(1)}, f32[2,32,1024]{2,1,0:T(8,128)S(1)}, u32[]{:S(2)}, u32[]{:S(2)}) collective-permute-start(f32[2,32,1024]{2,1,0:T(8,128)S(1)} %pad_maximum_fusion.13), channel_id=1, source_target_pairs={{0,32},{1,33},{2,34},{3,35},{4,36},{5,37},{6,38},{7,39},{8,40},{9,... | collective-permute-start | bytes 786440 | tf_op jit(solution)/shard_map/ppermute | solution.py:70
  104.0 7.0 %collective-permute-start.6 = (f32[2,32,1024]{2,1,0:T(8,128)S(1)}, f32[2,32,1024]{2,1,0:T(8,128)S(1)}, u32[]{:S(2)}, u32[]{:S(2)}) collective-permute-start(f32[2,32,1024]{2,1,0:T(8,128)S(1)} %pad_maximum_fusion.14), channel_id=1, source_target_pairs={{0,96},{1,97},{2,98},{3,99},{4,100},{5,101},{6,102},{7,103},{8,104... | collective-permute-start | bytes 786440 | tf_op jit(solution)/shard_map/ppermute | solution.py:70
  106.9 7.8 %collective-permute-start.15 = (f32[64,1024]{1,0:T(8,128)S(1)}, f32[64,1024]{1,0:T(8,128)S(1)}, u32[]{:S(2)}, u32[]{:S(2)}) collective-permute-start(f32[64,1024]{1,0:T(8,128)S(1)} %pad_maximum_fusion.15), channel_id=1, source_target_pairs={{0,16},{1,17},{2,18},{3,19},{4,20},{5,21},{6,22},{7,23},{8,24},{9,... | collective-permute-start | bytes 786440 | tf_op jit(solution)/shard_map/ppermute | solution.py:70
  111.1 5.7 %collective-permute-start.9 = (f32[32,1024]{1,0:T(8,128)S(1)}, f32[32,1024]{1,0:T(8,128)S(1)}, u32[]{:S(2)}, u32[]{:S(2)}) collective-permute-start(f32[32,1024]{1,0:T(8,128)S(1)} %slice_add_fusion.18), channel_id=1, source_target_pairs={{0,96},{1,97},{2,98},{3,99},{4,100},{5,101},{6,102},{7,103},{8,104... | collective-permute-start | bytes 393224 | tf_op jit(solution)/shard_map/ppermute | solution.py:70
  114.5 4.4 collective-permute-start.10
  126.7 9.0 %collective-permute-start.18 = (f32[1280,256]{1,0:T(8,128)S(1)}, f32[1280,256]{1,0:T(8,128)}, u32[]{:S(2)}, u32[]{:S(2)}) collective-permute-start(f32[1280,256]{1,0:T(8,128)S(1)} %bitcast.147), channel_id=1, source_target_pairs={{0,8},{1,9},{2,10},{3,11},{4,12},{5,13},{6,14},{7,15},{8,0},{9,1},... | collective-permute-start | bytes 3932168 | tf_op jit(solution)/shard_map/ppermute | solution.py:70
  130.4 15.4 %collective-permute-start.17 = (f32[128,1024]{1,0:T(8,128)S(1)}, f32[128,1024]{1,0:T(8,128)S(1)}, u32[]{:S(2)}, u32[]{:S(2)}) collective-permute-start(f32[128,1024]{1,0:T(8,128)S(1)} %copy-done.5), channel_id=1, source_target_pairs={{16,0},{32,16},{48,32},{64,48},{80,64},{96,80},{112,96},{8,112},{2... | collective-permute-start | bytes 1572872 | tf_op jit(solution)/shard_map/ppermute | solution.py:503
  132.3 24.9 %collective-permute-start.16 = (f32[128,1024]{1,0:T(8,128)S(1)}, f32[128,1024]{1,0:T(8,128)S(1)}, u32[]{:S(2)}, u32[]{:S(2)}) collective-permute-start(f32[128,1024]{1,0:T(8,128)S(1)} %copy-done.5), channel_id=1, source_target_pairs={{0,16},{16,32},{32,48},{48,64},{64,80},{80,96},{96,112},{112,8},{8... | collective-permute-start | bytes 1572872 | tf_op jit(solution)/shard_map/ppermute | solution.py:502
  159.0 12.2 %collective-permute-start.20 = (f32[320,256]{1,0:T(8,128)}, f32[320,256]{1,0:T(8,128)S(1)}, u32[]{:S(2)}, u32[]{:S(2)}) collective-permute-start(f32[320,256]{1,0:T(8,128)} %get-tuple-element.119), channel_id=1, source_target_pairs={{0,2},{1,3},{2,0},{3,1},{4,6},{5,7},{6,4},{7,5},{8,10},{9,11},{10,... | collective-permute-start | bytes 983048 | tf_op jit(solution)/shard_map/ppermute | solution.py:70
  159.0 19.2 %collective-permute-start.22 = (f32[320,256]{1,0:T(8,128)S(1)}, f32[320,256]{1,0:T(8,128)}, u32[]{:S(2)}, u32[]{:S(2)}) collective-permute-start(f32[320,256]{1,0:T(8,128)S(1)} %get-tuple-element.120), channel_id=1, source_target_pairs={{0,6},{1,7},{2,4},{3,5},{4,2},{5,3},{6,0},{7,1},{8,14},{9,15},{10,... | collective-permute-start | bytes 983048 | tf_op jit(solution)/shard_map/ppermute | solution.py:70
  164.3 13.9 %collective-permute-start.21 = (f32[320,256]{1,0:T(8,128)S(1)}, f32[320,256]{1,0:T(8,128)}, u32[]{:S(2)}, u32[]{:S(2)}) collective-permute-start(f32[320,256]{1,0:T(8,128)S(1)} %get-tuple-element.121), channel_id=1, source_target_pairs={{0,4},{1,5},{2,6},{3,7},{4,0},{5,1},{6,2},{7,3},{8,12},{9,13},{10,... | collective-permute-start | bytes 983048 | tf_op jit(solution)/shard_map/ppermute | solution.py:70
  165.5 26.4 %collective-permute-start.19 = (f32[128,1024]{1,0:T(8,128)S(1)}, f32[128,1024]{1,0:T(8,128)S(1)}, u32[]{:S(2)}, u32[]{:S(2)}) collective-permute-start(f32[128,1024]{1,0:T(8,128)S(1)} %copy-done.7), channel_id=1, source_target_pairs={{0,0},{8,8},{1,16},{9,24},{2,32},{10,40},{3,48},{11,56},{4,64},{12... | collective-permute-start | bytes 1572872 | tf_op jit(solution)/shard_map/ppermute | solution.py:513
  191.9 9.1 %collective-permute-start.27 = (f32[80,256]{1,0:T(8,128)S(1)}, f32[80,256]{1,0:T(8,128)S(1)}, u32[]{:S(2)}, u32[]{:S(2)}) collective-permute-start(f32[80,256]{1,0:T(8,128)S(1)} %get-tuple-element.142), channel_id=1, source_target_pairs={{0,16},{1,17},{2,18},{3,19},{4,20},{5,21},{6,22},{7,23},{8,24},{9,... | collective-permute-start | bytes 245768 | tf_op jit(solution)/shard_map/ppermute | solution.py:70
  192.0 15.1 %collective-permute-start.29 = (f32[80,256]{1,0:T(8,128)S(1)}, f32[80,256]{1,0:T(8,128)S(1)}, u32[]{:S(2)}, u32[]{:S(2)}) collective-permute-start(f32[80,256]{1,0:T(8,128)S(1)} %get-tuple-element.143), channel_id=1, source_target_pairs={{0,17},{1,16},{2,19},{3,18},{4,21},{5,20},{6,23},{7,22},{8,25},{9,... | collective-permute-start | bytes 245768 | tf_op jit(solution)/shard_map/ppermute | solution.py:70
  193.8 13.3 %collective-permute-start.28 = (f32[80,256]{1,0:T(8,128)S(1)}, f32[80,256]{1,0:T(8,128)S(1)}, u32[]{:S(2)}, u32[]{:S(2)}) collective-permute-start(f32[80,256]{1,0:T(8,128)S(1)} %get-tuple-element.144), channel_id=1, source_target_pairs={{0,1},{1,0},{2,3},{3,2},{4,5},{5,4},{6,7},{7,6},{8,9},{9,8},{10,11... | collective-permute-start | bytes 245768 | tf_op jit(solution)/shard_map/ppermute | solution.py:70
  195.4 11.7 %collective-permute-start.23 = (f32[64,1024]{1,0:T(8,128)S(1)}, f32[64,1024]{1,0:T(8,128)S(1)}, u32[]{:S(2)}, u32[]{:S(2)}) collective-permute-start(f32[64,1024]{1,0:T(8,128)S(1)} %get-tuple-element.133), channel_id=1, source_target_pairs={{0,1},{1,0},{2,3},{3,2},{4,5},{5,4},{6,7},{7,6},{8,9},{9,8},{10,11... | collective-permute-start | bytes 786440 | tf_op jit(solution)/shard_map/ppermute | solution.py:70
  197.0 10.2 %collective-permute-start.25 = (f32[64,1024]{1,0:T(8,128)S(1)}, f32[64,1024]{1,0:T(8,128)S(1)}, u32[]{:S(2)}, u32[]{:S(2)}) collective-permute-start(f32[64,1024]{1,0:T(8,128)S(1)} %get-tuple-element.132), channel_id=1, source_target_pairs={{0,4},{1,5},{2,6},{3,7},{4,0},{5,1},{6,2},{7,3},{8,12},{9,13},{10,... | collective-permute-start | bytes 786440 | tf_op jit(solution)/shard_map/ppermute | solution.py:70
  201.0 16.0 %collective-permute-start.24 = (f32[64,1024]{1,0:T(8,128)S(1)}, f32[64,1024]{1,0:T(8,128)S(1)}, u32[]{:S(2)}, u32[]{:S(2)}) collective-permute-start(f32[64,1024]{1,0:T(8,128)S(1)} %get-tuple-element.132), channel_id=1, source_target_pairs={{0,2},{1,3},{2,0},{3,1},{4,6},{5,7},{6,4},{7,5},{8,10},{9,11},{10,... | collective-permute-start | bytes 786440 | tf_op jit(solution)/shard_map/ppermute | solution.py:70
  207.1 11.2 %collective-permute-start.26 = (f32[64,1024]{1,0:T(8,128)S(1)}, f32[64,1024]{1,0:T(8,128)S(1)}, u32[]{:S(2)}, u32[]{:S(2)}) collective-permute-start(f32[64,1024]{1,0:T(8,128)S(1)} %get-tuple-element.132), channel_id=1, source_target_pairs={{0,6},{1,7},{2,4},{3,5},{4,2},{5,3},{6,0},{7,1},{8,14},{9,15},{10,... | collective-permute-start | bytes 786440 | tf_op jit(solution)/shard_map/ppermute | solution.py:70
  207.2 43.5 %copy-start.15 = (f32[2,64,1024]{2,1,0:T(8,128)}, f32[2,64,1024]{2,1,0:T(8,128)S(1)}, u32[]{:S(2)}) copy-start(f32[2,64,1024]{2,1,0:T(8,128)S(1)} %pad_maximum_fusion.10.own) | copy-start | bytes 1572868
  218.4 23.5 %copy-start.12 = (f32[4,64,1024]{2,1,0:T(8,128)}, f32[4,64,1024]{2,1,0:T(8,128)S(1)}, u32[]{:S(2)}) copy-start(f32[4,64,1024]{2,1,0:T(8,128)S(1)} %pad_maximum_fusion.4.quad) | copy-start | bytes 3145732
  218.5 10.8 %collective-permute-start.36 = (f32[80,256]{1,0:T(8,128)S(1)}, f32[80,256]{1,0:T(8,128)S(1)}, u32[]{:S(2)}, u32[]{:S(2)}) collective-permute-start(f32[80,256]{1,0:T(8,128)S(1)} %add_add_fusion.2), channel_id=1, source_target_pairs={{0,96},{1,97},{2,98},{3,99},{4,100},{5,101},{6,102},{7,103},{8,104... | collective-permute-start | bytes 245768 | tf_op jit(solution)/shard_map/ppermute | solution.py:70
  227.5 6.0 %collective-permute-start.35 = (f32[80,256]{1,0:T(8,128)S(1)}, f32[80,256]{1,0:T(8,128)S(1)}, u32[]{:S(2)}, u32[]{:S(2)}) collective-permute-start(f32[80,256]{1,0:T(8,128)S(1)} %add_add_fusion.2), channel_id=1, source_target_pairs={{0,64},{1,65},{2,66},{3,67},{4,68},{5,69},{6,70},{7,71},{8,72},{9,... | collective-permute-start | bytes 245768 | tf_op jit(solution)/shard_map/ppermute | solution.py:70
  227.5 7.7 %collective-permute-start.34 = (f32[80,256]{1,0:T(8,128)S(1)}, f32[80,256]{1,0:T(8,128)S(1)}, u32[]{:S(2)}, u32[]{:S(2)}) collective-permute-start(f32[80,256]{1,0:T(8,128)S(1)} %add_add_fusion.2), channel_id=1, source_target_pairs={{0,32},{1,33},{2,34},{3,35},{4,36},{5,37},{6,38},{7,39},{8,40},{9,... | collective-permute-start | bytes 245768 | tf_op jit(solution)/shard_map/ppermute | solution.py:70
  235.2 4.8 collective-permute-start.39
  237.1 4.8 collective-permute-start.38
  237.1 4.8 collective-permute-start.37
  238.5 40.3 %collective-permute-start.33 = (f32[4,64,1024]{2,1,0:T(8,128)S(1)}, f32[4,64,1024]{2,1,0:T(8,128)}, u32[]{:S(2)}, u32[]{:S(2)}) collective-permute-start(f32[4,64,1024]{2,1,0:T(8,128)S(1)} %pad_maximum_fusion.4.quad), channel_id=1, source_target_pairs={{0,1},{1,0},{2,3},{3,2},{4,5},{5,4},{6,7},{7,6},{8,9},{9,8},{10,11... | collective-permute-start | bytes 3145736 | tf_op jit(solution)/shard_map/ppermute | solution.py:70
  242.0 8.0 %collective-permute-start.41 = (f32[320,256]{1,0:T(8,128)S(1)}, f32[320,256]{1,0:T(8,128)S(1)}, u32[]{:S(2)}, u32[]{:S(2)}) collective-permute-start(f32[320,256]{1,0:T(8,128)S(1)} %get-tuple-element.137), channel_id=1, source_target_pairs={{0,4},{1,5},{2,6},{3,7},{4,0},{5,1},{6,2},{7,3},{8,12},{9,13},{10,... | collective-permute-start | bytes 983048 | tf_op jit(solution)/shard_map/ppermute | solution.py:70
  242.1 8.6 %collective-permute-start.40 = (f32[320,256]{1,0:T(8,128)S(1)}, f32[320,256]{1,0:T(8,128)S(1)}, u32[]{:S(2)}, u32[]{:S(2)}) collective-permute-start(f32[320,256]{1,0:T(8,128)S(1)} %get-tuple-element.137), channel_id=1, source_target_pairs={{0,2},{1,3},{2,0},{3,1},{4,6},{5,7},{6,4},{7,5},{8,10},{9,11},{10,... | collective-permute-start | bytes 983048 | tf_op jit(solution)/shard_map/ppermute | solution.py:70
  242.3 11.1 %collective-permute-start.42 = (f32[320,256]{1,0:T(8,128)S(1)}, f32[320,256]{1,0:T(8,128)S(1)}, u32[]{:S(2)}, u32[]{:S(2)}) collective-permute-start(f32[320,256]{1,0:T(8,128)S(1)} %get-tuple-element.137), channel_id=1, source_target_pairs={{0,6},{1,7},{2,4},{3,5},{4,2},{5,3},{6,0},{7,1},{8,14},{9,15},{10,... | collective-permute-start | bytes 983048 | tf_op jit(solution)/shard_map/ppermute | solution.py:70
  245.3 33.5 %collective-permute-start.32 = (f32[2,64,1024]{2,1,0:T(8,128)S(1)}, f32[2,64,1024]{2,1,0:T(8,128)S(1)}, u32[]{:S(2)}, u32[]{:S(2)}) collective-permute-start(f32[2,64,1024]{2,1,0:T(8,128)S(1)} %pad_maximum_fusion.10.own), channel_id=1, source_target_pairs={{0,6},{1,7},{2,4},{3,5},{4,2},{5,3},{6,0},{7,1},{8,14},{9,15},{10,... | collective-permute-start | bytes 1572872 | tf_op jit(solution)/shard_map/ppermute | solution.py:70
  249.9 28.8 %collective-permute-start.31 = (f32[2,64,1024]{2,1,0:T(8,128)S(1)}, f32[2,64,1024]{2,1,0:T(8,128)S(1)}, u32[]{:S(2)}, u32[]{:S(2)}) collective-permute-start(f32[2,64,1024]{2,1,0:T(8,128)S(1)} %pad_maximum_fusion.10.own), channel_id=1, source_target_pairs={{0,4},{1,5},{2,6},{3,7},{4,0},{5,1},{6,2},{7,3},{8,12},{9,13},{10,... | collective-permute-start | bytes 1572872 | tf_op jit(solution)/shard_map/ppermute | solution.py:70
  250.7 28.1 %collective-permute-start.30 = (f32[2,64,1024]{2,1,0:T(8,128)S(1)}, f32[2,64,1024]{2,1,0:T(8,128)S(1)}, u32[]{:S(2)}, u32[]{:S(2)}) collective-permute-start(f32[2,64,1024]{2,1,0:T(8,128)S(1)} %pad_maximum_fusion.10.own), channel_id=1, source_target_pairs={{0,2},{1,3},{2,0},{3,1},{4,6},{5,7},{6,4},{7,5},{8,10},{9,11},{10,... | collective-permute-start | bytes 1572872 | tf_op jit(solution)/shard_map/ppermute | solution.py:70
  278.8 12.2 %collective-permute-start.43 = (f32[1280,256]{1,0:T(8,128)S(1)}, f32[1280,256]{1,0:T(8,128)S(1)}, u32[]{:S(2)}, u32[]{:S(2)}) collective-permute-start(f32[1280,256]{1,0:T(8,128)S(1)} %pad_maximum_fusion.2), channel_id=1, source_target_pairs={{0,8},{1,9},{2,10},{3,11},{4,12},{5,13},{6,14},{7,15},{8,0},{9,1},... | collective-permute-start | bytes 3932168 | tf_op jit(solution)/shard_map/ppermute | solution.py:70
  (16 other events, 174.3 us)
Sparse Core Ops, SparseCore 0:
  158.3 82.0 all-gather.2

commit v6 on v5

--- a/solution.py
+++ b/solution.py
@@ -86,7 +86,7 @@
     return blocks[0] + got[0] + swap(kept, Y[far])
 
 
-def scatter_lines(even, odd, begun, first_wait, second_wait, third_wait):
+def scatter_lines(even, odd, begun, first_wait, third_wait):
     got = begun(swap(odd, CORE))
     quarter = LINE // 4
     cut = lambda i, q: even[i, q * quarter : (q + 1) * quarter] + got[i, q * quarter : (q + 1) * quarter]
@@ -97,7 +97,6 @@
     d = [pair(m, 3) for m in range(4)]
     c_got, d_got = first_wait(y_first(1, c), y_first(3, d))
     c, d = y_second(1, c, c_got), y_second(3, d, d_got)
-    came = second_wait(came)
     own = [half(2 * m, 0) + came[m] for m in range(4)]
     a = [o[:quarter] for o in own]
     b = [o[quarter:] for o in own]
@@ -135,11 +134,6 @@
 def sum_cores(x, core):
     keep, send = halves(x, core == 1)
     return keep + swap(send, CORE)
-
-
-def sum_rest(x, x_place, z):
-    x = x + swap(x, Y[1]) + swap(x, Y[2]) + swap(x, Y[3])
-    return gather_four(gather_four(x, x_place, X), z, Z)
 
 
 def gather_rows_start(line):
@@ -426,11 +420,6 @@
     )(*operands)
 
 
-def device_of(line):
-    chip_row, core, col = line % 8, (line // 8) % 2, line // 16
-    return (chip_row * 2 + core) * 8 + col
-
-
 def local(value_matrix, inputs, plant_diag, state_cost, control_weight):
     row_index = lax.axis_index("row")
     col_index = lax.axis_index("col")
@@ -444,8 +433,6 @@
     diag_cols = lax.dynamic_slice_in_dim(plant_diag, col_index * lines_cols, lines_cols, 0)
     me = row_index.astype(jnp.int32).reshape(1)
     trade = [((a * 2 + core) * 8 + b, (b * 2 + core) * 8 + a) for a in range(8) for b in range(8) for core in range(2)]
-    mine_inputs = lax.dynamic_slice_in_dim(inputs, col_index * LINE, LINE, 0)
-    mine_inputs = lax.ppermute(mine_inputs, both, trade)
 
     def shifted(x, axis, by):
         count = lax.axis_size(axis)
@@ -453,16 +440,13 @@
 
     above = shifted(value_matrix[-LINE:], "row", 1)
     below = shifted(value_matrix[:LINE], "row", -1)
-    tall = lambda cols: jnp.concatenate([above[:, cols], value_matrix[:, cols], below[:, cols]], 0)
-    left = shifted(tall(slice(-LINE, None)), "col", 1)
-    right = shifted(tall(slice(None, LINE)), "col", -1)
     operands = (
         jnp.stack([row_index * lines_rows, col_index * lines_cols]).astype(jnp.int32),
         value_matrix,
         above,
         below,
-        left,
-        right,
+        None,
+        None,
         jnp.broadcast_to(diag_rows.reshape(rows_block, 1), (rows_block, LINE)),
         diag_cols,
         state_cost.reshape(lines_rows, grid_side),
@@ -476,56 +460,55 @@
         return got
 
     def first_wait(c_got, d_got):
-        middle = (*operands[:2], held["above"], held["below"], None, None, *operands[6:])
+        middle = (*operands[:2], held["above"], held["below"], *operands[4:])
         base = plant_part(1, 7, *middle, None)
         base = plant_part(8, 7, *middle, base)
-        c_got, d_got, held["base"] = tied(c_got, d_got, base)
+        c_got, d_got, held["base"], above, below = tied(c_got, d_got, base, held["above"], held["below"])
+        tall = lambda cols: jnp.concatenate([above[:, cols], value_matrix[:, cols], below[:, cols]], 0)
+        held["left"] = shifted(tall(slice(-LINE, None)), "col", 1)
+        held["right"] = shifted(tall(slice(None, LINE)), "col", -1)
         return c_got, d_got
 
-    def second_wait(came):
-        came, held["inputs"] = tied(came, mine_inputs)
-        return came
-
     def third_wait(a_got, b_got):
-        a_got, b_got, held["left"], held["right"] = tied(a_got, b_got, left, right)
+        a_got, b_got, held["left"], held["right"] = tied(a_got, b_got, held["left"], held["right"])
         return a_got, b_got
 
-    product = scatter_lines(even, odd, begun, first_wait, second_wait, third_wait)
-    mine_inputs = held["inputs"]
+    product = scatter_lines(even, odd, begun, first_wait, third_wait)
     operands = (*operands[:2], held["above"], held["below"], held["left"], held["right"], *operands[6:])
 
     core, x_low, y = row_index & 1, (row_index >> 1) & 1, row_index >> 2
     x_high, z = col_index & 1, col_index >> 1
     x_place = x_high * 2 + x_low
 
-    lines = grid_side
-    over = lax.ppermute(product, both, [(device_of(i), device_of(i + 1)) for i in range(lines - 1)])
-    under = lax.ppermute(product, both, [(device_of(i + 1), device_of(i)) for i in range(lines - 1)])
+    product = lax.ppermute(product, both, trade)
+    count = grid_side
+    over = lax.ppermute(product, both, [(i, i + 1) for i in range(count - 1)])
+    under = lax.ppermute(product, both, [(i + 1, i) for i in range(count - 1)])
+    mine_inputs = lax.dynamic_slice_in_dim(inputs, col_index * LINE, LINE, 0)
     gram = gram_blocks(mine_inputs, product)
     total = sum_cores(gram.reshape(10 * PANEL, PANEL), core)
-    line = col_index * 16 + line_of(row_index)
-    diagonal = lax.dynamic_slice_in_dim(plant_diag, line, 1, 0)
+    total = scatter_four(total, z, Z)
     over, under, total = tied(over, under, total)
+    diagonal = lax.dynamic_slice_in_dim(plant_diag, row_index * 8 + col_index, 1, 0)
     gain = stencil_first(jnp.stack([over, product, under]), diagonal)[0]
     gain, total = tied(gain, total)
 
-    gain_cols = lax.all_gather(gain, "row", axis=0)
-    traded = lax.ppermute(gain, both, trade)
-    total = scatter_four(total, z, Z)
-    traded, total = tied(traded, total)
-
-    pair, quad = gather_rows_start(traded)
+    back = lax.ppermute(gain, both, trade)
     total = scatter_four(total, x_place, X)
+    total = total + swap(total, Y[1]) + swap(total, Y[2]) + swap(total, Y[3])
+    back, gain, total = tied(back, gain, total)
+
+    gain_cols = lax.all_gather(back, "row", axis=0)
+    pair, quad = gather_rows_start(gain)
+    total = gather_four(gather_four(total, x_place, X), z, Z)
     pair, quad, total = tied(pair, quad, total)
-
     sides = gather_rows_end(pair, quad)
-    total = sum_rest(total, x_place, z)
-    *sides, total = tied(*sides, total)
-    base = plant_part(0, 1, *operands, held["base"])
+    total = joined(total, swap(total, CORE), core == 1)
+    factors = factored(control_weight, total.reshape(10, PANEL, PANEL))
+    *factors, base = tied(*factors, held["base"])
+    base = plant_part(0, 1, *operands, base)
     base = plant_part(lines_cols - 1, 1, *operands, base)
-    total = joined(total, swap(total, CORE), core == 1)
-    total, base = tied(total, base)
-    factors = factored(control_weight, total.reshape(10, PANEL, PANEL))
+    *sides, base = tied(*sides, base)
     solved = solve(jnp.stack([z, x_high]).astype(jnp.int32), factors, sides)
     return downdate(solved, gain_cols, base)
 

time: 519 us -> 521 us (level)
  the two profiles are of different devices: /device:TPU:33 before, /device:TPU:1 now
where the time goes in v6:
time: 521 us; the launch traced here: 511 us
  Pallas kernels  260 us (50%)
  starting transfers between devices  102 us (20%)
  waiting for transfers between devices  95.2 us (18%)
  other arithmetic  23.3 us (4%)
  between operations  15.2 us (3%)
  local copies, waits for them, and re-layouts  14.8 us (3%)
    pallas_call x1, Pallas kernels, factored(): pl.pallas_call(factor_kernel, out_shape=[jax.ShapeDtypeStruct((10, PANEL,...  176 us
    ppermute x36, waiting for transfers between devices, swap(): return lax.ppermute(x, ('row', 'col'), [(i, i ^ mask) for i in range(128)])  84.1 us
    ppermute x36, starting transfers between devices, swap(): return lax.ppermute(x, ('row', 'col'), [(i, i ^ mask) for i in range(128)])  78.6 us
    pallas_call x4, Pallas kernels, plant_part(): pl.pallas_call(functools.partial(plant_kernel, start, [len(blocks) for bl...  24.8 us
    pallas_call x2, Pallas kernels, product_lines(): pl.pallas_call(product_kernel, grid_spec=pltpu.PrefetchScalarGridSpec(num...  23.4 us
    pallas_call x1, Pallas kernels, downdate(): pl.pallas_call(downdate_kernel, grid=(8,), in_specs=[whole, whole, pl.Blo...  19.3 us
    pallas_call x1, Pallas kernels, solve(): pl.pallas_call(solve_kernel, out_shape=[jax.ShapeDtypeStruct((size, 4 * P...  12.6 us
    ppermute x4, starting transfers between devices, shifted(): lax.ppermute(x, axis, [(i, i + by) for i in range(count) if 0 <= i + by <...  11.8 us
  transfers between devices with their start and end apart: 45, of which 21 were waited for; matrix products, arithmetic and copies ran while one was open for 5% of the time, Pallas kernels for 44%

profile of v6, /device:TPU:1, one launch (start us, length us, event | category | flops | bytes accessed | tf_op | source)
XLA Modules:
  0.0 511.1 jit_solution(1566558193374723578)
XLA Ops:
  6.5 11.8 %shard_map.56 = f32[8,128,1024]{2,1,0:T(8,128)} custom-call(s32[1]{0:T(128)} %bitcast.3.me_ref, f32[1024,2048]{1,0:T(8,128)} %refs_4_.5, f32[1024,2048]{1,0:T(8,128)} %refs_4_.5, f32[1024,1024]{1,0:T(8,128)} %inputs.3), custom_call_target="tpu_custom_call" | custom-call | flops 1048576 | bytes 1048576 | tf_op jit(solution)/shard_map/pallas_call | solution.py:50
  19.8 3.1 fusion.33
  22.8 3.1 collective-permute-start.1
  25.9 1.9 collective-permute-start.2
  27.9 11.7 %shard_map.55 = f32[8,128,1024]{2,1,0:T(8,128)} custom-call(s32[1]{0:T(128)} %bitcast.3.me_ref, f32[1024,2048]{1,0:T(8,128)} %refs_4_.5, f32[1024,2048]{1,0:T(8,128)} %refs_4_.5, f32[1024,1024]{1,0:T(8,128)} %inputs.3), custom_call_target="tpu_custom_call" | custom-call | flops 1048576 | bytes 1048576 | tf_op jit(solution)/shard_map/pallas_call | solution.py:50
  42.2 8.6 %collective-permute-done.2.refs_2_.refs_5_.refs_8_.refs_3_.refs_6_ = f32[128,2048]{1,0:T(8,128)S(1)} collective-permute-done((f32[128,2048]{1,0:T(8,128)}, f32[128,2048]{1,0:T(8,128)S(1)}, u32[]{:S(2)}, u32[]{:S(2)}) %collective-permute-start.2) | collective-permute-done | bytes 1048608 | tf_op jit(solution)/shard_map/ppermute | solution.py:439
  50.8 2.2 fusion.27
  53.1 2.2 fusion.13
  58.3 2.3 collective-permute-start.6
  63.1 9.1 %shard_map.57.refs_12_ = f32[1024,2048]{1,0:T(8,128)} custom-call(s32[2]{0:T(128)} %pad_add_fusion.1.place, f32[128,2048]{1,0:T(8,128)} %copy-done.2, f32[1024,2048]{1,0:T(8,128)} %refs_4_.5, f32[128,2048]{1,0:T(8,128)} %copy-done.3, f32[128,2048]{1,0:T(8,128)} %copy-done.2, f32[1024,2048]{1,0:T(8,128)} %refs_4_.5, f32[128,2048]{1,0:T(8,128)} %copy-done.3, ...), custom_call_target="tpu_custom_call" | custom-call | flops 33554432 | bytes 16777216 | tf_op jit(solution)/shard_map/pallas_call | solution.py:410
  72.2 9.2 %shard_map.58.refs_10_ = f32[1024,2048]{1,0:T(8,128)} custom-call(s32[2]{0:T(128)} %pad_add_fusion.1.place, f32[128,2048]{1,0:T(8,128)} %copy-done.2, f32[1024,2048]{1,0:T(8,128)} %refs_4_.5, f32[128,2048]{1,0:T(8,128)} %copy-done.3, f32[128,2048]{1,0:T(8,128)} %copy-done.2, f32[1024,2048]{1,0:T(8,128)} %refs_4_.5, ...), custom_call_target="tpu_custom_call", output_to_operand_aliasing={{}: (13, {})} | custom-call | flops 33554432 | bytes 16777216 | tf_op jit(solution)/shard_map/pallas_call | solution.py:410
  88.3 5.5 %collective-permute-start.8 = (f32[1280,128]{1,0:T(8,128)S(1)}, f32[1280,128]{1,0:T(8,128)S(1)}, u32[]{:S(2)}, u32[]{:S(2)}) collective-permute-start(f32[1280,128]{1,0:T(8,128)S(1)} %pad_maximum_fusion.5), channel_id=1, source_target_pairs={{0,1},{1,2},{2,3},{3,4},{4,5},{5,6},{6,7},{8,9},{9,10},{10,11},{11... | collective-permute-start | bytes 1966088 | tf_op jit(solution)/shard_map/ppermute | solution.py:439
  97.6 4.6 collective-permute-done.13
  103.5 1.7 collective-permute-start.5
  105.5 2.1 collective-permute-done.8.refs_0_
  107.6 3.6 collective-permute-done.5
  118.0 1.9 constant_dynamic-slice_fusion.6.inputs
  120.7 3.9 shard_map.59
  124.6 2.0 slice_select_fusion.1
  126.6 3.8 collective-permute-start.18
  130.4 2.8 collective-permute-done.18
  135.6 30.2 %collective-permute-start.19 = (f32[320,256]{1,0:T(8,128)}, f32[320,256]{1,0:T(8,128)}, u32[]{:S(2)}, u32[]{:S(2)}) collective-permute-start(f32[320,256]{1,0:T(8,128)} %get-tuple-element.123), channel_id=1, source_target_pairs={{0,2},{1,3},{2,0},{3,1},{4,6},{5,7},{6,4},{7,5},{8,10},{9,11},{10,... | collective-permute-start | bytes 983048 | tf_op jit(solution)/shard_map/ppermute | solution.py:70
  165.8 5.8 %collective-permute-start.20 = (f32[320,256]{1,0:T(8,128)}, f32[320,256]{1,0:T(8,128)}, u32[]{:S(2)}, u32[]{:S(2)}) collective-permute-start(f32[320,256]{1,0:T(8,128)} %get-tuple-element.125), channel_id=1, source_target_pairs={{0,4},{1,5},{2,6},{3,7},{4,0},{5,1},{6,2},{7,3},{8,12},{9,13},{10,... | collective-permute-start | bytes 983048 | tf_op jit(solution)/shard_map/ppermute | solution.py:70
  171.6 5.1 collective-permute-start.16
  176.7 5.4 %collective-permute-start.17 = (f32[128,1024]{1,0:T(8,128)S(1)}, f32[128,1024]{1,0:T(8,128)S(1)}, u32[]{:S(2)}, u32[]{:S(2)}) collective-permute-start(f32[128,1024]{1,0:T(8,128)S(1)} %copy-done.6), channel_id=1, source_target_pairs={{1,0},{2,1},{3,2},{4,3},{5,4},{6,5},{7,6},{8,7},{9,8},{10,9},{11,1... | collective-permute-start | bytes 1572872 | tf_op jit(solution)/shard_map/ppermute | solution.py:486
  182.1 15.5 %collective-permute-done.20 = f32[320,256]{1,0:T(8,128)} collective-permute-done((f32[320,256]{1,0:T(8,128)}, f32[320,256]{1,0:T(8,128)}, u32[]{:S(2)}, u32[]{:S(2)}) %collective-permute-start.20) | collective-permute-done | bytes 327712 | tf_op jit(solution)/shard_map/ppermute | solution.py:70
  199.5 1.8 collective-permute-start.23
  201.7 2.1 collective-permute-start.25
  204.5 2.1 collective-permute-done.24
  207.6 4.1 collective-permute-start.27
  211.9 11.0 %collective-permute-done.26 = f32[80,256]{1,0:T(8,128)S(1)} collective-permute-done((f32[80,256]{1,0:T(8,128)S(1)}, f32[80,256]{1,0:T(8,128)S(1)}, u32[]{:S(2)}, u32[]{:S(2)}) %collective-permute-start.26) | collective-permute-done | bytes 81952 | tf_op jit(solution)/shard_map/ppermute | solution.py:70
  222.9 4.5 collective-permute-done.27
  227.4 8.6 %collective-permute-done.28 = f32[80,256]{1,0:T(8,128)S(1)} collective-permute-done((f32[80,256]{1,0:T(8,128)S(1)}, f32[80,256]{1,0:T(8,128)S(1)}, u32[]{:S(2)}, u32[]{:S(2)}) %collective-permute-start.28) | collective-permute-done | bytes 81952 | tf_op jit(solution)/shard_map/ppermute | solution.py:70
  236.9 3.1 collective-permute-start.33
  239.9 2.2 collective-permute-start.34
  244.1 2.4 collective-permute-start.32
  246.5 1.7 collective-permute-start.29
  249.9 11.2 %collective-permute-done.29 = f32[64,1024]{1,0:T(8,128)S(1)} collective-permute-done((f32[64,1024]{1,0:T(8,128)S(1)}, f32[64,1024]{1,0:T(8,128)S(1)}, u32[]{:S(2)}, u32[]{:S(2)}) %collective-permute-start.29) | collective-permute-done | bytes 262176 | tf_op jit(solution)/shard_map/ppermute | solution.py:70
  262.5 5.1 %collective-permute-done.37 = f32[320,256]{1,0:T(8,128)S(1)} collective-permute-done((f32[320,256]{1,0:T(8,128)S(1)}, f32[320,256]{1,0:T(8,128)S(1)}, u32[]{:S(2)}, u32[]{:S(2)}) %collective-permute-start.37) | collective-permute-done | bytes 327712 | tf_op jit(solution)/shard_map/ppermute | solution.py:70
  267.7 8.2 %collective-permute-done.38 = f32[320,256]{1,0:T(8,128)S(1)} collective-permute-done((f32[320,256]{1,0:T(8,128)S(1)}, f32[320,256]{1,0:T(8,128)S(1)}, u32[]{:S(2)}, u32[]{:S(2)}) %collective-permute-start.38) | collective-permute-done | bytes 327712 | tf_op jit(solution)/shard_map/ppermute | solution.py:70
  278.8 3.0 collective-permute-start.41
  282.7 2.6 collective-permute-start.43
  285.5 1.7 pad_maximum_fusion
  287.2 176.1 %shard_map.60 = (f32[10,256,256]{2,1,0:T(8,128)}, f32[4,256,256]{2,1,0:T(8,128)}) custom-call(f32[1]{0:T(128)S(6)} %copy.12.weight, f32[10,256,256]{2,1,0:T(8,128)} %bitcast.152), custom_call_target="tpu_custom_call" | custom-call | flops 9663676416 | bytes 12582912 | tf_op jit(solution)/shard_map/pallas_call | solution.py:251
  463.4 3.1 shard_map.61.refs_10_
  466.5 3.4 shard_map.62.base
  472.0 12.6 %shard_map.63 = (bf16[1024,1024]{1,0:T(8,128)(2,1)}, bf16[1024,1024]{1,0:T(8,128)(2,1)}) custom-call(s32[2]{0:T(128)} %pad_add_fusion.place, f32[10,256,256]{2,1,0:T(8,128)} %get-tuple-element.62.factor, f32[4,256,256]{2,1,0:T(8,128)} %get-tuple-element.63.inverses, f32[2,64,1024]{2,1,0:T(8,128)} %copy-done.12, f32[2,64,1024]{2,1,0:T(8,128)} %copy-done.14, ...), custom_call_target="tpu_custom_call" | custom-call | flops 9663676416 | bytes 12582912 | tf_op jit(solution)/shard_map/pallas_call | solution.py:295
  484.5 19.3 %shard_map.64 = f32[1024,2048]{1,0:T(8,128)} custom-call(bf16[1024,1024]{1,0:T(8,128)(2,1)} %get-tuple-element.75.high, bf16[1024,1024]{1,0:T(8,128)(2,1)} %get-tuple-element.76.low, f32[16,128,1024]{2,1,0:T(8,128)} %bitcast.166, f32[16,128,1024]{2,1,0:T(8,128)} %bitcast.167, f32[1024,2048]{1,0:T(8,128)} %shard_map.62.base), custom_call_target="tpu_custom_call" | custom-call | flops 12884901888 | bytes 29360128 | tf_op jit(solution)/shard_map/pallas_call | solution.py:316
  (148 shorter events, 47.1 us)
Async XLA Ops:
  6.5 33.6 %copy-start = (f32[128,128]{1,0:T(8,128)S(1)}, f32[128,128]{1,0:T(8,128)}, u32[]{:S(2)}) copy-start(f32[128,128]{1,0:T(8,128)} %param.7) | copy-start | bytes 196612
  6.5 478.0 %all-gather.3.cloned.1.call-start = ((), (), s32[]{:S(2)}) async-start(), calls=%async_computation | async-start | bytes 8912896 | tf_op jit(solution)/shard_map/all_gather | solution.py:501
  18.3 32.5 %collective-permute-start = (f32[8,128,1024]{2,1,0:T(8,128)}, f32[8,128,1024]{2,1,0:T(8,128)}, u32[]{:S(2)}, u32[]{:S(2)}) collective-permute-start(f32[8,128,1024]{2,1,0:T(8,128)} %shard_map.56), channel_id=1, source_target_pairs={{0,8},{1,9},{2,10},{3,11},{4,12},{5,13},{6,14},{7,15},{8,0},{9,1},... | collective-permute-start | bytes 12582920 | tf_op jit(solution)/shard_map/ppermute | solution.py:70
  22.8 19.4 %collective-permute-start.1 = (f32[128,2048]{1,0:T(8,128)}, f32[128,2048]{1,0:T(8,128)S(1)}, u32[]{:S(2)}, u32[]{:S(2)}) collective-permute-start(f32[128,2048]{1,0:T(8,128)} %get-tuple-element.114), channel_id=1, source_target_pairs={{0,8},{8,16},{16,24},{24,32},{32,40},{40,48},{48,56},{56,64},{64,7... | collective-permute-start | bytes 3145736 | tf_op jit(solution)/shard_map/ppermute | solution.py:439
  25.9 24.9 %collective-permute-start.2 = (f32[128,2048]{1,0:T(8,128)}, f32[128,2048]{1,0:T(8,128)S(1)}, u32[]{:S(2)}, u32[]{:S(2)}) collective-permute-start(f32[128,2048]{1,0:T(8,128)} %get-tuple-element.113), channel_id=1, source_target_pairs={{8,0},{16,8},{24,16},{32,24},{40,32},{48,40},{56,48},{64,56},{72,6... | collective-permute-start | bytes 3145736 | tf_op jit(solution)/shard_map/ppermute | solution.py:439
  57.4 25.6 %collective-permute-start.7 = (f32[2,2,32,1024]{3,2,1,0:T(8,128)}, f32[2,2,32,1024]{3,2,1,0:T(8,128)}, u32[]{:S(2)}, u32[]{:S(2)}) collective-permute-start(f32[2,2,32,1024]{3,2,1,0:T(8,128)} %pad_maximum_fusion.8), channel_id=1, source_target_pairs={{0,96},{1,97},{2,98},{3,99},{4,100},{5,101},{6,102},{7,103},{8,104... | collective-permute-start | bytes 1572872 | tf_op jit(solution)/shard_map/ppermute | solution.py:70
  58.3 24.7 %collective-permute-start.6 = (f32[2,2,32,1024]{3,2,1,0:T(8,128)}, f32[2,2,32,1024]{3,2,1,0:T(8,128)}, u32[]{:S(2)}, u32[]{:S(2)}) collective-permute-start(f32[2,2,32,1024]{3,2,1,0:T(8,128)} %pad_maximum_fusion.7), channel_id=1, source_target_pairs={{0,32},{1,33},{2,34},{3,35},{4,36},{5,37},{6,38},{7,39},{8,40},{9,... | collective-permute-start | bytes 1572872 | tf_op jit(solution)/shard_map/ppermute | solution.py:70
  60.8 42.4 %collective-permute-start.3 = (f32[4,64,1024]{2,1,0:T(8,128)S(1)}, f32[4,64,1024]{2,1,0:T(8,128)S(1)}, u32[]{:S(2)}, u32[]{:S(2)}) collective-permute-start(f32[4,64,1024]{2,1,0:T(8,128)S(1)} %pad_maximum_fusion.3), channel_id=1, source_target_pairs={{0,16},{1,17},{2,18},{3,19},{4,20},{5,21},{6,22},{7,23},{8,24},{9,... | collective-permute-start | bytes 3145736 | tf_op jit(solution)/shard_map/ppermute | solution.py:70
  84.8 20.7 %collective-permute-start.9 = (f32[1280,128]{1,0:T(8,128)S(1)}, f32[1280,128]{1,0:T(8,128)S(1)}, u32[]{:S(2)}, u32[]{:S(2)}) collective-permute-start(f32[1280,128]{1,0:T(8,128)S(1)} %pad_maximum_fusion.6), channel_id=1, source_target_pairs={{1,0},{2,1},{3,2},{4,3},{5,4},{6,5},{7,6},{9,8},{10,9},{11,10},{12... | collective-permute-start | bytes 1966088 | tf_op jit(solution)/shard_map/ppermute | solution.py:439
  87.1 9.5 %collective-permute-start.12 = (f32[2,32,1024]{2,1,0:T(8,128)S(1)}, f32[2,32,1024]{2,1,0:T(8,128)S(1)}, u32[]{:S(2)}, u32[]{:S(2)}) collective-permute-start(f32[2,32,1024]{2,1,0:T(8,128)S(1)} %maximum_add_fusion.1), channel_id=1, source_target_pairs={{0,96},{1,97},{2,98},{3,99},{4,100},{5,101},{6,102},{7,103},{8,104... | collective-permute-start | bytes 786440 | tf_op jit(solution)/shard_map/ppermute | solution.py:70
  88.3 19.4 %collective-permute-start.8 = (f32[1280,128]{1,0:T(8,128)S(1)}, f32[1280,128]{1,0:T(8,128)S(1)}, u32[]{:S(2)}, u32[]{:S(2)}) collective-permute-start(f32[1280,128]{1,0:T(8,128)S(1)} %pad_maximum_fusion.5), channel_id=1, source_target_pairs={{0,1},{1,2},{2,3},{3,4},{4,5},{5,6},{6,7},{8,9},{9,10},{10,11},{11... | collective-permute-start | bytes 1966088 | tf_op jit(solution)/shard_map/ppermute | solution.py:439
  94.8 7.4 %collective-permute-start.13 = (f32[2,32,1024]{2,1,0:T(8,128)S(1)}, f32[2,32,1024]{2,1,0:T(8,128)S(1)}, u32[]{:S(2)}, u32[]{:S(2)}) collective-permute-start(f32[2,32,1024]{2,1,0:T(8,128)S(1)} %maximum_add_fusion.3), channel_id=1, source_target_pairs={{0,32},{1,33},{2,34},{3,35},{4,36},{5,37},{6,38},{7,39},{8,40},{9,... | collective-permute-start | bytes 786440 | tf_op jit(solution)/shard_map/ppermute | solution.py:70
  103.5 7.7 %collective-permute-start.5 = (f32[2,32,1024]{2,1,0:T(8,128)S(1)}, f32[2,32,1024]{2,1,0:T(8,128)S(1)}, u32[]{:S(2)}, u32[]{:S(2)}) collective-permute-start(f32[2,32,1024]{2,1,0:T(8,128)S(1)} %pad_maximum_fusion.14), channel_id=1, source_target_pairs={{0,96},{1,97},{2,98},{3,99},{4,100},{5,101},{6,102},{7,103},{8,104... | collective-permute-start | bytes 786440 | tf_op jit(solution)/shard_map/ppermute | solution.py:70
  105.2 6.2 %collective-permute-start.4 = (f32[2,32,1024]{2,1,0:T(8,128)S(1)}, f32[2,32,1024]{2,1,0:T(8,128)S(1)}, u32[]{:S(2)}, u32[]{:S(2)}) collective-permute-start(f32[2,32,1024]{2,1,0:T(8,128)S(1)} %pad_maximum_fusion.13), channel_id=1, source_target_pairs={{0,32},{1,33},{2,34},{3,35},{4,36},{5,37},{6,38},{7,39},{8,40},{9,... | collective-permute-start | bytes 786440 | tf_op jit(solution)/shard_map/ppermute | solution.py:70
  105.4 8.4 %collective-permute-start.14 = (f32[64,1024]{1,0:T(8,128)S(1)}, f32[64,1024]{1,0:T(8,128)S(1)}, u32[]{:S(2)}, u32[]{:S(2)}) collective-permute-start(f32[64,1024]{1,0:T(8,128)S(1)} %pad_maximum_fusion.15), channel_id=1, source_target_pairs={{0,16},{1,17},{2,18},{3,19},{4,20},{5,21},{6,22},{7,23},{8,24},{9,... | collective-permute-start | bytes 786440 | tf_op jit(solution)/shard_map/ppermute | solution.py:70
  111.5 3.9 collective-permute-start.11
  111.9 5.1 collective-permute-start.10
  117.1 2.8 collective-permute-start.15
  126.6 6.6 %collective-permute-start.18 = (f32[1280,256]{1,0:T(8,128)S(1)}, f32[1280,256]{1,0:T(8,128)}, u32[]{:S(2)}, u32[]{:S(2)}) collective-permute-start(f32[1280,256]{1,0:T(8,128)S(1)} %bitcast.153), channel_id=1, source_target_pairs={{0,8},{1,9},{2,10},{3,11},{4,12},{5,13},{6,14},{7,15},{8,0},{9,1},... | collective-permute-start | bytes 3932168 | tf_op jit(solution)/shard_map/ppermute | solution.py:70
  134.6 37.0 %copy-start.6 = (f32[128,1024]{1,0:T(8,128)S(1)}, f32[128,1024]{1,0:T(8,128)}, u32[]{:S(2)}) copy-start(f32[128,1024]{1,0:T(8,128)} %copy-done.5) | copy-start | bytes 1572868
  135.6 46.6 %collective-permute-start.19 = (f32[320,256]{1,0:T(8,128)}, f32[320,256]{1,0:T(8,128)}, u32[]{:S(2)}, u32[]{:S(2)}) collective-permute-start(f32[320,256]{1,0:T(8,128)} %get-tuple-element.123), channel_id=1, source_target_pairs={{0,2},{1,3},{2,0},{3,1},{4,6},{5,7},{6,4},{7,5},{8,10},{9,11},{10,... | collective-permute-start | bytes 983048 | tf_op jit(solution)/shard_map/ppermute | solution.py:70
  165.8 31.8 %collective-permute-start.20 = (f32[320,256]{1,0:T(8,128)}, f32[320,256]{1,0:T(8,128)}, u32[]{:S(2)}, u32[]{:S(2)}) collective-permute-start(f32[320,256]{1,0:T(8,128)} %get-tuple-element.125), channel_id=1, source_target_pairs={{0,4},{1,5},{2,6},{3,7},{4,0},{5,1},{6,2},{7,3},{8,12},{9,13},{10,... | collective-permute-start | bytes 983048 | tf_op jit(solution)/shard_map/ppermute | solution.py:70
  171.6 26.0 %collective-permute-start.21 = (f32[320,256]{1,0:T(8,128)S(1)}, f32[320,256]{1,0:T(8,128)}, u32[]{:S(2)}, u32[]{:S(2)}) collective-permute-start(f32[320,256]{1,0:T(8,128)S(1)} %get-tuple-element.124), channel_id=1, source_target_pairs={{0,6},{1,7},{2,4},{3,5},{4,2},{5,3},{6,0},{7,1},{8,14},{9,15},{10,... | collective-permute-start | bytes 983048 | tf_op jit(solution)/shard_map/ppermute | solution.py:70
  171.6 27.3 %collective-permute-start.16 = (f32[128,1024]{1,0:T(8,128)S(1)}, f32[128,1024]{1,0:T(8,128)S(1)}, u32[]{:S(2)}, u32[]{:S(2)}) collective-permute-start(f32[128,1024]{1,0:T(8,128)S(1)} %copy-done.6), channel_id=1, source_target_pairs={{0,1},{1,2},{2,3},{3,4},{4,5},{5,6},{6,7},{7,8},{8,9},{9,10},{10,1... | collective-permute-start | bytes 1572872 | tf_op jit(solution)/shard_map/ppermute | solution.py:485
  176.7 22.6 %collective-permute-start.17 = (f32[128,1024]{1,0:T(8,128)S(1)}, f32[128,1024]{1,0:T(8,128)S(1)}, u32[]{:S(2)}, u32[]{:S(2)}) collective-permute-start(f32[128,1024]{1,0:T(8,128)S(1)} %copy-done.6), channel_id=1, source_target_pairs={{1,0},{2,1},{3,2},{4,3},{5,4},{6,5},{7,6},{8,7},{9,8},{10,9},{11,1... | collective-permute-start | bytes 1572872 | tf_op jit(solution)/shard_map/ppermute | solution.py:486
  199.5 5.0 collective-permute-start.23
  201.3 5.3 %collective-permute-start.24 = (f32[80,256]{1,0:T(8,128)S(1)}, f32[80,256]{1,0:T(8,128)S(1)}, u32[]{:S(2)}, u32[]{:S(2)}) collective-permute-start(f32[80,256]{1,0:T(8,128)S(1)} %get-tuple-element.146), channel_id=1, source_target_pairs={{0,1},{1,0},{2,3},{3,2},{4,5},{5,4},{6,7},{7,6},{8,9},{9,8},{10,11... | collective-permute-start | bytes 245768 | tf_op jit(solution)/shard_map/ppermute | solution.py:70
  201.7 5.3 %collective-permute-start.25 = (f32[80,256]{1,0:T(8,128)S(1)}, f32[80,256]{1,0:T(8,128)S(1)}, u32[]{:S(2)}, u32[]{:S(2)}) collective-permute-start(f32[80,256]{1,0:T(8,128)S(1)} %get-tuple-element.145), channel_id=1, source_target_pairs={{0,17},{1,16},{2,19},{3,18},{4,21},{5,20},{6,23},{7,22},{8,25},{9,... | collective-permute-start | bytes 245768 | tf_op jit(solution)/shard_map/ppermute | solution.py:70
  203.8 32.2 %collective-permute-start.22 = (f32[128,1024]{1,0:T(8,128)S(1)}, f32[128,1024]{1,0:T(8,128)S(1)}, u32[]{:S(2)}, u32[]{:S(2)}) collective-permute-start(f32[128,1024]{1,0:T(8,128)S(1)} %fusion.4), channel_id=1, source_target_pairs={{0,0},{8,8},{1,16},{9,24},{2,32},{10,40},{3,48},{11,56},{4,64},{12... | collective-permute-start | bytes 1572872 | tf_op jit(solution)/shard_map/ppermute | solution.py:496
  207.0 15.9 %collective-permute-start.26 = (f32[80,256]{1,0:T(8,128)S(1)}, f32[80,256]{1,0:T(8,128)S(1)}, u32[]{:S(2)}, u32[]{:S(2)}) collective-permute-start(f32[80,256]{1,0:T(8,128)S(1)} %add_add_fusion.2), channel_id=1, source_target_pairs={{0,32},{1,33},{2,34},{3,35},{4,36},{5,37},{6,38},{7,39},{8,40},{9,... | collective-permute-start | bytes 245768 | tf_op jit(solution)/shard_map/ppermute | solution.py:70
  207.6 19.8 %collective-permute-start.27 = (f32[80,256]{1,0:T(8,128)S(1)}, f32[80,256]{1,0:T(8,128)S(1)}, u32[]{:S(2)}, u32[]{:S(2)}) collective-permute-start(f32[80,256]{1,0:T(8,128)S(1)} %add_add_fusion.2), channel_id=1, source_target_pairs={{0,64},{1,65},{2,66},{3,67},{4,68},{5,69},{6,70},{7,71},{8,72},{9,... | collective-permute-start | bytes 245768 | tf_op jit(solution)/shard_map/ppermute | solution.py:70
  211.7 24.2 %collective-permute-start.28 = (f32[80,256]{1,0:T(8,128)S(1)}, f32[80,256]{1,0:T(8,128)S(1)}, u32[]{:S(2)}, u32[]{:S(2)}) collective-permute-start(f32[80,256]{1,0:T(8,128)S(1)} %add_add_fusion.2), channel_id=1, source_target_pairs={{0,96},{1,97},{2,98},{3,99},{4,100},{5,101},{6,102},{7,103},{8,104... | collective-permute-start | bytes 245768 | tf_op jit(solution)/shard_map/ppermute | solution.py:70
  236.9 7.2 %collective-permute-start.33 = (f32[80,256]{1,0:T(8,128)S(1)}, f32[80,256]{1,0:T(8,128)S(1)}, u32[]{:S(2)}, u32[]{:S(2)}) collective-permute-start(f32[80,256]{1,0:T(8,128)S(1)} %add_add_fusion.1), channel_id=1, source_target_pairs={{0,16},{1,17},{2,18},{3,19},{4,20},{5,21},{6,22},{7,23},{8,24},{9,... | collective-permute-start | bytes 245768 | tf_op jit(solution)/shard_map/ppermute | solution.py:70
  239.9 6.6 %collective-permute-start.34 = (f32[80,256]{1,0:T(8,128)S(1)}, f32[80,256]{1,0:T(8,128)S(1)}, u32[]{:S(2)}, u32[]{:S(2)}) collective-permute-start(f32[80,256]{1,0:T(8,128)S(1)} %add_add_fusion.1), channel_id=1, source_target_pairs={{0,1},{1,0},{2,3},{3,2},{4,5},{5,4},{6,7},{7,6},{8,9},{9,8},{10,11... | collective-permute-start | bytes 245768 | tf_op jit(solution)/shard_map/ppermute | solution.py:70
  242.1 6.1 %collective-permute-start.35 = (f32[80,256]{1,0:T(8,128)S(1)}, f32[80,256]{1,0:T(8,128)S(1)}, u32[]{:S(2)}, u32[]{:S(2)}) collective-permute-start(f32[80,256]{1,0:T(8,128)S(1)} %add_add_fusion.1), channel_id=1, source_target_pairs={{0,17},{1,16},{2,19},{3,18},{4,21},{5,20},{6,23},{7,22},{8,25},{9,... | collective-permute-start | bytes 245768 | tf_op jit(solution)/shard_map/ppermute | solution.py:70
  242.5 6.8 %collective-permute-start.30 = (f32[64,1024]{1,0:T(8,128)S(1)}, f32[64,1024]{1,0:T(8,128)}, u32[]{:S(2)}, u32[]{:S(2)}) collective-permute-start(f32[64,1024]{1,0:T(8,128)S(1)} %get-tuple-element.136), channel_id=1, source_target_pairs={{0,2},{1,3},{2,0},{3,1},{4,6},{5,7},{6,4},{7,5},{8,10},{9,11},{10,... | collective-permute-start | bytes 786440 | tf_op jit(solution)/shard_map/ppermute | solution.py:70
  242.6 18.5 %collective-permute-start.31 = (f32[64,1024]{1,0:T(8,128)S(1)}, f32[64,1024]{1,0:T(8,128)}, u32[]{:S(2)}, u32[]{:S(2)}) collective-permute-start(f32[64,1024]{1,0:T(8,128)S(1)} %get-tuple-element.136), channel_id=1, source_target_pairs={{0,4},{1,5},{2,6},{3,7},{4,0},{5,1},{6,2},{7,3},{8,12},{9,13},{10,... | collective-permute-start | bytes 786440 | tf_op jit(solution)/shard_map/ppermute | solution.py:70
  244.1 17.0 %collective-permute-start.32 = (f32[64,1024]{1,0:T(8,128)S(1)}, f32[64,1024]{1,0:T(8,128)}, u32[]{:S(2)}, u32[]{:S(2)}) collective-permute-start(f32[64,1024]{1,0:T(8,128)S(1)} %get-tuple-element.136), channel_id=1, source_target_pairs={{0,6},{1,7},{2,4},{3,5},{4,2},{5,3},{6,0},{7,1},{8,14},{9,15},{10,... | collective-permute-start | bytes 786440 | tf_op jit(solution)/shard_map/ppermute | solution.py:70
  246.5 14.6 %collective-permute-start.29 = (f32[64,1024]{1,0:T(8,128)S(1)}, f32[64,1024]{1,0:T(8,128)S(1)}, u32[]{:S(2)}, u32[]{:S(2)}) collective-permute-start(f32[64,1024]{1,0:T(8,128)S(1)} %get-tuple-element.137), channel_id=1, source_target_pairs={{0,1},{1,0},{2,3},{3,2},{4,5},{5,4},{6,7},{7,6},{8,9},{9,8},{10,11... | collective-permute-start | bytes 786440 | tf_op jit(solution)/shard_map/ppermute | solution.py:70
  248.3 14.3 %collective-permute-start.36 = (f32[320,256]{1,0:T(8,128)S(1)}, f32[320,256]{1,0:T(8,128)S(1)}, u32[]{:S(2)}, u32[]{:S(2)}) collective-permute-start(f32[320,256]{1,0:T(8,128)S(1)} %get-tuple-element.139), channel_id=1, source_target_pairs={{0,2},{1,3},{2,0},{3,1},{4,6},{5,7},{6,4},{7,5},{8,10},{9,11},{10,... | collective-permute-start | bytes 983048 | tf_op jit(solution)/shard_map/ppermute | solution.py:70
  249.3 18.4 %collective-permute-start.37 = (f32[320,256]{1,0:T(8,128)S(1)}, f32[320,256]{1,0:T(8,128)S(1)}, u32[]{:S(2)}, u32[]{:S(2)}) collective-permute-start(f32[320,256]{1,0:T(8,128)S(1)} %get-tuple-element.139), channel_id=1, source_target_pairs={{0,4},{1,5},{2,6},{3,7},{4,0},{5,1},{6,2},{7,3},{8,12},{9,13},{10,... | collective-permute-start | bytes 983048 | tf_op jit(solution)/shard_map/ppermute | solution.py:70
  261.1 14.8 %collective-permute-start.38 = (f32[320,256]{1,0:T(8,128)S(1)}, f32[320,256]{1,0:T(8,128)S(1)}, u32[]{:S(2)}, u32[]{:S(2)}) collective-permute-start(f32[320,256]{1,0:T(8,128)S(1)} %get-tuple-element.139), channel_id=1, source_target_pairs={{0,6},{1,7},{2,4},{3,5},{4,2},{5,3},{6,0},{7,1},{8,14},{9,15},{10,... | collective-permute-start | bytes 983048 | tf_op jit(solution)/shard_map/ppermute | solution.py:70
  261.1 20.7 %copy-start.12 = (f32[2,64,1024]{2,1,0:T(8,128)}, f32[2,64,1024]{2,1,0:T(8,128)S(1)}, u32[]{:S(2)}) copy-start(f32[2,64,1024]{2,1,0:T(8,128)S(1)} %pad_maximum_fusion.10.own) | copy-start | bytes 1572868
  276.2 9.2 %collective-permute-start.39 = (f32[1280,256]{1,0:T(8,128)S(1)}, f32[1280,256]{1,0:T(8,128)S(1)}, u32[]{:S(2)}, u32[]{:S(2)}) collective-permute-start(f32[1280,256]{1,0:T(8,128)S(1)} %pad_maximum_fusion.2), channel_id=1, source_target_pairs={{0,8},{1,9},{2,10},{3,11},{4,12},{5,13},{6,14},{7,15},{8,0},{9,1},... | collective-permute-start | bytes 3932168 | tf_op jit(solution)/shard_map/ppermute | solution.py:70
  278.8 191.0 %collective-permute-start.40 = (f32[2,64,1024]{2,1,0:T(8,128)S(1)}, f32[2,64,1024]{2,1,0:T(8,128)S(1)}, u32[]{:S(2)}, u32[]{:S(2)}) collective-permute-start(f32[2,64,1024]{2,1,0:T(8,128)S(1)} %pad_maximum_fusion.10.own), channel_id=1, source_target_pairs={{0,2},{1,3},{2,0},{3,1},{4,6},{5,7},{6,4},{7,5},{8,10},{9,11},{10,... | collective-permute-start | bytes 1572872 | tf_op jit(solution)/shard_map/ppermute | solution.py:70
  278.8 191.0 %collective-permute-start.41 = (f32[2,64,1024]{2,1,0:T(8,128)S(1)}, f32[2,64,1024]{2,1,0:T(8,128)S(1)}, u32[]{:S(2)}, u32[]{:S(2)}) collective-permute-start(f32[2,64,1024]{2,1,0:T(8,128)S(1)} %pad_maximum_fusion.10.own), channel_id=1, source_target_pairs={{0,4},{1,5},{2,6},{3,7},{4,0},{5,1},{6,2},{7,3},{8,12},{9,13},{10,... | collective-permute-start | bytes 1572872 | tf_op jit(solution)/shard_map/ppermute | solution.py:70
  281.9 188.0 %collective-permute-start.42 = (f32[2,64,1024]{2,1,0:T(8,128)S(1)}, f32[2,64,1024]{2,1,0:T(8,128)S(1)}, u32[]{:S(2)}, u32[]{:S(2)}) collective-permute-start(f32[2,64,1024]{2,1,0:T(8,128)S(1)} %pad_maximum_fusion.10.own), channel_id=1, source_target_pairs={{0,6},{1,7},{2,4},{3,5},{4,2},{5,3},{6,0},{7,1},{8,14},{9,15},{10,... | collective-permute-start | bytes 1572872 | tf_op jit(solution)/shard_map/ppermute | solution.py:70
  282.7 187.2 %collective-permute-start.43 = (f32[4,64,1024]{2,1,0:T(8,128)S(1)}, f32[4,64,1024]{2,1,0:T(8,128)S(1)}, u32[]{:S(2)}, u32[]{:S(2)}) collective-permute-start(f32[4,64,1024]{2,1,0:T(8,128)S(1)} %pad_maximum_fusion.4.quad), channel_id=1, source_target_pairs={{0,1},{1,0},{2,3},{3,2},{4,5},{5,4},{6,7},{7,6},{8,9},{9,8},{10,11... | collective-permute-start | bytes 3145736 | tf_op jit(solution)/shard_map/ppermute | solution.py:70
  (14 other events, 98.0 us)
Sparse Core Ops, SparseCore 0:
  237.0 59.0 all-gather.2

commit v7 on v6

--- a/solution.py
+++ b/solution.py
@@ -86,8 +86,8 @@
     return blocks[0] + got[0] + swap(kept, Y[far])
 
 
-def scatter_lines(even, odd, begun, first_wait, third_wait):
-    got = begun(swap(odd, CORE))
+def scatter_lines(even, odd):
+    got = swap(odd, CORE)
     quarter = LINE // 4
     cut = lambda i, q: even[i, q * quarter : (q + 1) * quarter] + got[i, q * quarter : (q + 1) * quarter]
     half = lambda i, q: jnp.concatenate([cut(i, q), cut(i, q + 1)], 0)
@@ -95,13 +95,11 @@
     came = swap(jnp.stack([half(2 * m + 1, 0) for m in range(4)]), X_LOW)
     c = [pair(m, 2) for m in range(4)]
     d = [pair(m, 3) for m in range(4)]
-    c_got, d_got = first_wait(y_first(1, c), y_first(3, d))
-    c, d = y_second(1, c, c_got), y_second(3, d, d_got)
+    c, d = y_second(1, c, y_first(1, c)), y_second(3, d, y_first(3, d))
     own = [half(2 * m, 0) + came[m] for m in range(4)]
     a = [o[:quarter] for o in own]
     b = [o[quarter:] for o in own]
-    a_got, b_got = third_wait(y_first(1, a), y_first(3, b))
-    a, b = y_second(1, a, a_got), y_second(3, b, b_got)
+    a, b = y_second(1, a, y_first(1, a)), y_second(3, b, y_first(3, b))
     rest = jnp.concatenate([c[0], d[0]], 0) + swap(jnp.concatenate([c[1], d[1]], 0), X_LOW)
     return jnp.concatenate([a, b, rest], 0)
 
@@ -134,17 +132,6 @@
 def sum_cores(x, core):
     keep, send = halves(x, core == 1)
     return keep + swap(send, CORE)
-
-
-def gather_rows_start(line):
-    first, second = line[: LINE // 2], line[LINE // 2 :]
-    pair = jnp.stack([first, swap(first, X_HIGH)])
-    quad = jnp.stack([second] + [swap(second, Z[m]) for m in range(1, 4)])
-    return pair, quad
-
-
-def gather_rows_end(pair, quad):
-    return [pair] + [swap(pair, Z[m]) for m in range(1, 4)] + [quad, swap(quad, X_HIGH)]
 
 
 def gram_kernel(inputs, product, out):
@@ -262,21 +249,22 @@
     )(weight, gram)
 
 
-def solve_kernel(place, factor, inverses, own, near, across, far, quad, other, high, low, out):
+def solve_kernel(z, factor, inverses, first, first_near, first_far, second, second_near, second_far, high, low, out):
     size = PANEL
-    half = LINE // 2
     at = lambda k: slice(k * size, (k + 1) * size)
 
-    def put(step, e, second, value):
-        line = (place[0] ^ step) * 2 + (place[1] ^ e)
-        out[pl.ds(pl.multiple_of(line * LINE + second * half, half), half), :] = value
-
-    for step, pair in enumerate((own, near, across, far)):
-        for e in range(2):
-            put(step, e, 0, pair[e])
-    for e, lines in enumerate((quad, other)):
-        for step in range(4):
-            put(step, e, 1, lines[step])
+    def put(step, x_high, value):
+        line = (z[0] ^ step) * 2 + x_high
+        out[pl.ds(pl.multiple_of(line * LINE, LINE), LINE), :] = value
+
+    put(0, 0, first[...])
+    put(1, 0, first_near[...])
+    put(3, 0, first_far[0])
+    put(2, 0, first_far[1])
+    put(0, 1, second[...])
+    put(3, 1, second_near[...])
+    put(1, 1, second_far[0])
+    put(2, 1, second_far[1])
     for k in range(4):
         solved = split(out[:, at(k)])
         for i in range(k + 1, 4):
@@ -288,7 +276,7 @@
         high[:, at(k)], low[:, at(k)] = split(total)
 
 
-def solve(place, factors, sides):
+def solve(z, factors, sides):
     scalar = pl.BlockSpec(memory_space=pltpu.SMEM)
     array = pl.BlockSpec(memory_space=pltpu.VMEM)
     size = 8 * LINE
@@ -300,7 +288,7 @@
         scratch_shapes=[pltpu.VMEM((size, 4 * PANEL), F32)],
         compiler_params=pltpu.CompilerParams(vmem_limit_bytes=VMEM_LIMIT),
         cost_estimate=pl.CostEstimate(flops=9 << 30, bytes_accessed=12 << 20, transcendentals=0),
-    )(place, *factors, *sides)
+    )(z, *factors, *sides)
 
 
 def downdate_kernel(high, low, first, second, base, out):
@@ -443,73 +431,63 @@
     operands = (
         jnp.stack([row_index * lines_rows, col_index * lines_cols]).astype(jnp.int32),
         value_matrix,
-        above,
-        below,
-        None,
-        None,
         jnp.broadcast_to(diag_rows.reshape(rows_block, 1), (rows_block, LINE)),
         diag_cols,
         state_cost.reshape(lines_rows, grid_side),
     )
     odd = product_lines(me, value_matrix, inputs, 1)
     even = product_lines(me, value_matrix, inputs, 0)
-    held = {}
-
-    def begun(got):
-        got, held["above"], held["below"] = tied(got, above, below)
-        return got
-
-    def first_wait(c_got, d_got):
-        middle = (*operands[:2], held["above"], held["below"], *operands[4:])
-        base = plant_part(1, 7, *middle, None)
-        base = plant_part(8, 7, *middle, base)
-        c_got, d_got, held["base"], above, below = tied(c_got, d_got, base, held["above"], held["below"])
-        tall = lambda cols: jnp.concatenate([above[:, cols], value_matrix[:, cols], below[:, cols]], 0)
-        held["left"] = shifted(tall(slice(-LINE, None)), "col", 1)
-        held["right"] = shifted(tall(slice(None, LINE)), "col", -1)
-        return c_got, d_got
-
-    def third_wait(a_got, b_got):
-        a_got, b_got, held["left"], held["right"] = tied(a_got, b_got, held["left"], held["right"])
-        return a_got, b_got
-
-    product = scatter_lines(even, odd, begun, first_wait, third_wait)
-    operands = (*operands[:2], held["above"], held["below"], held["left"], held["right"], *operands[6:])
+    tall = lambda cols: jnp.concatenate([above[:, cols], value_matrix[:, cols], below[:, cols]], 0)
+    left = shifted(tall(slice(-LINE, None)), "col", 1)
+    right = shifted(tall(slice(None, LINE)), "col", -1)
+    product = scatter_lines(even, odd)
 
     core, x_low, y = row_index & 1, (row_index >> 1) & 1, row_index >> 2
     x_high, z = col_index & 1, col_index >> 1
     x_place = x_high * 2 + x_low
 
+    product, above, below, left, right = tied(product, above, below, left, right)
     product = lax.ppermute(product, both, trade)
+    around = (*operands[:2], above, below, left, right, *operands[2:])
+    base = None
+    for start, count in ((1, 7), (8, 7), (0, 1), (lines_cols - 1, 1)):
+        base = plant_part(start, count, *around, base)
+    product, base = tied(product, base)
+
     count = grid_side
     over = lax.ppermute(product, both, [(i, i + 1) for i in range(count - 1)])
     under = lax.ppermute(product, both, [(i + 1, i) for i in range(count - 1)])
     mine_inputs = lax.dynamic_slice_in_dim(inputs, col_index * LINE, LINE, 0)
     gram = gram_blocks(mine_inputs, product)
     total = sum_cores(gram.reshape(10 * PANEL, PANEL), core)
-    total = scatter_four(total, z, Z)
     over, under, total = tied(over, under, total)
     diagonal = lax.dynamic_slice_in_dim(plant_diag, row_index * 8 + col_index, 1, 0)
     gain = stencil_first(jnp.stack([over, product, under]), diagonal)[0]
     gain, total = tied(gain, total)
 
+    pair = joined(gain, swap(gain, X_HIGH), x_high == 1)
+    total = scatter_four(total, z, Z)
+    pair, total = tied(pair, total)
+
     back = lax.ppermute(gain, both, trade)
+    first, second = pair[:LINE], pair[LINE:]
+    first_near, second_near = swap(first, Z[1]), swap(second, Z[3])
     total = scatter_four(total, x_place, X)
+    first_near, second_near, total = tied(first_near, second_near, total)
+
+    first_far = swap(jnp.stack([first, first_near]), Z[3])
+    second_far = swap(jnp.stack([second, second_near]), Z[1])
     total = total + swap(total, Y[1]) + swap(total, Y[2]) + swap(total, Y[3])
-    back, gain, total = tied(back, gain, total)
-
+    back, total = tied(back, total)
     gain_cols = lax.all_gather(back, "row", axis=0)
-    pair, quad = gather_rows_start(gain)
-    total = gather_four(gather_four(total, x_place, X), z, Z)
-    pair, quad, total = tied(pair, quad, total)
-    sides = gather_rows_end(pair, quad)
+    total = gather_four(total, x_place, X)
+    first_far, second_far, total = tied(first_far, second_far, total)
+    total = gather_four(total, z, Z)
     total = joined(total, swap(total, CORE), core == 1)
+
     factors = factored(control_weight, total.reshape(10, PANEL, PANEL))
-    *factors, base = tied(*factors, held["base"])
-    base = plant_part(0, 1, *operands, base)
-    base = plant_part(lines_cols - 1, 1, *operands, base)
-    *sides, base = tied(*sides, base)
-    solved = solve(jnp.stack([z, x_high]).astype(jnp.int32), factors, sides)
+    sides = (first, first_near, first_far, second, second_near, second_far)
+    solved = solve(z.astype(jnp.int32).reshape(1), factors, sides)
     return downdate(solved, gain_cols, base)
 
 

time: 521 us -> 524 us (level)
  the two profiles are of different devices: /device:TPU:1 before, /device:TPU:7 now
where the time goes in v7:
time: 524 us; the launch traced here: 515 us
  Pallas kernels  260 us (50%)
  waiting for transfers between devices  147 us (28%)
  starting transfers between devices  65.6 us (13%)
  between operations  15.1 us (3%)
  other arithmetic  14.8 us (3%)
  local copies, waits for them, and re-layouts  12.2 us (2%)
    pallas_call x1, Pallas kernels, factored(): pl.pallas_call(factor_kernel, out_shape=[jax.ShapeDtypeStruct((10, PANEL,...  176 us
    ppermute x33, waiting for transfers between devices, swap(): return lax.ppermute(x, ('row', 'col'), [(i, i ^ mask) for i in range(128)])  107 us
    ppermute x33, starting transfers between devices, swap(): return lax.ppermute(x, ('row', 'col'), [(i, i ^ mask) for i in range(128)])  40.5 us
    pallas_call x4, Pallas kernels, plant_part(): pl.pallas_call(functools.partial(plant_kernel, start, [len(blocks) for bl...  24.6 us
    pallas_call x2, Pallas kernels, product_lines(): pl.pallas_call(product_kernel, grid_spec=pltpu.PrefetchScalarGridSpec(num...  23.3 us
    ppermute x4, waiting for transfers between devices, shifted(): lax.ppermute(x, axis, [(i, i + by) for i in range(count) if 0 <= i + by <...  22.5 us
    pallas_call x1, Pallas kernels, downdate(): pl.pallas_call(downdate_kernel, grid=(8,), in_specs=[whole, whole, pl.Blo...  19.2 us
    ppermute x4, starting transfers between devices, shifted(): lax.ppermute(x, axis, [(i, i + by) for i in range(count) if 0 <= i + by <...  15 us
  transfers between devices with their start and end apart: 42, of which 24 were waited for; matrix products, arithmetic and copies ran while one was open for 4% of the time, Pallas kernels for 44%

profile of v7, /device:TPU:7, one launch (start us, length us, event | category | flops | bytes accessed | tf_op | source)
XLA Modules:
  0.0 515.1 jit_solution(8124262507093958669)
XLA Ops:
  6.5 11.7 %shard_map.56 = f32[8,128,1024]{2,1,0:T(8,128)} custom-call(s32[1]{0:T(128)} %bitcast.2.me_ref, f32[1024,2048]{1,0:T(8,128)} %refs_4_.5, f32[1024,2048]{1,0:T(8,128)} %refs_4_.5, f32[1024,1024]{1,0:T(8,128)} %inputs.3), custom_call_target="tpu_custom_call" | custom-call | flops 1048576 | bytes 1048576 | tf_op jit(solution)/shard_map/pallas_call | solution.py:50
  18.9 2.8 fusion.40
  21.7 1.9 collective-permute-start.12
  23.6 4.5 collective-permute-start.11
  28.2 11.7 %shard_map.55 = f32[8,128,1024]{2,1,0:T(8,128)} custom-call(s32[1]{0:T(128)} %bitcast.2.me_ref, f32[1024,2048]{1,0:T(8,128)} %refs_4_.5, f32[1024,2048]{1,0:T(8,128)} %refs_4_.5, f32[1024,1024]{1,0:T(8,128)} %inputs.3), custom_call_target="tpu_custom_call" | custom-call | flops 1048576 | bytes 1048576 | tf_op jit(solution)/shard_map/pallas_call | solution.py:50
  41.1 6.9 %collective-permute-done.12.refs_2_.refs_5_.refs_8_.refs_3_.refs_6_ = f32[128,2048]{1,0:T(8,128)S(1)} collective-permute-done((f32[128,2048]{1,0:T(8,128)}, f32[128,2048]{1,0:T(8,128)S(1)}, u32[]{:S(2)}, u32[]{:S(2)}) %collective-permute-start.12) | collective-permute-done | bytes 1048608 | tf_op jit(solution)/shard_map/ppermute | solution.py:427
  48.1 2.2 fusion.36
  51.7 2.0 collective-permute-start.6
  54.8 8.8 %collective-permute-done.8 = f32[2,2,32,1024]{3,2,1,0:T(8,128)S(1)} collective-permute-done((f32[2,2,32,1024]{3,2,1,0:T(8,128)S(1)}, f32[2,2,32,1024]{3,2,1,0:T(8,128)S(1)}, u32[]{:S(2)}, u32[]{:S(2)}) %collective-permute-start.8) | collective-permute-done | bytes 524320 | tf_op jit(solution)/shard_map/ppermute | solution.py:70
  64.1 2.3 collective-permute-start.7
  66.5 5.1 collective-permute-start.13
  71.7 5.4 %collective-permute-done.1 = f32[4,64,1024]{2,1,0:T(8,128)S(1)} collective-permute-done((f32[4,64,1024]{2,1,0:T(8,128)S(1)}, f32[4,64,1024]{2,1,0:T(8,128)S(1)}, u32[]{:S(2)}, u32[]{:S(2)}) %collective-permute-start.1) | collective-permute-done | bytes 1048608 | tf_op jit(solution)/shard_map/ppermute | solution.py:70
  77.5 5.4 %collective-permute-done.2 = f32[2,32,1024]{2,1,0:T(8,128)S(1)} collective-permute-done((f32[2,32,1024]{2,1,0:T(8,128)S(1)}, f32[2,32,1024]{2,1,0:T(8,128)S(1)}, u32[]{:S(2)}, u32[]{:S(2)}) %collective-permute-start.2) | collective-permute-done | bytes 262176 | tf_op jit(solution)/shard_map/ppermute | solution.py:70
  83.0 2.0 collective-permute-start.4
  85.2 3.4 collective-permute-start.14
  89.9 6.8 %collective-permute-done.10 = f32[64,1024]{1,0:T(8,128)S(1)} collective-permute-done((f32[64,1024]{1,0:T(8,128)S(1)}, f32[64,1024]{1,0:T(8,128)S(1)}, u32[]{:S(2)}, u32[]{:S(2)}) %collective-permute-start.10) | collective-permute-done | bytes 262176 | tf_op jit(solution)/shard_map/ppermute | solution.py:70
  96.9 15.6 %collective-permute-done.14.refs_6_ = f32[1280,128]{1,0:T(8,128)S(1)} collective-permute-done((f32[1280,128]{1,0:T(8,128)S(1)}, f32[1280,128]{1,0:T(8,128)S(1)}, u32[]{:S(2)}, u32[]{:S(2)}) %collective-permute-start.14) | collective-permute-done | bytes 655392 | tf_op jit(solution)/shard_map/ppermute | solution.py:427
  114.7 2.0 constant_dynamic-slice_fusion.6.inputs
  117.7 9.1 %shard_map.57.refs_12_ = f32[1024,2048]{1,0:T(8,128)} custom-call(s32[2]{0:T(128)} %pad_add_fusion.place, f32[128,2048]{1,0:T(8,128)} %copy-done.2, f32[1024,2048]{1,0:T(8,128)} %refs_4_.5, f32[128,2048]{1,0:T(8,128)} %copy-done.1, f32[128,2048]{1,0:T(8,128)} %copy-done.2, f32[1024,2048]{1,0:T(8,128)} %refs_4_.5, f32[128,2048]{1,0:T(8,128)} %copy-done.1, ...), custom_call_target="tpu_custom_call" | custom-call | flops 33554432 | bytes 16777216 | tf_op jit(solution)/shard_map/pallas_call | solution.py:398
  126.9 9.2 %shard_map.58.refs_10_ = f32[1024,2048]{1,0:T(8,128)} custom-call(s32[2]{0:T(128)} %pad_add_fusion.place, f32[128,2048]{1,0:T(8,128)} %copy-done.2, f32[1024,2048]{1,0:T(8,128)} %refs_4_.5, f32[128,2048]{1,0:T(8,128)} %copy-done.1, f32[128,2048]{1,0:T(8,128)} %copy-done.2, f32[1024,2048]{1,0:T(8,128)} %refs_4_.5, ...), custom_call_target="tpu_custom_call", output_to_operand_aliasing={{}: (13, {})} | custom-call | flops 33554432 | bytes 16777216 | tf_op jit(solution)/shard_map/pallas_call | solution.py:398
  136.1 3.1 shard_map.59.refs_10_
  139.2 3.1 shard_map.60.base
  143.2 3.9 shard_map.61
  147.1 2.0 slice_select_fusion.1
  149.1 2.7 collective-permute-start.18
  151.8 5.8 %collective-permute-start.17 = (f32[128,1024]{1,0:T(8,128)S(1)}, f32[128,1024]{1,0:T(8,128)S(1)}, u32[]{:S(2)}, u32[]{:S(2)}) collective-permute-start(f32[128,1024]{1,0:T(8,128)S(1)} %copy-done.5), channel_id=1, source_target_pairs={{1,0},{2,1},{3,2},{4,3},{5,4},{6,5},{7,6},{8,7},{9,8},{10,9},{11,1... | collective-permute-start | bytes 1572872 | tf_op jit(solution)/shard_map/ppermute | solution.py:459
  157.7 2.7 collective-permute-start.16
  161.8 8.8 %collective-permute-done.17 = f32[128,1024]{1,0:T(8,128)S(1)} collective-permute-done((f32[128,1024]{1,0:T(8,128)S(1)}, f32[128,1024]{1,0:T(8,128)S(1)}, u32[]{:S(2)}, u32[]{:S(2)}) %collective-permute-start.17) | collective-permute-done | bytes 524320 | tf_op jit(solution)/shard_map/ppermute | solution.py:459
  170.7 9.5 %collective-permute-done.16 = f32[128,1024]{1,0:T(8,128)S(1)} collective-permute-done((f32[128,1024]{1,0:T(8,128)S(1)}, f32[128,1024]{1,0:T(8,128)S(1)}, u32[]{:S(2)}, u32[]{:S(2)}) %collective-permute-start.16) | collective-permute-done | bytes 524320 | tf_op jit(solution)/shard_map/ppermute | solution.py:458
  181.2 2.0 collective-permute-start.20
  183.2 6.4 %collective-permute-start.22 = (f32[320,256]{1,0:T(8,128)S(1)}, f32[320,256]{1,0:T(8,128)}, u32[]{:S(2)}, u32[]{:S(2)}) collective-permute-start(f32[320,256]{1,0:T(8,128)S(1)} %get-tuple-element.102), channel_id=1, source_target_pairs={{0,6},{1,7},{2,4},{3,5},{4,2},{5,3},{6,0},{7,1},{8,14},{9,15},{10,... | collective-permute-start | bytes 983048 | tf_op jit(solution)/shard_map/ppermute | solution.py:70
  191.0 12.0 %collective-permute-done.22 = f32[320,256]{1,0:T(8,128)} collective-permute-done((f32[320,256]{1,0:T(8,128)S(1)}, f32[320,256]{1,0:T(8,128)}, u32[]{:S(2)}, u32[]{:S(2)}) %collective-permute-start.22) | collective-permute-done | bytes 327712 | tf_op jit(solution)/shard_map/ppermute | solution.py:70
  203.0 2.1 collective-permute-done.21
  209.1 3.2 collective-permute-start.26
  216.2 6.0 %collective-permute-done.24.second_near = f32[128,1024]{1,0:T(8,128)} collective-permute-done((f32[128,1024]{1,0:T(8,128)S(1)}, f32[128,1024]{1,0:T(8,128)}, u32[]{:S(2)}, u32[]{:S(2)}) %collective-permute-start.24) | collective-permute-done | bytes 524320 | tf_op jit(solution)/shard_map/ppermute | solution.py:70
  222.2 19.6 %collective-permute-done.23.first_near = f32[128,1024]{1,0:T(8,128)} collective-permute-done((f32[128,1024]{1,0:T(8,128)S(1)}, f32[128,1024]{1,0:T(8,128)}, u32[]{:S(2)}, u32[]{:S(2)}) %collective-permute-start.23) | collective-permute-done | bytes 524320 | tf_op jit(solution)/shard_map/ppermute | solution.py:70
  241.7 4.2 collective-permute-start.32
  247.8 2.2 collective-permute-done.31
  254.8 2.1 collective-permute-start.34
  256.9 2.5 collective-permute-done.36
  260.1 15.5 %collective-permute-done.28.first_far = f32[2,128,1024]{2,1,0:T(8,128)} collective-permute-done((f32[2,128,1024]{2,1,0:T(8,128)S(1)}, f32[2,128,1024]{2,1,0:T(8,128)}, u32[]{:S(2)}, u32[]{:S(2)}) %collective-permute-start.28) | collective-permute-done | bytes 1048608 | tf_op jit(solution)/shard_map/ppermute | solution.py:70
  275.6 2.4 collective-permute-start.39
  278.8 12.9 %collective-permute-done.39 = f32[320,256]{1,0:T(8,128)S(1)} collective-permute-done((f32[320,256]{1,0:T(8,128)S(1)}, f32[320,256]{1,0:T(8,128)S(1)}, u32[]{:S(2)}, u32[]{:S(2)}) %collective-permute-start.39) | collective-permute-done | bytes 327712 | tf_op jit(solution)/shard_map/ppermute | solution.py:70
  292.0 3.1 collective-permute-start.40
  295.8 2.0 collective-permute-done.40
  299.6 176.5 %shard_map.62 = (f32[10,256,256]{2,1,0:T(8,128)}, f32[4,256,256]{2,1,0:T(8,128)}) custom-call(f32[1]{0:T(128)S(6)} %copy.12.weight, f32[10,256,256]{2,1,0:T(8,128)} %bitcast.172), custom_call_target="tpu_custom_call" | custom-call | flops 9663676416 | bytes 12582912 | tf_op jit(solution)/shard_map/pallas_call | solution.py:238
  476.1 12.5 %shard_map.63 = (bf16[1024,1024]{1,0:T(8,128)(2,1)}, bf16[1024,1024]{1,0:T(8,128)(2,1)}) custom-call(s32[1]{0:T(128)} %bitcast.z, f32[10,256,256]{2,1,0:T(8,128)} %get-tuple-element.49.factor, f32[4,256,256]{2,1,0:T(8,128)} %get-tuple-element.50.inverses, f32[128,1024]{1,0:T(8,128)} %copy-done.10, f32[128,1024]{1,0:T(8,128)} %collective-permute-done.23.first_near, ...), custom_call_target="tpu_custom_call" | custom-call | flops 9663676416 | bytes 12582912 | tf_op jit(solution)/shard_map/pallas_call | solution.py:283
  488.6 19.2 %shard_map.64 = f32[1024,2048]{1,0:T(8,128)} custom-call(bf16[1024,1024]{1,0:T(8,128)(2,1)} %get-tuple-element.53.high, bf16[1024,1024]{1,0:T(8,128)(2,1)} %get-tuple-element.54.low, f32[16,128,1024]{2,1,0:T(8,128)} %bitcast.186, f32[16,128,1024]{2,1,0:T(8,128)} %bitcast.187, f32[1024,2048]{1,0:T(8,128)} %shard_map.60.base), custom_call_target="tpu_custom_call" | custom-call | flops 12884901888 | bytes 29360128 | tf_op jit(solution)/shard_map/pallas_call | solution.py:304
  (130 shorter events, 32.9 us)
Async XLA Ops:
  6.5 107.6 %copy-start = (f32[128,128]{1,0:T(8,128)S(1)}, f32[128,128]{1,0:T(8,128)}, u32[]{:S(2)}) copy-start(f32[128,128]{1,0:T(8,128)} %param.7) | copy-start | bytes 196612
  6.5 482.1 %all-gather.3.cloned.1.call-start = ((), (), s32[]{:S(2)}) async-start(), calls=%async_computation | async-start | bytes 8912896 | tf_op jit(solution)/shard_map/all_gather | solution.py:482
  18.2 29.9 %collective-permute-start = (f32[8,128,1024]{2,1,0:T(8,128)}, f32[8,128,1024]{2,1,0:T(8,128)S(1)}, u32[]{:S(2)}, u32[]{:S(2)}) collective-permute-start(f32[8,128,1024]{2,1,0:T(8,128)} %shard_map.56), channel_id=1, source_target_pairs={{0,8},{1,9},{2,10},{3,11},{4,12},{5,13},{6,14},{7,15},{8,0},{9,1},... | collective-permute-start | bytes 12582920 | tf_op jit(solution)/shard_map/ppermute | solution.py:70
  21.7 26.3 %collective-permute-start.12 = (f32[128,2048]{1,0:T(8,128)}, f32[128,2048]{1,0:T(8,128)S(1)}, u32[]{:S(2)}, u32[]{:S(2)}) collective-permute-start(f32[128,2048]{1,0:T(8,128)} %get-tuple-element.59), channel_id=1, source_target_pairs={{8,0},{16,8},{24,16},{32,24},{40,32},{48,40},{56,48},{64,56},{72,6... | collective-permute-start | bytes 3145736 | tf_op jit(solution)/shard_map/ppermute | solution.py:427
  23.6 24.4 %collective-permute-start.11 = (f32[128,2048]{1,0:T(8,128)S(1)}, f32[128,2048]{1,0:T(8,128)S(1)}, u32[]{:S(2)}, u32[]{:S(2)}) collective-permute-start(f32[128,2048]{1,0:T(8,128)S(1)} %get-tuple-element.60), channel_id=1, source_target_pairs={{0,8},{8,16},{16,24},{24,32},{32,40},{40,48},{48,56},{56,64},{64,7... | collective-permute-start | bytes 3145736 | tf_op jit(solution)/shard_map/ppermute | solution.py:427
  50.4 13.2 %collective-permute-start.8 = (f32[2,2,32,1024]{3,2,1,0:T(8,128)S(1)}, f32[2,2,32,1024]{3,2,1,0:T(8,128)S(1)}, u32[]{:S(2)}, u32[]{:S(2)}) collective-permute-start(f32[2,2,32,1024]{3,2,1,0:T(8,128)S(1)} %pad_maximum_fusion.10), channel_id=1, source_target_pairs={{0,96},{1,97},{2,98},{3,99},{4,100},{5,101},{6,102},{7,103},{8,104... | collective-permute-start | bytes 1572872 | tf_op jit(solution)/shard_map/ppermute | solution.py:70
  51.7 12.4 %collective-permute-start.6 = (f32[2,2,32,1024]{3,2,1,0:T(8,128)S(1)}, f32[2,2,32,1024]{3,2,1,0:T(8,128)S(1)}, u32[]{:S(2)}, u32[]{:S(2)}) collective-permute-start(f32[2,2,32,1024]{3,2,1,0:T(8,128)S(1)} %pad_maximum_fusion.9), channel_id=1, source_target_pairs={{0,32},{1,33},{2,34},{3,35},{4,36},{5,37},{6,38},{7,39},{8,40},{9,... | collective-permute-start | bytes 1572872 | tf_op jit(solution)/shard_map/ppermute | solution.py:70
  54.3 22.8 %collective-permute-start.1 = (f32[4,64,1024]{2,1,0:T(8,128)S(1)}, f32[4,64,1024]{2,1,0:T(8,128)S(1)}, u32[]{:S(2)}, u32[]{:S(2)}) collective-permute-start(f32[4,64,1024]{2,1,0:T(8,128)S(1)} %pad_maximum_fusion.3), channel_id=1, source_target_pairs={{0,16},{1,17},{2,18},{3,19},{4,20},{5,21},{6,22},{7,23},{8,24},{9,... | collective-permute-start | bytes 3145736 | tf_op jit(solution)/shard_map/ppermute | solution.py:70
  63.7 7.9 %collective-permute-start.9 = (f32[2,32,1024]{2,1,0:T(8,128)S(1)}, f32[2,32,1024]{2,1,0:T(8,128)S(1)}, u32[]{:S(2)}, u32[]{:S(2)}) collective-permute-start(f32[2,32,1024]{2,1,0:T(8,128)S(1)} %fusion.5), channel_id=1, source_target_pairs={{0,32},{1,33},{2,34},{3,35},{4,36},{5,37},{6,38},{7,39},{8,40},{9,... | collective-permute-start | bytes 786440 | tf_op jit(solution)/shard_map/ppermute | solution.py:70
  64.1 7.5 %collective-permute-start.7 = (f32[2,32,1024]{2,1,0:T(8,128)S(1)}, f32[2,32,1024]{2,1,0:T(8,128)S(1)}, u32[]{:S(2)}, u32[]{:S(2)}) collective-permute-start(f32[2,32,1024]{2,1,0:T(8,128)S(1)} %fusion.8), channel_id=1, source_target_pairs={{0,96},{1,97},{2,98},{3,99},{4,100},{5,101},{6,102},{7,103},{8,104... | collective-permute-start | bytes 786440 | tf_op jit(solution)/shard_map/ppermute | solution.py:70
  66.5 30.5 %collective-permute-start.13 = (f32[1280,128]{1,0:T(8,128)S(1)}, f32[1280,128]{1,0:T(8,128)S(1)}, u32[]{:S(2)}, u32[]{:S(2)}) collective-permute-start(f32[1280,128]{1,0:T(8,128)S(1)} %pad_maximum_fusion.7), channel_id=1, source_target_pairs={{0,1},{1,2},{2,3},{3,4},{4,5},{5,6},{6,7},{8,9},{9,10},{10,11},{11... | collective-permute-start | bytes 1966088 | tf_op jit(solution)/shard_map/ppermute | solution.py:427
  77.4 5.6 %collective-permute-start.2 = (f32[2,32,1024]{2,1,0:T(8,128)S(1)}, f32[2,32,1024]{2,1,0:T(8,128)S(1)}, u32[]{:S(2)}, u32[]{:S(2)}) collective-permute-start(f32[2,32,1024]{2,1,0:T(8,128)S(1)} %pad_maximum_fusion.14), channel_id=1, source_target_pairs={{0,32},{1,33},{2,34},{3,35},{4,36},{5,37},{6,38},{7,39},{8,40},{9,... | collective-permute-start | bytes 786440 | tf_op jit(solution)/shard_map/ppermute | solution.py:70
  83.0 6.8 %collective-permute-start.4 = (f32[2,32,1024]{2,1,0:T(8,128)S(1)}, f32[2,32,1024]{2,1,0:T(8,128)S(1)}, u32[]{:S(2)}, u32[]{:S(2)}) collective-permute-start(f32[2,32,1024]{2,1,0:T(8,128)S(1)} %pad_maximum_fusion.15), channel_id=1, source_target_pairs={{0,96},{1,97},{2,98},{3,99},{4,100},{5,101},{6,102},{7,103},{8,104... | collective-permute-start | bytes 786440 | tf_op jit(solution)/shard_map/ppermute | solution.py:70
  85.0 11.7 %collective-permute-start.10 = (f32[64,1024]{1,0:T(8,128)S(1)}, f32[64,1024]{1,0:T(8,128)S(1)}, u32[]{:S(2)}, u32[]{:S(2)}) collective-permute-start(f32[64,1024]{1,0:T(8,128)S(1)} %pad_maximum_fusion.16), channel_id=1, source_target_pairs={{0,16},{1,17},{2,18},{3,19},{4,20},{5,21},{6,22},{7,23},{8,24},{9,... | collective-permute-start | bytes 786440 | tf_op jit(solution)/shard_map/ppermute | solution.py:70
  85.2 27.4 %collective-permute-start.14 = (f32[1280,128]{1,0:T(8,128)S(1)}, f32[1280,128]{1,0:T(8,128)S(1)}, u32[]{:S(2)}, u32[]{:S(2)}) collective-permute-start(f32[1280,128]{1,0:T(8,128)S(1)} %pad_maximum_fusion.8), channel_id=1, source_target_pairs={{1,0},{2,1},{3,2},{4,3},{5,4},{6,5},{7,6},{9,8},{10,9},{11,10},{12... | collective-permute-start | bytes 1966088 | tf_op jit(solution)/shard_map/ppermute | solution.py:427
  88.6 8.2 %collective-permute-start.3 = (f32[32,1024]{1,0:T(8,128)S(1)}, f32[32,1024]{1,0:T(8,128)S(1)}, u32[]{:S(2)}, u32[]{:S(2)}) collective-permute-start(f32[32,1024]{1,0:T(8,128)S(1)} %get-tuple-element.127), channel_id=1, source_target_pairs={{0,96},{1,97},{2,98},{3,99},{4,100},{5,101},{6,102},{7,103},{8,104... | collective-permute-start | bytes 393224 | tf_op jit(solution)/shard_map/ppermute | solution.py:70
  89.8 7.0 %collective-permute-start.5 = (f32[32,1024]{1,0:T(8,128)S(1)}, f32[32,1024]{1,0:T(8,128)S(1)}, u32[]{:S(2)}, u32[]{:S(2)}) collective-permute-start(f32[32,1024]{1,0:T(8,128)S(1)} %fusion.15), channel_id=1, source_target_pairs={{0,32},{1,33},{2,34},{3,35},{4,36},{5,37},{6,38},{7,39},{8,40},{9,... | collective-permute-start | bytes 393224 | tf_op jit(solution)/shard_map/ppermute | solution.py:70
  96.9 29.9 %copy-start.6 = (f32[1280,128]{1,0:T(8,128)}, f32[1280,128]{1,0:T(8,128)S(1)}, u32[]{:S(2)}) copy-start(f32[1280,128]{1,0:T(8,128)S(1)} %collective-permute-done.13.refs_0_) | copy-start | bytes 1966084
  112.6 14.3 %copy-start.7 = (f32[1280,128]{1,0:T(8,128)}, f32[1280,128]{1,0:T(8,128)S(1)}, u32[]{:S(2)}) copy-start(f32[1280,128]{1,0:T(8,128)S(1)} %collective-permute-done.14.refs_6_) | copy-start | bytes 1966084
  112.6 29.8 %collective-permute-start.15 = (f32[128,1024]{1,0:T(8,128)S(1)}, f32[128,1024]{1,0:T(8,128)S(1)}, u32[]{:S(2)}, u32[]{:S(2)}) collective-permute-start(f32[128,1024]{1,0:T(8,128)S(1)} %pad_maximum_fusion.11), channel_id=1, source_target_pairs={{0,0},{8,8},{1,16},{9,24},{2,32},{10,40},{3,48},{11,56},{4,64},{12... | collective-permute-start | bytes 1572872 | tf_op jit(solution)/shard_map/ppermute | solution.py:450
  147.1 4.7 copy-start.5
  149.1 11.2 %collective-permute-start.18 = (f32[1280,256]{1,0:T(8,128)S(1)}, f32[1280,256]{1,0:T(8,128)}, u32[]{:S(2)}, u32[]{:S(2)}) collective-permute-start(f32[1280,256]{1,0:T(8,128)S(1)} %bitcast.174), channel_id=1, source_target_pairs={{0,8},{1,9},{2,10},{3,11},{4,12},{5,13},{6,14},{7,15},{8,0},{9,1},... | collective-permute-start | bytes 3932168 | tf_op jit(solution)/shard_map/ppermute | solution.py:70
  151.8 18.8 %collective-permute-start.17 = (f32[128,1024]{1,0:T(8,128)S(1)}, f32[128,1024]{1,0:T(8,128)S(1)}, u32[]{:S(2)}, u32[]{:S(2)}) collective-permute-start(f32[128,1024]{1,0:T(8,128)S(1)} %copy-done.5), channel_id=1, source_target_pairs={{1,0},{2,1},{3,2},{4,3},{5,4},{6,5},{7,6},{8,7},{9,8},{10,9},{11,1... | collective-permute-start | bytes 1572872 | tf_op jit(solution)/shard_map/ppermute | solution.py:459
  157.7 22.5 %collective-permute-start.16 = (f32[128,1024]{1,0:T(8,128)S(1)}, f32[128,1024]{1,0:T(8,128)S(1)}, u32[]{:S(2)}, u32[]{:S(2)}) collective-permute-start(f32[128,1024]{1,0:T(8,128)S(1)} %copy-done.5), channel_id=1, source_target_pairs={{0,1},{1,2},{2,3},{3,4},{4,5},{5,6},{6,7},{7,8},{8,9},{9,10},{10,1... | collective-permute-start | bytes 1572872 | tf_op jit(solution)/shard_map/ppermute | solution.py:458
  181.2 9.8 %collective-permute-start.20 = (f32[320,256]{1,0:T(8,128)}, f32[320,256]{1,0:T(8,128)S(1)}, u32[]{:S(2)}, u32[]{:S(2)}) collective-permute-start(f32[320,256]{1,0:T(8,128)} %get-tuple-element.101), channel_id=1, source_target_pairs={{0,2},{1,3},{2,0},{3,1},{4,6},{5,7},{6,4},{7,5},{8,10},{9,11},{10,... | collective-permute-start | bytes 983048 | tf_op jit(solution)/shard_map/ppermute | solution.py:70
  183.2 19.8 %collective-permute-start.22 = (f32[320,256]{1,0:T(8,128)S(1)}, f32[320,256]{1,0:T(8,128)}, u32[]{:S(2)}, u32[]{:S(2)}) collective-permute-start(f32[320,256]{1,0:T(8,128)S(1)} %get-tuple-element.102), channel_id=1, source_target_pairs={{0,6},{1,7},{2,4},{3,5},{4,2},{5,3},{6,0},{7,1},{8,14},{9,15},{10,... | collective-permute-start | bytes 983048 | tf_op jit(solution)/shard_map/ppermute | solution.py:70
  189.6 15.6 %collective-permute-start.21 = (f32[320,256]{1,0:T(8,128)S(1)}, f32[320,256]{1,0:T(8,128)}, u32[]{:S(2)}, u32[]{:S(2)}) collective-permute-start(f32[320,256]{1,0:T(8,128)S(1)} %get-tuple-element.103), channel_id=1, source_target_pairs={{0,4},{1,5},{2,6},{3,7},{4,0},{5,1},{6,2},{7,3},{8,12},{9,13},{10,... | collective-permute-start | bytes 983048 | tf_op jit(solution)/shard_map/ppermute | solution.py:70
  190.8 15.6 %collective-permute-start.19 = (f32[128,1024]{1,0:T(8,128)S(1)}, f32[128,1024]{1,0:T(8,128)S(1)}, u32[]{:S(2)}, u32[]{:S(2)}) collective-permute-start(f32[128,1024]{1,0:T(8,128)S(1)} %fusion.4), channel_id=1, source_target_pairs={{0,1},{1,0},{2,3},{3,2},{4,5},{5,4},{6,7},{7,6},{8,9},{9,8},{10,11... | collective-permute-start | bytes 1572872 | tf_op jit(solution)/shard_map/ppermute | solution.py:70
  206.8 44.0 %copy-start.9 = (f32[128,1024]{1,0:T(8,128)}, f32[128,1024]{1,0:T(8,128)S(1)}, u32[]{:S(2)}) copy-start(f32[128,1024]{1,0:T(8,128)S(1)} %get-tuple-element.106.second) | copy-start | bytes 1572868
  206.9 44.0 %copy-start.10 = (f32[128,1024]{1,0:T(8,128)}, f32[128,1024]{1,0:T(8,128)S(1)}, u32[]{:S(2)}) copy-start(f32[128,1024]{1,0:T(8,128)S(1)} %get-tuple-element.107.first) | copy-start | bytes 1572868
  206.9 15.3 %collective-permute-start.24 = (f32[128,1024]{1,0:T(8,128)S(1)}, f32[128,1024]{1,0:T(8,128)}, u32[]{:S(2)}, u32[]{:S(2)}) collective-permute-start(f32[128,1024]{1,0:T(8,128)S(1)} %get-tuple-element.106.second), channel_id=1, source_target_pairs={{0,6},{1,7},{2,4},{3,5},{4,2},{5,3},{6,0},{7,1},{8,14},{9,15},{10,... | collective-permute-start | bytes 1572872 | tf_op jit(solution)/shard_map/ppermute | solution.py:70
  208.4 33.4 %collective-permute-start.23 = (f32[128,1024]{1,0:T(8,128)S(1)}, f32[128,1024]{1,0:T(8,128)}, u32[]{:S(2)}, u32[]{:S(2)}) collective-permute-start(f32[128,1024]{1,0:T(8,128)S(1)} %get-tuple-element.107.first), channel_id=1, source_target_pairs={{0,2},{1,3},{2,0},{3,1},{4,6},{5,7},{6,4},{7,5},{8,10},{9,11},{10,... | collective-permute-start | bytes 1572872 | tf_op jit(solution)/shard_map/ppermute | solution.py:70
  209.0 3.7 collective-permute-start.25
  209.0 6.2 %collective-permute-start.27 = (f32[80,256]{1,0:T(8,128)}, f32[80,256]{1,0:T(8,128)}, u32[]{:S(2)}, u32[]{:S(2)}) collective-permute-start(f32[80,256]{1,0:T(8,128)} %get-tuple-element.123), channel_id=1, source_target_pairs={{0,17},{1,16},{2,19},{3,18},{4,21},{5,20},{6,23},{7,22},{8,25},{9,... | collective-permute-start | bytes 245768 | tf_op jit(solution)/shard_map/ppermute | solution.py:70
  209.1 6.2 %collective-permute-start.26 = (f32[80,256]{1,0:T(8,128)}, f32[80,256]{1,0:T(8,128)}, u32[]{:S(2)}, u32[]{:S(2)}) collective-permute-start(f32[80,256]{1,0:T(8,128)} %get-tuple-element.124), channel_id=1, source_target_pairs={{0,1},{1,0},{2,3},{3,2},{4,5},{5,4},{6,7},{7,6},{8,9},{9,8},{10,11... | collective-permute-start | bytes 245768 | tf_op jit(solution)/shard_map/ppermute | solution.py:70
  212.7 37.3 %collective-permute-start.30 = (f32[128,1024]{1,0:T(8,128)S(1)}, f32[128,1024]{1,0:T(8,128)S(1)}, u32[]{:S(2)}, u32[]{:S(2)}) collective-permute-start(f32[128,1024]{1,0:T(8,128)S(1)} %fusion.4), channel_id=1, source_target_pairs={{0,0},{8,8},{1,16},{9,24},{2,32},{10,40},{3,48},{11,56},{4,64},{12... | collective-permute-start | bytes 1572872 | tf_op jit(solution)/shard_map/ppermute | solution.py:472
  241.7 4.5 collective-permute-start.33
  241.7 6.1 %collective-permute-start.32 = (f32[80,256]{1,0:T(8,128)S(1)}, f32[80,256]{1,0:T(8,128)S(1)}, u32[]{:S(2)}, u32[]{:S(2)}) collective-permute-start(f32[80,256]{1,0:T(8,128)S(1)} %add_add_fusion.2), channel_id=1, source_target_pairs={{0,64},{1,65},{2,66},{3,67},{4,68},{5,69},{6,70},{7,71},{8,72},{9,... | collective-permute-start | bytes 245768 | tf_op jit(solution)/shard_map/ppermute | solution.py:70
  245.9 4.1 collective-permute-start.31
  252.0 23.6 %collective-permute-start.28 = (f32[2,128,1024]{2,1,0:T(8,128)S(1)}, f32[2,128,1024]{2,1,0:T(8,128)}, u32[]{:S(2)}, u32[]{:S(2)}) collective-permute-start(f32[2,128,1024]{2,1,0:T(8,128)S(1)} %pad_maximum_fusion.5), channel_id=1, source_target_pairs={{0,6},{1,7},{2,4},{3,5},{4,2},{5,3},{6,0},{7,1},{8,14},{9,15},{10,... | collective-permute-start | bytes 3145736 | tf_op jit(solution)/shard_map/ppermute | solution.py:70
  253.2 22.3 %collective-permute-start.29 = (f32[2,128,1024]{2,1,0:T(8,128)S(1)}, f32[2,128,1024]{2,1,0:T(8,128)}, u32[]{:S(2)}, u32[]{:S(2)}) collective-permute-start(f32[2,128,1024]{2,1,0:T(8,128)S(1)} %pad_maximum_fusion.6), channel_id=1, source_target_pairs={{0,2},{1,3},{2,0},{3,1},{4,6},{5,7},{6,4},{7,5},{8,10},{9,11},{10,... | collective-permute-start | bytes 3145736 | tf_op jit(solution)/shard_map/ppermute | solution.py:70
  253.6 5.8 %collective-permute-start.36 = (f32[80,256]{1,0:T(8,128)S(1)}, f32[80,256]{1,0:T(8,128)S(1)}, u32[]{:S(2)}, u32[]{:S(2)}) collective-permute-start(f32[80,256]{1,0:T(8,128)S(1)} %add_add_fusion.1), channel_id=1, source_target_pairs={{0,17},{1,16},{2,19},{3,18},{4,21},{5,20},{6,23},{7,22},{8,25},{9,... | collective-permute-start | bytes 245768 | tf_op jit(solution)/shard_map/ppermute | solution.py:70
  253.6 5.8 %collective-permute-start.35 = (f32[80,256]{1,0:T(8,128)S(1)}, f32[80,256]{1,0:T(8,128)S(1)}, u32[]{:S(2)}, u32[]{:S(2)}) collective-permute-start(f32[80,256]{1,0:T(8,128)S(1)} %add_add_fusion.1), channel_id=1, source_target_pairs={{0,1},{1,0},{2,3},{3,2},{4,5},{5,4},{6,7},{7,6},{8,9},{9,8},{10,11... | collective-permute-start | bytes 245768 | tf_op jit(solution)/shard_map/ppermute | solution.py:70
  254.8 5.2 %collective-permute-start.34 = (f32[80,256]{1,0:T(8,128)S(1)}, f32[80,256]{1,0:T(8,128)S(1)}, u32[]{:S(2)}, u32[]{:S(2)}) collective-permute-start(f32[80,256]{1,0:T(8,128)S(1)} %add_add_fusion.1), channel_id=1, source_target_pairs={{0,16},{1,17},{2,18},{3,19},{4,20},{5,21},{6,22},{7,23},{8,24},{9,... | collective-permute-start | bytes 245768 | tf_op jit(solution)/shard_map/ppermute | solution.py:70
  275.6 16.2 %collective-permute-start.39 = (f32[320,256]{1,0:T(8,128)S(1)}, f32[320,256]{1,0:T(8,128)S(1)}, u32[]{:S(2)}, u32[]{:S(2)}) collective-permute-start(f32[320,256]{1,0:T(8,128)S(1)} %pad_maximum_fusion.13), channel_id=1, source_target_pairs={{0,6},{1,7},{2,4},{3,5},{4,2},{5,3},{6,0},{7,1},{8,14},{9,15},{10,... | collective-permute-start | bytes 983048 | tf_op jit(solution)/shard_map/ppermute | solution.py:70
  277.9 13.8 %collective-permute-start.38 = (f32[320,256]{1,0:T(8,128)S(1)}, f32[320,256]{1,0:T(8,128)S(1)}, u32[]{:S(2)}, u32[]{:S(2)}) collective-permute-start(f32[320,256]{1,0:T(8,128)S(1)} %pad_maximum_fusion.13), channel_id=1, source_target_pairs={{0,4},{1,5},{2,6},{3,7},{4,0},{5,1},{6,2},{7,3},{8,12},{9,13},{10,... | collective-permute-start | bytes 983048 | tf_op jit(solution)/shard_map/ppermute | solution.py:70
  277.9 13.8 %collective-permute-start.37 = (f32[320,256]{1,0:T(8,128)S(1)}, f32[320,256]{1,0:T(8,128)S(1)}, u32[]{:S(2)}, u32[]{:S(2)}) collective-permute-start(f32[320,256]{1,0:T(8,128)S(1)} %pad_maximum_fusion.13), channel_id=1, source_target_pairs={{0,2},{1,3},{2,0},{3,1},{4,6},{5,7},{6,4},{7,5},{8,10},{9,11},{10,... | collective-permute-start | bytes 983048 | tf_op jit(solution)/shard_map/ppermute | solution.py:70
  292.0 5.8 %collective-permute-start.40 = (f32[1280,256]{1,0:T(8,128)S(1)}, f32[1280,256]{1,0:T(8,128)S(1)}, u32[]{:S(2)}, u32[]{:S(2)}) collective-permute-start(f32[1280,256]{1,0:T(8,128)S(1)} %pad_maximum_fusion.2), channel_id=1, source_target_pairs={{0,8},{1,9},{2,10},{3,11},{4,12},{5,13},{6,14},{7,15},{8,0},{9,1},... | collective-permute-start | bytes 3932168 | tf_op jit(solution)/shard_map/ppermute | solution.py:70
  (5 other events, 9.6 us)
Sparse Core Ops, SparseCore 0:
  251.0 53.3 all-gather.2

commit v8 on v7

--- a/solution.py
+++ b/solution.py
@@ -32,10 +32,6 @@
     return dot1(a_high, b_high, dims) + dot1(a_high, b_low, dims) + dot1(a_low, b_high, dims)
 
 
-def line_of(device):
-    return (device & 1) * 8 + (device >> 1)
-
-
 def product_kernel(me_ref, first, second, inputs, out, high, low):
     @pl.when(pl.program_id(0) == 0)
     def _():
@@ -53,8 +49,8 @@
             num_scalar_prefetch=1,
             grid=(4,),
             in_specs=[
-                pl.BlockSpec((rows, LINE), lambda i, m: (0, line_of(m[0] ^ (4 * i + odd)))),
-                pl.BlockSpec((rows, LINE), lambda i, m: (0, line_of(m[0] ^ (4 * i + 2 + odd)))),
+                pl.BlockSpec((rows, LINE), lambda i, m: (0, m[0] ^ (4 * i + odd))),
+                pl.BlockSpec((rows, LINE), lambda i, m: (0, m[0] ^ (4 * i + 2 + odd))),
                 pl.BlockSpec((rows, acts), lambda i, m: (0, 0)),
             ],
             out_specs=pl.BlockSpec((2, LINE, acts), lambda i, m: (i, 0, 0)),
@@ -86,7 +82,7 @@
     return blocks[0] + got[0] + swap(kept, Y[far])
 
 
-def scatter_lines(even, odd):
+def scatter_lines(even, odd, wait):
     got = swap(odd, CORE)
     quarter = LINE // 4
     cut = lambda i, q: even[i, q * quarter : (q + 1) * quarter] + got[i, q * quarter : (q + 1) * quarter]
@@ -96,6 +92,7 @@
     c = [pair(m, 2) for m in range(4)]
     d = [pair(m, 3) for m in range(4)]
     c, d = y_second(1, c, y_first(1, c)), y_second(3, d, y_first(3, d))
+    came = wait(came)
     own = [half(2 * m, 0) + came[m] for m in range(4)]
     a = [o[:quarter] for o in own]
     b = [o[quarter:] for o in own]
@@ -299,7 +296,6 @@
 def downdate(solved, gain_cols, base):
     rows, acts = solved[0].shape
     whole = pl.BlockSpec((rows, acts), lambda b: (0, 0))
-    line = lambda b: (b % 8) * 2 + b // 8
     block = pl.BlockSpec((rows, 2 * LINE), lambda b: (0, b))
     return pl.pallas_call(
         downdate_kernel,
@@ -307,8 +303,8 @@
         in_specs=[
             whole,
             whole,
-            pl.BlockSpec((1, LINE, acts), lambda b: (line(2 * b), 0, 0)),
-            pl.BlockSpec((1, LINE, acts), lambda b: (line(2 * b + 1), 0, 0)),
+            pl.BlockSpec((1, LINE, acts), lambda b: (2 * b, 0, 0)),
+            pl.BlockSpec((1, LINE, acts), lambda b: (2 * b + 1, 0, 0)),
             block,
         ],
         out_specs=block,
@@ -420,7 +416,9 @@
     diag_rows = lax.dynamic_slice_in_dim(plant_diag, row_index * lines_rows, lines_rows, 0)
     diag_cols = lax.dynamic_slice_in_dim(plant_diag, col_index * lines_cols, lines_cols, 0)
     me = row_index.astype(jnp.int32).reshape(1)
-    trade = [((a * 2 + core) * 8 + b, (b * 2 + core) * 8 + a) for a in range(8) for b in range(8) for core in range(2)]
+    trade = [(r * 8 + c, (2 * c + r // 8) * 8 + r % 8) for r in range(16) for c in range(8)]
+    mine_inputs = lax.dynamic_slice_in_dim(inputs, col_index * LINE, LINE, 0)
+    mine_inputs = lax.ppermute(mine_inputs, both, [(b, a) for a, b in trade])
 
     def shifted(x, axis, by):
         count = lax.axis_size(axis)
@@ -437,55 +435,59 @@
     )
     odd = product_lines(me, value_matrix, inputs, 1)
     even = product_lines(me, value_matrix, inputs, 0)
+    held = {}
+
+    def wait(came):
+        came, held["inputs"], *held["rows"] = tied(came, mine_inputs, above, below)
+        return came
+
+    product = scatter_lines(even, odd, wait)
+    above, below = held["rows"]
     tall = lambda cols: jnp.concatenate([above[:, cols], value_matrix[:, cols], below[:, cols]], 0)
     left = shifted(tall(slice(-LINE, None)), "col", 1)
     right = shifted(tall(slice(None, LINE)), "col", -1)
-    product = scatter_lines(even, odd)
 
     core, x_low, y = row_index & 1, (row_index >> 1) & 1, row_index >> 2
     x_high, z = col_index & 1, col_index >> 1
     x_place = x_high * 2 + x_low
 
-    product, above, below, left, right = tied(product, above, below, left, right)
-    product = lax.ppermute(product, both, trade)
-    around = (*operands[:2], above, below, left, right, *operands[2:])
-    base = None
-    for start, count in ((1, 7), (8, 7), (0, 1), (lines_cols - 1, 1)):
-        base = plant_part(start, count, *around, base)
-    product, base = tied(product, base)
-
     count = grid_side
-    over = lax.ppermute(product, both, [(i, i + 1) for i in range(count - 1)])
-    under = lax.ppermute(product, both, [(i + 1, i) for i in range(count - 1)])
-    mine_inputs = lax.dynamic_slice_in_dim(inputs, col_index * LINE, LINE, 0)
-    gram = gram_blocks(mine_inputs, product)
+    device_of = lambda line: (line % 16) * 8 + line // 16
+    over = lax.ppermute(product, both, [(device_of(i), device_of(i + 1)) for i in range(count - 1)])
+    under = lax.ppermute(product, both, [(device_of(i + 1), device_of(i)) for i in range(count - 1)])
+    gram = gram_blocks(held["inputs"], product)
     total = sum_cores(gram.reshape(10 * PANEL, PANEL), core)
     over, under, total = tied(over, under, total)
-    diagonal = lax.dynamic_slice_in_dim(plant_diag, row_index * 8 + col_index, 1, 0)
+    diagonal = lax.dynamic_slice_in_dim(plant_diag, col_index * 16 + row_index, 1, 0)
     gain = stencil_first(jnp.stack([over, product, under]), diagonal)[0]
     gain, total = tied(gain, total)
 
-    pair = joined(gain, swap(gain, X_HIGH), x_high == 1)
-    total = scatter_four(total, z, Z)
-    pair, total = tied(pair, total)
-
-    back = lax.ppermute(gain, both, trade)
+    gain_cols = lax.all_gather(gain, "row", axis=0)
+    total = scatter_four(scatter_four(total, z, Z), x_place, X)
+    total = total + swap(total, Y[1]) + swap(total, Y[2]) + swap(total, Y[3])
+    total = gather_four(gather_four(total, x_place, X), z, Z)
+
+    gain, total = tied(gain, total)
+    traded = lax.ppermute(gain, both, trade)
+    total = joined(total, swap(total, CORE), core == 1)
+    factors = factored(control_weight, total.reshape(10, PANEL, PANEL))
+    around = (*operands[:2], above, below, left, right, *operands[2:])
+    *factors, value = tied(*factors, value_matrix)
+    base = plant_part(1, 7, around[0], value, *around[2:], None)
+    traded, base, left, right = tied(traded, base, left, right)
+    around = (*operands[:2], above, below, left, right, *operands[2:])
+
+    pair = joined(traded, swap(traded, X_HIGH), x_high == 1)
+    base = plant_part(8, 7, *around, base)
+    pair, base, gain_cols = tied(pair, base, gain_cols)
     first, second = pair[:LINE], pair[LINE:]
     first_near, second_near = swap(first, Z[1]), swap(second, Z[3])
-    total = scatter_four(total, x_place, X)
-    first_near, second_near, total = tied(first_near, second_near, total)
-
+    base = plant_part(0, 1, *around, base)
+    base = plant_part(lines_cols - 1, 1, *around, base)
+    first_near, second_near, base = tied(first_near, second_near, base)
     first_far = swap(jnp.stack([first, first_near]), Z[3])
     second_far = swap(jnp.stack([second, second_near]), Z[1])
-    total = total + swap(total, Y[1]) + swap(total, Y[2]) + swap(total, Y[3])
-    back, total = tied(back, total)
-    gain_cols = lax.all_gather(back, "row", axis=0)
-    total = gather_four(total, x_place, X)
-    first_far, second_far, total = tied(first_far, second_far, total)
-    total = gather_four(total, z, Z)
-    total = joined(total, swap(total, CORE), core == 1)
-
-    factors = factored(control_weight, total.reshape(10, PANEL, PANEL))
+
     sides = (first, first_near, first_far, second, second_near, second_far)
     solved = solve(z.astype(jnp.int32).reshape(1), factors, sides)
     return downdate(solved, gain_cols, base)

time: 524 us -> 544 us (1.038)
  the two profiles are of different devices: /device:TPU:7 before, /device:TPU:1 now
where the time goes in v8:
time: 544 us; the launch traced here: 534 us
  Pallas kernels  260 us (48%)
  waiting for transfers between devices  126 us (23%)
  starting transfers between devices  87.1 us (16%)
  other arithmetic  31.7 us (6%)
  between operations  15.3 us (3%)
  local copies, waits for them, and re-layouts  13.2 us (2%)
    pallas_call x1, Pallas kernels, factored(): pl.pallas_call(factor_kernel, out_shape=[jax.ShapeDtypeStruct((10, PANEL,...  177 us
    ppermute x33, waiting for transfers between devices, swap(): return lax.ppermute(x, ('row', 'col'), [(i, i ^ mask) for i in range(128)])  117 us
    ppermute x33, starting transfers between devices, swap(): return lax.ppermute(x, ('row', 'col'), [(i, i ^ mask) for i in range(128)])  61.9 us
    pallas_call x4, Pallas kernels, plant_part(): pl.pallas_call(functools.partial(plant_kernel, start, [len(blocks) for bl...  24.6 us
    pallas_call x2, Pallas kernels, product_lines(): pl.pallas_call(product_kernel, grid_spec=pltpu.PrefetchScalarGridSpec(num...  23.3 us
    pallas_call x1, Pallas kernels, downdate(): pl.pallas_call(downdate_kernel, grid=(8,), in_specs=[whole, whole, pl.Blo...  19.1 us
    pallas_call x1, Pallas kernels, solve(): pl.pallas_call(solve_kernel, out_shape=[jax.ShapeDtypeStruct((size, 4 * P...  12.6 us
  transfers between devices with their start and end apart: 42, of which 25 were waited for; matrix products, arithmetic and copies ran while one was open for 6% of the time, Pallas kernels for 40%

profile of v8, /device:TPU:1, one launch (start us, length us, event | category | flops | bytes accessed | tf_op | source)
XLA Modules:
  0.0 533.6 jit_solution(8543343766435379736)
XLA Ops:
  6.5 11.7 %shard_map.56 = f32[8,128,1024]{2,1,0:T(8,128)} custom-call(s32[1]{0:T(128)} %bitcast.2.me_ref, f32[1024,2048]{1,0:T(8,128)} %refs_4_.4, f32[1024,2048]{1,0:T(8,128)} %refs_4_.4, f32[1024,1024]{1,0:T(8,128)} %inputs.3), custom_call_target="tpu_custom_call" | custom-call | flops 1048576 | bytes 1048576 | tf_op jit(solution)/shard_map/pallas_call | solution.py:46
  19.6 3.1 fusion.38
  22.7 3.1 collective-permute-start.3
  27.7 11.7 %shard_map.55 = f32[8,128,1024]{2,1,0:T(8,128)} custom-call(s32[1]{0:T(128)} %bitcast.2.me_ref, f32[1024,2048]{1,0:T(8,128)} %refs_4_.4, f32[1024,2048]{1,0:T(8,128)} %refs_4_.4, f32[1024,1024]{1,0:T(8,128)} %inputs.3), custom_call_target="tpu_custom_call" | custom-call | flops 1048576 | bytes 1048576 | tf_op jit(solution)/shard_map/pallas_call | solution.py:46
  39.4 2.3 fusion.22
  53.5 6.4 %collective-permute-done.9 = f32[2,2,32,1024]{3,2,1,0:T(8,128)} collective-permute-done((f32[2,2,32,1024]{3,2,1,0:T(8,128)}, f32[2,2,32,1024]{3,2,1,0:T(8,128)}, u32[]{:S(2)}, u32[]{:S(2)}) %collective-permute-start.9) | collective-permute-done | bytes 524320 | tf_op jit(solution)/shard_map/ppermute | solution.py:66
  59.9 6.8 %collective-permute-start.2 = (f32[128,1024]{1,0:T(8,128)S(1)}, f32[128,1024]{1,0:T(8,128)S(1)}, u32[]{:S(2)}, u32[]{:S(2)}) collective-permute-start(f32[128,1024]{1,0:T(8,128)S(1)} %constant_dynamic-slice_fusion.8), channel_id=1, source_target_pairs={{0,0},{16,1},{32,2},{48,3},{64,4},{80,5},{96,6},{112,7},{1,8},{17,... | collective-permute-start | bytes 1572872 | tf_op jit(solution)/shard_map/ppermute | solution.py:421
  67.9 3.8 collective-permute-start.10
  72.7 21.4 %collective-permute-done.10 = f32[2,32,1024]{2,1,0:T(8,128)S(1)} collective-permute-done((f32[2,32,1024]{2,1,0:T(8,128)S(1)}, f32[2,32,1024]{2,1,0:T(8,128)S(1)}, u32[]{:S(2)}, u32[]{:S(2)}) %collective-permute-start.10) | collective-permute-done | bytes 262176 | tf_op jit(solution)/shard_map/ppermute | solution.py:66
  94.1 2.2 collective-permute-start.12
  101.1 5.1 collective-permute-done.5
  107.6 4.0 collective-permute-start.7
  112.4 3.6 collective-permute-done.7
  117.0 2.2 collective-permute-start.8
  119.2 2.6 collective-permute-done.8
  124.6 3.9 shard_map.57
  128.5 3.0 slice_select_fusion.1
  131.5 5.4 %collective-permute-start.16 = (f32[1280,256]{1,0:T(8,128)S(1)}, f32[1280,256]{1,0:T(8,128)}, u32[]{:S(2)}, u32[]{:S(2)}) collective-permute-start(f32[1280,256]{1,0:T(8,128)S(1)} %bitcast.168), channel_id=1, source_target_pairs={{0,8},{1,9},{2,10},{3,11},{4,12},{5,13},{6,14},{7,15},{8,0},{9,1},... | collective-permute-start | bytes 3932168 | tf_op jit(solution)/shard_map/ppermute | solution.py:66
  138.9 2.4 collective-permute-start.15
  145.3 7.6 %collective-permute-done.15 = f32[128,1024]{1,0:T(8,128)S(1)} collective-permute-done((f32[128,1024]{1,0:T(8,128)}, f32[128,1024]{1,0:T(8,128)S(1)}, u32[]{:S(2)}, u32[]{:S(2)}) %collective-permute-start.15) | collective-permute-done | bytes 524320 | tf_op jit(solution)/shard_map/ppermute | solution.py:457
  154.9 6.6 %collective-permute-start.17 = (f32[320,256]{1,0:T(8,128)}, f32[320,256]{1,0:T(8,128)}, u32[]{:S(2)}, u32[]{:S(2)}) collective-permute-start(f32[320,256]{1,0:T(8,128)} %get-tuple-element.105), channel_id=1, source_target_pairs={{0,2},{1,3},{2,0},{3,1},{4,6},{5,7},{6,4},{7,5},{8,10},{9,11},{10,... | collective-permute-start | bytes 983048 | tf_op jit(solution)/shard_map/ppermute | solution.py:66
  161.5 2.5 collective-permute-start.19
  164.0 6.1 %collective-permute-done.17 = f32[320,256]{1,0:T(8,128)} collective-permute-done((f32[320,256]{1,0:T(8,128)}, f32[320,256]{1,0:T(8,128)}, u32[]{:S(2)}, u32[]{:S(2)}) %collective-permute-start.17) | collective-permute-done | bytes 327712 | tf_op jit(solution)/shard_map/ppermute | solution.py:66
  170.1 3.7 collective-permute-done.18
  173.8 3.2 collective-permute-done.19
  179.0 3.6 collective-permute-start.20
  182.6 2.5 collective-permute-start.22
  185.1 2.2 collective-permute-done.20
  187.3 2.9 collective-permute-done.21
  191.2 3.3 collective-permute-start.24
  196.9 5.3 collective-permute-done.24
  204.1 2.2 collective-permute-start.28
  208.1 3.0 collective-permute-done.27
  212.6 3.3 collective-permute-start.30
  218.1 10.2 %collective-permute-done.30 = f32[320,256]{1,0:T(8,128)S(1)} collective-permute-done((f32[320,256]{1,0:T(8,128)}, f32[320,256]{1,0:T(8,128)S(1)}, u32[]{:S(2)}, u32[]{:S(2)}) %collective-permute-start.30) | collective-permute-done | bytes 327712 | tf_op jit(solution)/shard_map/ppermute | solution.py:66
  228.3 3.3 collective-permute-done.31
  231.9 3.0 collective-permute-start.32
  240.1 6.0 %collective-permute-start.33 = (f32[128,1024]{1,0:T(8,128)S(1)}, f32[128,1024]{1,0:T(8,128)}, u32[]{:S(2)}, u32[]{:S(2)}) collective-permute-start(f32[128,1024]{1,0:T(8,128)S(1)} %copy-done.8), channel_id=1, source_target_pairs={{0,0},{1,16},{2,32},{3,48},{4,64},{5,80},{6,96},{7,112},{8,1},{9,1... | collective-permute-start | bytes 1572872 | tf_op jit(solution)/shard_map/ppermute | solution.py:471
  247.9 176.5 %shard_map.58 = (f32[10,256,256]{2,1,0:T(8,128)}, f32[4,256,256]{2,1,0:T(8,128)}) custom-call(f32[1]{0:T(128)S(6)} %copy.12.weight, f32[10,256,256]{2,1,0:T(8,128)} %bitcast.166), custom_call_target="tpu_custom_call" | custom-call | flops 9663676416 | bytes 12582912 | tf_op jit(solution)/shard_map/pallas_call | solution.py:235
  425.5 9.2 %shard_map.59.refs_12_ = f32[1024,2048]{1,0:T(8,128)} custom-call(s32[2]{0:T(128)} %pad_add_fusion.place, f32[128,2048]{1,0:T(8,128)} %copy-done.2, f32[1024,2048]{1,0:T(8,128)} %refs_4_.4, f32[128,2048]{1,0:T(8,128)} %copy-done.3, f32[128,2048]{1,0:T(8,128)} %copy-done.2, f32[1024,2048]{1,0:T(8,128)} %refs_4_.4, f32[128,2048]{1,0:T(8,128)} %copy-done.3, ...), custom_call_target="tpu_custom_call" | custom-call | flops 33554432 | bytes 16777216 | tf_op jit(solution)/shard_map/pallas_call | solution.py:394
  437.0 9.2 %shard_map.60.refs_10_ = f32[1024,2048]{1,0:T(8,128)} custom-call(s32[2]{0:T(128)} %pad_add_fusion.place, f32[128,2048]{1,0:T(8,128)} %copy-done.2, f32[1024,2048]{1,0:T(8,128)} %refs_4_.4, f32[128,2048]{1,0:T(8,128)} %copy-done.3, f32[128,2048]{1,0:T(8,128)} %copy-done.2, f32[1024,2048]{1,0:T(8,128)} %refs_4_.4, ...), custom_call_target="tpu_custom_call", output_to_operand_aliasing={{}: (13, {})} | custom-call | flops 33554432 | bytes 16777216 | tf_op jit(solution)/shard_map/pallas_call | solution.py:394
  450.6 4.6 collective-permute-start.38
  455.2 3.1 shard_map.61.refs_10_
  458.3 3.1 shard_map.62.base
  463.0 4.5 collective-permute-done.38.second_near
  469.5 22.1 %collective-permute-done.40.second_far = f32[2,128,1024]{2,1,0:T(8,128)S(1)} collective-permute-done((f32[2,128,1024]{2,1,0:T(8,128)S(1)}, f32[2,128,1024]{2,1,0:T(8,128)S(1)}, u32[]{:S(2)}, u32[]{:S(2)}) %collective-permute-start.40) | collective-permute-done | bytes 1048608 | tf_op jit(solution)/shard_map/ppermute | solution.py:66
  494.7 12.6 %shard_map.63 = (bf16[1024,1024]{1,0:T(8,128)(2,1)}, bf16[1024,1024]{1,0:T(8,128)(2,1)}) custom-call(s32[1]{0:T(128)} %bitcast.z, f32[10,256,256]{2,1,0:T(8,128)} %get-tuple-element.43.factor, f32[4,256,256]{2,1,0:T(8,128)} %get-tuple-element.44.inverses, f32[128,1024]{1,0:T(8,128)} %copy-done.33, f32[128,1024]{1,0:T(8,128)} %copy-done.34, ...), custom_call_target="tpu_custom_call" | custom-call | flops 9663676416 | bytes 12582912 | tf_op jit(solution)/shard_map/pallas_call | solution.py:280
  507.2 19.1 %shard_map.64 = f32[1024,2048]{1,0:T(8,128)} custom-call(bf16[1024,1024]{1,0:T(8,128)(2,1)} %get-tuple-element.57.high, bf16[1024,1024]{1,0:T(8,128)(2,1)} %get-tuple-element.58.low, f32[16,128,1024]{2,1,0:T(8,128)} %bitcast.184, f32[16,128,1024]{2,1,0:T(8,128)} %bitcast.185, f32[1024,2048]{1,0:T(8,128)} %shard_map.62.base), custom_call_target="tpu_custom_call" | custom-call | flops 12884901888 | bytes 29360128 | tf_op jit(solution)/shard_map/pallas_call | solution.py:300
  (186 shorter events, 69.3 us)
Async XLA Ops:
  6.5 130.4 %copy-start = (f32[128,128]{1,0:T(8,128)S(1)}, f32[128,128]{1,0:T(8,128)}, u32[]{:S(2)}) copy-start(f32[128,128]{1,0:T(8,128)} %param.7) | copy-start | bytes 196612
  6.5 443.0 %all-gather.3.cloned.1.call-start = ((), (), s32[]{:S(2)}) async-start(), calls=%async_computation | async-start | bytes 8912896 | tf_op jit(solution)/shard_map/all_gather | solution.py:465
  18.2 21.2 %collective-permute-start = (f32[8,128,1024]{2,1,0:T(8,128)}, f32[8,128,1024]{2,1,0:T(8,128)S(1)}, u32[]{:S(2)}, u32[]{:S(2)}) collective-permute-start(f32[8,128,1024]{2,1,0:T(8,128)} %shard_map.56), channel_id=1, source_target_pairs={{0,8},{1,9},{2,10},{3,11},{4,12},{5,13},{6,14},{7,15},{8,0},{9,1},... | collective-permute-start | bytes 12582920 | tf_op jit(solution)/shard_map/ppermute | solution.py:66
  22.7 74.7 %collective-permute-start.3 = (f32[128,2048]{1,0:T(8,128)}, f32[128,2048]{1,0:T(8,128)S(1)}, u32[]{:S(2)}, u32[]{:S(2)}) collective-permute-start(f32[128,2048]{1,0:T(8,128)} %get-tuple-element.91), channel_id=1, source_target_pairs={{0,8},{8,16},{16,24},{24,32},{32,40},{40,48},{48,56},{56,64},{64,7... | collective-permute-start | bytes 3145736 | tf_op jit(solution)/shard_map/ppermute | solution.py:425
  25.8 71.6 %collective-permute-start.4 = (f32[128,2048]{1,0:T(8,128)}, f32[128,2048]{1,0:T(8,128)S(1)}, u32[]{:S(2)}, u32[]{:S(2)}) collective-permute-start(f32[128,2048]{1,0:T(8,128)} %get-tuple-element.90), channel_id=1, source_target_pairs={{8,0},{16,8},{24,16},{32,24},{40,32},{48,40},{56,48},{64,56},{72,6... | collective-permute-start | bytes 3145736 | tf_op jit(solution)/shard_map/ppermute | solution.py:425
  44.1 53.3 %collective-permute-start.1 = (f32[4,64,1024]{2,1,0:T(8,128)}, f32[4,64,1024]{2,1,0:T(8,128)S(1)}, u32[]{:S(2)}, u32[]{:S(2)}) collective-permute-start(f32[4,64,1024]{2,1,0:T(8,128)} %pad_maximum_fusion.3), channel_id=1, source_target_pairs={{0,16},{1,17},{2,18},{3,19},{4,20},{5,21},{6,22},{7,23},{8,24},{9,... | collective-permute-start | bytes 3145736 | tf_op jit(solution)/shard_map/ppermute | solution.py:66
  47.3 12.6 %collective-permute-start.9 = (f32[2,2,32,1024]{3,2,1,0:T(8,128)}, f32[2,2,32,1024]{3,2,1,0:T(8,128)}, u32[]{:S(2)}, u32[]{:S(2)}) collective-permute-start(f32[2,2,32,1024]{3,2,1,0:T(8,128)} %pad_maximum_fusion.9), channel_id=1, source_target_pairs={{0,32},{1,33},{2,34},{3,35},{4,36},{5,37},{6,38},{7,39},{8,40},{9,... | collective-permute-start | bytes 1572872 | tf_op jit(solution)/shard_map/ppermute | solution.py:66
  50.4 17.4 %collective-permute-start.11 = (f32[2,2,32,1024]{3,2,1,0:T(8,128)}, f32[2,2,32,1024]{3,2,1,0:T(8,128)}, u32[]{:S(2)}, u32[]{:S(2)}) collective-permute-start(f32[2,2,32,1024]{3,2,1,0:T(8,128)} %pad_maximum_fusion.10), channel_id=1, source_target_pairs={{0,96},{1,97},{2,98},{3,99},{4,100},{5,101},{6,102},{7,103},{8,104... | collective-permute-start | bytes 1572872 | tf_op jit(solution)/shard_map/ppermute | solution.py:66
  52.4 44.0 %copy-start.29 = (f32[1,32,1024]{2,1,0:T(8,128)S(1)}, f32[1,32,1024]{2,1,0:T(8,128)}, u32[]{:S(2)}) copy-start(f32[1,32,1024]{2,1,0:T(8,128)} %get-tuple-element.79) | copy-start | bytes 393220
  52.4 44.0 %copy-start.30 = (f32[1,32,1024]{2,1,0:T(8,128)S(1)}, f32[1,32,1024]{2,1,0:T(8,128)}, u32[]{:S(2)}) copy-start(f32[1,32,1024]{2,1,0:T(8,128)} %get-tuple-element.80) | copy-start | bytes 393220
  59.9 37.4 %collective-permute-start.2 = (f32[128,1024]{1,0:T(8,128)S(1)}, f32[128,1024]{1,0:T(8,128)S(1)}, u32[]{:S(2)}, u32[]{:S(2)}) collective-permute-start(f32[128,1024]{1,0:T(8,128)S(1)} %constant_dynamic-slice_fusion.8), channel_id=1, source_target_pairs={{0,0},{16,1},{32,2},{48,3},{64,4},{80,5},{96,6},{112,7},{1,8},{17,... | collective-permute-start | bytes 1572872 | tf_op jit(solution)/shard_map/ppermute | solution.py:421
  66.7 31.5 %copy-start.17 = (f32[32,1024]{1,0:T(8,128)S(1)}, f32[32,1024]{1,0:T(8,128)}, u32[]{:S(2)}) copy-start(f32[32,1024]{1,0:T(8,128)} %get-tuple-element.81) | copy-start | bytes 393220
  67.9 26.2 %collective-permute-start.10 = (f32[2,32,1024]{2,1,0:T(8,128)S(1)}, f32[2,32,1024]{2,1,0:T(8,128)S(1)}, u32[]{:S(2)}, u32[]{:S(2)}) collective-permute-start(f32[2,32,1024]{2,1,0:T(8,128)S(1)} %fusion.8), channel_id=1, source_target_pairs={{0,96},{1,97},{2,98},{3,99},{4,100},{5,101},{6,102},{7,103},{8,104... | collective-permute-start | bytes 786440 | tf_op jit(solution)/shard_map/ppermute | solution.py:66
  94.1 5.9 %collective-permute-start.12 = (f32[2,32,1024]{2,1,0:T(8,128)S(1)}, f32[2,32,1024]{2,1,0:T(8,128)S(1)}, u32[]{:S(2)}, u32[]{:S(2)}) collective-permute-start(f32[2,32,1024]{2,1,0:T(8,128)S(1)} %fusion.5), channel_id=1, source_target_pairs={{0,32},{1,33},{2,34},{3,35},{4,36},{5,37},{6,38},{7,39},{8,40},{9,... | collective-permute-start | bytes 786440 | tf_op jit(solution)/shard_map/ppermute | solution.py:66
  97.3 139.4 %copy-start.2 = (f32[128,2048]{1,0:T(8,128)}, f32[128,2048]{1,0:T(8,128)S(1)}, u32[]{:S(2)}) copy-start(f32[128,2048]{1,0:T(8,128)S(1)} %collective-permute-done.3.refs_0_.refs_3_.refs_6_.refs_1_.refs_4_) | copy-start | bytes 3145732
  97.4 139.4 %copy-start.3 = (f32[128,2048]{1,0:T(8,128)}, f32[128,2048]{1,0:T(8,128)S(1)}, u32[]{:S(2)}) copy-start(f32[128,2048]{1,0:T(8,128)S(1)} %collective-permute-done.4.refs_2_.refs_5_.refs_8_.refs_3_.refs_6_) | copy-start | bytes 3145732
  99.2 7.0 %collective-permute-start.5 = (f32[2,32,1024]{2,1,0:T(8,128)S(1)}, f32[2,32,1024]{2,1,0:T(8,128)S(1)}, u32[]{:S(2)}, u32[]{:S(2)}) collective-permute-start(f32[2,32,1024]{2,1,0:T(8,128)S(1)} %pad_maximum_fusion.14), channel_id=1, source_target_pairs={{0,32},{1,33},{2,34},{3,35},{4,36},{5,37},{6,38},{7,39},{8,40},{9,... | collective-permute-start | bytes 786440 | tf_op jit(solution)/shard_map/ppermute | solution.py:66
  107.6 8.4 %collective-permute-start.7 = (f32[2,32,1024]{2,1,0:T(8,128)}, f32[2,32,1024]{2,1,0:T(8,128)}, u32[]{:S(2)}, u32[]{:S(2)}) collective-permute-start(f32[2,32,1024]{2,1,0:T(8,128)} %pad_maximum_fusion.15), channel_id=1, source_target_pairs={{0,96},{1,97},{2,98},{3,99},{4,100},{5,101},{6,102},{7,103},{8,104... | collective-permute-start | bytes 786440 | tf_op jit(solution)/shard_map/ppermute | solution.py:66
  112.4 6.7 %collective-permute-start.13 = (f32[64,1024]{1,0:T(8,128)}, f32[64,1024]{1,0:T(8,128)S(1)}, u32[]{:S(2)}, u32[]{:S(2)}) collective-permute-start(f32[64,1024]{1,0:T(8,128)} %pad_maximum_fusion.16), channel_id=1, source_target_pairs={{0,16},{1,17},{2,18},{3,19},{4,20},{5,21},{6,22},{7,23},{8,24},{9,... | collective-permute-start | bytes 786440 | tf_op jit(solution)/shard_map/ppermute | solution.py:66
  112.4 6.8 %collective-permute-start.6 = (f32[32,1024]{1,0:T(8,128)}, f32[32,1024]{1,0:T(8,128)S(1)}, u32[]{:S(2)}, u32[]{:S(2)}) collective-permute-start(f32[32,1024]{1,0:T(8,128)} %get-tuple-element.135), channel_id=1, source_target_pairs={{0,96},{1,97},{2,98},{3,99},{4,100},{5,101},{6,102},{7,103},{8,104... | collective-permute-start | bytes 393224 | tf_op jit(solution)/shard_map/ppermute | solution.py:66
  117.0 4.8 collective-permute-start.8
  131.5 9.8 %collective-permute-start.16 = (f32[1280,256]{1,0:T(8,128)S(1)}, f32[1280,256]{1,0:T(8,128)}, u32[]{:S(2)}, u32[]{:S(2)}) collective-permute-start(f32[1280,256]{1,0:T(8,128)S(1)} %bitcast.168), channel_id=1, source_target_pairs={{0,8},{1,9},{2,10},{3,11},{4,12},{5,13},{6,14},{7,15},{8,0},{9,1},... | collective-permute-start | bytes 3932168 | tf_op jit(solution)/shard_map/ppermute | solution.py:66
  136.9 8.3 %collective-permute-start.14 = (f32[128,1024]{1,0:T(8,128)}, f32[128,1024]{1,0:T(8,128)S(1)}, u32[]{:S(2)}, u32[]{:S(2)}) collective-permute-start(f32[128,1024]{1,0:T(8,128)} %get-tuple-element.122.product), channel_id=1, source_target_pairs={{0,8},{8,16},{16,24},{24,32},{32,40},{40,48},{48,56},{56,64},{64,7... | collective-permute-start | bytes 1572872 | tf_op jit(solution)/shard_map/ppermute | solution.py:456
  138.9 14.0 %collective-permute-start.15 = (f32[128,1024]{1,0:T(8,128)}, f32[128,1024]{1,0:T(8,128)S(1)}, u32[]{:S(2)}, u32[]{:S(2)}) collective-permute-start(f32[128,1024]{1,0:T(8,128)} %get-tuple-element.122.product), channel_id=1, source_target_pairs={{8,0},{16,8},{24,16},{32,24},{40,32},{48,40},{56,48},{64,56},{72,6... | collective-permute-start | bytes 1572872 | tf_op jit(solution)/shard_map/ppermute | solution.py:457
  154.9 15.2 %collective-permute-start.17 = (f32[320,256]{1,0:T(8,128)}, f32[320,256]{1,0:T(8,128)}, u32[]{:S(2)}, u32[]{:S(2)}) collective-permute-start(f32[320,256]{1,0:T(8,128)} %get-tuple-element.105), channel_id=1, source_target_pairs={{0,2},{1,3},{2,0},{3,1},{4,6},{5,7},{6,4},{7,5},{8,10},{9,11},{10,... | collective-permute-start | bytes 983048 | tf_op jit(solution)/shard_map/ppermute | solution.py:66
  161.5 12.3 %collective-permute-start.18 = (f32[320,256]{1,0:T(8,128)}, f32[320,256]{1,0:T(8,128)}, u32[]{:S(2)}, u32[]{:S(2)}) collective-permute-start(f32[320,256]{1,0:T(8,128)} %get-tuple-element.107), channel_id=1, source_target_pairs={{0,4},{1,5},{2,6},{3,7},{4,0},{5,1},{6,2},{7,3},{8,12},{9,13},{10,... | collective-permute-start | bytes 983048 | tf_op jit(solution)/shard_map/ppermute | solution.py:66
  161.5 15.5 %collective-permute-start.19 = (f32[320,256]{1,0:T(8,128)}, f32[320,256]{1,0:T(8,128)}, u32[]{:S(2)}, u32[]{:S(2)}) collective-permute-start(f32[320,256]{1,0:T(8,128)} %get-tuple-element.106), channel_id=1, source_target_pairs={{0,6},{1,7},{2,4},{3,5},{4,2},{5,3},{6,0},{7,1},{8,14},{9,15},{10,... | collective-permute-start | bytes 983048 | tf_op jit(solution)/shard_map/ppermute | solution.py:66
  179.0 8.3 %collective-permute-start.20 = (f32[80,256]{1,0:T(8,128)S(1)}, f32[80,256]{1,0:T(8,128)S(1)}, u32[]{:S(2)}, u32[]{:S(2)}) collective-permute-start(f32[80,256]{1,0:T(8,128)S(1)} %get-tuple-element.130), channel_id=1, source_target_pairs={{0,16},{1,17},{2,18},{3,19},{4,20},{5,21},{6,22},{7,23},{8,24},{9,... | collective-permute-start | bytes 245768 | tf_op jit(solution)/shard_map/ppermute | solution.py:66
  182.6 7.6 %collective-permute-start.21 = (f32[80,256]{1,0:T(8,128)S(1)}, f32[80,256]{1,0:T(8,128)S(1)}, u32[]{:S(2)}, u32[]{:S(2)}) collective-permute-start(f32[80,256]{1,0:T(8,128)S(1)} %get-tuple-element.132), channel_id=1, source_target_pairs={{0,1},{1,0},{2,3},{3,2},{4,5},{5,4},{6,7},{7,6},{8,9},{9,8},{10,11... | collective-permute-start | bytes 245768 | tf_op jit(solution)/shard_map/ppermute | solution.py:66
  182.6 7.6 %collective-permute-start.22 = (f32[80,256]{1,0:T(8,128)S(1)}, f32[80,256]{1,0:T(8,128)S(1)}, u32[]{:S(2)}, u32[]{:S(2)}) collective-permute-start(f32[80,256]{1,0:T(8,128)S(1)} %get-tuple-element.131), channel_id=1, source_target_pairs={{0,17},{1,16},{2,19},{3,18},{4,21},{5,20},{6,23},{7,22},{8,25},{9,... | collective-permute-start | bytes 245768 | tf_op jit(solution)/shard_map/ppermute | solution.py:66
  191.2 5.8 %collective-permute-start.23 = (f32[80,256]{1,0:T(8,128)S(1)}, f32[80,256]{1,0:T(8,128)S(1)}, u32[]{:S(2)}, u32[]{:S(2)}) collective-permute-start(f32[80,256]{1,0:T(8,128)S(1)} %add_add_fusion.2), channel_id=1, source_target_pairs={{0,32},{1,33},{2,34},{3,35},{4,36},{5,37},{6,38},{7,39},{8,40},{9,... | collective-permute-start | bytes 245768 | tf_op jit(solution)/shard_map/ppermute | solution.py:66
  191.2 11.0 %collective-permute-start.24 = (f32[80,256]{1,0:T(8,128)S(1)}, f32[80,256]{1,0:T(8,128)S(1)}, u32[]{:S(2)}, u32[]{:S(2)}) collective-permute-start(f32[80,256]{1,0:T(8,128)S(1)} %add_add_fusion.2), channel_id=1, source_target_pairs={{0,64},{1,65},{2,66},{3,67},{4,68},{5,69},{6,70},{7,71},{8,72},{9,... | collective-permute-start | bytes 245768 | tf_op jit(solution)/shard_map/ppermute | solution.py:66
  194.6 7.7 %collective-permute-start.25 = (f32[80,256]{1,0:T(8,128)S(1)}, f32[80,256]{1,0:T(8,128)S(1)}, u32[]{:S(2)}, u32[]{:S(2)}) collective-permute-start(f32[80,256]{1,0:T(8,128)S(1)} %add_add_fusion.2), channel_id=1, source_target_pairs={{0,96},{1,97},{2,98},{3,99},{4,100},{5,101},{6,102},{7,103},{8,104... | collective-permute-start | bytes 245768 | tf_op jit(solution)/shard_map/ppermute | solution.py:66
  202.3 5.8 %collective-permute-start.26 = (f32[80,256]{1,0:T(8,128)S(1)}, f32[80,256]{1,0:T(8,128)S(1)}, u32[]{:S(2)}, u32[]{:S(2)}) collective-permute-start(f32[80,256]{1,0:T(8,128)S(1)} %add_add_fusion.1), channel_id=1, source_target_pairs={{0,16},{1,17},{2,18},{3,19},{4,20},{5,21},{6,22},{7,23},{8,24},{9,... | collective-permute-start | bytes 245768 | tf_op jit(solution)/shard_map/ppermute | solution.py:66
  202.4 8.7 %collective-permute-start.27 = (f32[80,256]{1,0:T(8,128)S(1)}, f32[80,256]{1,0:T(8,128)S(1)}, u32[]{:S(2)}, u32[]{:S(2)}) collective-permute-start(f32[80,256]{1,0:T(8,128)S(1)} %add_add_fusion.1), channel_id=1, source_target_pairs={{0,1},{1,0},{2,3},{3,2},{4,5},{5,4},{6,7},{7,6},{8,9},{9,8},{10,11... | collective-permute-start | bytes 245768 | tf_op jit(solution)/shard_map/ppermute | solution.py:66
  204.1 7.0 %collective-permute-start.28 = (f32[80,256]{1,0:T(8,128)S(1)}, f32[80,256]{1,0:T(8,128)S(1)}, u32[]{:S(2)}, u32[]{:S(2)}) collective-permute-start(f32[80,256]{1,0:T(8,128)S(1)} %add_add_fusion.1), channel_id=1, source_target_pairs={{0,17},{1,16},{2,19},{3,18},{4,21},{5,20},{6,23},{7,22},{8,25},{9,... | collective-permute-start | bytes 245768 | tf_op jit(solution)/shard_map/ppermute | solution.py:66
  212.0 6.1 %collective-permute-start.29 = (f32[320,256]{1,0:T(8,128)}, f32[320,256]{1,0:T(8,128)S(1)}, u32[]{:S(2)}, u32[]{:S(2)}) collective-permute-start(f32[320,256]{1,0:T(8,128)} %get-tuple-element.125), channel_id=1, source_target_pairs={{0,2},{1,3},{2,0},{3,1},{4,6},{5,7},{6,4},{7,5},{8,10},{9,11},{10,... | collective-permute-start | bytes 983048 | tf_op jit(solution)/shard_map/ppermute | solution.py:66
  212.6 15.7 %collective-permute-start.30 = (f32[320,256]{1,0:T(8,128)}, f32[320,256]{1,0:T(8,128)S(1)}, u32[]{:S(2)}, u32[]{:S(2)}) collective-permute-start(f32[320,256]{1,0:T(8,128)} %get-tuple-element.125), channel_id=1, source_target_pairs={{0,4},{1,5},{2,6},{3,7},{4,0},{5,1},{6,2},{7,3},{8,12},{9,13},{10,... | collective-permute-start | bytes 983048 | tf_op jit(solution)/shard_map/ppermute | solution.py:66
  215.9 15.7 %collective-permute-start.31 = (f32[320,256]{1,0:T(8,128)}, f32[320,256]{1,0:T(8,128)S(1)}, u32[]{:S(2)}, u32[]{:S(2)}) collective-permute-start(f32[320,256]{1,0:T(8,128)} %get-tuple-element.125), channel_id=1, source_target_pairs={{0,6},{1,7},{2,4},{3,5},{4,2},{5,3},{6,0},{7,1},{8,14},{9,15},{10,... | collective-permute-start | bytes 983048 | tf_op jit(solution)/shard_map/ppermute | solution.py:66
  231.9 14.2 %collective-permute-start.32 = (f32[1280,256]{1,0:T(8,128)S(1)}, f32[1280,256]{1,0:T(8,128)S(1)}, u32[]{:S(2)}, u32[]{:S(2)}) collective-permute-start(f32[1280,256]{1,0:T(8,128)S(1)} %pad_maximum_fusion.2), channel_id=1, source_target_pairs={{0,8},{1,9},{2,10},{3,11},{4,12},{5,13},{6,14},{7,15},{8,0},{9,1},... | collective-permute-start | bytes 3932168 | tf_op jit(solution)/shard_map/ppermute | solution.py:66
  236.9 197.7 %collective-permute-start.34 = (f32[1280,128]{1,0:T(8,128)S(1)}, f32[1280,128]{1,0:T(8,128)S(1)}, u32[]{:S(2)}, u32[]{:S(2)}) collective-permute-start(f32[1280,128]{1,0:T(8,128)S(1)} %pad_maximum_fusion.7), channel_id=1, source_target_pairs={{0,1},{1,2},{2,3},{3,4},{4,5},{5,6},{6,7},{8,9},{9,10},{10,11},{11... | collective-permute-start | bytes 1966088 | tf_op jit(solution)/shard_map/ppermute | solution.py:425
  238.8 195.8 %collective-permute-start.35 = (f32[1280,128]{1,0:T(8,128)S(1)}, f32[1280,128]{1,0:T(8,128)S(1)}, u32[]{:S(2)}, u32[]{:S(2)}) collective-permute-start(f32[1280,128]{1,0:T(8,128)S(1)} %pad_maximum_fusion.8), channel_id=1, source_target_pairs={{1,0},{2,1},{3,2},{4,3},{5,4},{6,5},{7,6},{9,8},{10,9},{11,10},{12... | collective-permute-start | bytes 1966088 | tf_op jit(solution)/shard_map/ppermute | solution.py:425
  240.1 194.5 %collective-permute-start.33 = (f32[128,1024]{1,0:T(8,128)S(1)}, f32[128,1024]{1,0:T(8,128)}, u32[]{:S(2)}, u32[]{:S(2)}) collective-permute-start(f32[128,1024]{1,0:T(8,128)S(1)} %copy-done.8), channel_id=1, source_target_pairs={{0,0},{1,16},{2,32},{3,48},{4,64},{5,80},{6,96},{7,112},{8,1},{9,1... | collective-permute-start | bytes 1572872 | tf_op jit(solution)/shard_map/ppermute | solution.py:471
  435.5 12.7 %collective-permute-start.36 = (f32[128,1024]{1,0:T(8,128)}, f32[128,1024]{1,0:T(8,128)S(1)}, u32[]{:S(2)}, u32[]{:S(2)}) collective-permute-start(f32[128,1024]{1,0:T(8,128)} %collective-permute-done.33), channel_id=1, source_target_pairs={{0,1},{1,0},{2,3},{3,2},{4,5},{5,4},{6,7},{7,6},{8,9},{9,8},{10,11... | collective-permute-start | bytes 1572872 | tf_op jit(solution)/shard_map/ppermute | solution.py:66
  449.8 13.1 %collective-permute-start.37 = (f32[128,1024]{1,0:T(8,128)S(1)}, f32[128,1024]{1,0:T(8,128)S(1)}, u32[]{:S(2)}, u32[]{:S(2)}) collective-permute-start(f32[128,1024]{1,0:T(8,128)S(1)} %get-tuple-element.111.first), channel_id=1, source_target_pairs={{0,2},{1,3},{2,0},{3,1},{4,6},{5,7},{6,4},{7,5},{8,10},{9,11},{10,... | collective-permute-start | bytes 1572872 | tf_op jit(solution)/shard_map/ppermute | solution.py:66
  450.6 16.8 %collective-permute-start.38 = (f32[128,1024]{1,0:T(8,128)S(1)}, f32[128,1024]{1,0:T(8,128)S(1)}, u32[]{:S(2)}, u32[]{:S(2)}) collective-permute-start(f32[128,1024]{1,0:T(8,128)S(1)} %get-tuple-element.110.second), channel_id=1, source_target_pairs={{0,6},{1,7},{2,4},{3,5},{4,2},{5,3},{6,0},{7,1},{8,14},{9,15},{10,... | collective-permute-start | bytes 1572872 | tf_op jit(solution)/shard_map/ppermute | solution.py:66
  467.5 24.1 %collective-permute-start.40 = (f32[2,128,1024]{2,1,0:T(8,128)S(1)}, f32[2,128,1024]{2,1,0:T(8,128)S(1)}, u32[]{:S(2)}, u32[]{:S(2)}) collective-permute-start(f32[2,128,1024]{2,1,0:T(8,128)S(1)} %pad_maximum_fusion.6), channel_id=1, source_target_pairs={{0,2},{1,3},{2,0},{3,1},{4,6},{5,7},{6,4},{7,5},{8,10},{9,11},{10,... | collective-permute-start | bytes 3145736 | tf_op jit(solution)/shard_map/ppermute | solution.py:66
  468.2 25.5 %collective-permute-start.39 = (f32[2,128,1024]{2,1,0:T(8,128)S(1)}, f32[2,128,1024]{2,1,0:T(8,128)S(1)}, u32[]{:S(2)}, u32[]{:S(2)}) collective-permute-start(f32[2,128,1024]{2,1,0:T(8,128)S(1)} %pad_maximum_fusion.5), channel_id=1, source_target_pairs={{0,6},{1,7},{2,4},{3,5},{4,2},{5,3},{6,0},{7,1},{8,14},{9,15},{10,... | collective-permute-start | bytes 3145736 | tf_op jit(solution)/shard_map/ppermute | solution.py:66
  (33 other events, 400.5 us)
Sparse Core Ops, SparseCore 0:
  154.0 61.7 all-gather.2

commit v9 on v7

--- a/solution.py
+++ b/solution.py
@@ -32,10 +32,6 @@
     return dot1(a_high, b_high, dims) + dot1(a_high, b_low, dims) + dot1(a_low, b_high, dims)
 
 
-def line_of(device):
-    return (device & 1) * 8 + (device >> 1)
-
-
 def product_kernel(me_ref, first, second, inputs, out, high, low):
     @pl.when(pl.program_id(0) == 0)
     def _():
@@ -53,8 +49,8 @@
             num_scalar_prefetch=1,
             grid=(4,),
             in_specs=[
-                pl.BlockSpec((rows, LINE), lambda i, m: (0, line_of(m[0] ^ (4 * i + odd)))),
-                pl.BlockSpec((rows, LINE), lambda i, m: (0, line_of(m[0] ^ (4 * i + 2 + odd)))),
+                pl.BlockSpec((rows, LINE), lambda i, m: (0, m[0] ^ (4 * i + odd))),
+                pl.BlockSpec((rows, LINE), lambda i, m: (0, m[0] ^ (4 * i + 2 + odd))),
                 pl.BlockSpec((rows, acts), lambda i, m: (0, 0)),
             ],
             out_specs=pl.BlockSpec((2, LINE, acts), lambda i, m: (i, 0, 0)),
@@ -86,7 +82,7 @@
     return blocks[0] + got[0] + swap(kept, Y[far])
 
 
-def scatter_lines(even, odd):
+def scatter_lines(even, odd, wait):
     got = swap(odd, CORE)
     quarter = LINE // 4
     cut = lambda i, q: even[i, q * quarter : (q + 1) * quarter] + got[i, q * quarter : (q + 1) * quarter]
@@ -96,6 +92,7 @@
     c = [pair(m, 2) for m in range(4)]
     d = [pair(m, 3) for m in range(4)]
     c, d = y_second(1, c, y_first(1, c)), y_second(3, d, y_first(3, d))
+    came = wait(came)
     own = [half(2 * m, 0) + came[m] for m in range(4)]
     a = [o[:quarter] for o in own]
     b = [o[quarter:] for o in own]
@@ -249,13 +246,15 @@
     )(weight, gram)
 
 
-def solve_kernel(z, factor, inverses, first, first_near, first_far, second, second_near, second_far, high, low, out):
+def solve_kernel(
+    z, factor, inverses, first, first_near, first_far, second, second_near, second_far, over, under, diag, high, low, raw, out
+):
     size = PANEL
     at = lambda k: slice(k * size, (k + 1) * size)
 
     def put(step, x_high, value):
         line = (z[0] ^ step) * 2 + x_high
-        out[pl.ds(pl.multiple_of(line * LINE, LINE), LINE), :] = value
+        raw[pl.ds(pl.multiple_of(line * LINE, LINE), LINE), :] = value
 
     put(0, 0, first[...])
     put(1, 0, first_near[...])
@@ -265,6 +264,11 @@
     put(3, 1, second_near[...])
     put(1, 1, second_far[0])
     put(2, 1, second_far[1])
+    for a in range(8):
+        line = lambda k: slice((a + k) * LINE, (a + k + 1) * LINE)
+        before = raw[line(-1), :] if a > 0 else over[...]
+        after = raw[line(1), :] if a < 7 else under[...]
+        out[line(0), :] = plant_line(before, raw[line(0), :], after, diag[line(0), :1])
     for k in range(4):
         solved = split(out[:, at(k)])
         for i in range(k + 1, 4):
@@ -283,46 +287,50 @@
     return pl.pallas_call(
         solve_kernel,
         out_shape=[jax.ShapeDtypeStruct((size, 4 * PANEL), BF16)] * 2,
-        in_specs=[scalar] + [array] * 8,
+        in_specs=[scalar] + [array] * 11,
         out_specs=[array, array],
-        scratch_shapes=[pltpu.VMEM((size, 4 * PANEL), F32)],
+        scratch_shapes=[pltpu.VMEM((size, 4 * PANEL), F32)] * 2,
         compiler_params=pltpu.CompilerParams(vmem_limit_bytes=VMEM_LIMIT),
         cost_estimate=pl.CostEstimate(flops=9 << 30, bytes_accessed=12 << 20, transcendentals=0),
     )(z, *factors, *sides)
 
 
-def downdate_kernel(high, low, first, second, base, out):
-    lines = split(jnp.concatenate([first[0], second[0]], 0))
+def downdate_kernel(high, low, before, first, second, after, over, under, diag, base, out):
+    b = pl.program_id(0)
+    before = jnp.where(b == 0, over[...], before[0])
+    after = jnp.where(b == pl.num_programs(0) - 1, under[...], after[0])
+    first, second = first[0], second[0]
+    upper = plant_line(before, first, second, diag[0][:, :1])
+    lower = plant_line(first, second, after, diag[1][:, :1])
+    lines = split(jnp.concatenate([upper, lower], 0))
     out[...] = base[...] - dot3((high[...], low[...]), lines, NT)
 
 
-def downdate(solved, gain_cols, base):
+def downdate(solved, lines, over, under, diag, base):
     rows, acts = solved[0].shape
-    whole = pl.BlockSpec((rows, acts), lambda b: (0, 0))
-    line = lambda b: (b % 8) * 2 + b // 8
+    last = lines.shape[0] - 1
+    whole = lambda x: pl.BlockSpec(x.shape, lambda b: (0, 0))
     block = pl.BlockSpec((rows, 2 * LINE), lambda b: (0, b))
+    line = lambda k: pl.BlockSpec((1, LINE, acts), lambda b: (jnp.clip(2 * b + k, 0, last), 0, 0))
     return pl.pallas_call(
         downdate_kernel,
         grid=(8,),
-        in_specs=[
-            whole,
-            whole,
-            pl.BlockSpec((1, LINE, acts), lambda b: (line(2 * b), 0, 0)),
-            pl.BlockSpec((1, LINE, acts), lambda b: (line(2 * b + 1), 0, 0)),
-            block,
-        ],
+        in_specs=[whole(solved[0]), whole(solved[1])]
+        + [line(k) for k in (-1, 0, 1, 2)]
+        + [whole(over), whole(under), pl.BlockSpec((2, LINE, LINE), lambda b: (b, 0, 0)), block],
         out_specs=block,
         out_shape=jax.ShapeDtypeStruct(base.shape, F32),
         compiler_params=pltpu.CompilerParams(vmem_limit_bytes=VMEM_LIMIT),
         cost_estimate=pl.CostEstimate(flops=12 << 30, bytes_accessed=28 << 20, transcendentals=0),
-    )(*solved, gain_cols, gain_cols, base)
-
-
-def stencil_first(field, diagonal):
-    centre = field[1:-1]
-    side_padded = jnp.pad(centre, ((0, 0), (1, 1), (0, 0)))
-    neighbours = field[:-2] + field[2:] + side_padded[:, :-2] + side_padded[:, 2:]
-    return diagonal[:, :, None] * centre + COUPLING * neighbours
+    )(*solved, lines, lines, lines, lines, over, under, diag, base)
+
+
+def plant_line(before, here, after, diagonal):
+    inner = lax.broadcasted_iota(jnp.int32, (LINE, 1), 0)
+    sides = jnp.where(inner == 0, 0.0, pltpu.roll(here, 1, 0)) + jnp.where(
+        inner == LINE - 1, 0.0, pltpu.roll(here, LINE - 1, 0)
+    )
+    return diagonal * here + COUPLING * (before + after + sides)
 
 
 def plant_kernel(start, sizes, place, *refs):
@@ -420,7 +428,7 @@
     diag_rows = lax.dynamic_slice_in_dim(plant_diag, row_index * lines_rows, lines_rows, 0)
     diag_cols = lax.dynamic_slice_in_dim(plant_diag, col_index * lines_cols, lines_cols, 0)
     me = row_index.astype(jnp.int32).reshape(1)
-    trade = [((a * 2 + core) * 8 + b, (b * 2 + core) * 8 + a) for a in range(8) for b in range(8) for core in range(2)]
+    trade = [(r * 8 + c, (2 * c + r // 8) * 8 + r % 8) for r in range(16) for c in range(8)]
 
     def shifted(x, axis, by):
         count = lax.axis_size(axis)
@@ -437,16 +445,24 @@
     )
     odd = product_lines(me, value_matrix, inputs, 1)
     even = product_lines(me, value_matrix, inputs, 0)
+    rows = []
+
+    def wait(came):
+        came, *rows[:] = tied(came, above, below)
+        return came
+
+    product = scatter_lines(even, odd, wait)
+    above, below = rows
     tall = lambda cols: jnp.concatenate([above[:, cols], value_matrix[:, cols], below[:, cols]], 0)
     left = shifted(tall(slice(-LINE, None)), "col", 1)
     right = shifted(tall(slice(None, LINE)), "col", -1)
-    product = scatter_lines(even, odd)
 
     core, x_low, y = row_index & 1, (row_index >> 1) & 1, row_index >> 2
     x_high, z = col_index & 1, col_index >> 1
     x_place = x_high * 2 + x_low
 
-    product, above, below, left, right = tied(product, above, below, left, right)
+    product, above, below = tied(product, above, below)
+    lines = lax.all_gather(product, "row", axis=0)
     product = lax.ppermute(product, both, trade)
     around = (*operands[:2], above, below, left, right, *operands[2:])
     base = None
@@ -454,41 +470,38 @@
         base = plant_part(start, count, *around, base)
     product, base = tied(product, base)
 
-    count = grid_side
-    over = lax.ppermute(product, both, [(i, i + 1) for i in range(count - 1)])
-    under = lax.ppermute(product, both, [(i + 1, i) for i in range(count - 1)])
     mine_inputs = lax.dynamic_slice_in_dim(inputs, col_index * LINE, LINE, 0)
+    pair = joined(product, swap(product, X_HIGH), x_high == 1)
     gram = gram_blocks(mine_inputs, product)
     total = sum_cores(gram.reshape(10 * PANEL, PANEL), core)
-    over, under, total = tied(over, under, total)
-    diagonal = lax.dynamic_slice_in_dim(plant_diag, row_index * 8 + col_index, 1, 0)
-    gain = stencil_first(jnp.stack([over, product, under]), diagonal)[0]
-    gain, total = tied(gain, total)
-
-    pair = joined(gain, swap(gain, X_HIGH), x_high == 1)
-    total = scatter_four(total, z, Z)
     pair, total = tied(pair, total)
 
-    back = lax.ppermute(gain, both, trade)
     first, second = pair[:LINE], pair[LINE:]
     first_near, second_near = swap(first, Z[1]), swap(second, Z[3])
-    total = scatter_four(total, x_place, X)
+    total = scatter_four(total, z, Z)
     first_near, second_near, total = tied(first_near, second_near, total)
 
     first_far = swap(jnp.stack([first, first_near]), Z[3])
     second_far = swap(jnp.stack([second, second_near]), Z[1])
+    total = scatter_four(total, x_place, X)
     total = total + swap(total, Y[1]) + swap(total, Y[2]) + swap(total, Y[3])
-    back, total = tied(back, total)
-    gain_cols = lax.all_gather(back, "row", axis=0)
     total = gather_four(total, x_place, X)
-    first_far, second_far, total = tied(first_far, second_far, total)
+    first_far, second_far, total, lines = tied(first_far, second_far, total, lines)
+
+    pick = lambda k, x: jnp.where(k < 2, jnp.where(k == 0, x[0], x[1]), jnp.where(k == 2, x[2], x[3]))
+    head = pick(z, (first, first_near, first_far[1], first_far[0]))
+    tail = pick(z ^ 3, (second, second_far[0], second_far[1], second_near))
+    row_over, row_under = shifted(tail, "row", 1), shifted(head, "row", -1)
+    col_over, col_under = shifted(lines[-1], "col", 1), shifted(lines[0], "col", -1)
     total = gather_four(total, z, Z)
+    row_over, row_under, col_over, col_under, total = tied(row_over, row_under, col_over, col_under, total)
+
     total = joined(total, swap(total, CORE), core == 1)
-
     factors = factored(control_weight, total.reshape(10, PANEL, PANEL))
-    sides = (first, first_near, first_far, second, second_near, second_far)
+    sides = (first, first_near, first_far, second, second_near, second_far, row_over, row_under, operands[2])
     solved = solve(z.astype(jnp.int32).reshape(1), factors, sides)
-    return downdate(solved, gain_cols, base)
+    wide_diag = jnp.broadcast_to(diag_cols[:, :, None], (lines_cols, LINE, LINE))
+    return downdate(solved, lines, col_over, col_under, wide_diag, base)
 
 
 def solution(mesh):

time: 524 us -> 538 us (1.027)
  the two profiles are of different devices: /device:TPU:7 before, /device:TPU:9 now
where the time goes in v9:
time: 538 us; the launch traced here: 530 us
  Pallas kernels  264 us (49%)
  starting transfers between devices  108 us (20%)
  waiting for transfers between devices  107 us (20%)
  other arithmetic  20.7 us (4%)
  local copies, waits for them, and re-layouts  15.2 us (3%)
  between operations  15.1 us (3%)
    pallas_call x1, Pallas kernels, factored(): pl.pallas_call(factor_kernel, out_shape=[jax.ShapeDtypeStruct((10, PANEL,...  176 us
    ppermute x33, waiting for transfers between devices, swap(): return lax.ppermute(x, ('row', 'col'), [(i, i ^ mask) for i in range(128)])  81.6 us
    ppermute x33, starting transfers between devices, swap(): return lax.ppermute(x, ('row', 'col'), [(i, i ^ mask) for i in range(128)])  65.4 us
    ppermute x8, starting transfers between devices, shifted(): lax.ppermute(x, axis, [(i, i + by) for i in range(count) if 0 <= i + by <...  27 us
    ppermute x8, waiting for transfers between devices, shifted(): lax.ppermute(x, axis, [(i, i + by) for i in range(count) if 0 <= i + by <...  25.1 us
    pallas_call x4, Pallas kernels, plant_part(): pl.pallas_call(functools.partial(plant_kernel, start, [len(blocks) for bl...  24.8 us
    pallas_call x2, Pallas kernels, product_lines(): pl.pallas_call(product_kernel, grid_spec=pltpu.PrefetchScalarGridSpec(num...  23.3 us
    pallas_call x1, Pallas kernels, downdate(): pl.pallas_call(downdate_kernel, grid=(8,), in_specs=[whole(solved[0]), wh...  22.8 us
  transfers between devices with their start and end apart: 43, of which 23 were waited for; matrix products, arithmetic and copies ran while one was open for 6% of the time, Pallas kernels for 8%

profile of v9, /device:TPU:9, one launch (start us, length us, event | category | flops | bytes accessed | tf_op | source)
XLA Modules:
  0.0 530.0 jit_solution(752518497805365367)
XLA Ops:
  6.5 11.7 %shard_map.56 = f32[8,128,1024]{2,1,0:T(8,128)} custom-call(s32[1]{0:T(128)} %bitcast.1.me_ref, f32[1024,2048]{1,0:T(8,128)} %refs_4_.5, f32[1024,2048]{1,0:T(8,128)} %refs_4_.5, f32[1024,1024]{1,0:T(8,128)} %inputs.3), custom_call_target="tpu_custom_call" | custom-call | flops 1048576 | bytes 1048576 | tf_op jit(solution)/shard_map/pallas_call | solution.py:46
  18.9 2.7 fusion.31
  21.6 3.0 collective-permute-start.2
  24.6 1.9 collective-permute-start.3
  26.5 11.7 %shard_map.55 = f32[8,128,1024]{2,1,0:T(8,128)} custom-call(s32[1]{0:T(128)} %bitcast.1.me_ref, f32[1024,2048]{1,0:T(8,128)} %refs_4_.5, f32[1024,2048]{1,0:T(8,128)} %refs_4_.5, f32[1024,1024]{1,0:T(8,128)} %inputs.3), custom_call_target="tpu_custom_call" | custom-call | flops 1048576 | bytes 1048576 | tf_op jit(solution)/shard_map/pallas_call | solution.py:46
  44.0 2.2 collective-permute-start.10
  46.2 10.1 %collective-permute-done.8 = f32[2,2,32,1024]{3,2,1,0:T(8,128)S(1)} collective-permute-done((f32[2,2,32,1024]{3,2,1,0:T(8,128)S(1)}, f32[2,2,32,1024]{3,2,1,0:T(8,128)S(1)}, u32[]{:S(2)}, u32[]{:S(2)}) %collective-permute-start.8) | collective-permute-done | bytes 524320 | tf_op jit(solution)/shard_map/ppermute | solution.py:66
  56.8 2.3 collective-permute-start.11
  59.1 3.1 collective-permute-done.9
  62.3 7.4 %collective-permute-done.1 = f32[4,64,1024]{2,1,0:T(8,128)S(1)} collective-permute-done((f32[4,64,1024]{2,1,0:T(8,128)S(1)}, f32[4,64,1024]{2,1,0:T(8,128)S(1)}, u32[]{:S(2)}, u32[]{:S(2)}) %collective-permute-start.1) | collective-permute-done | bytes 1048608 | tf_op jit(solution)/shard_map/ppermute | solution.py:66
  70.3 5.0 collective-permute-done.4
  77.1 3.5 collective-permute-done.6
  82.1 2.7 collective-permute-done.7
  87.1 5.9 %collective-permute-start.15 = (f32[1280,128]{1,0:T(8,128)S(1)}, f32[1280,128]{1,0:T(8,128)}, u32[]{:S(2)}, u32[]{:S(2)}) collective-permute-start(f32[1280,128]{1,0:T(8,128)S(1)} %pad_maximum_fusion.8), channel_id=1, source_target_pairs={{0,1},{1,2},{2,3},{3,4},{4,5},{5,6},{6,7},{8,9},{9,10},{10,11},{11... | collective-permute-start | bytes 1966088 | tf_op jit(solution)/shard_map/ppermute | solution.py:435
  94.4 15.5 %collective-permute-start.13 = (f32[128,1024]{1,0:T(8,128)S(1)}, f32[128,1024]{1,0:T(8,128)S(1)}, u32[]{:S(2)}, u32[]{:S(2)}) collective-permute-start(f32[128,1024]{1,0:T(8,128)S(1)} %copy-done.8), channel_id=1, source_target_pairs={{0,0},{1,16},{2,32},{3,48},{4,64},{5,80},{6,96},{7,112},{8,1},{9,1... | collective-permute-start | bytes 1572872 | tf_op jit(solution)/shard_map/ppermute | solution.py:466
  114.0 9.2 %shard_map.57.refs_12_ = f32[1024,2048]{1,0:T(8,128)} custom-call(s32[2]{0:T(128)} %pad_add_fusion.place, f32[128,2048]{1,0:T(8,128)} %copy-done.2, f32[1024,2048]{1,0:T(8,128)} %refs_4_.5, f32[128,2048]{1,0:T(8,128)} %copy-done.3, f32[128,2048]{1,0:T(8,128)} %copy-done.2, f32[1024,2048]{1,0:T(8,128)} %refs_4_.5, f32[128,2048]{1,0:T(8,128)} %copy-done.3, ...), custom_call_target="tpu_custom_call" | custom-call | flops 33554432 | bytes 16777216 | tf_op jit(solution)/shard_map/pallas_call | solution.py:406
  123.3 9.2 %shard_map.58.refs_10_ = f32[1024,2048]{1,0:T(8,128)} custom-call(s32[2]{0:T(128)} %pad_add_fusion.place, f32[128,2048]{1,0:T(8,128)} %copy-done.2, f32[1024,2048]{1,0:T(8,128)} %refs_4_.5, f32[128,2048]{1,0:T(8,128)} %copy-done.3, f32[128,2048]{1,0:T(8,128)} %copy-done.2, f32[1024,2048]{1,0:T(8,128)} %refs_4_.5, ...), custom_call_target="tpu_custom_call", output_to_operand_aliasing={{}: (13, {})} | custom-call | flops 33554432 | bytes 16777216 | tf_op jit(solution)/shard_map/pallas_call | solution.py:406
  132.5 3.2 shard_map.59.refs_10_
  135.7 3.1 shard_map.60.base
  139.6 3.9 shard_map.61
  143.5 3.2 slice_select_fusion.1
  146.7 17.7 %collective-permute-start.16 = (f32[128,1024]{1,0:T(8,128)S(1)}, f32[128,1024]{1,0:T(8,128)S(1)}, u32[]{:S(2)}, u32[]{:S(2)}) collective-permute-start(f32[128,1024]{1,0:T(8,128)S(1)} %copy-done.7), channel_id=1, source_target_pairs={{0,1},{1,0},{2,3},{3,2},{4,5},{5,4},{6,7},{7,6},{8,9},{9,8},{10,11... | collective-permute-start | bytes 1572872 | tf_op jit(solution)/shard_map/ppermute | solution.py:66
  164.4 12.3 %collective-permute-done.16 = f32[128,1024]{1,0:T(8,128)S(1)} collective-permute-done((f32[128,1024]{1,0:T(8,128)S(1)}, f32[128,1024]{1,0:T(8,128)S(1)}, u32[]{:S(2)}, u32[]{:S(2)}) %collective-permute-start.16) | collective-permute-done | bytes 524320 | tf_op jit(solution)/shard_map/ppermute | solution.py:66
  180.5 10.9 %collective-permute-start.20 = (f32[320,256]{1,0:T(8,128)}, f32[320,256]{1,0:T(8,128)}, u32[]{:S(2)}, u32[]{:S(2)}) collective-permute-start(f32[320,256]{1,0:T(8,128)} %get-tuple-element.103), channel_id=1, source_target_pairs={{0,2},{1,3},{2,0},{3,1},{4,6},{5,7},{6,4},{7,5},{8,10},{9,11},{10,... | collective-permute-start | bytes 983048 | tf_op jit(solution)/shard_map/ppermute | solution.py:66
  191.4 2.0 collective-permute-start.21
  195.3 2.0 collective-permute-start.19
  199.1 8.1 %collective-permute-done.21 = f32[320,256]{1,0:T(8,128)} collective-permute-done((f32[320,256]{1,0:T(8,128)}, f32[320,256]{1,0:T(8,128)}, u32[]{:S(2)}, u32[]{:S(2)}) %collective-permute-start.21) | collective-permute-done | bytes 327712 | tf_op jit(solution)/shard_map/ppermute | solution.py:66
  208.8 8.5 %collective-permute-done.18.first_near = f32[128,1024]{1,0:T(8,128)} collective-permute-done((f32[128,1024]{1,0:T(8,128)}, f32[128,1024]{1,0:T(8,128)}, u32[]{:S(2)}, u32[]{:S(2)}) %collective-permute-start.18) | collective-permute-done | bytes 524320 | tf_op jit(solution)/shard_map/ppermute | solution.py:66
  217.4 3.1 collective-permute-done.19.second_near
  220.5 4.0 collective-permute-start.25
  227.0 2.1 pad_maximum_fusion.6
  229.1 2.1 pad_maximum_fusion.5
  233.5 2.5 collective-permute-start.29
  241.9 2.0 collective-permute-start.33
  246.8 3.9 collective-permute-done.24.second_far
  250.7 3.2 collective-permute-done.23.first_far
  254.0 3.6 collective-permute-start.39
  259.6 7.1 %collective-permute-start.34 = (f32[128,1024]{1,0:T(8,128)S(1)}, f32[128,1024]{1,0:T(8,128)S(1)}, u32[]{:S(2)}, u32[]{:S(2)}) collective-permute-start(f32[128,1024]{1,0:T(8,128)S(1)} %get-tuple-element.107), channel_id=1, source_target_pairs={{0,8},{8,16},{16,24},{24,32},{32,40},{40,48},{48,56},{56,64},{64,7... | collective-permute-start | bytes 1572872 | tf_op jit(solution)/shard_map/ppermute | solution.py:435
  266.7 1.9 collective-permute-start.35
  269.9 4.4 collective-permute-start.36
  276.2 6.7 %collective-permute-done.35.under = f32[128,1024]{1,0:T(8,128)S(1)} collective-permute-done((f32[128,1024]{1,0:T(8,128)S(1)}, f32[128,1024]{1,0:T(8,128)S(1)}, u32[]{:S(2)}, u32[]{:S(2)}) %collective-permute-start.35) | collective-permute-done | bytes 524320 | tf_op jit(solution)/shard_map/ppermute | solution.py:435
  282.9 3.2 collective-permute-done.36.over
  286.1 15.2 %collective-permute-done.37.under = f32[128,1024]{1,0:T(8,128)S(1)} collective-permute-done((f32[128,1024]{1,0:T(8,128)S(1)}, f32[128,1024]{1,0:T(8,128)S(1)}, u32[]{:S(2)}, u32[]{:S(2)}) %collective-permute-start.37) | collective-permute-done | bytes 524320 | tf_op jit(solution)/shard_map/ppermute | solution.py:435
  301.3 3.2 collective-permute-start.41
  305.1 2.0 collective-permute-done.41
  309.0 176.4 %shard_map.62 = (f32[10,256,256]{2,1,0:T(8,128)}, f32[4,256,256]{2,1,0:T(8,128)}) custom-call(f32[1]{0:T(128)S(6)} %copy.12.weight, f32[10,256,256]{2,1,0:T(8,128)} %bitcast.173), custom_call_target="tpu_custom_call" | custom-call | flops 9663676416 | bytes 12582912 | tf_op jit(solution)/shard_map/pallas_call | solution.py:235
  485.5 13.1 %shard_map.63 = (bf16[1024,1024]{1,0:T(8,128)(2,1)}, bf16[1024,1024]{1,0:T(8,128)(2,1)}) custom-call(s32[1]{0:T(128)} %bitcast.z, f32[10,256,256]{2,1,0:T(8,128)} %get-tuple-element.48.factor, f32[4,256,256]{2,1,0:T(8,128)} %get-tuple-element.49.inverses, f32[128,1024]{1,0:T(8,128)} %get-tuple-element.110.first, ...), custom_call_target="tpu_custom_call" | custom-call | flops 9663676416 | bytes 12582912 | tf_op jit(solution)/shard_map/pallas_call | solution.py:287
  499.9 22.8 %shard_map.64 = f32[1024,2048]{1,0:T(8,128)} custom-call(bf16[1024,1024]{1,0:T(8,128)(2,1)} %get-tuple-element.52.high, bf16[1024,1024]{1,0:T(8,128)(2,1)} %get-tuple-element.53.low, f32[16,128,1024]{2,1,0:T(8,128)} %bitcast.169, f32[16,128,1024]{2,1,0:T(8,128)} %bitcast.170, f32[16,128,1024]{2,1,0:T(8,128)} %bitcast.171, f32[16,128,1024]{2,1,0:T(8,128)} %bitcast.172, ...), custom_call_target="tpu_custom_call" | custom-call | flops 12884901888 | bytes 29360128 | tf_op jit(solution)/shard_map/pallas_call | solution.py:315
  (143 shorter events, 50.3 us)
Async XLA Ops:
  6.5 104.0 %copy-start = (f32[128,128]{1,0:T(8,128)S(1)}, f32[128,128]{1,0:T(8,128)}, u32[]{:S(2)}) copy-start(f32[128,128]{1,0:T(8,128)} %param.7) | copy-start | bytes 196612
  6.5 247.4 %all-gather.3.cloned.1.call-start = ((), (), s32[]{:S(2)}) async-start(), calls=%async_computation | async-start | bytes 8912896 | tf_op jit(solution)/shard_map/all_gather | solution.py:465
  18.2 20.0 %collective-permute-start = (f32[8,128,1024]{2,1,0:T(8,128)}, f32[8,128,1024]{2,1,0:T(8,128)S(1)}, u32[]{:S(2)}, u32[]{:S(2)}) collective-permute-start(f32[8,128,1024]{2,1,0:T(8,128)} %shard_map.56), channel_id=1, source_target_pairs={{0,8},{1,9},{2,10},{3,11},{4,12},{5,13},{6,14},{7,15},{8,0},{9,1},... | collective-permute-start | bytes 12582920 | tf_op jit(solution)/shard_map/ppermute | solution.py:66
  21.6 40.6 %collective-permute-start.2 = (f32[128,2048]{1,0:T(8,128)}, f32[128,2048]{1,0:T(8,128)S(1)}, u32[]{:S(2)}, u32[]{:S(2)}) collective-permute-start(f32[128,2048]{1,0:T(8,128)} %get-tuple-element.89), channel_id=1, source_target_pairs={{0,8},{8,16},{16,24},{24,32},{32,40},{40,48},{48,56},{56,64},{64,7... | collective-permute-start | bytes 3145736 | tf_op jit(solution)/shard_map/ppermute | solution.py:435
  24.6 37.7 %collective-permute-start.3 = (f32[128,2048]{1,0:T(8,128)S(1)}, f32[128,2048]{1,0:T(8,128)S(1)}, u32[]{:S(2)}, u32[]{:S(2)}) collective-permute-start(f32[128,2048]{1,0:T(8,128)S(1)} %get-tuple-element.88), channel_id=1, source_target_pairs={{8,0},{16,8},{24,16},{32,24},{40,32},{48,40},{56,48},{64,56},{72,6... | collective-permute-start | bytes 3145736 | tf_op jit(solution)/shard_map/ppermute | solution.py:435
  41.2 28.5 %collective-permute-start.1 = (f32[4,64,1024]{2,1,0:T(8,128)S(1)}, f32[4,64,1024]{2,1,0:T(8,128)S(1)}, u32[]{:S(2)}, u32[]{:S(2)}) collective-permute-start(f32[4,64,1024]{2,1,0:T(8,128)S(1)} %pad_maximum_fusion.3), channel_id=1, source_target_pairs={{0,16},{1,17},{2,18},{3,19},{4,20},{5,21},{6,22},{7,23},{8,24},{9,... | collective-permute-start | bytes 3145736 | tf_op jit(solution)/shard_map/ppermute | solution.py:66
  43.4 12.8 %collective-permute-start.8 = (f32[2,2,32,1024]{3,2,1,0:T(8,128)S(1)}, f32[2,2,32,1024]{3,2,1,0:T(8,128)S(1)}, u32[]{:S(2)}, u32[]{:S(2)}) collective-permute-start(f32[2,2,32,1024]{3,2,1,0:T(8,128)S(1)} %pad_maximum_fusion.9), channel_id=1, source_target_pairs={{0,32},{1,33},{2,34},{3,35},{4,36},{5,37},{6,38},{7,39},{8,40},{9,... | collective-permute-start | bytes 1572872 | tf_op jit(solution)/shard_map/ppermute | solution.py:66
  44.0 12.8 %collective-permute-start.10 = (f32[2,2,32,1024]{3,2,1,0:T(8,128)S(1)}, f32[2,2,32,1024]{3,2,1,0:T(8,128)S(1)}, u32[]{:S(2)}, u32[]{:S(2)}) collective-permute-start(f32[2,2,32,1024]{3,2,1,0:T(8,128)S(1)} %pad_maximum_fusion.10), channel_id=1, source_target_pairs={{0,96},{1,97},{2,98},{3,99},{4,100},{5,101},{6,102},{7,103},{8,104... | collective-permute-start | bytes 1572872 | tf_op jit(solution)/shard_map/ppermute | solution.py:66
  56.3 5.9 %collective-permute-start.9 = (f32[2,32,1024]{2,1,0:T(8,128)S(1)}, f32[2,32,1024]{2,1,0:T(8,128)S(1)}, u32[]{:S(2)}, u32[]{:S(2)}) collective-permute-start(f32[2,32,1024]{2,1,0:T(8,128)S(1)} %fusion.4), channel_id=1, source_target_pairs={{0,96},{1,97},{2,98},{3,99},{4,100},{5,101},{6,102},{7,103},{8,104... | collective-permute-start | bytes 786440 | tf_op jit(solution)/shard_map/ppermute | solution.py:66
  56.8 13.4 %collective-permute-start.11 = (f32[2,32,1024]{2,1,0:T(8,128)S(1)}, f32[2,32,1024]{2,1,0:T(8,128)S(1)}, u32[]{:S(2)}, u32[]{:S(2)}) collective-permute-start(f32[2,32,1024]{2,1,0:T(8,128)S(1)} %fusion.1), channel_id=1, source_target_pairs={{0,32},{1,33},{2,34},{3,35},{4,36},{5,37},{6,38},{7,39},{8,40},{9,... | collective-permute-start | bytes 786440 | tf_op jit(solution)/shard_map/ppermute | solution.py:66
  62.2 24.8 %copy-start.2 = (f32[128,2048]{1,0:T(8,128)}, f32[128,2048]{1,0:T(8,128)S(1)}, u32[]{:S(2)}) copy-start(f32[128,2048]{1,0:T(8,128)S(1)} %collective-permute-done.2.refs_0_.refs_3_.refs_6_.refs_1_.refs_4_) | copy-start | bytes 3145732
  62.2 24.8 %copy-start.3 = (f32[128,2048]{1,0:T(8,128)}, f32[128,2048]{1,0:T(8,128)S(1)}, u32[]{:S(2)}) copy-start(f32[128,2048]{1,0:T(8,128)S(1)} %collective-permute-done.3.refs_2_.refs_5_.refs_8_.refs_3_.refs_6_) | copy-start | bytes 3145732
  69.9 5.3 %collective-permute-start.4 = (f32[2,32,1024]{2,1,0:T(8,128)S(1)}, f32[2,32,1024]{2,1,0:T(8,128)S(1)}, u32[]{:S(2)}, u32[]{:S(2)}) collective-permute-start(f32[2,32,1024]{2,1,0:T(8,128)S(1)} %pad_maximum_fusion.14), channel_id=1, source_target_pairs={{0,32},{1,33},{2,34},{3,35},{4,36},{5,37},{6,38},{7,39},{8,40},{9,... | collective-permute-start | bytes 786440 | tf_op jit(solution)/shard_map/ppermute | solution.py:66
  75.3 5.3 %collective-permute-start.6 = (f32[2,32,1024]{2,1,0:T(8,128)S(1)}, f32[2,32,1024]{2,1,0:T(8,128)S(1)}, u32[]{:S(2)}, u32[]{:S(2)}) collective-permute-start(f32[2,32,1024]{2,1,0:T(8,128)S(1)} %pad_maximum_fusion.15), channel_id=1, source_target_pairs={{0,96},{1,97},{2,98},{3,99},{4,100},{5,101},{6,102},{7,103},{8,104... | collective-permute-start | bytes 786440 | tf_op jit(solution)/shard_map/ppermute | solution.py:66
  76.1 6.0 %collective-permute-start.12 = (f32[64,1024]{1,0:T(8,128)S(1)}, f32[64,1024]{1,0:T(8,128)S(1)}, u32[]{:S(2)}, u32[]{:S(2)}) collective-permute-start(f32[64,1024]{1,0:T(8,128)S(1)} %pad_maximum_fusion.16), channel_id=1, source_target_pairs={{0,16},{1,17},{2,18},{3,19},{4,20},{5,21},{6,22},{7,23},{8,24},{9,... | collective-permute-start | bytes 786440 | tf_op jit(solution)/shard_map/ppermute | solution.py:66
  76.2 5.9 %collective-permute-start.5 = (f32[32,1024]{1,0:T(8,128)S(1)}, f32[32,1024]{1,0:T(8,128)S(1)}, u32[]{:S(2)}, u32[]{:S(2)}) collective-permute-start(f32[32,1024]{1,0:T(8,128)S(1)} %get-tuple-element.131), channel_id=1, source_target_pairs={{0,96},{1,97},{2,98},{3,99},{4,100},{5,101},{6,102},{7,103},{8,104... | collective-permute-start | bytes 393224 | tf_op jit(solution)/shard_map/ppermute | solution.py:66
  80.6 4.2 collective-permute-start.7
  87.1 45.4 %collective-permute-start.15 = (f32[1280,128]{1,0:T(8,128)S(1)}, f32[1280,128]{1,0:T(8,128)}, u32[]{:S(2)}, u32[]{:S(2)}) collective-permute-start(f32[1280,128]{1,0:T(8,128)S(1)} %pad_maximum_fusion.8), channel_id=1, source_target_pairs={{0,1},{1,2},{2,3},{3,4},{4,5},{5,6},{6,7},{8,9},{9,10},{10,11},{11... | collective-permute-start | bytes 1966088 | tf_op jit(solution)/shard_map/ppermute | solution.py:435
  93.1 42.6 %collective-permute-start.14 = (f32[1280,128]{1,0:T(8,128)S(1)}, f32[1280,128]{1,0:T(8,128)}, u32[]{:S(2)}, u32[]{:S(2)}) collective-permute-start(f32[1280,128]{1,0:T(8,128)S(1)} %pad_maximum_fusion.7), channel_id=1, source_target_pairs={{1,0},{2,1},{3,2},{4,3},{5,4},{6,5},{7,6},{9,8},{10,9},{11,10},{12... | collective-permute-start | bytes 1966088 | tf_op jit(solution)/shard_map/ppermute | solution.py:435
  94.4 44.5 %collective-permute-start.13 = (f32[128,1024]{1,0:T(8,128)S(1)}, f32[128,1024]{1,0:T(8,128)S(1)}, u32[]{:S(2)}, u32[]{:S(2)}) collective-permute-start(f32[128,1024]{1,0:T(8,128)S(1)} %copy-done.8), channel_id=1, source_target_pairs={{0,0},{1,16},{2,32},{3,48},{4,64},{5,80},{6,96},{7,112},{8,1},{9,1... | collective-permute-start | bytes 1572872 | tf_op jit(solution)/shard_map/ppermute | solution.py:466
  146.7 30.2 %collective-permute-start.17 = (f32[1280,256]{1,0:T(8,128)S(1)}, f32[1280,256]{1,0:T(8,128)}, u32[]{:S(2)}, u32[]{:S(2)}) collective-permute-start(f32[1280,256]{1,0:T(8,128)S(1)} %bitcast.175), channel_id=1, source_target_pairs={{0,8},{1,9},{2,10},{3,11},{4,12},{5,13},{6,14},{7,15},{8,0},{9,1},... | collective-permute-start | bytes 3932168 | tf_op jit(solution)/shard_map/ppermute | solution.py:66
  146.7 30.0 %collective-permute-start.16 = (f32[128,1024]{1,0:T(8,128)S(1)}, f32[128,1024]{1,0:T(8,128)S(1)}, u32[]{:S(2)}, u32[]{:S(2)}) collective-permute-start(f32[128,1024]{1,0:T(8,128)S(1)} %copy-done.7), channel_id=1, source_target_pairs={{0,1},{1,0},{2,3},{3,2},{4,5},{5,4},{6,7},{7,6},{8,9},{9,8},{10,11... | collective-permute-start | bytes 1572872 | tf_op jit(solution)/shard_map/ppermute | solution.py:66
  180.5 18.5 %collective-permute-start.20 = (f32[320,256]{1,0:T(8,128)}, f32[320,256]{1,0:T(8,128)}, u32[]{:S(2)}, u32[]{:S(2)}) collective-permute-start(f32[320,256]{1,0:T(8,128)} %get-tuple-element.103), channel_id=1, source_target_pairs={{0,2},{1,3},{2,0},{3,1},{4,6},{5,7},{6,4},{7,5},{8,10},{9,11},{10,... | collective-permute-start | bytes 983048 | tf_op jit(solution)/shard_map/ppermute | solution.py:66
  191.4 15.7 %collective-permute-start.21 = (f32[320,256]{1,0:T(8,128)}, f32[320,256]{1,0:T(8,128)}, u32[]{:S(2)}, u32[]{:S(2)}) collective-permute-start(f32[320,256]{1,0:T(8,128)} %get-tuple-element.105), channel_id=1, source_target_pairs={{0,4},{1,5},{2,6},{3,7},{4,0},{5,1},{6,2},{7,3},{8,12},{9,13},{10,... | collective-permute-start | bytes 983048 | tf_op jit(solution)/shard_map/ppermute | solution.py:66
  193.4 14.1 %collective-permute-start.22 = (f32[320,256]{1,0:T(8,128)}, f32[320,256]{1,0:T(8,128)}, u32[]{:S(2)}, u32[]{:S(2)}) collective-permute-start(f32[320,256]{1,0:T(8,128)} %get-tuple-element.104), channel_id=1, source_target_pairs={{0,6},{1,7},{2,4},{3,5},{4,2},{5,3},{6,0},{7,1},{8,14},{9,15},{10,... | collective-permute-start | bytes 983048 | tf_op jit(solution)/shard_map/ppermute | solution.py:66
  195.1 22.3 %collective-permute-start.18 = (f32[128,1024]{1,0:T(8,128)}, f32[128,1024]{1,0:T(8,128)}, u32[]{:S(2)}, u32[]{:S(2)}) collective-permute-start(f32[128,1024]{1,0:T(8,128)} %get-tuple-element.110.first), channel_id=1, source_target_pairs={{0,2},{1,3},{2,0},{3,1},{4,6},{5,7},{6,4},{7,5},{8,10},{9,11},{10,... | collective-permute-start | bytes 1572872 | tf_op jit(solution)/shard_map/ppermute | solution.py:66
  195.3 25.2 %collective-permute-start.19 = (f32[128,1024]{1,0:T(8,128)}, f32[128,1024]{1,0:T(8,128)}, u32[]{:S(2)}, u32[]{:S(2)}) collective-permute-start(f32[128,1024]{1,0:T(8,128)} %get-tuple-element.111.second), channel_id=1, source_target_pairs={{0,6},{1,7},{2,4},{3,5},{4,2},{5,3},{6,0},{7,1},{8,14},{9,15},{10,... | collective-permute-start | bytes 1572872 | tf_op jit(solution)/shard_map/ppermute | solution.py:66
  220.5 12.0 %collective-permute-start.25 = (f32[80,256]{1,0:T(8,128)S(1)}, f32[80,256]{1,0:T(8,128)S(1)}, u32[]{:S(2)}, u32[]{:S(2)}) collective-permute-start(f32[80,256]{1,0:T(8,128)S(1)} %get-tuple-element.126), channel_id=1, source_target_pairs={{0,16},{1,17},{2,18},{3,19},{4,20},{5,21},{6,22},{7,23},{8,24},{9,... | collective-permute-start | bytes 245768 | tf_op jit(solution)/shard_map/ppermute | solution.py:66
  224.5 8.0 %collective-permute-start.26 = (f32[80,256]{1,0:T(8,128)S(1)}, f32[80,256]{1,0:T(8,128)S(1)}, u32[]{:S(2)}, u32[]{:S(2)}) collective-permute-start(f32[80,256]{1,0:T(8,128)S(1)} %get-tuple-element.128), channel_id=1, source_target_pairs={{0,1},{1,0},{2,3},{3,2},{4,5},{5,4},{6,7},{7,6},{8,9},{9,8},{10,11... | collective-permute-start | bytes 245768 | tf_op jit(solution)/shard_map/ppermute | solution.py:66
  225.8 6.7 %collective-permute-start.27 = (f32[80,256]{1,0:T(8,128)S(1)}, f32[80,256]{1,0:T(8,128)}, u32[]{:S(2)}, u32[]{:S(2)}) collective-permute-start(f32[80,256]{1,0:T(8,128)S(1)} %get-tuple-element.127), channel_id=1, source_target_pairs={{0,17},{1,16},{2,19},{3,18},{4,21},{5,20},{6,23},{7,22},{8,25},{9,... | collective-permute-start | bytes 245768 | tf_op jit(solution)/shard_map/ppermute | solution.py:66
  229.1 21.6 %collective-permute-start.24 = (f32[2,128,1024]{2,1,0:T(8,128)}, f32[2,128,1024]{2,1,0:T(8,128)}, u32[]{:S(2)}, u32[]{:S(2)}) collective-permute-start(f32[2,128,1024]{2,1,0:T(8,128)} %pad_maximum_fusion.6), channel_id=1, source_target_pairs={{0,2},{1,3},{2,0},{3,1},{4,6},{5,7},{6,4},{7,5},{8,10},{9,11},{10,... | collective-permute-start | bytes 3145736 | tf_op jit(solution)/shard_map/ppermute | solution.py:66
  231.2 22.7 %collective-permute-start.23 = (f32[2,128,1024]{2,1,0:T(8,128)}, f32[2,128,1024]{2,1,0:T(8,128)S(1)}, u32[]{:S(2)}, u32[]{:S(2)}) collective-permute-start(f32[2,128,1024]{2,1,0:T(8,128)} %pad_maximum_fusion.5), channel_id=1, source_target_pairs={{0,6},{1,7},{2,4},{3,5},{4,2},{5,3},{6,0},{7,1},{8,14},{9,15},{10,... | collective-permute-start | bytes 3145736 | tf_op jit(solution)/shard_map/ppermute | solution.py:66
  233.5 3.8 collective-permute-start.28
  233.5 5.1 collective-permute-start.29
  236.0 3.9 collective-permute-start.30
  239.9 3.9 collective-permute-start.31
  240.0 4.9 collective-permute-start.32
  241.9 4.8 collective-permute-start.33
  253.9 16.0 %collective-permute-start.38 = (f32[320,256]{1,0:T(8,128)S(1)}, f32[320,256]{1,0:T(8,128)S(1)}, u32[]{:S(2)}, u32[]{:S(2)}) collective-permute-start(f32[320,256]{1,0:T(8,128)S(1)} %pad_maximum_fusion.13), channel_id=1, source_target_pairs={{0,2},{1,3},{2,0},{3,1},{4,6},{5,7},{6,4},{7,5},{8,10},{9,11},{10,... | collective-permute-start | bytes 983048 | tf_op jit(solution)/shard_map/ppermute | solution.py:66
  254.0 20.4 %collective-permute-start.39 = (f32[320,256]{1,0:T(8,128)S(1)}, f32[320,256]{1,0:T(8,128)S(1)}, u32[]{:S(2)}, u32[]{:S(2)}) collective-permute-start(f32[320,256]{1,0:T(8,128)S(1)} %pad_maximum_fusion.13), channel_id=1, source_target_pairs={{0,4},{1,5},{2,6},{3,7},{4,0},{5,1},{6,2},{7,3},{8,12},{9,13},{10,... | collective-permute-start | bytes 983048 | tf_op jit(solution)/shard_map/ppermute | solution.py:66
  257.6 18.2 %collective-permute-start.40 = (f32[320,256]{1,0:T(8,128)S(1)}, f32[320,256]{1,0:T(8,128)S(1)}, u32[]{:S(2)}, u32[]{:S(2)}) collective-permute-start(f32[320,256]{1,0:T(8,128)S(1)} %pad_maximum_fusion.13), channel_id=1, source_target_pairs={{0,6},{1,7},{2,4},{3,5},{4,2},{5,3},{6,0},{7,1},{8,14},{9,15},{10,... | collective-permute-start | bytes 983048 | tf_op jit(solution)/shard_map/ppermute | solution.py:66
  259.6 16.6 %collective-permute-start.34 = (f32[128,1024]{1,0:T(8,128)S(1)}, f32[128,1024]{1,0:T(8,128)S(1)}, u32[]{:S(2)}, u32[]{:S(2)}) collective-permute-start(f32[128,1024]{1,0:T(8,128)S(1)} %get-tuple-element.107), channel_id=1, source_target_pairs={{0,8},{8,16},{16,24},{24,32},{32,40},{40,48},{48,56},{56,64},{64,7... | collective-permute-start | bytes 1572872 | tf_op jit(solution)/shard_map/ppermute | solution.py:435
  266.7 16.2 %collective-permute-start.35 = (f32[128,1024]{1,0:T(8,128)S(1)}, f32[128,1024]{1,0:T(8,128)S(1)}, u32[]{:S(2)}, u32[]{:S(2)}) collective-permute-start(f32[128,1024]{1,0:T(8,128)S(1)} %get-tuple-element.106), channel_id=1, source_target_pairs={{8,0},{16,8},{24,16},{32,24},{40,32},{48,40},{56,48},{64,56},{72,6... | collective-permute-start | bytes 1572872 | tf_op jit(solution)/shard_map/ppermute | solution.py:435
  269.9 16.2 %collective-permute-start.36 = (f32[128,1024]{1,0:T(8,128)S(1)}, f32[128,1024]{1,0:T(8,128)S(1)}, u32[]{:S(2)}, u32[]{:S(2)}) collective-permute-start(f32[128,1024]{1,0:T(8,128)S(1)} %get-tuple-element.58), channel_id=1, source_target_pairs={{0,1},{1,2},{2,3},{3,4},{4,5},{5,6},{6,7},{8,9},{9,10},{10,11},{11... | collective-permute-start | bytes 1572872 | tf_op jit(solution)/shard_map/ppermute | solution.py:435
  274.3 26.9 %collective-permute-start.37 = (f32[128,1024]{1,0:T(8,128)S(1)}, f32[128,1024]{1,0:T(8,128)S(1)}, u32[]{:S(2)}, u32[]{:S(2)}) collective-permute-start(f32[128,1024]{1,0:T(8,128)S(1)} %get-tuple-element.57), channel_id=1, source_target_pairs={{1,0},{2,1},{3,2},{4,3},{5,4},{6,5},{7,6},{9,8},{10,9},{11,10},{12... | collective-permute-start | bytes 1572872 | tf_op jit(solution)/shard_map/ppermute | solution.py:435
  276.2 31.1 %copy-start.14 = (f32[128,1024]{1,0:T(8,128)}, f32[128,1024]{1,0:T(8,128)S(1)}, u32[]{:S(2)}) copy-start(f32[128,1024]{1,0:T(8,128)S(1)} %collective-permute-done.34.over) | copy-start | bytes 1572868
  282.9 24.4 %copy-start.15 = (f32[128,1024]{1,0:T(8,128)}, f32[128,1024]{1,0:T(8,128)S(1)}, u32[]{:S(2)}) copy-start(f32[128,1024]{1,0:T(8,128)S(1)} %collective-permute-done.35.under) | copy-start | bytes 1572868
  301.3 5.8 %collective-permute-start.41 = (f32[1280,256]{1,0:T(8,128)S(1)}, f32[1280,256]{1,0:T(8,128)S(1)}, u32[]{:S(2)}, u32[]{:S(2)}) collective-permute-start(f32[1280,256]{1,0:T(8,128)S(1)} %pad_maximum_fusion.2), channel_id=1, source_target_pairs={{0,8},{1,9},{2,10},{3,11},{4,12},{5,13},{6,14},{7,15},{8,0},{9,1},... | collective-permute-start | bytes 3932168 | tf_op jit(solution)/shard_map/ppermute | solution.py:66
  (11 other events, 106.0 us)
Sparse Core Ops, SparseCore 0:
  85.8 68.8 all-gather.2

commit v10 on v9

--- a/solution.py
+++ b/solution.py
@@ -462,24 +462,26 @@
     x_place = x_high * 2 + x_low
 
     product, above, below = tied(product, above, below)
+    traded = lax.ppermute(product, both, trade)
+    around = (*operands[:2], above, below, left, right, *operands[2:])
+    base = plant_part(1, 7, *around, None)
+    base = plant_part(8, 7, *around, base)
+    traded, product, base = tied(traded, product, base)
     lines = lax.all_gather(product, "row", axis=0)
-    product = lax.ppermute(product, both, trade)
-    around = (*operands[:2], above, below, left, right, *operands[2:])
-    base = None
-    for start, count in ((1, 7), (8, 7), (0, 1), (lines_cols - 1, 1)):
-        base = plant_part(start, count, *around, base)
-    product, base = tied(product, base)
 
     mine_inputs = lax.dynamic_slice_in_dim(inputs, col_index * LINE, LINE, 0)
-    pair = joined(product, swap(product, X_HIGH), x_high == 1)
-    gram = gram_blocks(mine_inputs, product)
+    pair = joined(traded, swap(traded, X_HIGH), x_high == 1)
+    gram = gram_blocks(mine_inputs, traded)
     total = sum_cores(gram.reshape(10 * PANEL, PANEL), core)
-    pair, total = tied(pair, total)
+    pair, total, left, right = tied(pair, total, left, right)
 
     first, second = pair[:LINE], pair[LINE:]
     first_near, second_near = swap(first, Z[1]), swap(second, Z[3])
     total = scatter_four(total, z, Z)
-    first_near, second_near, total = tied(first_near, second_near, total)
+    around = (*operands[:2], above, below, left, right, *operands[2:])
+    for start in (0, lines_cols - 1):
+        base = plant_part(start, 1, *around, base)
+    first_near, second_near, total, base = tied(first_near, second_near, total, base)
 
     first_far = swap(jnp.stack([first, first_near]), Z[3])
     second_far = swap(jnp.stack([second, second_near]), Z[1])
@@ -494,8 +496,6 @@
     row_over, row_under = shifted(tail, "row", 1), shifted(head, "row", -1)
     col_over, col_under = shifted(lines[-1], "col", 1), shifted(lines[0], "col", -1)
     total = gather_four(total, z, Z)
-    row_over, row_under, col_over, col_under, total = tied(row_over, row_under, col_over, col_under, total)
-
     total = joined(total, swap(total, CORE), core == 1)
     factors = factored(control_weight, total.reshape(10, PANEL, PANEL))
     sides = (first, first_near, first_far, second, second_near, second_far, row_over, row_under, operands[2])

time: 538 us -> 552 us (1.026)
  the two profiles are of different devices: /device:TPU:9 before, /device:TPU:1 now
where the time goes in v10:
time: 552 us; the launch traced here: 542 us
  Pallas kernels  264 us (48%)
  waiting for transfers between devices  138 us (25%)
  starting transfers between devices  89 us (16%)
  other arithmetic  19.9 us (4%)
  local copies, waits for them, and re-layouts  16.1 us (3%)
  between operations  15.1 us (3%)
    pallas_call x1, Pallas kernels, factored(): pl.pallas_call(factor_kernel, out_shape=[jax.ShapeDtypeStruct((10, PANEL,...  176 us
    ppermute x33, waiting for transfers between devices, swap(): return lax.ppermute(x, ('row', 'col'), [(i, i ^ mask) for i in range(128)])  83.3 us
    ppermute x33, starting transfers between devices, swap(): return lax.ppermute(x, ('row', 'col'), [(i, i ^ mask) for i in range(128)])  58.8 us
    ppermute x8, waiting for transfers between devices, shifted(): lax.ppermute(x, axis, [(i, i + by) for i in range(count) if 0 <= i + by <...  54.6 us
    pallas_call x4, Pallas kernels, plant_part(): pl.pallas_call(functools.partial(plant_kernel, start, [len(blocks) for bl...  24.6 us
    pallas_call x2, Pallas kernels, product_lines(): pl.pallas_call(product_kernel, grid_spec=pltpu.PrefetchScalarGridSpec(num...  23.3 us
    pallas_call x1, Pallas kernels, downdate(): pl.pallas_call(downdate_kernel, grid=(8,), in_specs=[whole(solved[0]), wh...  22.8 us
    ppermute x8, starting transfers between devices, shifted(): lax.ppermute(x, axis, [(i, i + by) for i in range(count) if 0 <= i + by <...  19.4 us
  transfers between devices with their start and end apart: 43, of which 23 were waited for; matrix products, arithmetic and copies ran while one was open for 6% of the time, Pallas kernels for 42%

profile of v10, /device:TPU:1, one launch (start us, length us, event | category | flops | bytes accessed | tf_op | source)
XLA Modules:
  0.0 542.2 jit_solution(12918393191888065392)
XLA Ops:
  6.5 11.7 %shard_map.56 = f32[8,128,1024]{2,1,0:T(8,128)} custom-call(s32[1]{0:T(128)} %bitcast.1.me_ref, f32[1024,2048]{1,0:T(8,128)} %refs_4_.5, f32[1024,2048]{1,0:T(8,128)} %refs_4_.5, f32[1024,1024]{1,0:T(8,128)} %inputs.3), custom_call_target="tpu_custom_call" | custom-call | flops 1048576 | bytes 1048576 | tf_op jit(solution)/shard_map/pallas_call | solution.py:46
  19.6 2.7 fusion.31
  22.4 3.1 collective-permute-start.2
  27.4 11.7 %shard_map.55 = f32[8,128,1024]{2,1,0:T(8,128)} custom-call(s32[1]{0:T(128)} %bitcast.1.me_ref, f32[1024,2048]{1,0:T(8,128)} %refs_4_.5, f32[1024,2048]{1,0:T(8,128)} %refs_4_.5, f32[1024,1024]{1,0:T(8,128)} %inputs.3), custom_call_target="tpu_custom_call" | custom-call | flops 1048576 | bytes 1048576 | tf_op jit(solution)/shard_map/pallas_call | solution.py:46
  48.0 8.7 %collective-permute-done.8 = f32[2,2,32,1024]{3,2,1,0:T(8,128)S(1)} collective-permute-done((f32[2,2,32,1024]{3,2,1,0:T(8,128)S(1)}, f32[2,2,32,1024]{3,2,1,0:T(8,128)S(1)}, u32[]{:S(2)}, u32[]{:S(2)}) %collective-permute-start.8) | collective-permute-done | bytes 524320 | tf_op jit(solution)/shard_map/ppermute | solution.py:66
  56.7 2.9 collective-permute-start.9
  59.8 4.9 collective-permute-done.9
  64.8 5.8 %collective-permute-done.1 = f32[4,64,1024]{2,1,0:T(8,128)S(1)} collective-permute-done((f32[4,64,1024]{2,1,0:T(8,128)S(1)}, f32[4,64,1024]{2,1,0:T(8,128)S(1)}, u32[]{:S(2)}, u32[]{:S(2)}) %collective-permute-start.1) | collective-permute-done | bytes 1048608 | tf_op jit(solution)/shard_map/ppermute | solution.py:66
  72.3 3.8 collective-permute-done.4
  78.6 2.7 collective-permute-start.5
  84.1 2.8 collective-permute-done.7
  87.0 10.8 %collective-permute-start.13 = (f32[128,1024]{1,0:T(8,128)S(1)}, f32[128,1024]{1,0:T(8,128)S(1)}, u32[]{:S(2)}, u32[]{:S(2)}) collective-permute-start(f32[128,1024]{1,0:T(8,128)S(1)} %pad_maximum_fusion.11), channel_id=1, source_target_pairs={{0,0},{1,16},{2,32},{3,48},{4,64},{5,80},{6,96},{7,112},{8,1},{9,1... | collective-permute-start | bytes 1572872 | tf_op jit(solution)/shard_map/ppermute | solution.py:465
  100.1 9.2 %shard_map.57.refs_12_ = f32[1024,2048]{1,0:T(8,128)} custom-call(s32[2]{0:T(128)} %pad_add_fusion.place, f32[128,2048]{1,0:T(8,128)} %copy-done.2, f32[1024,2048]{1,0:T(8,128)} %refs_4_.5, f32[128,2048]{1,0:T(8,128)} %copy-done.3, f32[128,2048]{1,0:T(8,128)} %copy-done.2, f32[1024,2048]{1,0:T(8,128)} %refs_4_.5, f32[128,2048]{1,0:T(8,128)} %copy-done.3, ...), custom_call_target="tpu_custom_call" | custom-call | flops 33554432 | bytes 16777216 | tf_op jit(solution)/shard_map/pallas_call | solution.py:406
  109.3 9.2 %shard_map.58.refs_10_ = f32[1024,2048]{1,0:T(8,128)} custom-call(s32[2]{0:T(128)} %pad_add_fusion.place, f32[128,2048]{1,0:T(8,128)} %copy-done.2, f32[1024,2048]{1,0:T(8,128)} %refs_4_.5, f32[128,2048]{1,0:T(8,128)} %copy-done.3, f32[128,2048]{1,0:T(8,128)} %copy-done.2, f32[1024,2048]{1,0:T(8,128)} %refs_4_.5, ...), custom_call_target="tpu_custom_call", output_to_operand_aliasing={{}: (13, {})} | custom-call | flops 33554432 | bytes 16777216 | tf_op jit(solution)/shard_map/pallas_call | solution.py:406
  121.9 3.9 shard_map.59
  128.8 2.5 collective-permute-start.14
  132.3 2.5 collective-permute-start.16
  136.1 10.4 %collective-permute-done.14 = f32[128,1024]{1,0:T(8,128)S(1)} collective-permute-done((f32[128,1024]{1,0:T(8,128)S(1)}, f32[128,1024]{1,0:T(8,128)S(1)}, u32[]{:S(2)}, u32[]{:S(2)}) %collective-permute-start.14) | collective-permute-done | bytes 524320 | tf_op jit(solution)/shard_map/ppermute | solution.py:66
  146.9 27.6 %collective-permute-done.16.refs_0_ = f32[1280,128]{1,0:T(8,128)S(1)} collective-permute-done((f32[1280,128]{1,0:T(8,128)S(1)}, f32[1280,128]{1,0:T(8,128)S(1)}, u32[]{:S(2)}, u32[]{:S(2)}) %collective-permute-start.16) | collective-permute-done | bytes 655392 | tf_op jit(solution)/shard_map/ppermute | solution.py:435
  174.5 27.0 %collective-permute-done.17.refs_6_ = f32[1280,128]{1,0:T(8,128)S(1)} collective-permute-done((f32[1280,128]{1,0:T(8,128)S(1)}, f32[1280,128]{1,0:T(8,128)S(1)}, u32[]{:S(2)}, u32[]{:S(2)}) %collective-permute-start.17) | collective-permute-done | bytes 655392 | tf_op jit(solution)/shard_map/ppermute | solution.py:435
  202.5 16.0 %collective-permute-start.20 = (f32[320,256]{1,0:T(8,128)}, f32[320,256]{1,0:T(8,128)}, u32[]{:S(2)}, u32[]{:S(2)}) collective-permute-start(f32[320,256]{1,0:T(8,128)} %get-tuple-element.101), channel_id=1, source_target_pairs={{0,2},{1,3},{2,0},{3,1},{4,6},{5,7},{6,4},{7,5},{8,10},{9,11},{10,... | collective-permute-start | bytes 983048 | tf_op jit(solution)/shard_map/ppermute | solution.py:66
  218.5 2.4 collective-permute-start.22
  223.0 3.1 shard_map.60.refs_10_
  226.1 3.1 shard_map.61.base
  229.3 3.0 collective-permute-done.21
  232.3 4.1 collective-permute-done.22
  237.6 7.0 %collective-permute-done.18.first_near = f32[128,1024]{1,0:T(8,128)} collective-permute-done((f32[128,1024]{1,0:T(8,128)}, f32[128,1024]{1,0:T(8,128)}, u32[]{:S(2)}, u32[]{:S(2)}) %collective-permute-start.18) | collective-permute-done | bytes 524320 | tf_op jit(solution)/shard_map/ppermute | solution.py:66
  244.6 3.0 collective-permute-done.19.second_near
  247.7 4.1 collective-permute-start.26
  252.0 2.1 pad_maximum_fusion.6
  254.1 2.1 pad_maximum_fusion.5
  259.2 3.9 collective-permute-start.29
  263.1 2.7 collective-permute-done.29
  265.8 2.1 collective-permute-done.30
  268.4 3.1 collective-permute-start.32
  271.9 2.3 collective-permute-done.32
  274.2 2.1 collective-permute-done.33
  277.9 2.8 collective-permute-done.23.first_far
  280.6 2.1 collective-permute-start.35
  284.5 2.8 collective-permute-done.34
  287.3 6.3 %collective-permute-done.35 = f32[320,256]{1,0:T(8,128)S(1)} collective-permute-done((f32[320,256]{1,0:T(8,128)S(1)}, f32[320,256]{1,0:T(8,128)S(1)}, u32[]{:S(2)}, u32[]{:S(2)}) %collective-permute-start.35) | collective-permute-done | bytes 327712 | tf_op jit(solution)/shard_map/ppermute | solution.py:66
  293.6 4.6 collective-permute-done.36
  299.5 3.1 collective-permute-start.37
  305.1 2.4 collective-permute-start.38
  310.8 5.0 collective-permute-start.40
  320.2 176.4 %shard_map.62 = (f32[10,256,256]{2,1,0:T(8,128)}, f32[4,256,256]{2,1,0:T(8,128)}) custom-call(f32[1]{0:T(128)S(6)} %copy.12.weight, f32[10,256,256]{2,1,0:T(8,128)} %bitcast.173), custom_call_target="tpu_custom_call" | custom-call | flops 9663676416 | bytes 12582912 | tf_op jit(solution)/shard_map/pallas_call | solution.py:235
  497.6 13.1 %shard_map.63 = (bf16[1024,1024]{1,0:T(8,128)(2,1)}, bf16[1024,1024]{1,0:T(8,128)(2,1)}) custom-call(s32[1]{0:T(128)} %bitcast.z, f32[10,256,256]{2,1,0:T(8,128)} %get-tuple-element.47.factor, f32[4,256,256]{2,1,0:T(8,128)} %get-tuple-element.48.inverses, f32[128,1024]{1,0:T(8,128)} %get-tuple-element.109.first, ...), custom_call_target="tpu_custom_call" | custom-call | flops 9663676416 | bytes 12582912 | tf_op jit(solution)/shard_map/pallas_call | solution.py:287
  512.1 22.8 %shard_map.64 = f32[1024,2048]{1,0:T(8,128)} custom-call(bf16[1024,1024]{1,0:T(8,128)(2,1)} %get-tuple-element.51.high, bf16[1024,1024]{1,0:T(8,128)(2,1)} %get-tuple-element.52.low, f32[16,128,1024]{2,1,0:T(8,128)} %bitcast.169, f32[16,128,1024]{2,1,0:T(8,128)} %bitcast.170, f32[16,128,1024]{2,1,0:T(8,128)} %bitcast.171, f32[16,128,1024]{2,1,0:T(8,128)} %bitcast.172, ...), custom_call_target="tpu_custom_call" | custom-call | flops 12884901888 | bytes 29360128 | tf_op jit(solution)/shard_map/pallas_call | solution.py:315
  (145 shorter events, 55.7 us)
Async XLA Ops:
  6.5 92.0 %copy-start = (f32[128,128]{1,0:T(8,128)S(1)}, f32[128,128]{1,0:T(8,128)}, u32[]{:S(2)}) copy-start(f32[128,128]{1,0:T(8,128)} %param.7) | copy-start | bytes 196612
  6.5 274.1 %all-gather.3.cloned.1.call-start = ((), (), s32[]{:S(2)}) async-start(), calls=%async_computation | async-start | bytes 8912896 | tf_op jit(solution)/shard_map/all_gather | solution.py:470
  18.2 20.9 %collective-permute-start = (f32[8,128,1024]{2,1,0:T(8,128)}, f32[8,128,1024]{2,1,0:T(8,128)S(1)}, u32[]{:S(2)}, u32[]{:S(2)}) collective-permute-start(f32[8,128,1024]{2,1,0:T(8,128)} %shard_map.56), channel_id=1, source_target_pairs={{0,8},{1,9},{2,10},{3,11},{4,12},{5,13},{6,14},{7,15},{8,0},{9,1},... | collective-permute-start | bytes 12582920 | tf_op jit(solution)/shard_map/ppermute | solution.py:66
  22.4 42.4 %collective-permute-start.2 = (f32[128,2048]{1,0:T(8,128)}, f32[128,2048]{1,0:T(8,128)S(1)}, u32[]{:S(2)}, u32[]{:S(2)}) collective-permute-start(f32[128,2048]{1,0:T(8,128)} %get-tuple-element.87), channel_id=1, source_target_pairs={{0,8},{8,16},{16,24},{24,32},{32,40},{40,48},{48,56},{56,64},{64,7... | collective-permute-start | bytes 3145736 | tf_op jit(solution)/shard_map/ppermute | solution.py:435
  25.4 39.3 %collective-permute-start.3 = (f32[128,2048]{1,0:T(8,128)S(1)}, f32[128,2048]{1,0:T(8,128)S(1)}, u32[]{:S(2)}, u32[]{:S(2)}) collective-permute-start(f32[128,2048]{1,0:T(8,128)S(1)} %get-tuple-element.86), channel_id=1, source_target_pairs={{8,0},{16,8},{24,16},{32,24},{40,32},{48,40},{56,48},{64,56},{72,6... | collective-permute-start | bytes 3145736 | tf_op jit(solution)/shard_map/ppermute | solution.py:435
  42.0 28.5 %collective-permute-start.1 = (f32[4,64,1024]{2,1,0:T(8,128)S(1)}, f32[4,64,1024]{2,1,0:T(8,128)S(1)}, u32[]{:S(2)}, u32[]{:S(2)}) collective-permute-start(f32[4,64,1024]{2,1,0:T(8,128)S(1)} %pad_maximum_fusion.3), channel_id=1, source_target_pairs={{0,16},{1,17},{2,18},{3,19},{4,20},{5,21},{6,22},{7,23},{8,24},{9,... | collective-permute-start | bytes 3145736 | tf_op jit(solution)/shard_map/ppermute | solution.py:66
  44.3 12.4 %collective-permute-start.8 = (f32[2,2,32,1024]{3,2,1,0:T(8,128)S(1)}, f32[2,2,32,1024]{3,2,1,0:T(8,128)S(1)}, u32[]{:S(2)}, u32[]{:S(2)}) collective-permute-start(f32[2,2,32,1024]{3,2,1,0:T(8,128)S(1)} %pad_maximum_fusion.9), channel_id=1, source_target_pairs={{0,32},{1,33},{2,34},{3,35},{4,36},{5,37},{6,38},{7,39},{8,40},{9,... | collective-permute-start | bytes 1572872 | tf_op jit(solution)/shard_map/ppermute | solution.py:66
  46.0 13.7 %collective-permute-start.10 = (f32[2,2,32,1024]{3,2,1,0:T(8,128)S(1)}, f32[2,2,32,1024]{3,2,1,0:T(8,128)S(1)}, u32[]{:S(2)}, u32[]{:S(2)}) collective-permute-start(f32[2,2,32,1024]{3,2,1,0:T(8,128)S(1)} %pad_maximum_fusion.10), channel_id=1, source_target_pairs={{0,96},{1,97},{2,98},{3,99},{4,100},{5,101},{6,102},{7,103},{8,104... | collective-permute-start | bytes 1572872 | tf_op jit(solution)/shard_map/ppermute | solution.py:66
  56.7 7.9 %collective-permute-start.9 = (f32[2,32,1024]{2,1,0:T(8,128)S(1)}, f32[2,32,1024]{2,1,0:T(8,128)S(1)}, u32[]{:S(2)}, u32[]{:S(2)}) collective-permute-start(f32[2,32,1024]{2,1,0:T(8,128)S(1)} %fusion.4), channel_id=1, source_target_pairs={{0,96},{1,97},{2,98},{3,99},{4,100},{5,101},{6,102},{7,103},{8,104... | collective-permute-start | bytes 786440 | tf_op jit(solution)/shard_map/ppermute | solution.py:66
  59.7 12.5 %collective-permute-start.11 = (f32[2,32,1024]{2,1,0:T(8,128)S(1)}, f32[2,32,1024]{2,1,0:T(8,128)S(1)}, u32[]{:S(2)}, u32[]{:S(2)}) collective-permute-start(f32[2,32,1024]{2,1,0:T(8,128)S(1)} %fusion.1), channel_id=1, source_target_pairs={{0,32},{1,33},{2,34},{3,35},{4,36},{5,37},{6,38},{7,39},{8,40},{9,... | collective-permute-start | bytes 786440 | tf_op jit(solution)/shard_map/ppermute | solution.py:66
  70.8 5.3 collective-permute-start.4
  76.2 6.5 %collective-permute-start.6 = (f32[2,32,1024]{2,1,0:T(8,128)S(1)}, f32[2,32,1024]{2,1,0:T(8,128)S(1)}, u32[]{:S(2)}, u32[]{:S(2)}) collective-permute-start(f32[2,32,1024]{2,1,0:T(8,128)S(1)} %pad_maximum_fusion.15), channel_id=1, source_target_pairs={{0,96},{1,97},{2,98},{3,99},{4,100},{5,101},{6,102},{7,103},{8,104... | collective-permute-start | bytes 786440 | tf_op jit(solution)/shard_map/ppermute | solution.py:66
  77.5 5.4 %collective-permute-start.12 = (f32[64,1024]{1,0:T(8,128)S(1)}, f32[64,1024]{1,0:T(8,128)S(1)}, u32[]{:S(2)}, u32[]{:S(2)}) collective-permute-start(f32[64,1024]{1,0:T(8,128)S(1)} %pad_maximum_fusion.16), channel_id=1, source_target_pairs={{0,16},{1,17},{2,18},{3,19},{4,20},{5,21},{6,22},{7,23},{8,24},{9,... | collective-permute-start | bytes 786440 | tf_op jit(solution)/shard_map/ppermute | solution.py:66
  78.6 5.5 %collective-permute-start.5 = (f32[32,1024]{1,0:T(8,128)S(1)}, f32[32,1024]{1,0:T(8,128)S(1)}, u32[]{:S(2)}, u32[]{:S(2)}) collective-permute-start(f32[32,1024]{1,0:T(8,128)S(1)} %get-tuple-element.129), channel_id=1, source_target_pairs={{0,96},{1,97},{2,98},{3,99},{4,100},{5,101},{6,102},{7,103},{8,104... | collective-permute-start | bytes 393224 | tf_op jit(solution)/shard_map/ppermute | solution.py:66
  82.7 4.2 collective-permute-start.7
  87.0 22.2 %copy-start.7 = (f32[128,1024]{1,0:T(8,128)}, f32[128,1024]{1,0:T(8,128)S(1)}, u32[]{:S(2)}) copy-start(f32[128,1024]{1,0:T(8,128)S(1)} %pad_maximum_fusion.11) | copy-start | bytes 1572868
  87.0 31.4 %collective-permute-start.13 = (f32[128,1024]{1,0:T(8,128)S(1)}, f32[128,1024]{1,0:T(8,128)S(1)}, u32[]{:S(2)}, u32[]{:S(2)}) collective-permute-start(f32[128,1024]{1,0:T(8,128)S(1)} %pad_maximum_fusion.11), channel_id=1, source_target_pairs={{0,0},{1,16},{2,32},{3,48},{4,64},{5,80},{6,96},{7,112},{8,1},{9,1... | collective-permute-start | bytes 1572872 | tf_op jit(solution)/shard_map/ppermute | solution.py:465
  127.8 18.8 %collective-permute-start.15 = (f32[1280,256]{1,0:T(8,128)S(1)}, f32[1280,256]{1,0:T(8,128)S(1)}, u32[]{:S(2)}, u32[]{:S(2)}) collective-permute-start(f32[1280,256]{1,0:T(8,128)S(1)} %bitcast.175), channel_id=1, source_target_pairs={{0,8},{1,9},{2,10},{3,11},{4,12},{5,13},{6,14},{7,15},{8,0},{9,1},... | collective-permute-start | bytes 3932168 | tf_op jit(solution)/shard_map/ppermute | solution.py:66
  128.8 17.6 %collective-permute-start.14 = (f32[128,1024]{1,0:T(8,128)S(1)}, f32[128,1024]{1,0:T(8,128)S(1)}, u32[]{:S(2)}, u32[]{:S(2)}) collective-permute-start(f32[128,1024]{1,0:T(8,128)S(1)} %copy-done.6), channel_id=1, source_target_pairs={{0,1},{1,0},{2,3},{3,2},{4,5},{5,4},{6,7},{7,6},{8,9},{9,8},{10,11... | collective-permute-start | bytes 1572872 | tf_op jit(solution)/shard_map/ppermute | solution.py:66
  132.3 42.3 %collective-permute-start.16 = (f32[1280,128]{1,0:T(8,128)S(1)}, f32[1280,128]{1,0:T(8,128)S(1)}, u32[]{:S(2)}, u32[]{:S(2)}) collective-permute-start(f32[1280,128]{1,0:T(8,128)S(1)} %pad_maximum_fusion.7), channel_id=1, source_target_pairs={{0,1},{1,2},{2,3},{3,4},{4,5},{5,6},{6,7},{8,9},{9,10},{10,11},{11... | collective-permute-start | bytes 1966088 | tf_op jit(solution)/shard_map/ppermute | solution.py:435
  134.8 66.7 %collective-permute-start.17 = (f32[1280,128]{1,0:T(8,128)S(1)}, f32[1280,128]{1,0:T(8,128)S(1)}, u32[]{:S(2)}, u32[]{:S(2)}) collective-permute-start(f32[1280,128]{1,0:T(8,128)S(1)} %pad_maximum_fusion.8), channel_id=1, source_target_pairs={{1,0},{2,1},{3,2},{4,3},{5,4},{6,5},{7,6},{9,8},{10,9},{11,10},{12... | collective-permute-start | bytes 1966088 | tf_op jit(solution)/shard_map/ppermute | solution.py:435
  174.5 47.6 %copy-start.10 = (f32[1280,128]{1,0:T(8,128)}, f32[1280,128]{1,0:T(8,128)S(1)}, u32[]{:S(2)}) copy-start(f32[1280,128]{1,0:T(8,128)S(1)} %collective-permute-done.16.refs_0_) | copy-start | bytes 1966084
  202.5 26.8 %collective-permute-start.20 = (f32[320,256]{1,0:T(8,128)}, f32[320,256]{1,0:T(8,128)}, u32[]{:S(2)}, u32[]{:S(2)}) collective-permute-start(f32[320,256]{1,0:T(8,128)} %get-tuple-element.101), channel_id=1, source_target_pairs={{0,2},{1,3},{2,0},{3,1},{4,6},{5,7},{6,4},{7,5},{8,10},{9,11},{10,... | collective-permute-start | bytes 983048 | tf_op jit(solution)/shard_map/ppermute | solution.py:66
  218.5 13.8 %collective-permute-start.21 = (f32[320,256]{1,0:T(8,128)}, f32[320,256]{1,0:T(8,128)}, u32[]{:S(2)}, u32[]{:S(2)}) collective-permute-start(f32[320,256]{1,0:T(8,128)} %get-tuple-element.103), channel_id=1, source_target_pairs={{0,4},{1,5},{2,6},{3,7},{4,0},{5,1},{6,2},{7,3},{8,12},{9,13},{10,... | collective-permute-start | bytes 983048 | tf_op jit(solution)/shard_map/ppermute | solution.py:66
  218.5 17.8 %collective-permute-start.22 = (f32[320,256]{1,0:T(8,128)}, f32[320,256]{1,0:T(8,128)}, u32[]{:S(2)}, u32[]{:S(2)}) collective-permute-start(f32[320,256]{1,0:T(8,128)} %get-tuple-element.102), channel_id=1, source_target_pairs={{0,6},{1,7},{2,4},{3,5},{4,2},{5,3},{6,0},{7,1},{8,14},{9,15},{10,... | collective-permute-start | bytes 983048 | tf_op jit(solution)/shard_map/ppermute | solution.py:66
  222.2 22.4 %collective-permute-start.18 = (f32[128,1024]{1,0:T(8,128)}, f32[128,1024]{1,0:T(8,128)}, u32[]{:S(2)}, u32[]{:S(2)}) collective-permute-start(f32[128,1024]{1,0:T(8,128)} %get-tuple-element.109.first), channel_id=1, source_target_pairs={{0,2},{1,3},{2,0},{3,1},{4,6},{5,7},{6,4},{7,5},{8,10},{9,11},{10,... | collective-permute-start | bytes 1572872 | tf_op jit(solution)/shard_map/ppermute | solution.py:66
  222.4 25.2 %collective-permute-start.19 = (f32[128,1024]{1,0:T(8,128)}, f32[128,1024]{1,0:T(8,128)}, u32[]{:S(2)}, u32[]{:S(2)}) collective-permute-start(f32[128,1024]{1,0:T(8,128)} %get-tuple-element.108.second), channel_id=1, source_target_pairs={{0,6},{1,7},{2,4},{3,5},{4,2},{5,3},{6,0},{7,1},{8,14},{9,15},{10,... | collective-permute-start | bytes 1572872 | tf_op jit(solution)/shard_map/ppermute | solution.py:66
  247.6 10.5 %collective-permute-start.25 = (f32[80,256]{1,0:T(8,128)S(1)}, f32[80,256]{1,0:T(8,128)S(1)}, u32[]{:S(2)}, u32[]{:S(2)}) collective-permute-start(f32[80,256]{1,0:T(8,128)S(1)} %get-tuple-element.124), channel_id=1, source_target_pairs={{0,16},{1,17},{2,18},{3,19},{4,20},{5,21},{6,22},{7,23},{8,24},{9,... | collective-permute-start | bytes 245768 | tf_op jit(solution)/shard_map/ppermute | solution.py:66
  247.7 10.5 %collective-permute-start.26 = (f32[80,256]{1,0:T(8,128)S(1)}, f32[80,256]{1,0:T(8,128)S(1)}, u32[]{:S(2)}, u32[]{:S(2)}) collective-permute-start(f32[80,256]{1,0:T(8,128)S(1)} %get-tuple-element.126), channel_id=1, source_target_pairs={{0,1},{1,0},{2,3},{3,2},{4,5},{5,4},{6,7},{7,6},{8,9},{9,8},{10,11... | collective-permute-start | bytes 245768 | tf_op jit(solution)/shard_map/ppermute | solution.py:66
  251.8 6.3 %collective-permute-start.27 = (f32[80,256]{1,0:T(8,128)S(1)}, f32[80,256]{1,0:T(8,128)S(1)}, u32[]{:S(2)}, u32[]{:S(2)}) collective-permute-start(f32[80,256]{1,0:T(8,128)S(1)} %get-tuple-element.125), channel_id=1, source_target_pairs={{0,17},{1,16},{2,19},{3,18},{4,21},{5,20},{6,23},{7,22},{8,25},{9,... | collective-permute-start | bytes 245768 | tf_op jit(solution)/shard_map/ppermute | solution.py:66
  254.1 23.8 %collective-permute-start.24 = (f32[2,128,1024]{2,1,0:T(8,128)}, f32[2,128,1024]{2,1,0:T(8,128)}, u32[]{:S(2)}, u32[]{:S(2)}) collective-permute-start(f32[2,128,1024]{2,1,0:T(8,128)} %pad_maximum_fusion.6), channel_id=1, source_target_pairs={{0,2},{1,3},{2,0},{3,1},{4,6},{5,7},{6,4},{7,5},{8,10},{9,11},{10,... | collective-permute-start | bytes 3145736 | tf_op jit(solution)/shard_map/ppermute | solution.py:66
  256.2 24.4 %collective-permute-start.23 = (f32[2,128,1024]{2,1,0:T(8,128)}, f32[2,128,1024]{2,1,0:T(8,128)S(1)}, u32[]{:S(2)}, u32[]{:S(2)}) collective-permute-start(f32[2,128,1024]{2,1,0:T(8,128)} %pad_maximum_fusion.5), channel_id=1, source_target_pairs={{0,6},{1,7},{2,4},{3,5},{4,2},{5,3},{6,0},{7,1},{8,14},{9,15},{10,... | collective-permute-start | bytes 3145736 | tf_op jit(solution)/shard_map/ppermute | solution.py:66
  259.1 4.0 collective-permute-start.28
  259.2 6.6 %collective-permute-start.29 = (f32[80,256]{1,0:T(8,128)S(1)}, f32[80,256]{1,0:T(8,128)S(1)}, u32[]{:S(2)}, u32[]{:S(2)}) collective-permute-start(f32[80,256]{1,0:T(8,128)S(1)} %add_add_fusion.2), channel_id=1, source_target_pairs={{0,64},{1,65},{2,66},{3,67},{4,68},{5,69},{6,70},{7,71},{8,72},{9,... | collective-permute-start | bytes 245768 | tf_op jit(solution)/shard_map/ppermute | solution.py:66
  263.1 4.8 collective-permute-start.30
  267.9 3.9 collective-permute-start.31
  268.4 5.8 %collective-permute-start.32 = (f32[80,256]{1,0:T(8,128)S(1)}, f32[80,256]{1,0:T(8,128)S(1)}, u32[]{:S(2)}, u32[]{:S(2)}) collective-permute-start(f32[80,256]{1,0:T(8,128)S(1)} %add_add_fusion.1), channel_id=1, source_target_pairs={{0,1},{1,0},{2,3},{3,2},{4,5},{5,4},{6,7},{7,6},{8,9},{9,8},{10,11... | collective-permute-start | bytes 245768 | tf_op jit(solution)/shard_map/ppermute | solution.py:66
  271.5 4.8 collective-permute-start.33
  280.6 22.6 %copy-start.9 = (f32[2,128,1024]{2,1,0:T(8,128)}, f32[2,128,1024]{2,1,0:T(8,128)S(1)}, u32[]{:S(2)}) copy-start(f32[2,128,1024]{2,1,0:T(8,128)S(1)} %collective-permute-done.23.first_far) | copy-start | bytes 3145732
  280.6 6.6 %collective-permute-start.34 = (f32[320,256]{1,0:T(8,128)S(1)}, f32[320,256]{1,0:T(8,128)S(1)}, u32[]{:S(2)}, u32[]{:S(2)}) collective-permute-start(f32[320,256]{1,0:T(8,128)S(1)} %pad_maximum_fusion.13), channel_id=1, source_target_pairs={{0,2},{1,3},{2,0},{3,1},{4,6},{5,7},{6,4},{7,5},{8,10},{9,11},{10,... | collective-permute-start | bytes 983048 | tf_op jit(solution)/shard_map/ppermute | solution.py:66
  280.6 12.9 %collective-permute-start.35 = (f32[320,256]{1,0:T(8,128)S(1)}, f32[320,256]{1,0:T(8,128)S(1)}, u32[]{:S(2)}, u32[]{:S(2)}) collective-permute-start(f32[320,256]{1,0:T(8,128)S(1)} %pad_maximum_fusion.13), channel_id=1, source_target_pairs={{0,4},{1,5},{2,6},{3,7},{4,0},{5,1},{6,2},{7,3},{8,12},{9,13},{10,... | collective-permute-start | bytes 983048 | tf_op jit(solution)/shard_map/ppermute | solution.py:66
  282.7 15.5 %collective-permute-start.36 = (f32[320,256]{1,0:T(8,128)S(1)}, f32[320,256]{1,0:T(8,128)S(1)}, u32[]{:S(2)}, u32[]{:S(2)}) collective-permute-start(f32[320,256]{1,0:T(8,128)S(1)} %pad_maximum_fusion.13), channel_id=1, source_target_pairs={{0,6},{1,7},{2,4},{3,5},{4,2},{5,3},{6,0},{7,1},{8,14},{9,15},{10,... | collective-permute-start | bytes 983048 | tf_op jit(solution)/shard_map/ppermute | solution.py:66
  299.5 17.5 %collective-permute-start.37 = (f32[1280,256]{1,0:T(8,128)}, f32[1280,256]{1,0:T(8,128)}, u32[]{:S(2)}, u32[]{:S(2)}) collective-permute-start(f32[1280,256]{1,0:T(8,128)} %pad_maximum_fusion.2), channel_id=1, source_target_pairs={{0,8},{1,9},{2,10},{3,11},{4,12},{5,13},{6,14},{7,15},{8,0},{9,1},... | collective-permute-start | bytes 3932168 | tf_op jit(solution)/shard_map/ppermute | solution.py:66
  305.1 191.6 %collective-permute-start.38 = (f32[128,1024]{1,0:T(8,128)S(1)}, f32[128,1024]{1,0:T(8,128)S(1)}, u32[]{:S(2)}, u32[]{:S(2)}) collective-permute-start(f32[128,1024]{1,0:T(8,128)S(1)} %get-tuple-element.105), channel_id=1, source_target_pairs={{0,8},{8,16},{16,24},{24,32},{32,40},{40,48},{48,56},{56,64},{64,7... | collective-permute-start | bytes 1572872 | tf_op jit(solution)/shard_map/ppermute | solution.py:435
  307.5 189.2 %collective-permute-start.39 = (f32[128,1024]{1,0:T(8,128)S(1)}, f32[128,1024]{1,0:T(8,128)S(1)}, u32[]{:S(2)}, u32[]{:S(2)}) collective-permute-start(f32[128,1024]{1,0:T(8,128)S(1)} %get-tuple-element.104), channel_id=1, source_target_pairs={{8,0},{16,8},{24,16},{32,24},{40,32},{48,40},{56,48},{64,56},{72,6... | collective-permute-start | bytes 1572872 | tf_op jit(solution)/shard_map/ppermute | solution.py:435
  310.8 200.0 %collective-permute-start.40 = (f32[128,1024]{1,0:T(8,128)S(1)}, f32[128,1024]{1,0:T(8,128)S(1)}, u32[]{:S(2)}, u32[]{:S(2)}) collective-permute-start(f32[128,1024]{1,0:T(8,128)S(1)} %get-tuple-element.56), channel_id=1, source_target_pairs={{0,1},{1,2},{2,3},{3,4},{4,5},{5,6},{6,7},{8,9},{9,10},{10,11},{11... | collective-permute-start | bytes 1572872 | tf_op jit(solution)/shard_map/ppermute | solution.py:435
  315.8 195.0 %collective-permute-start.41 = (f32[128,1024]{1,0:T(8,128)S(1)}, f32[128,1024]{1,0:T(8,128)S(1)}, u32[]{:S(2)}, u32[]{:S(2)}) collective-permute-start(f32[128,1024]{1,0:T(8,128)S(1)} %get-tuple-element.55), channel_id=1, source_target_pairs={{1,0},{2,1},{3,2},{4,3},{5,4},{6,5},{7,6},{9,8},{10,9},{11,10},{12... | collective-permute-start | bytes 1572872 | tf_op jit(solution)/shard_map/ppermute | solution.py:435
  512.1 22.8 %copy-start.1 = (f32[128,128]{1,0:T(8,128)S(1)}, f32[128,128]{1,0:T(8,128)}, u32[]{:S(2)}) copy-start(f32[128,128]{1,0:T(8,128)} %param.7) | copy-start | bytes 196612
  (12 other events, 77.4 us)
Sparse Core Ops, SparseCore 0:
  118.6 83.4 all-gather.2

commit v11 on v9

--- a/solution.py
+++ b/solution.py
@@ -462,17 +462,17 @@
     x_place = x_high * 2 + x_low
 
     product, above, below = tied(product, above, below)
-    lines = lax.all_gather(product, "row", axis=0)
-    product = lax.ppermute(product, both, trade)
+    traded = lax.ppermute(product, both, trade)
     around = (*operands[:2], above, below, left, right, *operands[2:])
     base = None
     for start, count in ((1, 7), (8, 7), (0, 1), (lines_cols - 1, 1)):
         base = plant_part(start, count, *around, base)
-    product, base = tied(product, base)
+    traded, product, base = tied(traded, product, base)
+    lines = lax.all_gather(product, "row", axis=0)
 
     mine_inputs = lax.dynamic_slice_in_dim(inputs, col_index * LINE, LINE, 0)
-    pair = joined(product, swap(product, X_HIGH), x_high == 1)
-    gram = gram_blocks(mine_inputs, product)
+    pair = joined(traded, swap(traded, X_HIGH), x_high == 1)
+    gram = gram_blocks(mine_inputs, traded)
     total = sum_cores(gram.reshape(10 * PANEL, PANEL), core)
     pair, total = tied(pair, total)
 
@@ -494,8 +494,6 @@
     row_over, row_under = shifted(tail, "row", 1), shifted(head, "row", -1)
     col_over, col_under = shifted(lines[-1], "col", 1), shifted(lines[0], "col", -1)
     total = gather_four(total, z, Z)
-    row_over, row_under, col_over, col_under, total = tied(row_over, row_under, col_over, col_under, total)
-
     total = joined(total, swap(total, CORE), core == 1)
     factors = factored(control_weight, total.reshape(10, PANEL, PANEL))
     sides = (first, first_near, first_far, second, second_near, second_far, row_over, row_under, operands[2])

time: 538 us -> 523 us (0.972)
  the two profiles are of different devices: /device:TPU:9 before, /device:TPU:120 now
where the time goes in v11:
time: 523 us; the launch traced here: 515 us
  Pallas kernels  264 us (50%)
  waiting for transfers between devices  116 us (22%)
  starting transfers between devices  82.9 us (16%)
  other arithmetic  21.3 us (4%)
  local copies, waits for them, and re-layouts  15.1 us (3%)
  between operations  15.1 us (3%)
    pallas_call x1, Pallas kernels, factored(): pl.pallas_call(factor_kernel, out_shape=[jax.ShapeDtypeStruct((10, PANEL,...  176 us
    ppermute x33, waiting for transfers between devices, swap(): return lax.ppermute(x, ('row', 'col'), [(i, i ^ mask) for i in range(128)])  116 us
    ppermute x33, starting transfers between devices, swap(): return lax.ppermute(x, ('row', 'col'), [(i, i ^ mask) for i in range(128)])  51.4 us
    ppermute x8, starting transfers between devices, shifted(): lax.ppermute(x, axis, [(i, i + by) for i in range(count) if 0 <= i + by <...  29.4 us
    pallas_call x4, Pallas kernels, plant_part(): pl.pallas_call(functools.partial(plant_kernel, start, [len(blocks) for bl...  24.6 us
    pallas_call x2, Pallas kernels, product_lines(): pl.pallas_call(product_kernel, grid_spec=pltpu.PrefetchScalarGridSpec(num...  23.3 us
    pallas_call x1, Pallas kernels, downdate(): pl.pallas_call(downdate_kernel, grid=(8,), in_specs=[whole(solved[0]), wh...  22.8 us
    pallas_call x1, Pallas kernels, solve(): pl.pallas_call(solve_kernel, out_shape=[jax.ShapeDtypeStruct((size, 4 * P...  13.1 us
  transfers between devices with their start and end apart: 43, of which 20 were waited for; matrix products, arithmetic and copies ran while one was open for 6% of the time, Pallas kernels for 45%

profile of v11, /device:TPU:120, one launch (start us, length us, event | category | flops | bytes accessed | tf_op | source)
XLA Modules:
  0.0 514.7 jit_solution(9211198544872179485)
XLA Ops:
  6.5 11.6 %shard_map.56 = f32[8,128,1024]{2,1,0:T(8,128)} custom-call(s32[1]{0:T(128)} %bitcast.1.me_ref, f32[1024,2048]{1,0:T(8,128)} %refs_4_.5, f32[1024,2048]{1,0:T(8,128)} %refs_4_.5, f32[1024,1024]{1,0:T(8,128)} %inputs.3), custom_call_target="tpu_custom_call" | custom-call | flops 1048576 | bytes 1048576 | tf_op jit(solution)/shard_map/pallas_call | solution.py:46
  18.2 2.7 fusion.31
  20.9 2.4 collective-permute-start.2
  23.4 4.0 collective-permute-start.3
  27.4 11.7 %shard_map.55 = f32[8,128,1024]{2,1,0:T(8,128)} custom-call(s32[1]{0:T(128)} %bitcast.1.me_ref, f32[1024,2048]{1,0:T(8,128)} %refs_4_.5, f32[1024,2048]{1,0:T(8,128)} %refs_4_.5, f32[1024,1024]{1,0:T(8,128)} %inputs.3), custom_call_target="tpu_custom_call" | custom-call | flops 1048576 | bytes 1048576 | tf_op jit(solution)/shard_map/pallas_call | solution.py:46
  44.8 11.6 %collective-permute-done.8 = f32[2,2,32,1024]{3,2,1,0:T(8,128)S(1)} collective-permute-done((f32[2,2,32,1024]{3,2,1,0:T(8,128)S(1)}, f32[2,2,32,1024]{3,2,1,0:T(8,128)S(1)}, u32[]{:S(2)}, u32[]{:S(2)}) %collective-permute-start.8) | collective-permute-done | bytes 524320 | tf_op jit(solution)/shard_map/ppermute | solution.py:66
  56.6 5.0 collective-permute-start.1
  62.0 3.0 collective-permute-done.9
  65.1 4.0 collective-permute-done.11
  69.5 16.2 %collective-permute-done.1 = f32[4,64,1024]{2,1,0:T(8,128)S(1)} collective-permute-done((f32[4,64,1024]{2,1,0:T(8,128)S(1)}, f32[4,64,1024]{2,1,0:T(8,128)S(1)}, u32[]{:S(2)}, u32[]{:S(2)}) %collective-permute-start.1) | collective-permute-done | bytes 1048608 | tf_op jit(solution)/shard_map/ppermute | solution.py:66
  86.3 6.1 %collective-permute-done.4 = f32[2,32,1024]{2,1,0:T(8,128)S(1)} collective-permute-done((f32[2,32,1024]{2,1,0:T(8,128)S(1)}, f32[2,32,1024]{2,1,0:T(8,128)S(1)}, u32[]{:S(2)}, u32[]{:S(2)}) %collective-permute-start.4) | collective-permute-done | bytes 262176 | tf_op jit(solution)/shard_map/ppermute | solution.py:66
  93.6 4.9 collective-permute-start.15
  98.6 3.3 collective-permute-start.14
  101.9 2.3 collective-permute-start.5
  104.4 3.8 collective-permute-done.5
  113.7 9.2 %shard_map.57.refs_12_ = f32[1024,2048]{1,0:T(8,128)} custom-call(s32[2]{0:T(128)} %pad_add_fusion.place, f32[128,2048]{1,0:T(8,128)} %copy-done.2, f32[1024,2048]{1,0:T(8,128)} %refs_4_.5, f32[128,2048]{1,0:T(8,128)} %copy-done.3, f32[128,2048]{1,0:T(8,128)} %copy-done.2, f32[1024,2048]{1,0:T(8,128)} %refs_4_.5, f32[128,2048]{1,0:T(8,128)} %copy-done.3, ...), custom_call_target="tpu_custom_call" | custom-call | flops 33554432 | bytes 16777216 | tf_op jit(solution)/shard_map/pallas_call | solution.py:406
  122.9 9.2 %shard_map.58.refs_10_ = f32[1024,2048]{1,0:T(8,128)} custom-call(s32[2]{0:T(128)} %pad_add_fusion.place, f32[128,2048]{1,0:T(8,128)} %copy-done.2, f32[1024,2048]{1,0:T(8,128)} %refs_4_.5, f32[128,2048]{1,0:T(8,128)} %copy-done.3, f32[128,2048]{1,0:T(8,128)} %copy-done.2, f32[1024,2048]{1,0:T(8,128)} %refs_4_.5, ...), custom_call_target="tpu_custom_call", output_to_operand_aliasing={{}: (13, {})} | custom-call | flops 33554432 | bytes 16777216 | tf_op jit(solution)/shard_map/pallas_call | solution.py:406
  132.1 3.1 shard_map.59.refs_10_
  135.2 3.1 shard_map.60.base
  140.5 3.9 shard_map.61
  144.4 3.1 slice_select_fusion.1
  147.5 4.2 collective-permute-start.17
  151.7 2.7 collective-permute-start.16
  154.5 21.9 %collective-permute-done.16 = f32[128,1024]{1,0:T(8,128)S(1)} collective-permute-done((f32[128,1024]{1,0:T(8,128)S(1)}, f32[128,1024]{1,0:T(8,128)S(1)}, u32[]{:S(2)}, u32[]{:S(2)}) %collective-permute-start.16) | collective-permute-done | bytes 524320 | tf_op jit(solution)/shard_map/ppermute | solution.py:66
  180.2 8.8 %collective-permute-start.21 = (f32[320,256]{1,0:T(8,128)}, f32[320,256]{1,0:T(8,128)}, u32[]{:S(2)}, u32[]{:S(2)}) collective-permute-start(f32[320,256]{1,0:T(8,128)} %get-tuple-element.97), channel_id=1, source_target_pairs={{0,4},{1,5},{2,6},{3,7},{4,0},{5,1},{6,2},{7,3},{8,12},{9,13},{10,... | collective-permute-start | bytes 983048 | tf_op jit(solution)/shard_map/ppermute | solution.py:66
  191.7 2.6 collective-permute-start.19
  194.4 10.6 %collective-permute-done.21 = f32[320,256]{1,0:T(8,128)} collective-permute-done((f32[320,256]{1,0:T(8,128)}, f32[320,256]{1,0:T(8,128)}, u32[]{:S(2)}, u32[]{:S(2)}) %collective-permute-start.21) | collective-permute-done | bytes 327712 | tf_op jit(solution)/shard_map/ppermute | solution.py:66
  205.0 3.3 collective-permute-done.22
  209.5 8.5 %collective-permute-done.19.second_near = f32[128,1024]{1,0:T(8,128)} collective-permute-done((f32[128,1024]{1,0:T(8,128)}, f32[128,1024]{1,0:T(8,128)}, u32[]{:S(2)}, u32[]{:S(2)}) %collective-permute-start.19) | collective-permute-done | bytes 524320 | tf_op jit(solution)/shard_map/ppermute | solution.py:66
  218.1 3.4 collective-permute-start.26
  222.8 2.1 pad_maximum_fusion.6
  224.9 2.1 pad_maximum_fusion.5
  228.9 2.5 collective-permute-start.29
  231.4 2.2 collective-permute-start.30
  234.9 2.1 collective-permute-done.30
  245.5 2.6 collective-permute-done.24.second_far
  248.1 3.2 collective-permute-done.23.first_far
  251.9 2.5 collective-permute-start.35
  256.0 5.3 %collective-permute-done.34 = f32[320,256]{1,0:T(8,128)S(1)} collective-permute-done((f32[320,256]{1,0:T(8,128)S(1)}, f32[320,256]{1,0:T(8,128)S(1)}, u32[]{:S(2)}, u32[]{:S(2)}) %collective-permute-start.34) | collective-permute-done | bytes 327712 | tf_op jit(solution)/shard_map/ppermute | solution.py:66
  261.4 5.4 %collective-permute-done.35 = f32[320,256]{1,0:T(8,128)S(1)} collective-permute-done((f32[320,256]{1,0:T(8,128)S(1)}, f32[320,256]{1,0:T(8,128)S(1)}, u32[]{:S(2)}, u32[]{:S(2)}) %collective-permute-start.35) | collective-permute-done | bytes 327712 | tf_op jit(solution)/shard_map/ppermute | solution.py:66
  266.8 2.6 collective-permute-done.36
  273.5 2.4 collective-permute-start.38
  275.9 4.1 collective-permute-start.39
  281.3 4.0 collective-permute-start.40
  285.3 4.2 collective-permute-start.41
  292.7 176.4 %shard_map.62 = (f32[10,256,256]{2,1,0:T(8,128)}, f32[4,256,256]{2,1,0:T(8,128)}) custom-call(f32[1]{0:T(128)S(6)} %copy.12.weight, f32[10,256,256]{2,1,0:T(8,128)} %bitcast.173), custom_call_target="tpu_custom_call" | custom-call | flops 9663676416 | bytes 12582912 | tf_op jit(solution)/shard_map/pallas_call | solution.py:235
  470.1 13.1 %shard_map.63 = (bf16[1024,1024]{1,0:T(8,128)(2,1)}, bf16[1024,1024]{1,0:T(8,128)(2,1)}) custom-call(s32[1]{0:T(128)} %bitcast.z, f32[10,256,256]{2,1,0:T(8,128)} %get-tuple-element.41.factor, f32[4,256,256]{2,1,0:T(8,128)} %get-tuple-element.42.inverses, f32[128,1024]{1,0:T(8,128)} %get-tuple-element.103.first, ...), custom_call_target="tpu_custom_call" | custom-call | flops 9663676416 | bytes 12582912 | tf_op jit(solution)/shard_map/pallas_call | solution.py:287
  484.6 22.8 %shard_map.64 = f32[1024,2048]{1,0:T(8,128)} custom-call(bf16[1024,1024]{1,0:T(8,128)(2,1)} %get-tuple-element.45.high, bf16[1024,1024]{1,0:T(8,128)(2,1)} %get-tuple-element.46.low, f32[16,128,1024]{2,1,0:T(8,128)} %bitcast.169, f32[16,128,1024]{2,1,0:T(8,128)} %bitcast.170, f32[16,128,1024]{2,1,0:T(8,128)} %bitcast.171, f32[16,128,1024]{2,1,0:T(8,128)} %bitcast.172, ...), custom_call_target="tpu_custom_call" | custom-call | flops 12884901888 | bytes 29360128 | tf_op jit(solution)/shard_map/pallas_call | solution.py:315
  (143 shorter events, 49.5 us)
Async XLA Ops:
  6.5 105.6 %copy-start = (f32[128,128]{1,0:T(8,128)S(1)}, f32[128,128]{1,0:T(8,128)}, u32[]{:S(2)}) copy-start(f32[128,128]{1,0:T(8,128)} %param.7) | copy-start | bytes 196612
  6.5 244.8 %all-gather.3.cloned.1.call-start = ((), (), s32[]{:S(2)}) async-start(), calls=%async_computation | async-start | bytes 8912896 | tf_op jit(solution)/shard_map/all_gather | solution.py:471
  18.2 22.2 %collective-permute-start = (f32[8,128,1024]{2,1,0:T(8,128)}, f32[8,128,1024]{2,1,0:T(8,128)S(1)}, u32[]{:S(2)}, u32[]{:S(2)}) collective-permute-start(f32[8,128,1024]{2,1,0:T(8,128)} %shard_map.56), channel_id=1, source_target_pairs={{0,8},{1,9},{2,10},{3,11},{4,12},{5,13},{6,14},{7,15},{8,0},{9,1},... | collective-permute-start | bytes 12582920 | tf_op jit(solution)/shard_map/ppermute | solution.py:66
  20.9 48.6 %collective-permute-start.2 = (f32[128,2048]{1,0:T(8,128)}, f32[128,2048]{1,0:T(8,128)S(1)}, u32[]{:S(2)}, u32[]{:S(2)}) collective-permute-start(f32[128,2048]{1,0:T(8,128)} %get-tuple-element.81), channel_id=1, source_target_pairs={{0,8},{8,16},{16,24},{24,32},{32,40},{40,48},{48,56},{56,64},{64,7... | collective-permute-start | bytes 3145736 | tf_op jit(solution)/shard_map/ppermute | solution.py:435
  23.4 46.2 %collective-permute-start.3 = (f32[128,2048]{1,0:T(8,128)S(1)}, f32[128,2048]{1,0:T(8,128)S(1)}, u32[]{:S(2)}, u32[]{:S(2)}) collective-permute-start(f32[128,2048]{1,0:T(8,128)S(1)} %get-tuple-element.80), channel_id=1, source_target_pairs={{8,0},{16,8},{24,16},{32,24},{40,32},{48,40},{56,48},{64,56},{72,6... | collective-permute-start | bytes 3145736 | tf_op jit(solution)/shard_map/ppermute | solution.py:435
  42.1 14.3 %collective-permute-start.8 = (f32[2,2,32,1024]{3,2,1,0:T(8,128)S(1)}, f32[2,2,32,1024]{3,2,1,0:T(8,128)S(1)}, u32[]{:S(2)}, u32[]{:S(2)}) collective-permute-start(f32[2,2,32,1024]{3,2,1,0:T(8,128)S(1)} %pad_maximum_fusion.9), channel_id=1, source_target_pairs={{0,32},{1,33},{2,34},{3,35},{4,36},{5,37},{6,38},{7,39},{8,40},{9,... | collective-permute-start | bytes 1572872 | tf_op jit(solution)/shard_map/ppermute | solution.py:66
  43.3 18.4 %collective-permute-start.10 = (f32[2,2,32,1024]{3,2,1,0:T(8,128)S(1)}, f32[2,2,32,1024]{3,2,1,0:T(8,128)S(1)}, u32[]{:S(2)}, u32[]{:S(2)}) collective-permute-start(f32[2,2,32,1024]{3,2,1,0:T(8,128)S(1)} %pad_maximum_fusion.10), channel_id=1, source_target_pairs={{0,96},{1,97},{2,98},{3,99},{4,100},{5,101},{6,102},{7,103},{8,104... | collective-permute-start | bytes 1572872 | tf_op jit(solution)/shard_map/ppermute | solution.py:66
  56.4 8.6 %collective-permute-start.9 = (f32[2,32,1024]{2,1,0:T(8,128)S(1)}, f32[2,32,1024]{2,1,0:T(8,128)S(1)}, u32[]{:S(2)}, u32[]{:S(2)}) collective-permute-start(f32[2,32,1024]{2,1,0:T(8,128)S(1)} %fusion.4), channel_id=1, source_target_pairs={{0,96},{1,97},{2,98},{3,99},{4,100},{5,101},{6,102},{7,103},{8,104... | collective-permute-start | bytes 786440 | tf_op jit(solution)/shard_map/ppermute | solution.py:66
  56.6 29.1 %collective-permute-start.1 = (f32[4,64,1024]{2,1,0:T(8,128)S(1)}, f32[4,64,1024]{2,1,0:T(8,128)S(1)}, u32[]{:S(2)}, u32[]{:S(2)}) collective-permute-start(f32[4,64,1024]{2,1,0:T(8,128)S(1)} %pad_maximum_fusion.3), channel_id=1, source_target_pairs={{0,16},{1,17},{2,18},{3,19},{4,20},{5,21},{6,22},{7,23},{8,24},{9,... | collective-permute-start | bytes 3145736 | tf_op jit(solution)/shard_map/ppermute | solution.py:66
  61.7 7.3 %collective-permute-start.11 = (f32[2,32,1024]{2,1,0:T(8,128)S(1)}, f32[2,32,1024]{2,1,0:T(8,128)S(1)}, u32[]{:S(2)}, u32[]{:S(2)}) collective-permute-start(f32[2,32,1024]{2,1,0:T(8,128)S(1)} %fusion.1), channel_id=1, source_target_pairs={{0,32},{1,33},{2,34},{3,35},{4,36},{5,37},{6,38},{7,39},{8,40},{9,... | collective-permute-start | bytes 786440 | tf_op jit(solution)/shard_map/ppermute | solution.py:66
  69.1 35.2 %collective-permute-start.12 = (f32[64,1024]{1,0:T(8,128)S(1)}, f32[64,1024]{1,0:T(8,128)S(1)}, u32[]{:S(2)}, u32[]{:S(2)}) collective-permute-start(f32[64,1024]{1,0:T(8,128)S(1)} %pad_maximum_fusion.16), channel_id=1, source_target_pairs={{0,16},{1,17},{2,18},{3,19},{4,20},{5,21},{6,22},{7,23},{8,24},{9,... | collective-permute-start | bytes 786440 | tf_op jit(solution)/shard_map/ppermute | solution.py:66
  69.5 16.8 %copy-start.3 = (f32[128,2048]{1,0:T(8,128)}, f32[128,2048]{1,0:T(8,128)S(1)}, u32[]{:S(2)}) copy-start(f32[128,2048]{1,0:T(8,128)S(1)} %collective-permute-done.3.refs_2_.refs_5_.refs_8_.refs_3_.refs_6_) | copy-start | bytes 3145732
  86.0 6.5 %collective-permute-start.4 = (f32[2,32,1024]{2,1,0:T(8,128)S(1)}, f32[2,32,1024]{2,1,0:T(8,128)S(1)}, u32[]{:S(2)}, u32[]{:S(2)}) collective-permute-start(f32[2,32,1024]{2,1,0:T(8,128)S(1)} %pad_maximum_fusion.14), channel_id=1, source_target_pairs={{0,32},{1,33},{2,34},{3,35},{4,36},{5,37},{6,38},{7,39},{8,40},{9,... | collective-permute-start | bytes 786440 | tf_op jit(solution)/shard_map/ppermute | solution.py:66
  92.5 11.8 %collective-permute-start.6 = (f32[2,32,1024]{2,1,0:T(8,128)S(1)}, f32[2,32,1024]{2,1,0:T(8,128)S(1)}, u32[]{:S(2)}, u32[]{:S(2)}) collective-permute-start(f32[2,32,1024]{2,1,0:T(8,128)S(1)} %pad_maximum_fusion.15), channel_id=1, source_target_pairs={{0,96},{1,97},{2,98},{3,99},{4,100},{5,101},{6,102},{7,103},{8,104... | collective-permute-start | bytes 786440 | tf_op jit(solution)/shard_map/ppermute | solution.py:66
  93.6 38.5 %collective-permute-start.15 = (f32[1280,128]{1,0:T(8,128)S(1)}, f32[1280,128]{1,0:T(8,128)}, u32[]{:S(2)}, u32[]{:S(2)}) collective-permute-start(f32[1280,128]{1,0:T(8,128)S(1)} %pad_maximum_fusion.8), channel_id=1, source_target_pairs={{0,1},{1,2},{2,3},{3,4},{4,5},{5,6},{6,7},{8,9},{9,10},{10,11},{11... | collective-permute-start | bytes 1966088 | tf_op jit(solution)/shard_map/ppermute | solution.py:435
  98.6 36.6 %collective-permute-start.14 = (f32[1280,128]{1,0:T(8,128)S(1)}, f32[1280,128]{1,0:T(8,128)}, u32[]{:S(2)}, u32[]{:S(2)}) collective-permute-start(f32[1280,128]{1,0:T(8,128)S(1)} %pad_maximum_fusion.7), channel_id=1, source_target_pairs={{1,0},{2,1},{3,2},{4,3},{5,4},{6,5},{7,6},{9,8},{10,9},{11,10},{12... | collective-permute-start | bytes 1966088 | tf_op jit(solution)/shard_map/ppermute | solution.py:435
  101.9 6.3 %collective-permute-start.5 = (f32[32,1024]{1,0:T(8,128)S(1)}, f32[32,1024]{1,0:T(8,128)S(1)}, u32[]{:S(2)}, u32[]{:S(2)}) collective-permute-start(f32[32,1024]{1,0:T(8,128)S(1)} %get-tuple-element.123), channel_id=1, source_target_pairs={{0,96},{1,97},{2,98},{3,99},{4,100},{5,101},{6,102},{7,103},{8,104... | collective-permute-start | bytes 393224 | tf_op jit(solution)/shard_map/ppermute | solution.py:66
  104.3 5.0 collective-permute-start.7
  109.4 28.9 %collective-permute-start.13 = (f32[128,1024]{1,0:T(8,128)S(1)}, f32[128,1024]{1,0:T(8,128)S(1)}, u32[]{:S(2)}, u32[]{:S(2)}) collective-permute-start(f32[128,1024]{1,0:T(8,128)S(1)} %pad_maximum_fusion.11), channel_id=1, source_target_pairs={{0,0},{1,16},{2,32},{3,48},{4,64},{5,80},{6,96},{7,112},{8,1},{9,1... | collective-permute-start | bytes 1572872 | tf_op jit(solution)/shard_map/ppermute | solution.py:465
  147.5 29.1 %collective-permute-start.17 = (f32[1280,256]{1,0:T(8,128)S(1)}, f32[1280,256]{1,0:T(8,128)}, u32[]{:S(2)}, u32[]{:S(2)}) collective-permute-start(f32[1280,256]{1,0:T(8,128)S(1)} %bitcast.175), channel_id=1, source_target_pairs={{0,8},{1,9},{2,10},{3,11},{4,12},{5,13},{6,14},{7,15},{8,0},{9,1},... | collective-permute-start | bytes 3932168 | tf_op jit(solution)/shard_map/ppermute | solution.py:66
  151.7 24.6 %collective-permute-start.16 = (f32[128,1024]{1,0:T(8,128)S(1)}, f32[128,1024]{1,0:T(8,128)S(1)}, u32[]{:S(2)}, u32[]{:S(2)}) collective-permute-start(f32[128,1024]{1,0:T(8,128)S(1)} %copy-done.7), channel_id=1, source_target_pairs={{0,1},{1,0},{2,3},{3,2},{4,5},{5,4},{6,7},{7,6},{8,9},{9,8},{10,11... | collective-permute-start | bytes 1572872 | tf_op jit(solution)/shard_map/ppermute | solution.py:66
  180.2 14.1 %collective-permute-start.20 = (f32[320,256]{1,0:T(8,128)}, f32[320,256]{1,0:T(8,128)}, u32[]{:S(2)}, u32[]{:S(2)}) collective-permute-start(f32[320,256]{1,0:T(8,128)} %get-tuple-element.95), channel_id=1, source_target_pairs={{0,2},{1,3},{2,0},{3,1},{4,6},{5,7},{6,4},{7,5},{8,10},{9,11},{10,... | collective-permute-start | bytes 983048 | tf_op jit(solution)/shard_map/ppermute | solution.py:66
  180.2 24.7 %collective-permute-start.21 = (f32[320,256]{1,0:T(8,128)}, f32[320,256]{1,0:T(8,128)}, u32[]{:S(2)}, u32[]{:S(2)}) collective-permute-start(f32[320,256]{1,0:T(8,128)} %get-tuple-element.97), channel_id=1, source_target_pairs={{0,4},{1,5},{2,6},{3,7},{4,0},{5,1},{6,2},{7,3},{8,12},{9,13},{10,... | collective-permute-start | bytes 983048 | tf_op jit(solution)/shard_map/ppermute | solution.py:66
  189.1 19.2 %collective-permute-start.22 = (f32[320,256]{1,0:T(8,128)}, f32[320,256]{1,0:T(8,128)}, u32[]{:S(2)}, u32[]{:S(2)}) collective-permute-start(f32[320,256]{1,0:T(8,128)} %get-tuple-element.96), channel_id=1, source_target_pairs={{0,6},{1,7},{2,4},{3,5},{4,2},{5,3},{6,0},{7,1},{8,14},{9,15},{10,... | collective-permute-start | bytes 983048 | tf_op jit(solution)/shard_map/ppermute | solution.py:66
  190.9 18.6 %collective-permute-start.18 = (f32[128,1024]{1,0:T(8,128)}, f32[128,1024]{1,0:T(8,128)}, u32[]{:S(2)}, u32[]{:S(2)}) collective-permute-start(f32[128,1024]{1,0:T(8,128)} %get-tuple-element.103.first), channel_id=1, source_target_pairs={{0,2},{1,3},{2,0},{3,1},{4,6},{5,7},{6,4},{7,5},{8,10},{9,11},{10,... | collective-permute-start | bytes 1572872 | tf_op jit(solution)/shard_map/ppermute | solution.py:66
  191.7 26.3 %collective-permute-start.19 = (f32[128,1024]{1,0:T(8,128)}, f32[128,1024]{1,0:T(8,128)}, u32[]{:S(2)}, u32[]{:S(2)}) collective-permute-start(f32[128,1024]{1,0:T(8,128)} %get-tuple-element.102.second), channel_id=1, source_target_pairs={{0,6},{1,7},{2,4},{3,5},{4,2},{5,3},{6,0},{7,1},{8,14},{9,15},{10,... | collective-permute-start | bytes 1572872 | tf_op jit(solution)/shard_map/ppermute | solution.py:66
  209.5 17.5 %copy-start.9 = (f32[320,256]{1,0:T(8,128)}, f32[320,256]{1,0:T(8,128)S(1)}, u32[]{:S(2)}) copy-start(f32[320,256]{1,0:T(8,128)S(1)} %add_add_fusion) | copy-start | bytes 983044
  218.0 9.8 %collective-permute-start.25 = (f32[80,256]{1,0:T(8,128)S(1)}, f32[80,256]{1,0:T(8,128)S(1)}, u32[]{:S(2)}, u32[]{:S(2)}) collective-permute-start(f32[80,256]{1,0:T(8,128)S(1)} %get-tuple-element.118), channel_id=1, source_target_pairs={{0,16},{1,17},{2,18},{3,19},{4,20},{5,21},{6,22},{7,23},{8,24},{9,... | collective-permute-start | bytes 245768 | tf_op jit(solution)/shard_map/ppermute | solution.py:66
  218.1 9.7 %collective-permute-start.26 = (f32[80,256]{1,0:T(8,128)S(1)}, f32[80,256]{1,0:T(8,128)S(1)}, u32[]{:S(2)}, u32[]{:S(2)}) collective-permute-start(f32[80,256]{1,0:T(8,128)S(1)} %get-tuple-element.120), channel_id=1, source_target_pairs={{0,1},{1,0},{2,3},{3,2},{4,5},{5,4},{6,7},{7,6},{8,9},{9,8},{10,11... | collective-permute-start | bytes 245768 | tf_op jit(solution)/shard_map/ppermute | solution.py:66
  221.6 6.3 %collective-permute-start.27 = (f32[80,256]{1,0:T(8,128)S(1)}, f32[80,256]{1,0:T(8,128)S(1)}, u32[]{:S(2)}, u32[]{:S(2)}) collective-permute-start(f32[80,256]{1,0:T(8,128)S(1)} %get-tuple-element.119), channel_id=1, source_target_pairs={{0,17},{1,16},{2,19},{3,18},{4,21},{5,20},{6,23},{7,22},{8,25},{9,... | collective-permute-start | bytes 245768 | tf_op jit(solution)/shard_map/ppermute | solution.py:66
  224.9 23.2 %collective-permute-start.24 = (f32[2,128,1024]{2,1,0:T(8,128)}, f32[2,128,1024]{2,1,0:T(8,128)}, u32[]{:S(2)}, u32[]{:S(2)}) collective-permute-start(f32[2,128,1024]{2,1,0:T(8,128)} %pad_maximum_fusion.6), channel_id=1, source_target_pairs={{0,2},{1,3},{2,0},{3,1},{4,6},{5,7},{6,4},{7,5},{8,10},{9,11},{10,... | collective-permute-start | bytes 3145736 | tf_op jit(solution)/shard_map/ppermute | solution.py:66
  227.0 24.3 %collective-permute-start.23 = (f32[2,128,1024]{2,1,0:T(8,128)}, f32[2,128,1024]{2,1,0:T(8,128)S(1)}, u32[]{:S(2)}, u32[]{:S(2)}) collective-permute-start(f32[2,128,1024]{2,1,0:T(8,128)} %pad_maximum_fusion.5), channel_id=1, source_target_pairs={{0,6},{1,7},{2,4},{3,5},{4,2},{5,3},{6,0},{7,1},{8,14},{9,15},{10,... | collective-permute-start | bytes 3145736 | tf_op jit(solution)/shard_map/ppermute | solution.py:66
  228.8 4.8 collective-permute-start.28
  228.9 6.0 %collective-permute-start.29 = (f32[80,256]{1,0:T(8,128)S(1)}, f32[80,256]{1,0:T(8,128)S(1)}, u32[]{:S(2)}, u32[]{:S(2)}) collective-permute-start(f32[80,256]{1,0:T(8,128)S(1)} %add_add_fusion.2), channel_id=1, source_target_pairs={{0,64},{1,65},{2,66},{3,67},{4,68},{5,69},{6,70},{7,71},{8,72},{9,... | collective-permute-start | bytes 245768 | tf_op jit(solution)/shard_map/ppermute | solution.py:66
  231.4 5.7 %collective-permute-start.30 = (f32[80,256]{1,0:T(8,128)S(1)}, f32[80,256]{1,0:T(8,128)S(1)}, u32[]{:S(2)}, u32[]{:S(2)}) collective-permute-start(f32[80,256]{1,0:T(8,128)S(1)} %add_add_fusion.2), channel_id=1, source_target_pairs={{0,96},{1,97},{2,98},{3,99},{4,100},{5,101},{6,102},{7,103},{8,104... | collective-permute-start | bytes 245768 | tf_op jit(solution)/shard_map/ppermute | solution.py:66
  237.0 4.8 collective-permute-start.31
  237.8 5.9 %collective-permute-start.32 = (f32[80,256]{1,0:T(8,128)S(1)}, f32[80,256]{1,0:T(8,128)S(1)}, u32[]{:S(2)}, u32[]{:S(2)}) collective-permute-start(f32[80,256]{1,0:T(8,128)S(1)} %add_add_fusion.1), channel_id=1, source_target_pairs={{0,1},{1,0},{2,3},{3,2},{4,5},{5,4},{6,7},{7,6},{8,9},{9,8},{10,11... | collective-permute-start | bytes 245768 | tf_op jit(solution)/shard_map/ppermute | solution.py:66
  239.8 5.7 %collective-permute-start.33 = (f32[80,256]{1,0:T(8,128)S(1)}, f32[80,256]{1,0:T(8,128)S(1)}, u32[]{:S(2)}, u32[]{:S(2)}) collective-permute-start(f32[80,256]{1,0:T(8,128)S(1)} %add_add_fusion.1), channel_id=1, source_target_pairs={{0,17},{1,16},{2,19},{3,18},{4,21},{5,20},{6,23},{7,22},{8,25},{9,... | collective-permute-start | bytes 245768 | tf_op jit(solution)/shard_map/ppermute | solution.py:66
  251.3 20.2 %copy-start.10 = (f32[2,128,1024]{2,1,0:T(8,128)}, f32[2,128,1024]{2,1,0:T(8,128)S(1)}, u32[]{:S(2)}) copy-start(f32[2,128,1024]{2,1,0:T(8,128)S(1)} %collective-permute-done.23.first_far) | copy-start | bytes 3145732
  251.3 10.0 %collective-permute-start.34 = (f32[320,256]{1,0:T(8,128)S(1)}, f32[320,256]{1,0:T(8,128)S(1)}, u32[]{:S(2)}, u32[]{:S(2)}) collective-permute-start(f32[320,256]{1,0:T(8,128)S(1)} %pad_maximum_fusion.13), channel_id=1, source_target_pairs={{0,2},{1,3},{2,0},{3,1},{4,6},{5,7},{6,4},{7,5},{8,10},{9,11},{10,... | collective-permute-start | bytes 983048 | tf_op jit(solution)/shard_map/ppermute | solution.py:66
  251.9 14.9 %collective-permute-start.35 = (f32[320,256]{1,0:T(8,128)S(1)}, f32[320,256]{1,0:T(8,128)S(1)}, u32[]{:S(2)}, u32[]{:S(2)}) collective-permute-start(f32[320,256]{1,0:T(8,128)S(1)} %pad_maximum_fusion.13), channel_id=1, source_target_pairs={{0,4},{1,5},{2,6},{3,7},{4,0},{5,1},{6,2},{7,3},{8,12},{9,13},{10,... | collective-permute-start | bytes 983048 | tf_op jit(solution)/shard_map/ppermute | solution.py:66
  254.4 14.9 %collective-permute-start.36 = (f32[320,256]{1,0:T(8,128)S(1)}, f32[320,256]{1,0:T(8,128)S(1)}, u32[]{:S(2)}, u32[]{:S(2)}) collective-permute-start(f32[320,256]{1,0:T(8,128)S(1)} %pad_maximum_fusion.13), channel_id=1, source_target_pairs={{0,6},{1,7},{2,4},{3,5},{4,2},{5,3},{6,0},{7,1},{8,14},{9,15},{10,... | collective-permute-start | bytes 983048 | tf_op jit(solution)/shard_map/ppermute | solution.py:66
  270.7 18.9 %collective-permute-start.37 = (f32[1280,256]{1,0:T(8,128)}, f32[1280,256]{1,0:T(8,128)}, u32[]{:S(2)}, u32[]{:S(2)}) collective-permute-start(f32[1280,256]{1,0:T(8,128)} %pad_maximum_fusion.2), channel_id=1, source_target_pairs={{0,8},{1,9},{2,10},{3,11},{4,12},{5,13},{6,14},{7,15},{8,0},{9,1},... | collective-permute-start | bytes 3932168 | tf_op jit(solution)/shard_map/ppermute | solution.py:66
  273.5 195.7 %collective-permute-start.38 = (f32[128,1024]{1,0:T(8,128)S(1)}, f32[128,1024]{1,0:T(8,128)S(1)}, u32[]{:S(2)}, u32[]{:S(2)}) collective-permute-start(f32[128,1024]{1,0:T(8,128)S(1)} %get-tuple-element.99), channel_id=1, source_target_pairs={{0,8},{8,16},{16,24},{24,32},{32,40},{40,48},{48,56},{56,64},{64,7... | collective-permute-start | bytes 1572872 | tf_op jit(solution)/shard_map/ppermute | solution.py:435
  275.9 193.3 %collective-permute-start.39 = (f32[128,1024]{1,0:T(8,128)S(1)}, f32[128,1024]{1,0:T(8,128)S(1)}, u32[]{:S(2)}, u32[]{:S(2)}) collective-permute-start(f32[128,1024]{1,0:T(8,128)S(1)} %get-tuple-element.98), channel_id=1, source_target_pairs={{8,0},{16,8},{24,16},{32,24},{40,32},{48,40},{56,48},{64,56},{72,6... | collective-permute-start | bytes 1572872 | tf_op jit(solution)/shard_map/ppermute | solution.py:435
  281.3 202.0 %collective-permute-start.40 = (f32[128,1024]{1,0:T(8,128)S(1)}, f32[128,1024]{1,0:T(8,128)S(1)}, u32[]{:S(2)}, u32[]{:S(2)}) collective-permute-start(f32[128,1024]{1,0:T(8,128)S(1)} %get-tuple-element.50), channel_id=1, source_target_pairs={{0,1},{1,2},{2,3},{3,4},{4,5},{5,6},{6,7},{8,9},{9,10},{10,11},{11... | collective-permute-start | bytes 1572872 | tf_op jit(solution)/shard_map/ppermute | solution.py:435
  285.3 198.0 %collective-permute-start.41 = (f32[128,1024]{1,0:T(8,128)S(1)}, f32[128,1024]{1,0:T(8,128)S(1)}, u32[]{:S(2)}, u32[]{:S(2)}) collective-permute-start(f32[128,1024]{1,0:T(8,128)S(1)} %get-tuple-element.49), channel_id=1, source_target_pairs={{1,0},{2,1},{3,2},{4,3},{5,4},{6,5},{7,6},{9,8},{10,9},{11,10},{12... | collective-permute-start | bytes 1572872 | tf_op jit(solution)/shard_map/ppermute | solution.py:435
  484.6 22.8 %copy-start.1 = (f32[128,128]{1,0:T(8,128)S(1)}, f32[128,128]{1,0:T(8,128)}, u32[]{:S(2)}) copy-start(f32[128,128]{1,0:T(8,128)} %param.7) | copy-start | bytes 196612
  (11 other events, 61.2 us)
Sparse Core Ops, SparseCore 0:
  138.5 70.6 all-gather.2
